TPU v7x, 32 devices: a whole 2x2x4 slice. The times are simulated.
32 devices in a mesh: seq: 16 (over z, y, core), chan: 2 (over x).
Axes of the slice: x: 2, y: 2, z: 4, core: 2. Of those that a mesh axis runs over, the one named last changes fastest.
Arguments:
- block_in: bfloat16 [10240, 1152], P(('seq', 'chan')), may hold values from -6 to 6
- routes: int32 [10240, 1], P(('seq', 'chan')), may hold values from 0 to 7; in each aligned block of 320 rows (0 to 319, 320 to 639, ...) at most 51 rows name the same one
- doc_lengths: int32 [4], replicated, may hold values from 64 to 10048, as said below
- norm_gain: float32 [1152], replicated, may hold values from 0.5 to 1.5
- in_weight: bfloat16 [2, 1152, 2304], P(None, None, 'chan'), may hold values from -0.1875 to 0.1875
- conv_weight: float32 [4, 2304], P(None, 'chan'), may hold values from -3 to 3
- conv_bias: float32 [2304], P('chan'), may hold values from -1.5 to 1.5
- xproj_weight: bfloat16 [2304, 104], P('chan'), may hold values from -0.125 to 0.125
- dt_weight: float32 [72, 2304], P(None, 'chan'), may hold values from -0.75 to 0.75
- dt_bias: float32 [2304], P('chan'), may hold values from -5 to 0.5
- a_log: float32 [2304, 16], P('chan'), may hold values from -5.8 to -2.3
- skip_gain: float32 [2304], P('chan'), may hold values from 0.5 to 1.5
- out_weight: bfloat16 [2304, 1152], P('chan'), may hold values from -0.125 to 0.125
- moe_gain: float32 [1152], replicated, may hold values from 0.5 to 1.5
- router_weight: float32 [1152, 8], replicated, may hold values from -0.125 to 0.125
- up_weight: bfloat16 [8, 1152, 3072], P('chan', 'seq'), may hold values from -0.1875 to 0.1875
- down_weight: bfloat16 [8, 1152, 3072], P('chan', 'seq'), may hold values from -0.109375 to 0.109375
- out_grad: bfloat16 [10240, 1152], P(('seq', 'chan')), may hold values from -6 to 6
Outputs:
- block_out: bfloat16 [10240, 1152], P(('seq', 'chan'))
- in_grad: float32 [10240, 1152], P(('seq', 'chan'))
- norm_gain_grad: float32 [1152], replicated
- in_weight_grad: float32 [2, 1152, 2304], P(None, None, 'chan')
- conv_weight_grad: float32 [4, 2304], P(None, 'chan')
- conv_bias_grad: float32 [2304], P('chan')
- xproj_grad: float32 [2304, 104], P('chan')
- dt_weight_grad: float32 [72, 2304], P(None, 'chan')
- dt_bias_grad: float32 [2304], P('chan')
- a_log_grad: float32 [2304, 16], P('chan')
- skip_grad: float32 [2304], P('chan')
- out_weight_grad: float32 [2304, 1152], P('chan')
- moe_gain_grad: float32 [1152], replicated
- router_grad: float32 [1152, 8], replicated
- up_grad: float32 [8, 1152, 3072], P('chan', 'seq')
- down_grad: float32 [8, 1152, 3072], P('chan', 'seq')
Inputs may be any that keep to these rules, and one draw needn't show every extreme that they name: `doc_lengths`: document lengths in time order; each is a multiple of 64, they add up to 10240, and one of them is longer than 9600. `routes`: among the 320 tokens of one device (aligned blocks) no expert is chosen more than 51 times, and in every draw some expert is chosen exactly 51 times in some block.
All inputs are finite; a program needn't handle non-finite values.
Results may differ from a plain program's by a relative error of at most 0.017.
Values may be sent and summed in bfloat16 or wider, within the bound.
A program may use at most 768 MiB of HBM per device.

v0:
```python
from functools import partial

import jax
import jax.numpy as jnp
from jax import lax
from jax.sharding import PartitionSpec as P

STATE = 16
CONV = 4
DT_RANK = 72
EXPERTS = 8
ALIGN = 64
SINK = 8


EPS = 1e-05
HIGH = lax.Precision.HIGHEST


def passed_along(value, axis, steps):
    count = lax.axis_size(axis)
    leading, last = (max(0, -steps), min(count, count - steps))
    return lax.ppermute(value, axis, [(source, source + steps) for source in range(leading, last)])


def entering(value, axis, combine, identity):
    count, index = (lax.axis_size(axis), lax.axis_index(axis))
    everything = jax.tree.map(lambda part: lax.all_gather(part, axis), value)
    start = jax.tree.map(
        lambda part, zero: jnp.broadcast_to(jnp.asarray(zero, part.dtype), part.shape),
        value,
        identity,
    )

    def turn(k, before):
        reached = k < index
        new = combine(before, jax.tree.map(lambda part: part[k], everything))
        return jax.tree.map(lambda a, b: jnp.where(reached, a, b), new, before)

    return lax.fori_loop(0, count, turn, start)


def carried_in(value, axis, join, neutral):
    count = lax.axis_size(axis)
    place = lax.axis_index(axis)
    ahead = count - 1 - place
    gathered = jax.tree.map(
        lambda a, kind: lax.all_gather(a.astype(kind), axis), value, (jnp.bfloat16, jnp.bfloat16)
    )
    state = jax.tree.map(lambda a, e: jnp.zeros_like(a) + jnp.asarray(e, a.dtype), value, neutral)

    def one(turn, state):
        source = count - 1 - turn
        return join(
            state,
            jax.tree.map(
                lambda a, own: lax.dynamic_index_in_dim(a, source, 0, False).astype(own.dtype),
                gathered,
                value,
            ),
        )

    return lax.fori_loop(0, ahead, one, state)


def affine_join(earlier, later):
    return (earlier[0] * later[0], later[0] * earlier[1] + later[1])


def norm_apply(values, gain):
    return values * lax.rsqrt(jnp.mean(values * values, -1, keepdims=True) + EPS) * gain


def silu_grad(values):
    sigma = jax.nn.sigmoid(values)
    return sigma * (1.0 + values * (1.0 - sigma))


def gelu_grad(values, upstream):
    return jax.vjp(partial(jax.nn.gelu, approximate=True), values)[1](upstream)[0]


def chan_rows(values):
    return lax.all_gather(values, "chan", axis=0, tiled=True)


def chan_sums(term_fn, rows):
    return lax.psum_scatter(
        term_fn(jnp.int32(0), rows * lax.axis_size("chan")), "chan", scatter_dimension=0, tiled=True
    )


def proj_total(values):
    return lax.psum(values, "chan")


def edge_rows(values, offset):
    return passed_along(values, "seq", offset)


def column_total(values):
    return lax.psum(values, ("seq", "chan"))


def route_rows(values):
    return lax.all_to_all(values, "chan", split_axis=0, concat_axis=0, tiled=True)


def lower_ones(length):
    row_ids = lax.broadcasted_iota(jnp.int32, (length, length), 0)
    col_ids = lax.broadcasted_iota(jnp.int32, (length, length), 1)
    return (col_ids <= row_ids).astype(jnp.float32)


def running_sum(lower, values):
    return jnp.einsum("ij,bjk->bik", lower, values, precision=HIGH)


def decay_terms(step_size, rates):
    blocks, length, channels = step_size.shape
    return (-step_size[..., None] * rates).reshape(blocks, length, -1)


def drive_terms(step_size, mixed, b_in):
    blocks, length, channels = step_size.shape
    return ((step_size * mixed)[..., None] * b_in[:, :, None, :]).reshape(blocks, length, -1)


def emitted_terms(grad_out, c_out):
    blocks, length, channels = grad_out.shape
    return (grad_out[..., None] * c_out[:, :, None, :]).reshape(blocks, length, -1)


def block_maps(parts, rates, lower):
    step_size, mixed, b_in = parts
    summed = running_sum(lower, decay_terms(step_size, rates))
    total = jnp.sum(jnp.exp(summed[:, -1:] - summed) * drive_terms(step_size, mixed, b_in), 1)
    return (jnp.exp(summed[:, -1]), total)


def block_states(step_size, mixed, b_in, entry, rates, lower):
    log_decay = decay_terms(step_size, rates)
    summed = running_sum(lower, log_decay)
    inside = running_sum(lower, jnp.exp(-summed) * drive_terms(step_size, mixed, b_in))
    states = jnp.exp(summed) * (inside + entry[:, None, :])
    return (log_decay, summed, states)


def block_outputs(parts, rates, lower):
    step_size, mixed, b_in, c_out, entry = parts
    blocks, length, channels = step_size.shape
    log_decay, summed, states = block_states(step_size, mixed, b_in, entry, rates, lower)
    return jnp.sum(states.reshape(blocks, length, channels, -1) * c_out[:, :, None, :], 3)


def block_back_maps(parts, rates, lower):
    step_size, c_out, grad_out = parts
    summed = running_sum(lower, decay_terms(step_size, rates))
    return jnp.sum(jnp.exp(summed) * emitted_terms(grad_out, c_out), 1)


def block_grads(parts, rates, lower):
    step_size, mixed, b_in, c_out, entry, grad_out, exit_grad = parts
    blocks, length, channels = step_size.shape
    upper = lower.T
    log_decay, summed, states = block_states(step_size, mixed, b_in, entry, rates, lower)
    later = running_sum(upper, jnp.exp(summed) * emitted_terms(grad_out, c_out))
    grads = jnp.exp(-summed) * later + jnp.exp(summed[:, -1:] - summed) * exit_grad[:, None, :]
    before = jnp.concatenate([entry[:, None, :], states[:, :-1]], 1)
    log_grad = (grads * jnp.exp(log_decay) * before).reshape(blocks, length, channels, -1)
    grads = grads.reshape(blocks, length, channels, -1)
    states = states.reshape(blocks, length, channels, -1)
    weighted = jnp.sum(grads * b_in[:, :, None, :], 3)
    step_grad = jnp.sum(log_grad * -rates, 3) + weighted * mixed
    mixed_grad = weighted * step_size
    b_grad = jnp.sum(grads * (step_size * mixed)[..., None], 2)
    c_grad = jnp.sum(grad_out[..., None] * states, 2)
    rate_grad = jnp.sum(log_grad * -step_size[..., None], (0, 1))
    return (step_grad, mixed_grad, b_grad, c_grad, rate_grad)


def expert_forward(rows_in, first_weight, second_weight):
    pre = jnp.einsum("secd,edf->secf", rows_in, first_weight, preferred_element_type=jnp.float32)
    act_b = jax.nn.gelu(pre, approximate=True).astype(jnp.bfloat16)
    expert_out = jnp.einsum(
        "secf,edf->secd", act_b, second_weight, preferred_element_type=jnp.float32
    )
    return (pre, act_b, expert_out)


def expert_backward(rows_in, grad_rows, pre, act_b, first_weight, second_weight):
    grad_act = jnp.einsum(
        "secd,edf->secf", grad_rows, second_weight, preferred_element_type=jnp.float32
    )
    grad_pre = gelu_grad(pre, grad_act).astype(jnp.bfloat16)
    grad_second = jnp.einsum("secd,secf->edf", grad_rows, act_b, preferred_element_type=jnp.float32)
    grad_first = jnp.einsum("secd,secf->edf", rows_in, grad_pre, preferred_element_type=jnp.float32)
    grad_in = jnp.einsum(
        "secf,edf->secd", grad_pre, first_weight, preferred_element_type=jnp.float32
    )
    return (grad_first, grad_second, grad_in)


def on_device(
    block_in,
    routes,
    doc_lengths,
    norm_gain,
    in_weight,
    conv_weight,
    conv_bias,
    xproj_weight,
    dt_weight,
    dt_bias,
    a_log,
    skip_gain,
    out_weight,
    moe_gain,
    router_weight,
    up_weight,
    down_weight,
    out_grad,
):
    tok_dev, model_width = block_in.shape
    chan_count = lax.axis_size("chan")
    seq_place = lax.axis_index("seq")
    residual = block_in.astype(jnp.float32)
    normed, norm_back = jax.vjp(norm_apply, residual, norm_gain)
    gathered = chan_rows(normed.astype(jnp.bfloat16))
    tok_seq = gathered.shape[0]
    projected = jnp.einsum("td,kde->kte", gathered, in_weight, preferred_element_type=jnp.float32)
    inner_b = projected[0].astype(jnp.bfloat16)
    gate_z = projected[1]
    channels = inner_b.shape[1]
    position = seq_place * tok_seq + lax.broadcasted_iota(jnp.int32, (tok_seq,), 0)
    starts = jnp.cumsum(doc_lengths) - doc_lengths
    doc_first = jnp.max(jnp.where(starts[None, :] <= position[:, None], starts[None, :], 0), axis=1)
    reach = CONV - 1
    previous = edge_rows(inner_b[tok_seq - reach :].astype(jnp.float32), 1)
    padded = jnp.concatenate([previous, inner_b.astype(jnp.float32)], 0)
    delays = reach - lax.broadcasted_iota(jnp.int32, (CONV, 1), 0)
    tap_masks = (position[None, :] - delays >= doc_first[None, :]).astype(jnp.float32)

    def convolve(padded_rows, weights, bias):
        total = bias[None, :] + jnp.zeros((tok_seq, channels), jnp.float32)
        for offset in range(CONV):
            total = (
                total
                + weights[offset][None, :]
                * padded_rows[offset : offset + tok_seq]
                * tap_masks[offset][:, None]
            )
        return total

    conv_pre, conv_back = jax.vjp(convolve, padded, conv_weight, conv_bias)
    mixed_b = jax.nn.silu(conv_pre).astype(jnp.bfloat16)
    mixed = mixed_b.astype(jnp.float32)
    proj_all = proj_total(jnp.dot(mixed_b, xproj_weight, preferred_element_type=jnp.float32))
    low_rank = proj_all[:, :DT_RANK]
    b_in = proj_all[:, DT_RANK : DT_RANK + STATE]
    c_out = proj_all[:, DT_RANK + STATE :]
    step_pre = jnp.dot(low_rank, dt_weight, precision=HIGH) + dt_bias
    step_size = jax.nn.softplus(step_pre)
    decay_rates = jnp.exp(a_log)
    length = ALIGN
    blocks = tok_seq // length
    groups = tok_seq // tok_seq
    per_group = tok_seq // length
    span = channels * STATE
    block_first = seq_place * tok_seq + length * lax.broadcasted_iota(jnp.int32, (blocks,), 0)
    keep = 1.0 - jnp.any(block_first[:, None] == starts[None, :], axis=1).astype(jnp.float32)
    lower = lower_ones(length)

    def grouped(values):
        return values.reshape((groups, per_group, length) + values.shape[1:])

    def by_group(values):
        return values.reshape(groups, per_group, span)

    ones_span = jnp.ones((1, span), jnp.float32)
    zeros_span = jnp.zeros((1, span), jnp.float32)
    block_end_mult, block_end_add = lax.map(
        lambda parts: block_maps(parts, decay_rates, lower),
        (grouped(step_size), grouped(mixed), grouped(b_in)),
    )
    block_mult = block_end_mult.reshape(blocks, span) * keep[:, None]
    block_add = block_end_add.reshape(blocks, span)
    incl_mult, incl_add = lax.associative_scan(affine_join, (block_mult, block_add))
    carried = entering(
        (incl_mult[-1], incl_add[-1]), "seq", affine_join, (ones_span[0], zeros_span[0])
    )
    device_state = carried[1]
    prior_mult = jnp.concatenate([ones_span, incl_mult[:-1]], 0)
    prior_add = jnp.concatenate([zeros_span, incl_add[:-1]], 0)
    entry = keep[:, None] * (prior_mult * device_state[None, :] + prior_add)
    scanned = lax.map(
        lambda parts: block_outputs(parts, decay_rates, lower),
        (grouped(step_size), grouped(mixed), grouped(b_in), grouped(c_out), by_group(entry)),
    )
    scan_out = scanned.reshape(tok_seq, channels) + skip_gain * mixed
    gate_act = jax.nn.silu(gate_z)
    gated_b = (scan_out * gate_act).astype(jnp.bfloat16)
    mixer_rows = chan_sums(
        lambda first, count: jnp.dot(gated_b, out_weight, preferred_element_type=jnp.float32),
        tok_dev,
    )
    hidden_one = residual + mixer_rows
    moe_in, moe_back = jax.vjp(norm_apply, hidden_one, moe_gain)
    logits = jnp.dot(moe_in, router_weight, precision=HIGH)
    route_col = routes[:, 0]
    expert_ids = lax.broadcasted_iota(jnp.int32, (1, EXPERTS), 1)
    chosen_int = (route_col[:, None] == expert_ids).astype(jnp.int32)
    chosen = chosen_int.astype(jnp.float32)
    probs = jnp.exp(logits)
    saved = []
    for sweep in range(SINK):
        column = column_total(jnp.sum(probs, 0))
        scaled = probs / column[None, :]
        row_total = jnp.sum(scaled, 1, keepdims=True)
        saved.append((column, scaled, row_total))
        probs = scaled / row_total
    gate = EXPERTS * jnp.sum(probs * chosen, 1)
    capacity = tok_dev * 5 // (4 * EXPERTS) + 1
    counts = jnp.cumsum(chosen_int, 0)
    rank = jnp.sum((counts - 1) * chosen_int, 1)
    slot = route_col * capacity + rank
    slot_ids = lax.broadcasted_iota(jnp.int32, (1, EXPERTS * capacity), 1)
    placer = (slot[:, None] == slot_ids).astype(jnp.bfloat16)
    moe_b = moe_in.astype(jnp.bfloat16)
    packed = jnp.einsum("ts,td->sd", placer, moe_b, preferred_element_type=jnp.float32).astype(
        jnp.bfloat16
    )
    arrived = route_rows(packed.reshape(EXPERTS, capacity, model_width)).reshape(
        chan_count, EXPERTS // chan_count, capacity, model_width
    )
    full_up, full_down = (
        lax.all_gather(up_weight, "seq", axis=1, tiled=True),
        lax.all_gather(down_weight, "seq", axis=1, tiled=True),
    )
    pre, act_b, expert_out = expert_forward(arrived, full_up, full_down)
    returned = route_rows(expert_out.astype(jnp.bfloat16).reshape(EXPERTS, capacity, model_width))
    expert_tok = jnp.einsum(
        "ts,sd->td",
        placer,
        returned.reshape(EXPERTS * capacity, model_width),
        preferred_element_type=jnp.float32,
    )
    block_out = (hidden_one + gate[:, None] * expert_tok).astype(jnp.bfloat16)
    grad_two = out_grad.astype(jnp.float32)
    grad_expert_tok = (gate[:, None] * grad_two).astype(jnp.bfloat16)
    grad_gate = jnp.sum(expert_tok * grad_two, 1)
    grad_packed = jnp.einsum(
        "ts,td->sd", placer, grad_expert_tok, preferred_element_type=jnp.float32
    ).astype(jnp.bfloat16)
    grad_arrived = route_rows(grad_packed.reshape(EXPERTS, capacity, model_width)).reshape(
        chan_count, EXPERTS // chan_count, capacity, model_width
    )
    back_up, back_down = (
        lax.all_gather(up_weight, "seq", axis=1, tiled=True),
        lax.all_gather(down_weight, "seq", axis=1, tiled=True),
    )
    grad_first, grad_second, grad_rows_in = expert_backward(
        arrived, grad_arrived, pre, act_b, back_up, back_down
    )
    up_grad, down_grad = (
        lax.psum_scatter(
            grad_first.astype(jnp.bfloat16), "seq", scatter_dimension=1, tiled=True
        ).astype(jnp.float32),
        lax.psum_scatter(
            grad_second.astype(jnp.bfloat16), "seq", scatter_dimension=1, tiled=True
        ).astype(jnp.float32),
    )
    grad_back = route_rows(
        grad_rows_in.astype(jnp.bfloat16).reshape(EXPERTS, capacity, model_width)
    )
    grad_moe_in = jnp.einsum(
        "ts,sd->td",
        placer,
        grad_back.reshape(EXPERTS * capacity, model_width),
        preferred_element_type=jnp.float32,
    )
    grad_probs = EXPERTS * grad_gate[:, None] * chosen
    for sweep in reversed(range(SINK)):
        column, scaled, row_total = saved[sweep]
        row_normed = scaled / row_total
        grad_scaled = (grad_probs - jnp.sum(grad_probs * row_normed, 1, keepdims=True)) / row_total
        along = column_total(jnp.sum(grad_scaled * scaled, 0))
        grad_probs = (grad_scaled - along[None, :]) / column[None, :]
    grad_logits = grad_probs * jnp.exp(logits)
    router_grad = jnp.einsum("td,te->de", moe_in, grad_logits, precision=HIGH)
    grad_moe_in = grad_moe_in + jnp.einsum("te,de->td", grad_logits, router_weight, precision=HIGH)
    grad_hidden, moe_gain_grad = moe_back(grad_moe_in)
    grad_hidden = grad_hidden + grad_two
    grad_mix = chan_rows(grad_hidden.astype(jnp.bfloat16))
    grad_gated = jnp.einsum("td,ed->te", grad_mix, out_weight, preferred_element_type=jnp.float32)
    out_weight_grad = jnp.einsum("te,td->ed", gated_b, grad_mix, preferred_element_type=jnp.float32)
    grad_scan = grad_gated * gate_act
    grad_gate_z = grad_gated * scan_out * silu_grad(gate_z)
    skip_grad = jnp.sum(grad_scan * mixed, 0)
    exit_first = lax.map(
        lambda parts: block_back_maps(parts, decay_rates, lower),
        (grouped(step_size), grouped(c_out), grouped(grad_scan)),
    )
    back_add = keep[:, None] * exit_first.reshape(blocks, span)
    suffix_mult, suffix_add = lax.associative_scan(
        affine_join, (block_mult, back_add), reverse=True
    )
    returned_carry = carried_in(
        (suffix_mult[0], suffix_add[0]), "seq", affine_join, (ones_span[0], zeros_span[0])
    )
    device_grad = returned_carry[1]
    later_mult = jnp.concatenate([suffix_mult[1:], ones_span], 0)
    later_add = jnp.concatenate([suffix_add[1:], zeros_span], 0)
    exit_grad = later_mult * device_grad[None, :] + later_add
    step_grad, mixed_grad, b_grad, c_grad, rate_grad = lax.map(
        lambda parts: block_grads(parts, decay_rates, lower),
        (
            grouped(step_size),
            grouped(mixed),
            grouped(b_in),
            grouped(c_out),
            by_group(entry),
            grouped(grad_scan),
            by_group(exit_grad),
        ),
    )
    step_grad = step_grad.reshape(tok_seq, channels)
    mixed_grad = mixed_grad.reshape(tok_seq, channels) + skip_gain * grad_scan
    b_grad = b_grad.reshape(tok_seq, STATE)
    c_grad = c_grad.reshape(tok_seq, STATE)
    a_log_grad = jnp.sum(rate_grad, 0) * decay_rates
    step_pre_grad = step_grad * jax.nn.sigmoid(step_pre)
    dt_bias_grad = jnp.sum(step_pre_grad, 0)
    dt_weight_grad = jnp.einsum("tr,te->re", low_rank, step_pre_grad, precision=HIGH)
    rank_grad = jnp.einsum("te,re->tr", step_pre_grad, dt_weight, precision=HIGH)
    proj_grad_b = proj_total(jnp.concatenate([rank_grad, b_grad, c_grad], 1)).astype(jnp.bfloat16)
    mixed_grad = mixed_grad + jnp.einsum(
        "tp,ep->te", proj_grad_b, xproj_weight, preferred_element_type=jnp.float32
    )
    xproj_grad = jnp.einsum("te,tp->ep", mixed_b, proj_grad_b, preferred_element_type=jnp.float32)
    conv_pre_grad = mixed_grad * silu_grad(conv_pre)
    padded_grad, conv_weight_grad, conv_bias_grad = conv_back(conv_pre_grad)
    from_next = edge_rows(padded_grad[:reach], -1)
    inner_grad = padded_grad[reach:].at[tok_seq - reach :].add(from_next)
    proj_in_grad = jnp.stack([inner_grad, grad_gate_z]).astype(jnp.bfloat16)
    in_weight_grad = jnp.einsum(
        "td,kte->kde", gathered, proj_in_grad, preferred_element_type=jnp.float32
    )
    normed_grad = chan_sums(
        lambda first, count: jnp.einsum(
            "kte,kde->td", proj_in_grad, in_weight, preferred_element_type=jnp.float32
        ),
        tok_dev,
    )
    residual_grad, norm_gain_grad = norm_back(normed_grad)
    in_grad = residual_grad + grad_hidden
    (
        in_weight_grad,
        conv_weight_grad,
        conv_bias_grad,
        xproj_grad,
        dt_weight_grad,
        dt_bias_grad,
        a_log_grad,
        skip_grad,
        out_weight_grad,
    ) = (
        lax.psum(in_weight_grad.astype(jnp.bfloat16), "seq").astype(jnp.float32),
        lax.psum(conv_weight_grad.astype(jnp.bfloat16), "seq").astype(jnp.float32),
        lax.psum(conv_bias_grad.astype(jnp.bfloat16), "seq").astype(jnp.float32),
        lax.psum(xproj_grad.astype(jnp.bfloat16), "seq").astype(jnp.float32),
        lax.psum(dt_weight_grad.astype(jnp.bfloat16), "seq").astype(jnp.float32),
        lax.psum(dt_bias_grad.astype(jnp.bfloat16), "seq").astype(jnp.float32),
        lax.psum(a_log_grad.astype(jnp.bfloat16), "seq").astype(jnp.float32),
        lax.psum(skip_grad.astype(jnp.bfloat16), "seq").astype(jnp.float32),
        lax.psum(out_weight_grad.astype(jnp.bfloat16), "seq").astype(jnp.float32),
    )
    norm_gain_grad, moe_gain_grad, router_grad = lax.psum(
        (norm_gain_grad, moe_gain_grad, router_grad), ("seq", "chan")
    )
    return (
        block_out,
        in_grad,
        norm_gain_grad,
        in_weight_grad,
        conv_weight_grad,
        conv_bias_grad,
        xproj_grad,
        dt_weight_grad,
        dt_bias_grad,
        a_log_grad,
        skip_grad,
        out_weight_grad,
        moe_gain_grad,
        router_grad,
        up_grad,
        down_grad,
    )


def solution(mesh):
    in_specs = (
        P(("seq", "chan"), None),
        P(("seq", "chan"), None),
        P(),
        P(),
        P(None, None, "chan"),
        P(None, "chan"),
        P("chan"),
        P("chan", None),
        P(None, "chan"),
        P("chan"),
        P("chan", None),
        P("chan"),
        P("chan", None),
        P(),
        P(),
        P("chan", "seq", None),
        P("chan", "seq", None),
        P(("seq", "chan"), None),
    )
    out_specs = (
        P(("seq", "chan"), None),
        P(("seq", "chan"), None),
        P(),
        P(None, None, "chan"),
        P(None, "chan"),
        P("chan"),
        P("chan", None),
        P(None, "chan"),
        P("chan"),
        P("chan", None),
        P("chan"),
        P("chan", None),
        P(),
        P(),
        P("chan", "seq", None),
        P("chan", "seq", None),
    )
    return jax.shard_map(
        on_device, mesh=mesh, in_specs=in_specs, out_specs=out_specs, check_vma=False
    )
```

profile of v0, /device:TPU:0, one launch (start us, length us, event | category | flops | bytes accessed | tf_op | source)
XLA Modules:
  0.0 3993.1 jit_solution(10633437056419052735)
XLA Ops:
  12.8 28.3 all-gather.11.cloned.1.call-done
  41.1 9.5 fusion.174
  63.6 22.5 all-reduce.46.cloned.1.call-done
  86.1 9.3 convert_multiply_fusion.3
  101.4 31.5 mul.897
  132.9 68.4 %copy.144 = f32[10,64,18432]{2,1,0:T(8,128)} copy(f32[10,64,18432]{1,2,0:T(8,128)} %bitcast.10) | data formatting | bytes 94371840 | tf_op jit(solution)/shard_map/while/body/eval_jaxpr/mul | solution.py:121
  201.3 42.3 %fusion.7 = f32[10,64,18432]{2,1,0:T(8,128)} fusion(f32[10,64,18432]{2,1,0:T(8,128)} %copy.144, f32[18432]{0:T(1024)S(1)} %mul.899), kind=kOutput, calls=%fused_computation.28 | convolution fusion | flops 9071497216 | bytes 94445568 | tf_op jit(solution)/shard_map/while/body/eval_jaxpr/ij,bjk->bik/dot_general | solution.py:116
  269.2 31.6 broadcast_multiply_fusion.1
  300.8 68.3 %copy.148 = f32[10,64,18432]{2,1,0:T(8,128)} copy(f32[10,64,18432]{1,2,0:T(8,128)} %bitcast.14) | data formatting | bytes 94371840 | tf_op jit(solution)/shard_map/while/body/eval_jaxpr/mul | solution.py:126
  369.2 29.9 multiply_reduce_fusion.6
  489.1 34.0 all-gather.21.cloned.1.call-done
  525.8 37.6 all-gather.19.cloned.1.call-done
  566.1 22.8 while.20
  591.9 66.2 %bitcast_multiply_fusion.1 = f32[10,64,18432]{2,1,0:T(8,128)} fusion(f32[10,64,18432]{2,1,0:T(8,128)} %fusion.7, f32[10,64,18432]{2,1,0:T(8,128)} %copy.148, f32[10,18432]{1,0:T(8,128)} %add_multiply_fusion), kind=kOutput, calls=%fused_computation.16 | convolution fusion | flops 9106886656 | bytes 142295040 | tf_op jit(solution)/shard_map/while/body/eval_jaxpr/ij,bjk->bik/dot_general | solution.py:116
  658.1 61.9 %copy.152 = f32[10,64,18432]{1,2,0:T(8,128)} copy(f32[10,64,18432]{2,1,0:T(8,128)} %bitcast_multiply_fusion.1) | data formatting | bytes 94371840 | tf_op jit(solution)/shard_map/while/body/eval_jaxpr/mul | solution.py:145
  720.0 65.6 %multiply_reduce_fusion.4 = f32[10,64,1152]{1,2,0:T(8,128)} fusion(f32[10,64,1152,16]{1,3,2,0:T(8,128)} %bitcast.20, f32[10,64,16]{1,2,0:T(8,128)S(1)} %copy-done.48), kind=kLoop, calls=%fused_computation.10 | loop fusion | flops 22855680 | bytes 50176000 | tf_op jit(solution)/shard_map/while/body/eval_jaxpr/reduce_sum | solution.py:153
  803.4 37.5 reduce-scatter.5.cloned.1.call-done
  845.3 40.5 %psum.211 = f32[8]{0:T(128)S(1)} all-reduce(f32[8]{0:T(128)S(1)} %get-tuple-element.574), channel_id=1, replica_groups=mesh['seq'=16,'chan'=2] {'seq','chan'}, use_global_device_ids=true, to_apply=%region_12.13 | all-reduce | flops 8 | bytes 64 | tf_op jit(solution)/shard_map/psum | solution.py:102
  886.1 41.7 %psum.212 = f32[8]{0:T(128)S(1)} all-reduce(f32[8]{0:T(128)S(1)} %fusion.130), channel_id=1, replica_groups=mesh['seq'=16,'chan'=2] {'seq','chan'}, use_global_device_ids=true, to_apply=%region_15.16 | all-reduce | flops 8 | bytes 64 | tf_op jit(solution)/shard_map/psum | solution.py:102
  928.7 40.4 %psum.213 = f32[8]{0:T(128)S(1)} all-reduce(f32[8]{0:T(128)S(1)} %get-tuple-element.515), channel_id=1, replica_groups=mesh['seq'=16,'chan'=2] {'seq','chan'}, use_global_device_ids=true, to_apply=%region_18.19 | all-reduce | flops 8 | bytes 64 | tf_op jit(solution)/shard_map/psum | solution.py:102
  970.6 40.9 %psum.214 = f32[8]{0:T(128)S(1)} all-reduce(f32[8]{0:T(128)S(1)} %get-tuple-element.511), channel_id=1, replica_groups=mesh['seq'=16,'chan'=2] {'seq','chan'}, use_global_device_ids=true, to_apply=%region_21.22 | all-reduce | flops 8 | bytes 64 | tf_op jit(solution)/shard_map/psum | solution.py:102
  1013.1 40.5 %psum.215 = f32[8]{0:T(128)S(1)} all-reduce(f32[8]{0:T(128)S(1)} %get-tuple-element.507), channel_id=1, replica_groups=mesh['seq'=16,'chan'=2] {'seq','chan'}, use_global_device_ids=true, to_apply=%region_24.25 | all-reduce | flops 8 | bytes 64 | tf_op jit(solution)/shard_map/psum | solution.py:102
  1065.2 46.2 %psum.216 = f32[8]{0:T(128)S(1)} all-reduce(f32[8]{0:T(128)S(1)} %get-tuple-element.503), channel_id=1, replica_groups=mesh['seq'=16,'chan'=2] {'seq','chan'}, use_global_device_ids=true, to_apply=%region_27.28 | all-reduce | flops 8 | bytes 64 | tf_op jit(solution)/shard_map/psum | solution.py:102
  1112.2 40.4 %psum.217 = f32[8]{0:T(128)S(1)} all-reduce(f32[8]{0:T(128)S(1)} %get-tuple-element.499), channel_id=1, replica_groups=mesh['seq'=16,'chan'=2] {'seq','chan'}, use_global_device_ids=true, to_apply=%region_30.31 | all-reduce | flops 8 | bytes 64 | tf_op jit(solution)/shard_map/psum | solution.py:102
  1152.6 16.2 fusion.12
  1168.8 14.8 fusion.52
  1189.3 45.7 %psum.218 = f32[8]{0:T(128)S(1)} all-reduce(f32[8]{0:T(128)S(1)} %get-tuple-element.497), channel_id=1, replica_groups=mesh['seq'=16,'chan'=2] {'seq','chan'}, use_global_device_ids=true, to_apply=%region_33.34 | all-reduce | flops 8 | bytes 64 | tf_op jit(solution)/shard_map/psum | solution.py:102
  1242.5 39.9 psum.219
  1284.0 40.6 %psum.220 = f32[8]{0:T(128)S(1)} all-reduce(f32[8]{0:T(128)S(1)} %multiply_reduce_fusion.26), channel_id=1, replica_groups=mesh['seq'=16,'chan'=2] {'seq','chan'}, use_global_device_ids=true, to_apply=%region_45.46 | all-reduce | flops 8 | bytes 64 | tf_op jit(solution)/shard_map/psum | solution.py:102
  1326.3 39.8 psum.221
  1368.5 40.3 %psum.222 = f32[8]{0:T(128)} all-reduce(f32[8]{0:T(128)S(1)} %multiply_reduce_fusion.22), channel_id=1, replica_groups=mesh['seq'=16,'chan'=2] {'seq','chan'}, use_global_device_ids=true, to_apply=%region_51.52 | all-reduce | flops 8 | bytes 64 | tf_op jit(solution)/shard_map/psum | solution.py:102
  1420.5 43.5 %psum.223 = f32[8]{0:T(128)S(1)} all-reduce(f32[8]{0:T(128)S(1)} %multiply_reduce_fusion.20), channel_id=1, replica_groups=mesh['seq'=16,'chan'=2] {'seq','chan'}, use_global_device_ids=true, to_apply=%region_54.55 | all-reduce | flops 8 | bytes 64 | tf_op jit(solution)/shard_map/psum | solution.py:102
  1465.6 40.4 %psum.224 = f32[8]{0:T(128)S(1)} all-reduce(f32[8]{0:T(128)S(1)} %multiply_reduce_fusion.18), channel_id=1, replica_groups=mesh['seq'=16,'chan'=2] {'seq','chan'}, use_global_device_ids=true, to_apply=%region_57.58 | all-reduce | flops 8 | bytes 64 | tf_op jit(solution)/shard_map/psum | solution.py:102
  1506.1 16.0 fusion.27
  1522.1 15.4 fusion.49
  1544.6 45.7 %psum.225 = f32[8]{0:T(128)S(1)} all-reduce(f32[8]{0:T(128)S(1)} %multiply_reduce_fusion.16), channel_id=1, replica_groups=mesh['seq'=16,'chan'=2] {'seq','chan'}, use_global_device_ids=true, to_apply=%region_60.61 | all-reduce | flops 8 | bytes 64 | tf_op jit(solution)/shard_map/psum | solution.py:102
  1590.6 38.9 psum.226
  1643.2 49.4 %slice.344 = f32[5,18432]{1,0:T(8,128)S(1)} reverse(f32[5,18432]{1,0:T(8,128)} %slice.312), dimensions={0} | reverse | bytes 737280 | tf_op jit(solution)/shard_map/slice | solution.py:405
  1692.6 61.6 %slice.343 = f32[5,18432]{1,0:T(8,128)} reverse(f32[5,18432]{1,0:T(8,128)} %copy-done.22), dimensions={0} | reverse | bytes 737280 | tf_op jit(solution)/shard_map/slice | solution.py:405
  1754.2 50.5 %slice.353 = f32[4,18432]{1,0:T(4,128)S(1)} reverse(f32[4,18432]{1,0:T(4,128)} %slice.352), dimensions={0} | reverse | bytes 589824 | tf_op jit(solution)/shard_map/slice | solution.py:405
  1807.3 9.1 fusion.40
  1822.0 64.4 %multiply_reduce_fusion = (f32[10,64,16]{1,2,0:T(8,128)}, f32[10,64,1152,16]{1,3,2,0:T(8,128)}) fusion(f32[10,64,1152,16]{1,3,2,0:T(8,128)} %bitcast.20, f32[10,64,1152]{1,2,0:T(8,128)} %copy.163, f32[10,64,16]{1,2,0:T(8,128)S(1)} %copy-done.49), kind=kLoop, calls=%fused_computation.6 | loop fusion | flops 35379200 | bytes 97402880 | tf_op jit(solution)/shard_map/while/body/eval_jaxpr/reduce_sum | solution.py:177
  1886.4 68.3 %copy.164 = f32[10,64,18432]{2,1,0:T(8,128)} copy(f32[10,64,18432]{1,2,0:T(8,128)} %bitcast.41) | data formatting | bytes 94371840 | tf_op jit(solution)/shard_map/while/body/eval_jaxpr/mul | solution.py:131
  1954.7 29.4 fusion.19
  1992.8 50.0 %slice.359 = f32[5,18432]{1,0:T(8,128)S(1)} reverse(f32[5,18432]{1,0:T(8,128)} %slice.358), dimensions={0} | reverse | bytes 737280 | tf_op jit(solution)/shard_map/slice | solution.py:405
  2042.8 50.0 %slice.361 = f32[5,18432]{1,0:T(8,128)S(1)} reverse(f32[5,18432]{1,0:T(8,128)} %slice.360), dimensions={0} | reverse | bytes 737280 | tf_op jit(solution)/shard_map/slice | solution.py:405
  2107.5 50.5 %slice.370 = f32[4,18432]{1,0:T(4,128)S(1)} reverse(f32[4,18432]{1,0:T(4,128)} %slice.369), dimensions={0} | reverse | bytes 589824 | tf_op jit(solution)/shard_map/slice | solution.py:405
  2176.8 62.9 %slice.373 = f32[9,18432]{1,0:T(8,128)} reverse(f32[9,18432]{1,0:T(8,128)} %slice_add_fusion.5), dimensions={0} | reverse | bytes 1327104 | tf_op jit(solution)/shard_map/slice | solution.py:413
  2241.0 24.1 all-gather.3
  2266.8 43.5 %slice.355 = f32[9,18432]{1,0:T(8,128)} reverse(f32[9,18432]{1,0:T(8,128)S(1)} %slice_add_fusion), dimensions={0} | reverse | bytes 1327104 | tf_op jit(solution)/shard_map/slice | solution.py:412
  2310.3 21.4 all-gather.2
  2336.8 111.1 %multiply_reduce_fusion.5 = (f32[18432]{0:T(1024)S(1)}, f32[10,64,18432]{2,1,0:T(8,128)}, f32[10,64,18432]{2,1,0:T(8,128)}) fusion(f32[10,64,18432]{2,1,0:T(8,128)} %copy.144, f32[10,63,18432]{2,1,0:T(8,128)} %bitcast.241, f32[10,1,18432]{2,1,0:T(1,128)} %broadcast_in_dim.71, f32[18432]{0:T(1024)S(1)} %copy-done.13, f32[10,18432]{1,0:T(8,128)S(1)} %pad_add_fusion.1, ...), kind=kOutput, calls=%fused_computation.17 | convolution fusion | flops 9201240064 | bytes 284737536 | tf_op jit(solution)/shard_map/while/body/eval_jaxpr/ij,bjk->bik/dot_general | solution.py:116
  2448.9 61.8 %copy.167 = f32[10,64,18432]{1,2,0:T(8,128)} copy(f32[10,64,18432]{2,1,0:T(8,128)} %get-tuple-element.486) | data formatting | bytes 94371840 | tf_op jit(solution)/shard_map/while/body/eval_jaxpr/mul | solution.py:170
  2510.8 125.3 %multiply_reduce_fusion.2 = f32[10,64,1152]{1,2,0:T(8,128)} fusion(f32[10,64,1152,16]{1,3,2,0:T(8,128)} %bitcast.48, f32[1152,16]{1,0:T(8,128)S(1)} %get-tuple-element.540), kind=kLoop, calls=%fused_computation.8 | loop fusion | flops 22855680 | bytes 50208768 | tf_op jit(solution)/shard_map/while/body/eval_jaxpr/reduce_sum | solution.py:174
  2642.0 61.9 %copy.165 = f32[10,64,18432]{1,2,0:T(8,128)} copy(f32[10,64,18432]{2,1,0:T(8,128)} %get-tuple-element.579) | data formatting | bytes 94371840 | tf_op jit(solution)/shard_map/while/body/eval_jaxpr/add | solution.py:168
  2703.8 82.9 %multiply_reduce_fusion.1 = (f32[10,64,16]{1,2,0:T(8,128)S(1)}, f32[10,64,1152]{1,2,0:T(8,128)}) fusion(f32[10,64,1152,16]{1,3,2,0:T(8,128)} %bitcast.46, f32[10,64,1152]{1,2,0:T(8,128)} %copy.146, f32[10,64,16]{1,2,0:T(8,128)S(1)} %copy-done.47), kind=kLoop, calls=%fused_computation.7 | loop fusion | flops 46438400 | bytes 53166080 | tf_op jit(solution)/shard_map/while/body/eval_jaxpr/reduce_sum | solution.py:176
  2804.5 13.1 all-reduce.49
  2817.7 9.9 fusion.141
  2842.5 14.7 bitcast_convert_fusion.1
  2857.2 15.2 bitcast_convert_fusion
  2889.8 70.2 %all-reduce.40 = (bf16[1152,16]{1,0:T(8,128)(2,1)}, bf16[4,1152]{1,0:T(4,128)(2,1)S(1)}, bf16[1152]{0:T(1024)(128)(2,1)S(1)}, bf16[1152]{0:T(1024)(128)(2,1)S(1)}, bf16[1152]{0:T(1024)(128)(2,1)S(1)}) all-reduce(bf16[1152,16]{1,0:T(8,128)(2,1)S(1)} %copy-done.41, ...), channel_id=1, replica_groups=mesh['seq'=16,'chan'=2] {'seq'}, use_global_device_ids=true, to_apply=%region_90.91 | all-reduce | flops 26496 | bytes 105984 | tf_op jit(solution)/shard_map/psum | solution.py:474
  2966.2 40.4 %all-reduce.39 = (f32[1152]{0:T(1024)}, f32[1152]{0:T(1024)}, f32[1152,8]{0,1:T(8,128)}) all-reduce(f32[1152]{0:T(1024)S(1)} %get-tuple-element.435, f32[1152]{0:T(1024)S(1)} %copy-done.82, f32[1152,8]{0,1:T(8,128)S(1)} %fusion.67), channel_id=1, replica_groups=mesh['seq'=16,'chan'=2] {'seq','chan'}, use_global_device_ids=true, to_apply=%region_76.77 | all-reduce | flops 11520 | bytes 92160 | tf_op jit(solution)/shard_map/psum | solution.py:478
  3011.2 950.0 %all-reduce.48.cloned.1.call-done = (bf16[2,1152,1152]{1,2,0:T(8,128)(2,1)}, bf16[1152,104]{0,1:T(8,128)(2,1)}, bf16[72,1152]{1,0:T(8,128)(2,1)}, bf16[1152,1152...) async-done(((bf16[2,1152,1152]{1,2,0:T(8,128)(2,1)}, bf16[1152,104]{0,1:T(8,128)(2,1)}, bf16[72,1152]{1,0:T(8,128)(2,1)}, ...) | async-done | bytes 64991248 | tf_op jit(solution)/shard_map/psum | solution.py:468
  3972.0 9.4 copy.175
  (574 shorter events, 404.8 us)
Async XLA Ops:
  7.2 789.5 %copy-start = (bf16[1152,1152]{1,0:T(8,128)(2,1)S(1)}, bf16[1152,1152]{1,0:T(8,128)(2,1)}, u32[]{:S(2)}) copy-start(bf16[1152,1152]{1,0:T(8,128)(2,1)} %param.36) | copy-start | bytes 7962628
  7.2 33.9 all-gather.11.cloned.1.call-start
  12.2 74.0 %all-reduce.46.cloned.1.call-start = ((), (), s32[]{:S(2)}) async-start(), calls=%async_computation.7 | async-start | bytes 532480 | tf_op jit(solution)/shard_map/psum | solution.py:94
  12.6 40.6 %copy-start.101 = (f32[640]{0:T(1024)}, f32[640]{0:T(1024)S(1)}, u32[]{:S(2)}) copy-start(f32[640]{0:T(1024)S(1)} %get-tuple-element.443) | copy-start | bytes 7684
  12.6 40.6 %copy-start.103 = (f32[640]{0:T(1024)}, f32[640]{0:T(1024)S(1)}, u32[]{:S(2)}) copy-start(f32[640]{0:T(1024)S(1)} %get-tuple-element.444) | copy-start | bytes 7684
  12.7 40.6 %copy-start.105 = (f32[640]{0:T(1024)}, f32[640]{0:T(1024)S(1)}, u32[]{:S(2)}) copy-start(f32[640]{0:T(1024)S(1)} %get-tuple-element.445) | copy-start | bytes 7684
  12.7 40.6 %copy-start.107 = (f32[640]{0:T(1024)}, f32[640]{0:T(1024)S(1)}, u32[]{:S(2)}) copy-start(f32[640]{0:T(1024)S(1)} %get-tuple-element.446) | copy-start | bytes 7684
  12.7 40.5 %copy-start.74 = (f32[1152]{0:T(1024)}, f32[1152]{0:T(1024)S(1)}, u32[]{:S(2)}) copy-start(f32[1152]{0:T(1024)S(1)} %get-tuple-element.437) | copy-start | bytes 13828
  12.7 40.5 %copy-start.76 = (f32[1152]{0:T(1024)}, f32[1152]{0:T(1024)S(1)}, u32[]{:S(2)}) copy-start(f32[1152]{0:T(1024)S(1)} %get-tuple-element.438) | copy-start | bytes 13828
  12.8 40.5 %copy-start.78 = (f32[1152]{0:T(1024)}, f32[1152]{0:T(1024)S(1)}, u32[]{:S(2)}) copy-start(f32[1152]{0:T(1024)S(1)} %get-tuple-element.439) | copy-start | bytes 13828
  12.8 40.5 %copy-start.80 = (f32[1152]{0:T(1024)}, f32[1152]{0:T(1024)S(1)}, u32[]{:S(2)}) copy-start(f32[1152]{0:T(1024)S(1)} %get-tuple-element.440) | copy-start | bytes 13828
  50.6 2.6 collective-permute-start
  57.7 28.4 copy-start.113
  60.2 462.9 %all-gather.21.cloned.1.call-start = ((), (), s32[]{:S(2)}) async-start(), calls=%async_computation.14 | async-start | bytes 1253376 | tf_op jit(solution)/shard_map/all_gather | solution.py:28
  63.6 137.7 %copy-start.12 = (f32[18432]{0:T(1024)}, f32[18432]{0:T(1024)S(1)}, u32[]{:S(2)}) copy-start(f32[18432]{0:T(1024)S(1)} %mul.899) | copy-start | bytes 221188
  63.6 525.3 %copy-start.116 = (f32[10]{0:T(128)}, f32[10]{0:T(128)S(1)}, u32[]{:S(2)}) copy-start(f32[10]{0:T(128)S(1)} %convert_subtract_fusion) | copy-start | bytes 124
  257.8 154.5 %copy-start.22 = (f32[5,18432]{1,0:T(8,128)}, f32[5,18432]{1,0:T(8,128)S(1)}, u32[]{:S(2)}) copy-start(f32[5,18432]{1,0:T(8,128)S(1)} %slice.313) | copy-start | bytes 1105924
  484.4 79.0 %all-gather.19.cloned.1.call-start = ((), (), s32[]{:S(2)}) async-start(), calls=%async_computation.13 | async-start | bytes 1253376 | tf_op jit(solution)/shard_map/all_gather | solution.py:28
  486.2 354.7 %reduce-scatter.5.cloned.1.call-start = ((), (), s32[]{:S(2)}) async-start(), calls=%async_computation.8 | async-start | bytes 4423680 | tf_op jit(solution)/shard_map/reduce_scatter | solution.py:88
  489.1 77.0 %copy-start.29 = (f32[18432]{0:T(1024)S(1)}, f32[18432]{0:T(1024)}, u32[]{:S(2)}) copy-start(f32[18432]{0:T(1024)} %custom-call) | copy-start | bytes 221188
  658.1 61.9 %copy-start.48 = (f32[10,64,16]{1,2,0:T(8,128)S(1)}, f32[10,64,16]{1,2,0:T(8,128)}, u32[]{:S(2)}) copy-start(f32[10,64,16]{1,2,0:T(8,128)} %copy.153) | copy-start | bytes 122884
  800.6 40.3 %copy-start.10 = (bf16[320,1152]{1,0:T(8,128)(2,1)S(1)}, bf16[320,1152]{1,0:T(8,128)(2,1)}, u32[]{:S(2)}) copy-start(bf16[320,1152]{1,0:T(8,128)(2,1)} %param.24) | copy-start | bytes 2211844
  800.6 352.0 %all-gather.13.cloned.1.call-start = ((), (), s32[]{:S(2)}) async-start(), calls=%async_computation.9 | async-start | bytes 30081024 | tf_op jit(solution)/shard_map/all_gather | solution.py:337
  801.2 42.5 %copy-start.51 = (f32[1152]{0:T(1024)S(1)}, f32[1152]{0:T(1024)}, u32[]{:S(2)}) copy-start(f32[1152]{0:T(1024)} %param.37) | copy-start | bytes 13828
  801.2 42.5 %copy-start.62 = (f32[1152,8]{0,1:T(8,128)S(1)}, f32[1152,8]{0,1:T(8,128)}, u32[]{:S(2)}) copy-start(f32[1152,8]{0,1:T(8,128)} %param.38) | copy-start | bytes 110596
  801.2 367.6 %all-gather.15.cloned.1.call-start = ((), (), s32[]{:S(2)}) async-start(), calls=%async_computation.10 | async-start | bytes 30081024 | tf_op jit(solution)/shard_map/all_gather | solution.py:338
  842.6 216.6 %copy-start.96 = (f32[320]{0:T(512)}, f32[320]{0:T(512)S(1)}, u32[]{:S(2)}) copy-start(f32[320]{0:T(512)S(1)} %get-tuple-element.517) | copy-start | bytes 3844
  842.6 793.7 %copy-start.63 = (f32[320]{0:T(512)}, f32[320]{0:T(512)S(1)}, u32[]{:S(2)}) copy-start(f32[320]{0:T(512)S(1)} %fusion.129) | copy-start | bytes 3844
  845.3 788.7 %copy-start.19 = (f32[320,8]{0,1:T(8,128)}, f32[320,8]{0,1:T(8,128)S(1)}, u32[]{:S(2)}) copy-start(f32[320,8]{0,1:T(8,128)S(1)} %get-tuple-element.575) | copy-start | bytes 30724
  885.8 748.1 %copy-start.55 = (f32[8]{0:T(128)}, f32[8]{0:T(128)S(1)}, u32[]{:S(2)}) copy-start(f32[8]{0:T(128)S(1)} %psum.211) | copy-start | bytes 100
  885.9 748.1 %copy-start.42 = (f32[320]{0:T(512)}, f32[320]{0:T(512)S(1)}, u32[]{:S(2)}) copy-start(f32[320]{0:T(512)S(1)} %fusion.127) | copy-start | bytes 3844
  886.1 352.1 %copy-start.87 = (s32[320]{0:T(512)}, s32[320]{0:T(512)S(1)}, u32[]{:S(2)}) copy-start(s32[320]{0:T(512)S(1)} %add_reduce_fusion) | copy-start | bytes 3844
  1059.2 93.4 %all-to-all-start = ((bf16[8,51,1152]{2,1,0:T(8,128)(2,1)}), bf16[8,51,1152]{2,1,0:T(8,128)(2,1)}, u32[]{:S(2)}, u32[]{:S(2)}) async-start(bf16[8,51,1152]{2,1,0:T(8,128)(2,1)} %reshape.404), calls=%async_computation.1 | async-start | bytes 2064384 | tf_op jit(solution)/shard_map/all_to_all | solution.py:106
  1183.6 54.6 %copy-start.17 = (bf16[320,1152]{1,0:T(8,128)(2,1)S(1)}, bf16[320,1152]{1,0:T(8,128)(2,1)}, u32[]{:S(2)}) copy-start(bf16[320,1152]{1,0:T(8,128)(2,1)} %param.41) | copy-start | bytes 2211844
  1184.6 51.1 %all-to-all-start.1 = ((bf16[8,51,1152]{2,1,0:T(8,128)(2,1)}), bf16[8,51,1152]{2,1,0:T(8,128)(2,1)}, u32[]{:S(2)}, u32[]{:S(2)}) async-start(bf16[8,51,1152]{2,1,0:T(8,128)(2,1)} %bitcast.252), calls=%async_computation.2 | async-start | bytes 2064384 | tf_op jit(solution)/shard_map/all_to_all | solution.py:106
  1235.0 47.4 %copy-start.69 = (f32[8]{0:T(128)}, f32[8]{0:T(128)S(1)}, u32[]{:S(2)}) copy-start(f32[8]{0:T(128)S(1)} %psum.218) | copy-start | bytes 100
  1324.6 43.9 %copy-start.109 = (f32[8]{0:T(128)}, f32[8]{0:T(128)S(1)}, u32[]{:S(2)}) copy-start(f32[8]{0:T(128)S(1)} %psum.220) | copy-start | bytes 100
  1366.9 46.9 %copy-start.100 = (f32[320]{0:T(512)}, f32[320]{0:T(512)S(1)}, u32[]{:S(2)}) copy-start(f32[320]{0:T(512)S(1)} %multiply_reduce_fusion.23) | copy-start | bytes 3844
  1368.5 45.2 %copy-start.111 = (f32[320]{0:T(512)}, f32[320]{0:T(512)S(1)}, u32[]{:S(2)}) copy-start(f32[320]{0:T(512)S(1)} %broadcast_multiply_fusion.4) | copy-start | bytes 3844
  1413.8 92.3 %all-to-all-start.2 = ((bf16[8,51,1152]{2,1,0:T(8,128)(2,1)}), bf16[8,51,1152]{2,1,0:T(8,128)(2,1)}, u32[]{:S(2)}, u32[]{:S(2)}) async-start(bf16[8,51,1152]{2,1,0:T(8,128)(2,1)} %reshape.408), calls=%async_computation.3 | async-start | bytes 2064384 | tf_op jit(solution)/shard_map/all_to_all | solution.py:106
  1537.5 94.5 %copy-start.88 = (s32[320]{0:T(512)S(1)}, s32[320]{0:T(512)}, u32[]{:S(2)}) copy-start(s32[320]{0:T(512)} %copy-done.87) | copy-start | bytes 3844
  1539.8 89.7 %all-to-all-start.3 = ((bf16[8,51,1152]{2,1,0:T(8,128)(2,1)}), bf16[8,51,1152]{2,1,0:T(8,128)(2,1)}, u32[]{:S(2)}, u32[]{:S(2)}) async-start(bf16[8,51,1152]{2,1,0:T(8,128)(2,1)} %bitcast.251), calls=%async_computation.4 | async-start | bytes 2064384 | tf_op jit(solution)/shard_map/all_to_all | solution.py:106
  1544.2 263.1 %all-gather.17.cloned.1.call-start = ((), (), s32[]{:S(2)}) async-start(), calls=%async_computation.11 | async-start | bytes 2211840 | tf_op jit(solution)/shard_map/all_gather | solution.py:84
  1590.4 45.9 %copy-start.59 = (f32[320,8]{0,1:T(8,128)}, f32[320,8]{0,1:T(8,128)S(1)}, u32[]{:S(2)}) copy-start(f32[320,8]{0,1:T(8,128)S(1)} %get-tuple-element.488) | copy-start | bytes 30724
  1590.4 45.9 %copy-start.83 = (f32[320]{0:T(512)}, f32[320]{0:T(512)S(1)}, u32[]{:S(2)}) copy-start(f32[320]{0:T(512)S(1)} %get-tuple-element.487) | copy-start | bytes 3844
  1636.3 56.3 %copy-start.90 = (f32[320]{0:T(512)}, f32[320]{0:T(512)S(1)}, u32[]{:S(2)}) copy-start(f32[320]{0:T(512)S(1)} %multiply_multiply_fusion.14) | copy-start | bytes 3844
  1638.7 168.6 %copy-start.72 = (f32[1152]{0:T(1024)S(1)}, f32[1152]{0:T(1024)}, u32[]{:S(2)}) copy-start(f32[1152]{0:T(1024)} %param.35) | copy-start | bytes 13828
  1638.7 1325.4 %reduce-scatter.7.cloned.1.call-start = ((), (), s32[]{:S(2)}) async-start(), calls=%async_computation.12 | async-start | bytes 4423680 | tf_op jit(solution)/shard_map/reduce_scatter | solution.py:88
  1954.7 29.4 copy-start.117
  1984.3 108.5 %copy-start.30 = (f32[5,18432]{1,0:T(8,128)S(1)}, f32[5,18432]{1,0:T(8,128)}, u32[]{:S(2)}) copy-start(f32[5,18432]{1,0:T(8,128)} %slice.343) | copy-start | bytes 1105924
  2239.8 26.9 copy-start.25
  2336.8 111.3 %copy-start.24 = (f32[1152,16]{1,0:T(8,128)S(1)}, f32[1152,16]{1,0:T(8,128)}, u32[]{:S(2)}) copy-start(f32[1152,16]{1,0:T(8,128)} %copy-done.23) | copy-start | bytes 221188
  2641.9 61.9 %copy-start.47 = (f32[10,64,16]{1,2,0:T(8,128)S(1)}, f32[10,64,16]{1,2,0:T(8,128)}, u32[]{:S(2)}) copy-start(f32[10,64,16]{1,2,0:T(8,128)} %copy-done.46) | copy-start | bytes 122884
  2799.9 17.7 copy-start.58
  2828.5 3.1 collective-permute-start.1
  2842.4 1118.7 %all-reduce.48.cloned.1.call-start = ((), (), s32[]{:S(2)}) async-start(), calls=%async_computation.15 | async-start | bytes 129982464 | tf_op jit(solution)/shard_map/psum | solution.py:468
  2886.8 77.4 %copy-start.11 = (bf16[320,1152]{1,0:T(8,128)(2,1)S(1)}, bf16[320,1152]{1,0:T(8,128)(2,1)}, u32[]{:S(2)}) copy-start(bf16[320,1152]{1,0:T(8,128)(2,1)} %param.24) | copy-start | bytes 2211844
  2886.8 77.4 %copy-start.65 = (f32[1152]{0:T(1024)S(1)}, f32[1152]{0:T(1024)}, u32[]{:S(2)}) copy-start(f32[1152]{0:T(1024)} %param.27) | copy-start | bytes 13828
  2886.8 77.4 %copy-start.86 = (f32[320]{0:T(512)S(1)}, f32[320]{0:T(512)}, u32[]{:S(2)}) copy-start(f32[320]{0:T(512)} %copy-done.85) | copy-start | bytes 3844
  2886.8 79.3 %copy-start.82 = (f32[1152]{0:T(1024)S(1)}, f32[1152]{0:T(1024)}, u32[]{:S(2)}) copy-start(f32[1152]{0:T(1024)} %get-tuple-element.428) | copy-start | bytes 13828
  2886.8 119.8 %copy-start.95 = (f32[320]{0:T(512)S(1)}, f32[320]{0:T(512)}, u32[]{:S(2)}) copy-start(f32[320]{0:T(512)} %copy-done.94) | copy-start | bytes 3844
  2886.8 119.8 %copy-start.18 = (bf16[320,1152]{1,0:T(8,128)(2,1)S(1)}, bf16[320,1152]{1,0:T(8,128)(2,1)}, u32[]{:S(2)}) copy-start(bf16[320,1152]{1,0:T(8,128)(2,1)} %param.41) | copy-start | bytes 2211844
  2886.8 119.8 %copy-start.91 = (f32[320]{0:T(512)S(1)}, f32[320]{0:T(512)}, u32[]{:S(2)}) copy-start(f32[320]{0:T(512)} %copy-done.90) | copy-start | bytes 3844
  2886.9 119.8 %copy-start.112 = (f32[320]{0:T(512)S(1)}, f32[320]{0:T(512)}, u32[]{:S(2)}) copy-start(f32[320]{0:T(512)} %copy-done.111) | copy-start | bytes 3844
  (79 other events, 448.0 us)
Sparse Core Ops, SparseCore 0:
  12.3 28.7 all-gather.10
  60.3 25.7 all-reduce.45
  484.6 38.5 all-gather.20
  526.1 37.2 all-gather.18
  800.7 40.1 reduce-scatter.4
  842.3 148.0 all-gather.12
  991.9 147.1 all-gather.14
  1638.8 26.9 all-gather.16
  2842.6 38.4 reduce-scatter.6
  2888.6 1072.5 all-reduce.47
where the time goes:
time: 4030 us; the launch traced here: 3990 us
  waiting for transfers between devices  1110 us (28%)
  local copies, waits for them, and re-layouts  1070 us (27%)
  blocking collectives  835 us (21%)
  other arithmetic  536 us (13%)
  matrix products  397 us (10%)
    psum x1, waiting for transfers between devices, on_device(): lax.psum(in_weight_grad.astype(jnp.bfloat16), 'seq').astype(jnp.float32)  950 us
    psum x16, blocking collectives, column_total(): return lax.psum(values, ('seq', 'chan'))  666 us
    slice x20, local copies, waits for them, and re-layouts, on_device(): lax.associative_scan(affine_join, (block_mult, back_add), reverse=True)  339 us
    dot_general x3, matrix products, running_sum(): return jnp.einsum('ij,bjk->bik', lower, values, precision=HIGH)  220 us
    reduce_sum x1, other arithmetic, block_grads(): step_grad = jnp.sum(log_grad * -rates, 3) + weighted * mixed  125 us
    mul x3, local copies, waits for them, and re-layouts, decay_terms(): return (-step_size[..., None] * rates).reshape(blocks, length, -1)  101 us
    reduce_sum x1, other arithmetic, block_grads(): b_grad = jnp.sum(grads * (step_size * mixed)[..., None], 2)  82.9 us
  transfers between devices with their start and end apart: 16, of which 8 were waited for; matrix products, arithmetic and copies ran while one was open for 7% of the time, Pallas kernels for 0%

commit v1 on v0

v1 whole, which is shorter than its diff:
```python
from functools import partial

import jax
import jax.numpy as jnp
from jax import lax
from jax.experimental import pallas as pl
from jax.experimental.pallas import tpu as pltpu
from jax.sharding import PartitionSpec as P

STATE = 16
CONV = 4
DT_RANK = 72
EXPERTS = 8
SINK = 8
CHUNKS = 8
LANES = 128
VMEM_LIMIT = 56 * 1024 * 1024

EPS = 1e-05
HIGH = lax.Precision.HIGHEST
LOG2E = 1.4426950408889634
LN2 = 0.6931471805599453
BREAK = 1e30


def passed_along(value, axis, steps):
    count = lax.axis_size(axis)
    leading, last = (max(0, -steps), min(count, count - steps))
    return lax.ppermute(value, axis, [(source, source + steps) for source in range(leading, last)])


def swapped(value, axis, bit):
    count = lax.axis_size(axis)
    return lax.ppermute(value, axis, [(source, source ^ bit) for source in range(count)])


def chan_rows(values):
    if lax.axis_size("chan") != 2:
        return lax.all_gather(values, "chan", axis=0, tiled=True)
    first = lax.axis_index("chan") == 0
    other = swapped(values, "chan", 1)
    return jnp.concatenate([jnp.where(first, values, other), jnp.where(first, other, values)], 0)


def chan_sums(term_fn, operand):
    count, place = lax.axis_size("chan"), lax.axis_index("chan")
    rows = operand.shape[0] // count
    if count != 2:
        return lax.psum_scatter(term_fn(operand), "chan", scatter_dimension=0, tiled=True)
    theirs = term_fn(lax.dynamic_slice_in_dim(operand, (1 - place) * rows, rows, 0))
    arrived = swapped(theirs.astype(jnp.bfloat16), "chan", 1)
    return term_fn(lax.dynamic_slice_in_dim(operand, place * rows, rows, 0)) + arrived.astype(
        jnp.float32
    )


def proj_total(values):
    if lax.axis_size("chan") != 2:
        return lax.psum(values, "chan")
    return values + swapped(values, "chan", 1)


def expert_groups():
    own = EXPERTS // lax.axis_size("chan")
    return own, lax.axis_size("seq") // own


def across_experts(values):
    own, share = expert_groups()
    if own == 1:
        return values
    groups = [[k * share + q for k in range(own)] for q in range(share)]
    return lax.all_to_all(
        values, "seq", split_axis=0, concat_axis=0, tiled=True, axis_index_groups=groups
    )


def to_experts(packed):
    own, share = expert_groups()
    count = lax.axis_size("chan")
    slots, width = packed.shape[1:]
    arrived = lax.all_to_all(packed, "chan", split_axis=0, concat_axis=0, tiled=True)
    arrived = jnp.swapaxes(arrived.reshape(count, own, slots, width), 0, 1)
    return across_experts(arrived).reshape(own * count * slots, width)


def to_tokens(rows):
    own, share = expert_groups()
    count = lax.axis_size("chan")
    width = rows.shape[1]
    slots = rows.shape[0] // (own * count)
    back = across_experts(rows.reshape(own, count, slots, width))
    back = jnp.swapaxes(back, 0, 1).reshape(count * own, slots, width)
    return lax.all_to_all(back, "chan", split_axis=0, concat_axis=0, tiled=True)


def whole_expert(weight):
    own, share = expert_groups()
    mine = across_experts(weight)
    groups = [[k * share + q for q in range(share)] for k in range(own)]
    full = lax.all_gather(mine, "seq", axis=1, axis_index_groups=groups)
    return full.reshape(own * share * weight.shape[1], weight.shape[2])


def expert_grad_total(grad):
    own, share = expert_groups()
    place = lax.rem(lax.axis_index("seq"), share)
    hidden = grad.shape[1]
    features = grad.shape[0] // (own * share)
    held = grad.reshape(own, share, features, hidden)
    bit = 1
    while bit < share:
        pairs = held.reshape(own, held.shape[1] // 2, 2, features, hidden)
        side = lax.rem(place // bit, 2)
        sent = lax.dynamic_index_in_dim(pairs, 1 - side, 2, False)
        kept = lax.dynamic_index_in_dim(pairs, side, 2, False)
        came = swapped(sent, "seq", bit)
        held = (kept.astype(jnp.float32) + came.astype(jnp.float32)).astype(grad.dtype)
        bit *= 2
    return across_experts(held.reshape(own, features, hidden)).astype(jnp.float32)


def to_steps(values):
    rows = values.shape[0]
    parts = values.reshape((CHUNKS, rows // CHUNKS) + values.shape[1:])
    return jnp.swapaxes(parts, 0, 1).reshape(values.shape)


def from_steps(values):
    rows = values.shape[0]
    parts = values.reshape((rows // CHUNKS, CHUNKS) + values.shape[1:])
    return jnp.swapaxes(parts, 0, 1).reshape(values.shape)


def norm_apply(values, gain):
    return values * lax.rsqrt(jnp.mean(values * values, -1, keepdims=True) + EPS) * gain


def silu_grad(values):
    sigma = jax.nn.sigmoid(values)
    return sigma * (1.0 + values * (1.0 - sigma))


def gelu_grad(values, upstream):
    return jax.vjp(partial(jax.nn.gelu, approximate=True), values)[1](upstream)[0]


def spread(target, source):
    for n in range(STATE):
        target[n] = jnp.broadcast_to(source[:, n : n + 1], target.shape[1:])


def full(row):
    return jnp.broadcast_to(row, (CHUNKS, LANES))


def shifted(values, by, down):
    sub = lax.broadcasted_iota(jnp.int32, (CHUNKS, LANES), 0)
    if down:
        return jnp.where(sub >= by, pltpu.roll(values, by, 0), 0.0)
    return jnp.where(sub < CHUNKS - by, pltpu.roll(values, CHUNKS - by, 0), 0.0)


def chunk_windows(sums, down):
    windows = []
    for by in (1, 2, 4):
        windows.append(sums)
        sums = sums + shifted(sums, by, down)
    return windows, sums


def chunk_prefix(ends, windows, rate, down):
    for by, window in zip((1, 2, 4), windows):
        ends = ends + jnp.exp2(rate * window) * shifted(ends, by, down)
    return ends


def ends_kernel(halves, reverse, step_ref, drive_ref, break_ref, map_ref, rate_ref, part_ref, sum_ref, tot_ref, wide):
    rows = step_ref.shape[0]
    steps = rows // (halves * CHUNKS)

    @pl.when(pl.program_id(0) == 0)
    def _():
        spread(wide, map_ref)

    rates = [full(rate_ref[n : n + 1, :]) for n in range(STATE)]
    zero = jnp.zeros((CHUNKS, LANES), jnp.float32)

    def half(turn, carry):
        h = halves - 1 - turn if reverse else turn
        before_sum, before = carry[0], carry[1:]

        def body(k, state):
            s = steps - 1 - k if reverse else k
            at = pl.ds(pl.multiple_of((h * steps + s) * CHUNKS, CHUNKS), CHUNKS)
            step = step_ref[at, :]
            decay_step = step + break_ref[at, :]
            drive = drive_ref[at, :]
            if not reverse:
                drive = drive * step
            new = [state[0] + decay_step]
            for n in range(STATE):
                decay = jnp.exp2(decay_step * rates[n])
                if reverse:
                    new.append(decay * (state[n + 1] + drive * wide[n, at, :]))
                else:
                    new.append(decay * state[n + 1] + drive * wide[n, at, :])
            return tuple(new)

        out = lax.fori_loop(0, steps, body, (zero,) * (STATE + 1), unroll=2)
        windows, sums = chunk_windows(out[0], not reverse)
        prior = shifted(sums, 1, not reverse)
        last = slice(0, 1) if reverse else slice(CHUNKS - 1, CHUNKS)
        sum_ref[h] = prior + before_sum
        new = [before_sum + full(sums[last])]
        for n in range(STATE):
            joined = chunk_prefix(out[n + 1], windows, rates[n], not reverse)
            part_ref[h, n] = shifted(joined, 1, not reverse) + jnp.exp2(rates[n] * prior) * before[n]
            new.append(full(joined[last]) + jnp.exp2(rates[n] * full(sums[last])) * before[n])
        return tuple(new)

    total = lax.fori_loop(0, halves, half, (zero,) * (STATE + 1))
    for n in range(STATE):
        tot_ref[n : n + 1, :] = total[n + 1][0:1]
    tot_ref[STATE:, :] = total[0]


def joined_over_devices(place_ref, all_ref, rate_ref, reverse):
    count = all_ref.shape[0]
    place = place_ref[0]
    rates = rate_ref[...]

    def turn(k, state):
        source = count - 1 - k if reverse else k
        part = all_ref[source]
        reached = source > place if reverse else source < place
        new = jnp.exp2(rates * part[STATE : STATE + 1]) * state + part[:STATE]
        return jnp.where(reached, new, state)

    return lax.fori_loop(0, count, turn, jnp.zeros((STATE, LANES), jnp.float32))


def outputs_kernel(
    halves, place_ref, step_ref, mixed_ref, break_ref, b_ref, c_ref, rate_ref, part_ref, sum_ref, all_ref,
    skip_ref, gate_ref, scan_ref, gated_ref, entry_ref, b_wide, c_wide, device,
):
    rows = step_ref.shape[0]
    steps = rows // (halves * CHUNKS)

    @pl.when(pl.program_id(0) == 0)
    def _():
        spread(b_wide, b_ref)
        spread(c_wide, c_ref)

    rates = [full(rate_ref[n : n + 1, :]) for n in range(STATE)]
    device[...] = joined_over_devices(place_ref, all_ref, rate_ref, False)

    def half(h, carry):
        state = []
        for n in range(STATE):
            state.append(
                part_ref[h, n] + jnp.exp2(rates[n] * sum_ref[h]) * full(device[n : n + 1, :])
            )
            entry_ref[h, n] = state[n]

        def body(s, state):
            at = pl.ds(pl.multiple_of((h * steps + s) * CHUNKS, CHUNKS), CHUNKS)
            step = step_ref[at, :]
            decay_step = step + break_ref[at, :]
            drive = mixed_ref[at, :] * step
            total = None
            new = []
            for n in range(STATE):
                value = jnp.exp2(decay_step * rates[n]) * state[n] + drive * b_wide[n, at, :]
                term = value * c_wide[n, at, :]
                total = term if total is None else total + term
                new.append(value)
            scan_ref[at, :] = total
            return tuple(new)

        lax.fori_loop(0, steps, body, tuple(state), unroll=2)
        return carry

    lax.fori_loop(0, halves, half, 0)
    gate = gate_ref[...]
    out = scan_ref[...] + skip_ref[...] * mixed_ref[...]
    scan_ref[...] = out
    gated_ref[...] = (out * (gate * jax.nn.sigmoid(gate))).astype(gated_ref.dtype)


def grads_kernel(
    halves, place_ref, step_ref, mixed_ref, break_ref, grad_ref, b_ref, c_ref, rate_ref, entry_ref, part_ref,
    sum_ref, all_ref, step_out, mixed_out, b_out, c_out, rate_out, b_wide, c_wide, b_sum, c_sum, decays,
    states, device,
):
    rows = step_ref.shape[0]
    steps = rows // (halves * CHUNKS)
    group = pl.program_id(0)
    block = STATE // 2

    @pl.when(group == 0)
    def _():
        spread(b_wide, b_ref)
        spread(c_wide, c_ref)
        b_sum[...] = jnp.zeros_like(b_sum)
        c_sum[...] = jnp.zeros_like(c_sum)

    device[...] = joined_over_devices(place_ref, all_ref, rate_ref, True)
    zero = jnp.zeros((CHUNKS, LANES), jnp.float32)

    for first in (0, block):
        rates = [full(rate_ref[first + n : first + n + 1, :]) for n in range(block)]

        def half(h, rate_sums):
            entry = []
            for n in range(block):
                entry.append(entry_ref[h, first + n])
                states[0, n] = entry[n]

            def ahead(s, state):
                at = pl.ds(pl.multiple_of((h * steps + s) * CHUNKS, CHUNKS), CHUNKS)
                step = step_ref[at, :]
                decay_step = step + break_ref[at, :]
                drive = mixed_ref[at, :] * step
                new = []
                for n in range(block):
                    decay = jnp.exp2(decay_step * rates[n])
                    value = decay * state[n] + drive * b_wide[first + n, at, :]
                    decays[s, n] = decay
                    states[s + 1, n] = value
                    new.append(value)
                return tuple(new)

            lax.fori_loop(0, steps, ahead, tuple(entry), unroll=2)

            exits = [
                part_ref[h, first + n]
                + jnp.exp2(rates[n] * sum_ref[h]) * full(device[first + n : first + n + 1, :])
                for n in range(block)
            ]

            def back(k, carry):
                s = steps - 1 - k
                at = pl.ds(pl.multiple_of((h * steps + s) * CHUNKS, CHUNKS), CHUNKS)
                step = step_ref[at, :]
                mixed = mixed_ref[at, :]
                grad = grad_ref[at, :]
                drive = mixed * step
                by_rate, by_map = zero, zero
                flows, sums = [], []
                for n in range(block):
                    b_now, c_now = b_wide[first + n, at, :], c_wide[first + n, at, :]
                    here = carry[n] + c_now * grad
                    flow = decays[s, n] * here
                    log_grad = flow * states[s, n]
                    by_rate = by_rate + rates[n] * log_grad
                    by_map = by_map + b_now * here
                    b_sum[first + n, at, :] += drive * here
                    c_sum[first + n, at, :] += grad * states[s + 1, n]
                    flows.append(flow)
                    sums.append(carry[block + n] + step * log_grad)
                by_rate = by_rate * LN2 + mixed * by_map
                by_map = step * by_map
                if first == 0:
                    step_out[at, :] = by_rate
                    mixed_out[at, :] = by_map
                else:
                    step_out[at, :] += by_rate
                    mixed_out[at, :] += by_map
                return tuple(flows + sums)

            out = lax.fori_loop(0, steps, back, tuple(exits) + rate_sums)
            return out[block:]

        rate_sums = lax.fori_loop(0, halves, half, (zero,) * block)
        for n in range(block):
            rate_out[first + n : first + n + 1, :] = jnp.sum(rate_sums[n], 0, keepdims=True)

    @pl.when(group == pl.num_programs(0) - 1)
    def _():
        for n in range(STATE):
            b_out[:, n : n + 1] = jnp.sum(b_sum[n], -1, keepdims=True)
            c_out[:, n : n + 1] = jnp.sum(c_sum[n], -1, keepdims=True)


class Scan:
    def __init__(self, rows, channels, halves, seq):
        self.rows, self.channels, self.halves, self.seq = rows, channels, halves, seq
        self.groups = channels // LANES
        row_spec = pl.BlockSpec((rows, LANES), lambda g: (0, g))
        fixed = lambda *shape: pl.BlockSpec(shape, lambda g: (0,) * len(shape))
        self.row_spec = row_spec
        self.break_spec = fixed(rows, LANES)
        self.map_spec = fixed(rows, STATE)
        self.rate_spec = pl.BlockSpec((STATE, LANES), lambda g: (0, g))
        self.part_spec = pl.BlockSpec((halves, STATE, CHUNKS, LANES), lambda g: (0, 0, 0, g))
        self.sum_spec = pl.BlockSpec((halves, CHUNKS, LANES), lambda g: (0, 0, g))
        self.tot_spec = pl.BlockSpec((STATE + CHUNKS, LANES), lambda g: (0, g))
        self.all_spec = pl.BlockSpec((seq, STATE + CHUNKS, LANES), lambda g: (0, 0, g))
        self.skip_spec = pl.BlockSpec((1, LANES), lambda g: (0, g))
        self.place_spec = pl.BlockSpec(memory_space=pltpu.SMEM)
        self.row_f32 = jax.ShapeDtypeStruct((rows, channels), jnp.float32)
        self.part_f32 = jax.ShapeDtypeStruct((halves, STATE, CHUNKS, channels), jnp.float32)
        self.sum_f32 = jax.ShapeDtypeStruct((halves, CHUNKS, channels), jnp.float32)
        self.tot_f32 = jax.ShapeDtypeStruct((STATE + CHUNKS, channels), jnp.float32)
        self.wide = pltpu.VMEM((STATE, rows, LANES), jnp.float32)
        self.device = pltpu.VMEM((STATE, LANES), jnp.float32)

    def params(self):
        return pltpu.CompilerParams(
            dimension_semantics=("arbitrary",), vmem_limit_bytes=VMEM_LIMIT
        )

    def cost(self, per_element):
        count = self.rows * self.channels * STATE
        return pl.CostEstimate(
            flops=per_element * count, bytes_accessed=12 * self.rows * self.channels, transcendentals=count
        )

    def ends(self, reverse, step, drive, breaks, maps, rates):
        return pl.pallas_call(
            partial(ends_kernel, self.halves, reverse),
            grid=(self.groups,),
            in_specs=[self.row_spec, self.row_spec, self.break_spec, self.map_spec, self.rate_spec],
            out_specs=[self.part_spec, self.sum_spec, self.tot_spec],
            out_shape=[self.part_f32, self.sum_f32, self.tot_f32],
            scratch_shapes=[self.wide],
            compiler_params=self.params(),
            cost_estimate=self.cost(5),
            name="scan_ends_back" if reverse else "scan_ends",
        )(step, drive, breaks, maps, rates)

    def outputs(self, place, step, mixed, breaks, b_in, c_out, rates, part, sums, every, skip, gate):
        return pl.pallas_call(
            partial(outputs_kernel, self.halves),
            grid=(self.groups,),
            in_specs=[
                self.place_spec, self.row_spec, self.row_spec, self.break_spec, self.map_spec, self.map_spec,
                self.rate_spec, self.part_spec, self.sum_spec, self.all_spec, self.skip_spec, self.row_spec,
            ],
            out_specs=[self.row_spec, self.row_spec, self.part_spec],
            out_shape=[
                self.row_f32,
                jax.ShapeDtypeStruct((self.rows, self.channels), jnp.bfloat16),
                self.part_f32,
            ],
            scratch_shapes=[self.wide, self.wide, self.device],
            compiler_params=self.params(),
            cost_estimate=self.cost(7),
            name="scan_outputs",
        )(place, step, mixed, breaks, b_in, c_out, rates, part, sums, every, skip, gate)

    def grads(self, place, step, mixed, breaks, grad, b_in, c_out, rates, entry, part, sums, every):
        steps = self.rows // (self.halves * CHUNKS)
        block = STATE // 2
        return pl.pallas_call(
            partial(grads_kernel, self.halves),
            grid=(self.groups,),
            in_specs=[
                self.place_spec, self.row_spec, self.row_spec, self.break_spec, self.row_spec, self.map_spec,
                self.map_spec, self.rate_spec, self.part_spec, self.part_spec, self.sum_spec, self.all_spec,
            ],
            out_specs=[self.row_spec, self.row_spec, self.map_spec, self.map_spec, self.rate_spec],
            out_shape=[
                self.row_f32,
                self.row_f32,
                jax.ShapeDtypeStruct((self.rows, STATE), jnp.float32),
                jax.ShapeDtypeStruct((self.rows, STATE), jnp.float32),
                jax.ShapeDtypeStruct((STATE, self.channels), jnp.float32),
            ],
            scratch_shapes=[
                self.wide, self.wide, self.wide, self.wide,
                pltpu.VMEM((steps, block, CHUNKS, LANES), jnp.float32),
                pltpu.VMEM((steps + 1, block, CHUNKS, LANES), jnp.float32),
                self.device,
            ],
            compiler_params=self.params(),
            cost_estimate=self.cost(20),
            name="scan_grads",
        )(place, step, mixed, breaks, grad, b_in, c_out, rates, entry, part, sums, every)


def over_tokens(values):
    return jnp.sum(jnp.sum(values, 0), -1, keepdims=True)


def sinkhorn_kernel(place_ref, logit_ref, route_ref, gate_ref, scaled_ref, row_ref, column_ref):
    probs = jnp.exp(logit_ref[...])
    for sweep in range(SINK):
        column = over_tokens(probs)
        scaled = probs / column[None]
        row = jnp.sum(scaled, 1, keepdims=True)
        scaled_ref[sweep] = scaled
        row_ref[sweep] = row
        column_ref[sweep] = jnp.broadcast_to(column, column_ref.shape[1:])
        probs = scaled / row
    place = place_ref[0]
    own = scaled_ref[SINK - 1, place] / row_ref[SINK - 1, place]
    ids = lax.broadcasted_iota(jnp.int32, own.shape, 0)
    gate_ref[...] = EXPERTS * jnp.sum(jnp.where(ids == route_ref[...], own, 0.0), 0, keepdims=True)


def sinkhorn_back_kernel(place_ref, logit_ref, scaled_ref, row_ref, column_ref, route_ref, grad_ref, out_ref, held):
    shape = logit_ref.shape
    ids = lax.broadcasted_iota(jnp.int32, shape, 1)
    grad = jnp.where(ids == route_ref[...], EXPERTS * grad_ref[...], 0.0)
    for sweep in reversed(range(SINK)):
        scaled, row = scaled_ref[sweep], row_ref[sweep]
        inner = jnp.sum(grad * (scaled / row), 1, keepdims=True)
        grad = (grad - inner) / row
        along = over_tokens(grad * scaled)
        grad = (grad - along[None]) / column_ref[sweep][:, 0:1][None]
    held[...] = grad
    place = place_ref[0]
    out_ref[...] = held[place] * jnp.exp(logit_ref[place])


def in_vmem(count):
    return [pl.BlockSpec(memory_space=pltpu.SMEM)] + [pl.BlockSpec(memory_space=pltpu.VMEM)] * count


def sinkhorn(place, logits, routes):
    devices, experts, tokens = logits.shape
    f32 = lambda *shape: jax.ShapeDtypeStruct(shape, jnp.float32)
    return pl.pallas_call(
        sinkhorn_kernel,
        in_specs=in_vmem(2),
        out_specs=in_vmem(4)[1:],
        out_shape=[
            f32(1, tokens),
            f32(SINK, devices, experts, tokens),
            f32(SINK, devices, 1, tokens),
            f32(SINK, experts, LANES),
        ],
        compiler_params=pltpu.CompilerParams(vmem_limit_bytes=VMEM_LIMIT),
        name="sinkhorn",
    )(place, logits, routes)


def sinkhorn_back(place, logits, scaled, rows, columns, routes, grad):
    devices, experts, tokens = logits.shape
    return pl.pallas_call(
        sinkhorn_back_kernel,
        in_specs=in_vmem(6),
        out_specs=in_vmem(1)[1],
        out_shape=jax.ShapeDtypeStruct((experts, tokens), jnp.float32),
        scratch_shapes=[pltpu.VMEM(logits.shape, jnp.float32)],
        compiler_params=pltpu.CompilerParams(vmem_limit_bytes=VMEM_LIMIT),
        name="sinkhorn_back",
    )(place, logits, scaled, rows, columns, routes, grad)


def on_device(
    block_in,
    routes,
    doc_lengths,
    norm_gain,
    in_weight,
    conv_weight,
    conv_bias,
    xproj_weight,
    dt_weight,
    dt_bias,
    a_log,
    skip_gain,
    out_weight,
    moe_gain,
    router_weight,
    up_weight,
    down_weight,
    out_grad,
):
    tok_dev, model_width = block_in.shape
    chan_count, seq_count = lax.axis_size("chan"), lax.axis_size("seq")
    chan_place, seq_place = lax.axis_index("chan"), lax.axis_index("seq")
    seq_ref = seq_place.astype(jnp.int32).reshape(1)
    dev_ref = (seq_place * chan_count + chan_place).astype(jnp.int32).reshape(1)
    steps = tok_dev // CHUNKS
    tok_seq = tok_dev * chan_count
    channels = in_weight.shape[2]
    padded_channels = -(-channels // LANES) * LANES
    f32, bf16 = jnp.float32, jnp.bfloat16

    route_col = routes[:, 0]
    expert_ids = lax.broadcasted_iota(jnp.int32, (1, EXPERTS), 1)
    chosen = (route_col[:, None] == expert_ids).astype(bf16)
    row_ids = lax.broadcasted_iota(jnp.int32, (tok_dev, tok_dev), 0)
    col_ids = lax.broadcasted_iota(jnp.int32, (tok_dev, tok_dev), 1)
    counts = jnp.dot((col_ids <= row_ids).astype(bf16), chosen, preferred_element_type=f32)
    rank = (jnp.sum(counts * chosen.astype(f32), 1) - 1.0).astype(jnp.int32)
    capacity = tok_dev * 5 // (4 * EXPERTS) + 1
    capacity = -(-capacity // 8) * 8
    slot = to_steps(route_col * capacity + rank)
    route_steps = to_steps(route_col)
    slot_ids = lax.broadcasted_iota(jnp.int32, (1, EXPERTS * capacity), 1)
    placer = (slot[:, None] == slot_ids).astype(bf16)

    def pack(values):
        rows = jnp.einsum("ts,td->sd", placer, values, preferred_element_type=f32).astype(bf16)
        return rows.reshape(EXPERTS, capacity, model_width)

    def unpack(values):
        return jnp.einsum(
            "ts,sd->td",
            placer,
            values.reshape(EXPERTS * capacity, model_width),
            preferred_element_type=f32,
        )

    block_steps = to_steps(block_in)
    grad_steps = to_steps(out_grad)
    residual = block_steps.astype(f32)
    normed, norm_back = jax.vjp(norm_apply, residual, norm_gain)
    gathered = chan_rows(normed.astype(bf16))
    full_up = whole_expert(up_weight)
    full_down = whole_expert(down_weight)
    grad_arrived = to_experts(pack(grad_steps))
    every_route = lax.all_gather(route_steps.reshape(1, tok_dev), ("seq", "chan"))

    inner_b = jnp.dot(gathered, in_weight[0], preferred_element_type=f32).astype(bf16)
    gate_z = jnp.dot(gathered, in_weight[1], preferred_element_type=f32)

    shape4 = (chan_count, steps, CHUNKS)
    ids = [lax.broadcasted_iota(jnp.int32, shape4, axis) for axis in range(3)]
    position = seq_place * tok_seq + ids[0] * tok_dev + ids[2] * steps + ids[1]
    starts = jnp.cumsum(doc_lengths) - doc_lengths
    doc_first = jnp.max(
        jnp.where(starts <= position[..., None], starts, 0), axis=-1
    )
    reach = CONV - 1
    inner = inner_b.astype(f32).reshape(shape4 + (channels,))
    tails = jnp.swapaxes(inner[:, steps - reach :], 0, 1).reshape(reach, chan_count * CHUNKS, channels)
    previous = passed_along(tails[:, -1], "seq", 1)
    heads = jnp.concatenate([previous[:, None], tails[:, :-1]], 1)
    heads = jnp.swapaxes(heads.reshape(reach, chan_count, CHUNKS, channels), 0, 1)
    padded = jnp.concatenate([heads, inner], 1)
    masks = [
        (position - (reach - offset) >= doc_first).astype(f32)[..., None] for offset in range(CONV)
    ]
    conv_pre = conv_bias
    for offset in range(CONV):
        conv_pre = conv_pre + conv_weight[offset] * padded[:, offset : offset + steps] * masks[offset]
    conv_pre = conv_pre.reshape(tok_seq, channels)
    mixed_b = jax.nn.silu(conv_pre).astype(bf16)
    mixed = mixed_b.astype(f32)
    proj_all = proj_total(jnp.dot(mixed_b, xproj_weight, preferred_element_type=f32))
    low_rank = proj_all[:, :DT_RANK]
    b_in = proj_all[:, DT_RANK : DT_RANK + STATE]
    c_out = proj_all[:, DT_RANK + STATE :]
    step_pre = jnp.dot(low_rank, dt_weight, precision=HIGH) + dt_bias
    step_size = jax.nn.softplus(step_pre)

    def widened(values, axis=-1):
        more = padded_channels - channels
        if not more:
            return values
        pads = [(0, 0)] * values.ndim
        pads[axis] = (0, more)
        return jnp.pad(values, pads)

    scan = Scan(tok_seq, padded_channels, chan_count, seq_count)
    decay_rates = jnp.exp(a_log)
    rates = widened((-LOG2E * decay_rates).T)
    breaks = jnp.any(position[..., None] == starts, axis=-1).astype(f32) * BREAK
    breaks = jnp.broadcast_to(breaks.reshape(tok_seq, 1), (tok_seq, LANES))
    step_w, mixed_w = widened(step_size), widened(mixed)
    part, sums, total = scan.ends(False, step_w, mixed_w, breaks, b_in, rates)
    every = lax.all_gather(total, "seq")
    scan_out, gated_b, entry = scan.outputs(
        seq_ref, step_w, mixed_w, breaks, b_in, c_out, rates, part, sums, every,
        widened(skip_gain[None]), widened(gate_z),
    )
    scan_out, gated_b = scan_out[:, :channels], gated_b[:, :channels]

    mixer_rows = chan_sums(
        lambda rows: jnp.dot(rows, out_weight, preferred_element_type=f32), gated_b
    )
    hidden_one = residual + mixer_rows
    moe_in, moe_back = jax.vjp(norm_apply, hidden_one, moe_gain)
    logits = jnp.einsum("td,de->et", moe_in, router_weight, precision=HIGH)
    every_logit = lax.all_gather(logits, ("seq", "chan"))
    gate_row, scaled, row_totals, columns = sinkhorn(
        dev_ref, every_logit, route_steps.reshape(1, tok_dev)
    )
    gate = gate_row.reshape(tok_dev)

    arrived = to_experts(pack(moe_in.astype(bf16)))
    pre = jnp.dot(arrived, full_up, preferred_element_type=f32)
    act_b = jax.nn.gelu(pre, approximate=True).astype(bf16)
    expert_out = jnp.einsum("sf,df->sd", act_b, full_down, preferred_element_type=f32).astype(bf16)
    grad_act = jnp.dot(grad_arrived, full_down, preferred_element_type=f32)
    plain_grad_pre = gelu_grad(pre, grad_act)
    grad_rows_in = jnp.einsum(
        "sf,df->sd", plain_grad_pre.astype(bf16), full_up, preferred_element_type=f32
    ).astype(bf16)
    expert_tok = unpack(to_tokens(expert_out))
    plain_grad_part = unpack(to_tokens(grad_rows_in))

    gate_slots = jnp.einsum("ts,t->s", placer.astype(f32), gate, precision=HIGH)
    gate_slots = jnp.broadcast_to(gate_slots.reshape(EXPERTS, capacity, 1), (EXPERTS, capacity, LANES))
    gate_arrived = to_experts(gate_slots)[:, 0:1]
    grad_gated_rows = (grad_arrived.astype(f32) * gate_arrived).astype(bf16)
    grad_pre_b = (plain_grad_pre * gate_arrived).astype(bf16)
    down_part = jnp.einsum("sd,sf->df", grad_gated_rows, act_b, preferred_element_type=f32)
    up_part = jnp.einsum("sd,sf->df", arrived, grad_pre_b, preferred_element_type=f32)
    down_grad = expert_grad_total(down_part.astype(bf16))
    up_grad = expert_grad_total(up_part.astype(bf16))

    block_out = from_steps((hidden_one + gate[:, None] * expert_tok).astype(bf16))
    grad_two = grad_steps.astype(f32)
    grad_gate = jnp.sum(expert_tok * grad_two, 1)
    every_grad = lax.all_gather(grad_gate.reshape(1, tok_dev), ("seq", "chan"))
    grad_logits = sinkhorn_back(
        dev_ref, every_logit, scaled, row_totals, columns, every_route, every_grad
    )
    router_grad = jnp.einsum("td,et->de", moe_in, grad_logits, precision=HIGH)
    grad_moe_in = gate[:, None] * plain_grad_part + jnp.einsum(
        "et,de->td", grad_logits, router_weight, precision=HIGH
    )
    grad_hidden, moe_gain_grad = moe_back(grad_moe_in)
    grad_hidden = grad_hidden + grad_two

    grad_mix = chan_rows(grad_hidden.astype(bf16))
    grad_gated = jnp.einsum("td,ed->te", grad_mix, out_weight, preferred_element_type=f32)
    out_weight_grad = jnp.einsum("te,td->ed", gated_b, grad_mix, preferred_element_type=f32)
    grad_scan = grad_gated * jax.nn.silu(gate_z)
    grad_gate_z = (grad_gated * scan_out * silu_grad(gate_z)).astype(bf16)
    skip_grad = jnp.sum(grad_scan * mixed, 0)
    gate_weight_grad = jnp.einsum("td,te->de", gathered, grad_gate_z, preferred_element_type=f32)
    early = lax.psum(
        (out_weight_grad.astype(bf16), gate_weight_grad.astype(bf16), skip_grad.astype(bf16)), "seq"
    )
    grad_scan_w = widened(grad_scan)
    back_part, back_sums, back_total = scan.ends(True, step_w, grad_scan_w, breaks, c_out, rates)
    back_every = lax.all_gather(back_total, "seq")
    step_grad, mixed_grad, b_grad, c_grad, rate_grad = scan.grads(
        seq_ref, step_w, mixed_w, breaks, grad_scan_w, b_in, c_out, rates, entry, back_part, back_sums,
        back_every,
    )
    step_grad, mixed_grad = step_grad[:, :channels], mixed_grad[:, :channels]
    mixed_grad = mixed_grad + skip_gain * grad_scan
    a_log_grad = -decay_rates * rate_grad[:, :channels].T
    step_pre_grad = step_grad * jax.nn.sigmoid(step_pre)
    dt_bias_grad = jnp.sum(step_pre_grad, 0)
    dt_weight_grad = jnp.einsum("tr,te->re", low_rank, step_pre_grad, precision=HIGH)
    rank_grad = jnp.einsum("te,re->tr", step_pre_grad, dt_weight, precision=HIGH)
    proj_grad_b = proj_total(jnp.concatenate([rank_grad, b_grad, c_grad], 1)).astype(bf16)
    mixed_grad = mixed_grad + jnp.einsum(
        "tp,ep->te", proj_grad_b, xproj_weight, preferred_element_type=f32
    )
    xproj_grad = jnp.einsum("te,tp->ep", mixed_b, proj_grad_b, preferred_element_type=f32)
    conv_grad = (mixed_grad * silu_grad(conv_pre)).reshape(shape4 + (channels,))
    conv_bias_grad = jnp.sum(conv_grad, (0, 1, 2))
    conv_weight_grad = jnp.stack(
        [
            jnp.sum(conv_grad * masks[offset] * padded[:, offset : offset + steps], (0, 1, 2))
            for offset in range(CONV)
        ]
    )
    padded_grad = 0.0
    for offset in range(CONV):
        padded_grad = padded_grad + jnp.pad(
            conv_weight[offset] * conv_grad * masks[offset],
            ((0, 0), (offset, reach - offset), (0, 0), (0, 0)),
        )
    head_grad = jnp.swapaxes(padded_grad[:, :reach], 0, 1).reshape(
        reach, chan_count * CHUNKS, channels
    )
    from_next = passed_along(head_grad[:, 0], "seq", -1)
    tail_grad = jnp.concatenate([head_grad[:, 1:], from_next[:, None]], 1)
    tail_grad = jnp.swapaxes(tail_grad.reshape(reach, chan_count, CHUNKS, channels), 0, 1)
    inner_grad = padded_grad[:, reach:] + jnp.pad(
        tail_grad, ((0, 0), (steps - reach, 0), (0, 0), (0, 0))
    )
    inner_grad_b = inner_grad.reshape(tok_seq, channels).astype(bf16)
    inner_weight_grad = jnp.einsum("td,te->de", gathered, inner_grad_b, preferred_element_type=f32)
    both_grad = jnp.concatenate([inner_grad_b, grad_gate_z], 1)
    normed_grad = chan_sums(
        lambda rows: jnp.dot(rows[:, :channels], in_weight[0].T, preferred_element_type=f32)
        + jnp.dot(rows[:, channels:], in_weight[1].T, preferred_element_type=f32),
        both_grad,
    )
    residual_grad, norm_gain_grad = norm_back(normed_grad)
    in_grad = from_steps(residual_grad + grad_hidden)

    late = (
        inner_weight_grad, xproj_grad, dt_weight_grad, a_log_grad,
        conv_weight_grad, conv_bias_grad, dt_bias_grad,
    )
    late, early = lax.optimization_barrier((tuple(part.astype(bf16) for part in late), early))
    late = lax.psum(late, "seq")
    (
        inner_weight_grad, xproj_grad, dt_weight_grad, a_log_grad,
        conv_weight_grad, conv_bias_grad, dt_bias_grad,
    ) = (part.astype(f32) for part in late)
    out_weight_grad, gate_weight_grad, skip_grad = (part.astype(f32) for part in early)
    in_weight_grad = jnp.stack([inner_weight_grad, gate_weight_grad])
    norm_gain_grad, moe_gain_grad, router_grad = lax.psum(
        (norm_gain_grad, moe_gain_grad, router_grad), ("seq", "chan")
    )
    return (
        block_out,
        in_grad,
        norm_gain_grad,
        in_weight_grad,
        conv_weight_grad,
        conv_bias_grad,
        xproj_grad,
        dt_weight_grad,
        dt_bias_grad,
        a_log_grad,
        skip_grad,
        out_weight_grad,
        moe_gain_grad,
        router_grad,
        up_grad,
        down_grad,
    )


def solution(mesh):
    in_specs = (
        P(("seq", "chan"), None),
        P(("seq", "chan"), None),
        P(),
        P(),
        P(None, None, "chan"),
        P(None, "chan"),
        P("chan"),
        P("chan", None),
        P(None, "chan"),
        P("chan"),
        P("chan", None),
        P("chan"),
        P("chan", None),
        P(),
        P(),
        P("chan", "seq", None),
        P("chan", "seq", None),
        P(("seq", "chan"), None),
    )
    out_specs = (
        P(("seq", "chan"), None),
        P(("seq", "chan"), None),
        P(),
        P(None, None, "chan"),
        P(None, "chan"),
        P("chan"),
        P("chan", None),
        P(None, "chan"),
        P("chan"),
        P("chan", None),
        P("chan"),
        P("chan", None),
        P(),
        P(),
        P("chan", "seq", None),
        P("chan", "seq", None),
    )
    return jax.shard_map(
        on_device, mesh=mesh, in_specs=in_specs, out_specs=out_specs, check_vma=False
    )
```

time: 4030 us -> 1150 us (0.29)
  local copies, waits for them, and re-layouts: 1070 us -> 51.4 us
  waiting for transfers between devices: 1110 us -> 126 us
  other arithmetic: 536 us -> 67.2 us
  blocking collectives: 835 us -> 529 us
  matrix products: 397 us -> 140 us
  Pallas kernels: 0 us -> 143 us
  starting transfers between devices: 21.1 us -> 70.5 us
    psum x2, waiting for transfers between devices: 973 us -> 50 us  [the longest x1 50 us: on_device(): late = lax.psum(late, 'seq')]
    psum x18 -> x2, blocking collectives: 749 us -> 165 us  [the longest x1 107 us: on_device(): lax.psum((out_weight_grad.astype(bf16), gate_weight_grad.astype(bf16), sk...]
    slice x43 -> x5, local copies, waits for them, and re-layouts: 502 us -> 1.17 us  [the longest x1 1.08 us: on_device(): gate_arrived = to_experts(gate_slots)[:, 0:1]]
    reduce_sum x39 -> x1, other arithmetic: 417 us -> 2.22 us  [on_device(): jnp.sum(conv_grad * masks[offset] * padded[:, offset:offset + steps], (0,...]
    mul x13 -> x2, local copies, waits for them, and re-layouts: 374 us -> 0.17 us  [on_device(): breaks = jnp.any(position[..., None] == starts, axis=-1).astype(f32) * BREAK]
    dot_general x24 -> x29, matrix products: 372 us -> 127 us  [the longest x1 12 us: on_device(): jnp.einsum('sf,df->sd', plain_grad_pre.astype(bf16), full_up, preferred_e...]
    pallas_call x0 -> x6, Pallas kernels: none -> 143 us  [the longest x1 75.1 us: grads(): pl.pallas_call(partial(grads_kernel, self.halves), grid=(self.groups,), i...]
    all_to_all x0 -> x2, blocking collectives: none -> 105 us  [across_experts(): lax.all_to_all(values, 'seq', split_axis=0, concat_axis=0, tiled=True, ax...]
  transfers between devices with their start and end apart: 16 -> 30, of which waited for: 8 -> 13; matrix products, arithmetic and copies ran while one was open for 7% -> 19% of each run, Pallas kernels for 0% -> 11%
where the time goes in v1:
time: 1150 us; the launch traced here: 1140 us
  blocking collectives  529 us (46%)
  Pallas kernels  143 us (12%)
  matrix products  140 us (12%)
  waiting for transfers between devices  126 us (11%)
  starting transfers between devices  70.5 us (6%)
  other arithmetic  67.2 us (6%)
  local copies, waits for them, and re-layouts  51.4 us (4%)
  between operations  15.9 us (1%)
    psum x1, blocking collectives, on_device(): lax.psum((out_weight_grad.astype(bf16), gate_weight_grad.astype(bf16), sk...  107 us
    all_to_all x2, blocking collectives, across_experts(): lax.all_to_all(values, 'seq', split_axis=0, concat_axis=0, tiled=True, ax...  105 us
    all_gather x1, blocking collectives, on_device(): lax.all_gather(route_steps.reshape(1, tok_dev), ('seq', 'chan'))  77.5 us
    pallas_call x1, Pallas kernels, grads(): pl.pallas_call(partial(grads_kernel, self.halves), grid=(self.groups,), i...  75.1 us
    all_gather x1, blocking collectives, on_device(): every_logit = lax.all_gather(logits, ('seq', 'chan'))  71.9 us
    psum x1, blocking collectives, on_device(): lax.psum((norm_gain_grad, moe_gain_grad, router_grad), ('seq', 'chan'))  66.4 us
    psum x1, blocking collectives, on_device(): late = lax.psum(late, 'seq')  58.6 us
    ppermute x10, waiting for transfers between devices, swapped(): lax.ppermute(value, axis, [(source, source ^ bit) for source in range(cou...  50.4 us
  transfers between devices with their start and end apart: 30, of which 13 were waited for; matrix products, arithmetic and copies ran while one was open for 19% of the time, Pallas kernels for 11%

profile of v1, /device:TPU:0, one launch (start us, length us, event | category | flops | bytes accessed | tf_op | source)
XLA Modules:
  0.0 1143.4 jit_solution(8302032620580063011)
XLA Ops:
  17.5 16.2 %collective-permute-done = bf16[320,1152]{1,0:T(8,128)(2,1)S(1)} collective-permute-done((bf16[320,1152]{1,0:T(8,128)(2,1)}, bf16[320,1152]{1,0:T(8,128)(2,1)S(1)}, u32[]{:S(2)}, u32[]{:S(2)}) %collective-permute-start) | collective-permute-done | bytes 737312 | tf_op jit(solution)/shard_map/ppermute | solution.py:34
  35.5 4.6 fusion.8
  53.4 6.6 collective-permute-done.2
  61.1 5.5 compare_select_fusion
  67.5 16.9 %scan_ends.1 = (f32[2,16,8,1152]{3,2,1,0:T(8,128)}, f32[2,8,1152]{2,1,0:T(8,128)}, f32[24,1152]{1,0:T(8,128)}) custom-call(f32[640,1152]{1,0:T(8,128)} %get-tuple-element.127.step_ref, f32[640,1152]{1,0:T(8,128)} %get-tuple-element.102.drive_ref.mixed_ref, f32[640,128]{1,0:T(8,128)} %broadcast_in_dim.22.break_ref, ...), custom_call_target="tpu_custom_call" | custom-call | flops 58982400 | bytes 8847360 | tf_op jit(solution)/shard_map/scan_ends/pallas_call | solution.py:421
  84.5 59.7 %all_to_all.70 = bf16[4,72,3072]{2,1,0:T(8,128)(2,1)} all-to-all(bf16[4,72,3072]{2,1,0:T(8,128)(2,1)} %param.33), channel_id=1, replica_groups={{0,8,16,24},{2,10,18,26},{4,12,20,28},{6,14,22,30},{1,9,17,25},{3,11,19..., dimensions={0} | all-to-all | bytes 3538944 | tf_op jit(solution)/shard_map/all_to_all | solution.py:73
  144.3 45.5 %all_to_all.71 = bf16[4,72,3072]{2,1,0:T(8,128)(2,1)} all-to-all(bf16[4,72,3072]{2,1,0:T(8,128)(2,1)} %param.34), channel_id=1, replica_groups={{0,8,16,24},{2,10,18,26},{4,12,20,28},{6,14,22,30},{1,9,17,25},{3,11,19..., dimensions={0} | all-to-all | bytes 3538944 | tf_op jit(solution)/shard_map/all_to_all | solution.py:73
  190.7 5.9 fusion.25.gate_ref
  196.6 24.1 %scan_outputs.1 = (f32[640,1152]{1,0:T(8,128)}, bf16[640,1152]{1,0:T(8,128)(2,1)}, f32[2,16,8,1152]{3,2,1,0:T(8,128)}) custom-call(s32[1]{0:T(128)} %bitcast.3.place_ref, f32[640,1152]{1,0:T(8,128)} %get-tuple-element.127.step_ref, f32[640,1152]{1,0:T(8,128)} %get-tuple-element.102.drive_ref.mixed_ref, f32[640,128]{1,0:T(8,128)} %broadcast_in_dim.22.break_ref, ...), custom_call_target="tpu_custom_call" | custom-call | flops 82575360 | bytes 8847360 | tf_op jit(solution)/shard_map/scan_outputs/pallas_call | solution.py:434
  220.7 3.3 convolution_convert_fusion.10
  227.5 4.4 all-to-all-start.6
  232.7 11.0 collective-permute-done.3
  243.7 3.2 multiply_reduce_fusion.8
  249.5 71.9 %all-gather.1 = f32[256,320]{1,0:T(8,128)} all-gather(f32[8,320]{1,0:T(8,128)S(1)} %fusion.49), channel_id=3, replica_groups=mesh['seq'=16,'chan'=2] {'seq','chan'}, dimensions={0}, use_global_device_ids=true | all-gather | bytes 337920 | tf_op jit(solution)/shard_map/all_gather | solution.py:681
  321.3 4.8 sinkhorn.1
  328.4 4.3 all-to-all-start.10
  332.7 3.2 convolution_convert_fusion.9
  337.7 4.4 all-to-all-start
  343.8 8.3 all-to-all-done
  352.1 4.0 all-to-all-start.11
  358.4 4.3 all-to-all-done.11
  362.7 4.2 all-to-all-start.1
  367.0 77.5 %all_gather.44.route_ref = s32[32,1,320]{2,1,0:T(1,128)} all-gather(s32[1,1,320]{2,1,0:T(1,128)S(1)} %all_gather_reshape_reshape.3), channel_id=1, replica_groups=mesh['seq'=16,'chan'=2] {'seq','chan'}, dimensions={0}, use_global_device_ids=true | all-gather | bytes 42240 | tf_op jit(solution)/shard_map/all_gather | solution.py:618
  447.9 4.2 all-to-all-start.7
  452.2 9.4 fusion.111
  461.6 10.4 convolution_convert_fusion.7
  471.9 3.3 all-to-all-done.7
  475.3 4.5 all-to-all-start.4
  479.7 6.2 fusion.112
  488.4 12.0 %convolution_convert_fusion.6 = bf16[448,1152]{1,0:T(8,128)(2,1)} fusion(bf16[1152,3072]{1,0:T(8,128)(2,1)} %bitcast.247, f32[448,3072]{1,0:T(8,128)} %fusion.111, f32[448,3072]{1,0:T(8,128)S(1)} %fusion.112), kind=kOutput, calls=%fused_computation.72 | convolution fusion | flops 3198935040 | bytes 19120128 | tf_op jit(solution)/shard_map/sf,df->sd/dot_general | solution.py:693
  500.4 4.2 all-to-all-done.4
  504.7 4.2 all-to-all-start.8
  508.9 11.0 convolution_convert_fusion.1
  519.9 9.9 convolution_convert_fusion
  533.8 4.9 all-to-all-start.5
  538.8 9.5 constant_dynamic-slice_fusion.2
  552.7 4.4 all-to-all-start.9
  560.3 43.0 %all-reduce.5 = f32[10240]{0:T(1024)S(1)} all-reduce(f32[10240]{0:T(1024)S(1)} %dynamic-update-slice), channel_id=6, replica_groups=mesh['seq'=16,'chan'=2] {'seq','chan'}, use_global_device_ids=true, to_apply=%add.5 | all-reduce | flops 10240 | bytes 81920
  604.0 5.3 sinkhorn_back.1
  609.3 3.2 fusion.113
  621.5 14.2 %collective-permute-done.4 = bf16[320,1152]{1,0:T(8,128)(2,1)} collective-permute-done((bf16[320,1152]{1,0:T(8,128)(2,1)}, bf16[320,1152]{1,0:T(8,128)(2,1)}, u32[]{:S(2)}, u32[]{:S(2)}) %collective-permute-start.4) | collective-permute-done | bytes 737312 | tf_op jit(solution)/shard_map/ppermute | solution.py:34
  637.2 7.0 multiply_reduce_fusion
  644.2 17.1 %scan_ends_back.1 = (f32[2,16,8,1152]{3,2,1,0:T(8,128)}, f32[2,8,1152]{2,1,0:T(8,128)}, f32[24,1152]{1,0:T(8,128)}) custom-call(f32[640,1152]{1,0:T(8,128)} %get-tuple-element.127.step_ref, f32[640,1152]{1,0:T(8,128)} %get-tuple-element.98.drive_ref.grad_ref, f32[640,128]{1,0:T(8,128)} %broadcast_in_dim.22.break_ref, ...), custom_call_target="tpu_custom_call" | custom-call | flops 58982400 | bytes 8847360 | tf_op jit(solution)/shard_map/scan_ends_back/pallas_call | solution.py:421
  661.6 4.4 fusion.1
  670.0 3.3 fusion
  677.6 3.9 convolution_convert_fusion.3
  681.5 3.9 convolution_convert_fusion.2
  685.5 106.8 %psum.94 = bf16[1152]{0:T(1024)(128)(2,1)S(1)} all-reduce(bf16[1152]{0:T(1024)(128)(2,1)S(1)} %get-tuple-element.97), channel_id=1, replica_groups=mesh['seq'=16,'chan'=2] {'seq'}, use_global_device_ids=true, to_apply=%region_20.21 | all-reduce | flops 1152 | bytes 4608 | tf_op jit(solution)/shard_map/psum | solution.py:730
  792.3 4.0 fusion.38
  796.3 4.4 all-to-all-start.12
  800.7 4.1 fusion.39
  804.8 75.1 %scan_grads.1 = (f32[640,1152]{1,0:T(8,128)}, f32[640,1152]{1,0:T(8,128)}, f32[640,16]{1,0:T(8,128)}, f32[640,16]{1,0:T(8,128)}, f32[16,1152]{1,0:T(8,128)}) custom-call(s32[1]{0:T(128)} %bitcast.3.place_ref, f32[640,1152]{1,0:T(8,128)} %get-tuple-element.127.step_ref, f32[640,1152]{1,0:T(8,128)} %get-tuple-element.102.drive_ref.mixed_ref, ...), custom_call_target="tpu_custom_call" | custom-call | flops 235929600 | bytes 8847360 | tf_op jit(solution)/shard_map/scan_grads/pallas_call | solution.py:456
  882.1 3.7 fusion.105
  914.4 3.9 convolution_convert_fusion.4
  918.4 58.6 %all-reduce.7 = (bf16[4,1152]{1,0:T(4,128)(2,1)S(1)}, bf16[1152]{0:T(1024)(128)(2,1)S(1)}, bf16[1152]{0:T(1024)(128)(2,1)S(1)}, bf16[1152,16]{0,1:T(8,128)(2,1)S(1)}) all-reduce(bf16[4,1152]{1,0:T(4,128)(2,1)S(1)} %pad_maximum_fusion.6, bf16[1152]{0:T(1024)(128)(2,1)S(1)} %get-tuple-element.65, ...), channel_id=1, replica_groups=mesh['seq'=16,'chan'=2] {'seq'}, use_global_device_ids=true, to_apply=%region_22.23 | all-reduce | flops 25344 | bytes 101376 | tf_op jit(solution)/shard_map/psum | solution.py:791
  980.1 4.5 convert_element_type.322
  984.6 4.4 fusion.29
  988.9 4.4 all-to-all-start.13
  993.4 4.8 multiply_reduce_fusion.6
  1001.7 66.4 %all-reduce.6 = (f32[1152]{0:T(1024)}, f32[1152]{0:T(1024)}, f32[1152,8]{0,1:T(8,128)}) all-reduce(f32[1152]{0:T(1024)S(1)} %get-tuple-element.79, f32[1152]{0:T(1024)S(1)} %get-tuple-element.75, f32[1152,8]{0,1:T(8,128)S(1)} %fusion.46), channel_id=1, replica_groups=mesh['seq'=16,'chan'=2] {'seq','chan'}, use_global_device_ids=true, to_apply=%region_10.11 | all-reduce | flops 11520 | bytes 92160 | tf_op jit(solution)/shard_map/psum | solution.py:798
  1068.1 50.0 %all-reduce.13.cloned.1.call-done = (bf16[1,1152,1152]{2,1,0:T(8,128)(2,1)}, bf16[1152,104]{0,1:T(8,128)(2,1)}, bf16[72,1152]{1,0:T(8,128)(2,1)}) async-done(((bf16[1,1152,1152]{2,1,0:T(8,128)(2,1)}, bf16[1152,104]{0,1:T(8,128)(2,1)}, bf16[72,1152]{1,0:T(8,128)(2,1)}), (bf16[1,1152,1152]{2,1,0:T(8,128)(2,1)}, bf16[1152,104]{0,1:T(8,128)(2,1)}, bf16[72,1152]{1,0:T(8,128)(2,1)})) %all-reduce.13.cloned.1.call-update) | async-done | bytes 3059728 | tf_op jit(solution)/shard_map/psum | solution.py:791
  1121.5 7.4 maximum_convert_fusion
  1128.9 3.8 convert_element_type.332
  1132.7 3.7 convert_element_type.343
  (329 shorter events, 120.4 us)
Async XLA Ops:
  7.2 213.5 %copy-start = (bf16[1152,1152]{1,0:T(8,128)(2,1)S(1)}, bf16[1152,1152]{1,0:T(8,128)(2,1)}, u32[]{:S(2)}) copy-start(bf16[1152,1152]{1,0:T(8,128)(2,1)} %param.30) | copy-start | bytes 7962628
  7.2 9.8 copy-start.76
  7.2 189.3 %all-gather.11.cloned.1.call-start = ((), (), s32[]{:S(2)}) async-start(), calls=%async_computation.14 | async-start | bytes 1880064 | tf_op jit(solution)/shard_map/all_gather | solution.py:668
  11.4 5.6 copy-start.68
  11.4 24.1 %copy-start.65 = (f32[320]{0:T(512)}, f32[320]{0:T(512)S(1)}, u32[]{:S(2)}) copy-start(f32[320]{0:T(512)S(1)} %rsqrt.20) | copy-start | bytes 3844
  14.0 19.6 %collective-permute-start = (bf16[320,1152]{1,0:T(8,128)(2,1)}, bf16[320,1152]{1,0:T(8,128)(2,1)S(1)}, u32[]{:S(2)}, u32[]{:S(2)}) collective-permute-start(bf16[320,1152]{1,0:T(8,128)(2,1)} %multiply_convert_fusion.5), channel_id=1, source_target_pairs={{0,1},{1,0},{2,3},{3,2},{4,5},{5,4},{6,7},{7,6},{8,9},{9,8},{10,11... | collective-permute-start | bytes 2211848 | tf_op jit(solution)/shard_map/ppermute | solution.py:34
  35.5 4.6 copy-start.27
  35.5 4.6 copy-start.30
  35.5 7.6 copy-start.67
  41.8 4.1 collective-permute-start.1
  47.9 4.8 copy-start.48
  50.3 16.3 %copy-start.12 = (bf16[640,1152]{1,0:T(8,128)(2,1)}, bf16[640,1152]{1,0:T(8,128)(2,1)S(1)}, u32[]{:S(2)}) copy-start(bf16[640,1152]{1,0:T(8,128)(2,1)S(1)} %get-tuple-element.103) | copy-start | bytes 4423684
  50.3 10.8 copy-start.45
  50.3 10.8 copy-start.75
  50.9 9.0 collective-permute-start.2
  60.0 6.7 copy-start.21
  84.4 367.7 %all-gather.13.cloned.1.call-start = ((), (), s32[]{:S(2)}) async-start(), calls=%async_computation.15 | async-start | bytes 8847360 | tf_op jit(solution)/shard_map/all_gather | solution.py:101
  144.2 45.6 %copy-start.71 = (f32[1152]{0:T(1024)S(1)}, f32[1152]{0:T(1024)}, u32[]{:S(2)}) copy-start(f32[1152]{0:T(1024)} %param.29) | copy-start | bytes 13828
  144.2 46.2 %copy-start.73 = (s32[320,1]{0,1:T(1,128)S(1)}, s32[320,1]{0,1:T(1,128)}, u32[]{:S(2)}) copy-start(s32[320,1]{0,1:T(1,128)} %param.19) | copy-start | bytes 3844
  144.2 46.5 %copy-start.28 = (bf16[320,1152]{1,0:T(8,128)(2,1)S(1)}, bf16[320,1152]{1,0:T(8,128)(2,1)}, u32[]{:S(2)}) copy-start(bf16[320,1152]{1,0:T(8,128)(2,1)} %copy-done.27) | copy-start | bytes 2211844
  144.2 317.3 %all-gather.15.cloned.1.call-start = ((), (), s32[]{:S(2)}) async-start(), calls=%async_computation.16 | async-start | bytes 8847360 | tf_op jit(solution)/shard_map/all_gather | solution.py:101
  220.7 5.0 copy-start.19
  224.0 19.7 %collective-permute-start.3 = (bf16[320,1152]{1,0:T(8,128)(2,1)}, bf16[320,1152]{1,0:T(8,128)(2,1)}, u32[]{:S(2)}, u32[]{:S(2)}) collective-permute-start(bf16[320,1152]{1,0:T(8,128)(2,1)} %convolution_convert_fusion.10), channel_id=1, source_target_pairs={{0,1},{1,0},{2,3},{3,2},{4,5},{5,4},{6,7},{7,6},{8,9},{9,8},{10,11... | collective-permute-start | bytes 2211848 | tf_op jit(solution)/shard_map/ppermute | solution.py:34
  227.5 100.0 %all-to-all-start.6 = ((bf16[8,56,1152]{2,1,0:T(8,128)(2,1)}), bf16[8,56,1152]{2,1,0:T(8,128)(2,1)}, u32[]{:S(2)}, u32[]{:S(2)}) async-start(bf16[8,56,1152]{2,1,0:T(8,128)(2,1)} %bitcast.235), calls=%async_computation.6 | async-start | bytes 2064384 | tf_op jit(solution)/shard_map/all_to_all | solution.py:82
  232.7 15.4 %copy-start.47 = (f32[1152]{0:T(1024)S(1)}, f32[1152]{0:T(1024)}, u32[]{:S(2)}) copy-start(f32[1152]{0:T(1024)} %param.31) | copy-start | bytes 13828
  232.7 15.4 %copy-start.52 = (f32[1152,8]{0,1:T(8,128)S(1)}, f32[1152,8]{0,1:T(8,128)}, u32[]{:S(2)}) copy-start(f32[1152,8]{0,1:T(8,128)} %param.32) | copy-start | bytes 110596
  328.4 9.3 all-to-all-start.10
  337.7 14.3 %all-to-all-start = ((bf16[8,56,1152]{2,1,0:T(8,128)(2,1)}), bf16[8,56,1152]{2,1,0:T(8,128)(2,1)}, u32[]{:S(2)}, u32[]{:S(2)}) async-start(bf16[8,56,1152]{2,1,0:T(8,128)(2,1)} %bitcast.225), calls=%async_computation | async-start | bytes 2064384 | tf_op jit(solution)/shard_map/all_to_all | solution.py:82
  352.1 10.6 all-to-all-start.11
  356.1 90.7 %copy-start.74 = (f32[1,320]{1,0:T(1,128)S(1)}, f32[1,320]{1,0:T(1,128)}, u32[]{:S(2)}) copy-start(f32[1,320]{1,0:T(1,128)} %get-tuple-element.48) | copy-start | bytes 3844
  362.7 85.2 %all-to-all-start.1 = ((bf16[4,2,56,1152]{3,2,1,0:T(8,128)(2,1)}), bf16[4,2,56,1152]{3,2,1,0:T(8,128)(2,1)}, u32[]{:S(2)}, u32[]{:S(2)}) async-start(bf16[4,2,56,1152]{3,2,1,0:T(8,128)(2,1)} %copy.177), calls=%async_computation.1 | async-start | bytes 2064384 | tf_op jit(solution)/shard_map/all_to_all | solution.py:73
  447.9 27.4 %all-to-all-start.7 = ((bf16[4,2,56,1152]{3,2,1,0:T(8,128)(2,1)}), bf16[4,2,56,1152]{3,2,1,0:T(8,128)(2,1)}, u32[]{:S(2)}, u32[]{:S(2)}) async-start(bf16[4,2,56,1152]{3,2,1,0:T(8,128)(2,1)} %copy.181), calls=%async_computation.7 | async-start | bytes 2064384 | tf_op jit(solution)/shard_map/all_to_all | solution.py:73
  475.3 29.4 %all-to-all-start.4 = ((bf16[4,2,56,1152]{3,2,1,0:T(8,128)(2,1)}), bf16[4,2,56,1152]{3,2,1,0:T(8,128)(2,1)}, u32[]{:S(2)}, u32[]{:S(2)}) async-start(bf16[4,2,56,1152]{3,2,1,0:T(8,128)(2,1)} %bitcast.237), calls=%async_computation.4 | async-start | bytes 2064384 | tf_op jit(solution)/shard_map/all_to_all | solution.py:73
  504.7 29.2 %all-to-all-start.8 = ((bf16[4,2,56,1152]{3,2,1,0:T(8,128)(2,1)}), bf16[4,2,56,1152]{3,2,1,0:T(8,128)(2,1)}, u32[]{:S(2)}, u32[]{:S(2)}) async-start(bf16[4,2,56,1152]{3,2,1,0:T(8,128)(2,1)} %bitcast.236), calls=%async_computation.8 | async-start | bytes 2064384 | tf_op jit(solution)/shard_map/all_to_all | solution.py:73
  533.8 18.8 %all-to-all-start.5 = ((bf16[8,56,1152]{2,1,0:T(8,128)(2,1)}), bf16[8,56,1152]{2,1,0:T(8,128)(2,1)}, u32[]{:S(2)}, u32[]{:S(2)}) async-start(bf16[8,56,1152]{2,1,0:T(8,128)(2,1)} %bitcast.227), calls=%async_computation.5 | async-start | bytes 2064384 | tf_op jit(solution)/shard_map/all_to_all | solution.py:94
  550.4 111.3 %collective-permute-start.8 = (bf16[4,2,72,3072]{3,2,0,1:T(8,128)(2,1)}, bf16[4,2,72,3072]{3,2,0,1:T(8,128)(2,1)}, u32[]{:S(2)}, u32[]{:S(2)}) collective-permute-start(bf16[4,2,72,3072]{3,2,0,1:T(8,128)(2,1)} %bitcast.210), channel_id=1, source_target_pairs={{0,2},{2,0},{4,6},{6,4},{8,10},{10,8},{12,14},{14,12},{16,18},{18,... | collective-permute-start | bytes 10616840 | tf_op jit(solution)/shard_map/ppermute | solution.py:34
  552.7 59.8 %all-to-all-start.9 = ((bf16[8,56,1152]{2,1,0:T(8,128)(2,1)}), bf16[8,56,1152]{2,1,0:T(8,128)(2,1)}, u32[]{:S(2)}, u32[]{:S(2)}) async-start(bf16[8,56,1152]{2,1,0:T(8,128)(2,1)} %bitcast.226), calls=%async_computation.9 | async-start | bytes 2064384 | tf_op jit(solution)/shard_map/all_to_all | solution.py:94
  557.1 247.7 %all-gather.17.cloned.1.call-start = ((), (), s32[]{:S(2)}) async-start(), calls=%async_computation.17 | async-start | bytes 1880064 | tf_op jit(solution)/shard_map/all_gather | solution.py:735
  617.0 18.7 %collective-permute-start.4 = (bf16[320,1152]{1,0:T(8,128)(2,1)}, bf16[320,1152]{1,0:T(8,128)(2,1)}, u32[]{:S(2)}, u32[]{:S(2)}) collective-permute-start(bf16[320,1152]{1,0:T(8,128)(2,1)} %fusion.101), channel_id=1, source_target_pairs={{0,1},{1,0},{2,3},{3,2},{4,5},{5,4},{6,7},{7,6},{8,9},{9,8},{10,11... | collective-permute-start | bytes 2211848 | tf_op jit(solution)/shard_map/ppermute | solution.py:34
  621.3 47.9 %collective-permute-start.10 = (bf16[4,2,72,3072]{3,2,0,1:T(8,128)(2,1)}, bf16[4,2,72,3072]{3,2,0,1:T(8,128)(2,1)}, u32[]{:S(2)}, u32[]{:S(2)}) collective-permute-start(bf16[4,2,72,3072]{3,2,0,1:T(8,128)(2,1)} %bitcast.209), channel_id=1, source_target_pairs={{0,2},{2,0},{4,6},{6,4},{8,10},{10,8},{12,14},{14,12},{16,18},{18,... | collective-permute-start | bytes 10616840 | tf_op jit(solution)/shard_map/ppermute | solution.py:34
  621.5 15.7 %copy-start.13 = (bf16[640,1152]{1,0:T(8,128)(2,1)S(1)}, bf16[640,1152]{1,0:T(8,128)(2,1)}, u32[]{:S(2)}) copy-start(bf16[640,1152]{1,0:T(8,128)(2,1)} %copy-done.12) | copy-start | bytes 4423684
  637.1 7.1 copy-start.33
  637.2 7.1 copy-start.35
  661.4 257.0 %all-reduce.15.cloned.1.call-start = ((), (), s32[]{:S(2)}) async-start(), calls=%async_computation.19 | async-start | bytes 10616832 | tf_op jit(solution)/shard_map/psum | solution.py:730
  667.4 124.9 %collective-permute-start.9 = (bf16[4,1,72,3072]{3,2,0,1:T(8,128)(2,1)}, bf16[4,1,72,3072]{3,2,0,1:T(8,128)(2,1)}, u32[]{:S(2)}, u32[]{:S(2)}) collective-permute-start(bf16[4,1,72,3072]{3,2,0,1:T(8,128)(2,1)} %constant_dynamic-slice_fusion.3), channel_id=1, source_target_pairs={{0,4},{2,6},{4,0},{6,2},{8,12},{10,14},{12,8},{14,10},{16,20},{18,... | collective-permute-start | bytes 5308424 | tf_op jit(solution)/shard_map/ppermute | solution.py:34
  673.3 8.2 copy-start.6
  674.7 126.0 %collective-permute-start.11 = (bf16[4,1,72,3072]{3,2,0,1:T(8,128)(2,1)}, bf16[4,1,72,3072]{3,2,0,1:T(8,128)(2,1)}, u32[]{:S(2)}, u32[]{:S(2)}) collective-permute-start(bf16[4,1,72,3072]{3,2,0,1:T(8,128)(2,1)} %constant_dynamic-slice_fusion), channel_id=1, source_target_pairs={{0,4},{2,6},{4,0},{6,2},{8,12},{10,14},{12,8},{14,10},{16,20},{18,... | collective-permute-start | bytes 5308424 | tf_op jit(solution)/shard_map/ppermute | solution.py:34
  796.3 192.7 %all-to-all-start.12 = ((bf16[4,72,3072]{2,1,0:T(8,128)(2,1)}), bf16[4,72,3072]{2,1,0:T(8,128)(2,1)}, u32[]{:S(2)}, u32[]{:S(2)}) async-start(bf16[4,72,3072]{2,1,0:T(8,128)(2,1)} %fusion.38), calls=%async_computation.12 | async-start | bytes 3538944 | tf_op jit(solution)/shard_map/all_to_all | solution.py:73
  800.6 317.4 %all-reduce.13.cloned.1.call-start = ((), (), s32[]{:S(2)}) async-start(), calls=%async_computation.18 | async-start | bytes 6119424 | tf_op jit(solution)/shard_map/psum | solution.py:791
  882.0 13.3 %copy-start.79 = (f32[640,1152]{1,0:T(8,128)S(1)}, f32[640,1152]{1,0:T(8,128)}, u32[]{:S(2)}) copy-start(f32[640,1152]{1,0:T(8,128)} %get-tuple-element.98.drive_ref.grad_ref) | copy-start | bytes 8847364
  882.1 13.3 %copy-start.80 = (f32[640,1152]{1,0:T(8,128)S(1)}, f32[640,1152]{1,0:T(8,128)}, u32[]{:S(2)}) copy-start(f32[640,1152]{1,0:T(8,128)} %get-tuple-element.56) | copy-start | bytes 8847364
  885.8 9.6 copy-start.18
  888.8 6.6 copy-start.16
  888.8 6.6 copy-start.51
  888.8 6.6 copy-start.72
  888.8 6.5 collective-permute-start.5
  902.9 3.1 collective-permute-start.6
  913.0 80.4 %collective-permute-start.7 = (bf16[320,1152]{1,0:T(8,128)(2,1)}, bf16[320,1152]{1,0:T(8,128)(2,1)}, u32[]{:S(2)}, u32[]{:S(2)}) collective-permute-start(bf16[320,1152]{1,0:T(8,128)(2,1)} %fusion.22), channel_id=1, source_target_pairs={{0,1},{1,0},{2,3},{3,2},{4,5},{5,4},{6,7},{7,6},{8,9},{9,8},{10,11... | collective-permute-start | bytes 2211848 | tf_op jit(solution)/shard_map/ppermute | solution.py:34
  988.9 143.8 %all-to-all-start.13 = ((bf16[4,72,3072]{2,1,0:T(8,128)(2,1)}), bf16[4,72,3072]{2,1,0:T(8,128)(2,1)}, u32[]{:S(2)}, u32[]{:S(2)}) async-start(bf16[4,72,3072]{2,1,0:T(8,128)(2,1)} %fusion.39), calls=%async_computation.13 | async-start | bytes 3538944 | tf_op jit(solution)/shard_map/all_to_all | solution.py:73
  993.3 4.9 copy-start.69
  993.3 4.9 copy-start.5
  993.4 4.9 copy-start.11
  993.4 4.9 copy-start.20
  1128.9 7.5 copy-start.1
  (49 other events, 142.3 us)
Sparse Core Ops, SparseCore 0:
  84.6 53.0 all-gather.10
  144.3 49.6 all-gather.12
  195.6 50.8 all-gather.14
  661.5 43.6 all-gather.16
  710.0 159.5 all-reduce.14
  984.7 133.3 all-reduce.12

commit v2 on v1

--- a/solution.py
+++ b/solution.py
@@ -21,6 +21,7 @@
 LOG2E = 1.4426950408889634
 LN2 = 0.6931471805599453
 BREAK = 1e30
+MESH = pl.DeviceIdType.MESH
 
 
 def passed_along(value, axis, steps):
@@ -65,59 +66,357 @@
     return own, lax.axis_size("seq") // own
 
 
-def across_experts(values):
+def across_experts(values, axis, wait=None):
+    own, share = expert_groups()
+    place = lax.div(lax.axis_index("seq"), share)
+    out = values
+    for d in range(1, own):
+        peer = lax.bitwise_xor(place, d)
+        came = swapped(lax.dynamic_slice_in_dim(values, peer, 1, axis), "seq", d * share)
+        if wait is not None:
+            came = after(came, wait)
+        out = lax.dynamic_update_slice_in_dim(out, came, peer, axis)
+    return out
+
+
+def to_owners(grad):
     own, share = expert_groups()
     if own == 1:
-        return values
+        return grad
     groups = [[k * share + q for k in range(own)] for q in range(share)]
     return lax.all_to_all(
-        values, "seq", split_axis=0, concat_axis=0, tiled=True, axis_index_groups=groups
-    )
-
-
-def to_experts(packed):
+        grad, "seq", split_axis=0, concat_axis=0, tiled=True, axis_index_groups=groups
+    )
+
+
+def expert_rows_early(packed):
     own, share = expert_groups()
     count = lax.axis_size("chan")
     slots, width = packed.shape[1:]
-    arrived = lax.all_to_all(packed, "chan", split_axis=0, concat_axis=0, tiled=True)
-    arrived = jnp.swapaxes(arrived.reshape(count, own, slots, width), 0, 1)
-    return across_experts(arrived).reshape(own * count * slots, width)
-
-
-def to_tokens(rows):
+    if count == 2:
+        place = lax.axis_index("chan")
+        halves = packed.reshape(2, own, slots, width)
+        kept = lax.dynamic_index_in_dim(halves, place, 0, False)
+        came = swapped(lax.dynamic_index_in_dim(halves, 1 - place, 0, False), "chan", 1)
+        first = place == 0
+        arrived = jnp.stack([jnp.where(first, kept, came), jnp.where(first, came, kept)])
+    else:
+        arrived = lax.all_to_all(packed, "chan", split_axis=0, concat_axis=0, tiled=True)
+        arrived = arrived.reshape(count, own, slots, width)
+    return across_experts(arrived, 1).reshape(count * own, slots, width)
+
+
+def expert_rows(ident, *arrays):
+    return exchange(ident, arrays)
+
+
+def whole_expert(weight, start, wait):
     own, share = expert_groups()
-    count = lax.axis_size("chan")
-    width = rows.shape[1]
-    slots = rows.shape[0] // (own * count)
-    back = across_experts(rows.reshape(own, count, slots, width))
-    back = jnp.swapaxes(back, 0, 1).reshape(count * own, slots, width)
-    return lax.all_to_all(back, "chan", split_axis=0, concat_axis=0, tiled=True)
-
-
-def whole_expert(weight):
-    own, share = expert_groups()
-    mine = across_experts(weight)
+    features, hidden = weight.shape[1:]
+    if start is not None:
+        weight = after(weight, start)
+    mine = across_experts(weight, 0, wait)
     groups = [[k * share + q for q in range(share)] for k in range(own)]
     full = lax.all_gather(mine, "seq", axis=1, axis_index_groups=groups)
-    return full.reshape(own * share * weight.shape[1], weight.shape[2])
-
-
-def expert_grad_total(grad):
+    return full.reshape(own * share * features, hidden)
+
+
+def halved(grad, stage):
     own, share = expert_groups()
-    place = lax.rem(lax.axis_index("seq"), share)
-    hidden = grad.shape[1]
-    features = grad.shape[0] // (own * share)
-    held = grad.reshape(own, share, features, hidden)
-    bit = 1
-    while bit < share:
-        pairs = held.reshape(own, held.shape[1] // 2, 2, features, hidden)
-        side = lax.rem(place // bit, 2)
-        sent = lax.dynamic_index_in_dim(pairs, 1 - side, 2, False)
-        kept = lax.dynamic_index_in_dim(pairs, side, 2, False)
-        came = swapped(sent, "seq", bit)
-        held = (kept.astype(jnp.float32) + came.astype(jnp.float32)).astype(grad.dtype)
-        bit *= 2
-    return across_experts(held.reshape(own, features, hidden)).astype(jnp.float32)
+    bit = 1 << stage
+    pairs = grad.reshape(own, grad.shape[1] // 2, 2, *grad.shape[2:])
+    side = lax.rem(lax.div(lax.axis_index("seq"), bit), 2)
+    sent = lax.dynamic_index_in_dim(pairs, 1 - side, 2, False)
+    kept = lax.dynamic_index_in_dim(pairs, side, 2, False)
+    came = swapped(sent, "seq", bit)
+    return (kept.astype(jnp.float32) + came.astype(jnp.float32)).astype(grad.dtype)
+
+
+def after(value, *others):
+    return lax.optimization_barrier((value,) + others)[0]
+
+
+def opposite(place, bit):
+    return place + bit - 2 * bit * lax.rem(lax.div(place, bit), 2)
+
+
+def greet(targets):
+    barrier = pltpu.get_barrier_semaphore()
+    for target in targets:
+        pl.semaphore_signal(barrier, inc=1, device_id=target, device_id_type=MESH)
+    pl.semaphore_wait(barrier, len(targets))
+
+
+def exchange_kernel(own, share, chans, count, *refs):
+    sources, results = refs[:count], refs[count : 2 * count]
+    send_sem, recv_sem, own_sem = refs[2 * count :]
+    seq, chan = lax.axis_index("seq"), lax.axis_index("chan")
+    column = lax.rem(seq, share)
+    me = chan * own + lax.div(seq, share)
+    total = own * chans
+    peers = [lax.rem(me + d, total) for d in range(1, total)]
+    targets = [(lax.rem(peer, own) * share + column, lax.div(peer, own)) for peer in peers]
+    greet(targets)
+    copies = []
+    for k in range(count):
+        for d in range(total - 1):
+            copies.append(
+                pltpu.make_async_remote_copy(
+                    src_ref=sources[k].at[peers[d]],
+                    dst_ref=results[k].at[me],
+                    send_sem=send_sem.at[k, d],
+                    recv_sem=recv_sem.at[k, d],
+                    device_id=targets[d],
+                    device_id_type=MESH,
+                )
+            )
+        copies.append(pltpu.make_async_copy(sources[k].at[me], results[k].at[me], own_sem.at[k]))
+    for copy in copies:
+        copy.start()
+    for copy in copies:
+        copy.wait()
+
+
+def exchange(ident, arrays):
+    own, share = expert_groups()
+    chans, count = lax.axis_size("chan"), len(arrays)
+    anywhere = pl.BlockSpec(memory_space=pl.ANY)
+    others = own * chans - 1
+    return pl.pallas_call(
+        partial(exchange_kernel, own, share, chans, count),
+        in_specs=[anywhere] * count,
+        out_specs=[anywhere] * count,
+        out_shape=[jax.ShapeDtypeStruct(part.shape, part.dtype) for part in arrays],
+        scratch_shapes=[
+            pltpu.SemaphoreType.DMA((count, others)),
+            pltpu.SemaphoreType.DMA((count, others)),
+            pltpu.SemaphoreType.DMA((count,)),
+        ],
+        compiler_params=pltpu.CompilerParams(collective_id=ident, has_side_effects=True),
+        name="expert_rows",
+    )(*arrays)
+
+
+def gather_kernel(devices, chans, own_ref, every_ref, send_sem, recv_sem):
+    me = lax.axis_index("seq") * chans + lax.axis_index("chan")
+    barrier = pltpu.get_barrier_semaphore()
+
+    def target(d):
+        peer = lax.rem(me + d, devices)
+        return (lax.div(peer, chans), lax.rem(peer, chans))
+
+    def copy(d):
+        return pltpu.make_async_remote_copy(
+            src_ref=own_ref,
+            dst_ref=every_ref.at[me],
+            send_sem=send_sem.at[d - 1],
+            recv_sem=recv_sem.at[d - 1],
+            device_id=target(d),
+            device_id_type=MESH,
+        )
+
+    def signal(d, carry):
+        pl.semaphore_signal(barrier, inc=1, device_id=target(d), device_id_type=MESH)
+        return carry
+
+    def start(d, carry):
+        copy(d).start()
+        return carry
+
+    def finish(d, carry):
+        copy(d).wait()
+        return carry
+
+    lax.fori_loop(1, devices, signal, 0)
+    every_ref[me] = own_ref[...]
+    pl.semaphore_wait(barrier, devices - 1)
+    lax.fori_loop(1, devices, start, 0)
+    lax.fori_loop(1, devices, finish, 0)
+
+
+def gathered_everywhere(values):
+    chans = lax.axis_size("chan")
+    devices = lax.axis_size("seq") * chans
+    return pl.pallas_call(
+        partial(gather_kernel, devices, chans),
+        in_specs=[pl.BlockSpec(memory_space=pltpu.VMEM)],
+        out_specs=pl.BlockSpec(memory_space=pltpu.VMEM),
+        out_shape=jax.ShapeDtypeStruct((devices,) + values.shape, values.dtype),
+        scratch_shapes=[
+            pltpu.SemaphoreType.DMA((devices - 1,)),
+            pltpu.SemaphoreType.DMA((devices - 1,)),
+        ],
+        compiler_params=pltpu.CompilerParams(
+            collective_id=3, has_side_effects=True, vmem_limit_bytes=VMEM_LIMIT
+        ),
+        name="gather_small",
+    )(values)
+
+
+def carry_kernel(
+    count, reverse, total_ref, rate_ref, entry_ref, ends_out, ends_in, sums_out, sums_in, ends_sems, sums_sems
+):
+    me = lax.axis_index("seq")
+    bits = [1 << k for k in range(count.bit_length() - 1)]
+    greet([{"seq": opposite(me, bit)} for bit in bits])
+    rates = rate_ref[...]
+    ends, sums = total_ref[:STATE], total_ref[STATE : STATE + 1]
+    before, before_sum = jnp.zeros_like(ends), jnp.zeros_like(sums)
+    for k, bit in enumerate(bits):
+        ends_out[k] = ends.astype(ends_out.dtype)
+        sums_out[k] = sums
+        copies = [
+            pltpu.make_async_remote_copy(
+                src_ref=out.at[k],
+                dst_ref=into.at[k],
+                send_sem=sems.at[0, k],
+                recv_sem=sems.at[1, k],
+                device_id={"seq": opposite(me, bit)},
+                device_id_type=MESH,
+            )
+            for out, into, sems in ((ends_out, ends_in, ends_sems), (sums_out, sums_in, sums_sems))
+        ]
+        for copy in copies:
+            copy.start()
+        for copy in copies:
+            copy.wait()
+        their_ends, their_sums = ends_in[k].astype(jnp.float32), sums_in[k]
+        theirs_first = lax.rem(lax.div(me, bit), 2) == (0 if reverse else 1)
+        before = jnp.where(theirs_first, jnp.exp2(rates * before_sum) * their_ends + before, before)
+        before_sum = jnp.where(theirs_first, before_sum + their_sums, before_sum)
+        ends = jnp.where(
+            theirs_first,
+            jnp.exp2(rates * sums) * their_ends + ends,
+            jnp.exp2(rates * their_sums) * ends + their_ends,
+        )
+        sums = sums + their_sums
+    entry_ref[...] = before
+
+
+def carried(total, rates, reverse):
+    count = lax.axis_size("seq")
+    rounds = count.bit_length() - 1
+    channels = rates.shape[1]
+    vmem = pl.BlockSpec(memory_space=pltpu.VMEM)
+    return pl.pallas_call(
+        partial(carry_kernel, count, reverse),
+        in_specs=[vmem, vmem],
+        out_specs=vmem,
+        out_shape=jax.ShapeDtypeStruct(rates.shape, jnp.float32),
+        scratch_shapes=[
+            pltpu.VMEM((rounds, STATE, channels), jnp.bfloat16),
+            pltpu.VMEM((rounds, STATE, channels), jnp.bfloat16),
+            pltpu.VMEM((rounds, 1, channels), jnp.float32),
+            pltpu.VMEM((rounds, 1, channels), jnp.float32),
+            pltpu.SemaphoreType.DMA((2, rounds)),
+            pltpu.SemaphoreType.DMA((2, rounds)),
+        ],
+        compiler_params=pltpu.CompilerParams(
+            collective_id=5 if reverse else 4, has_side_effects=True, vmem_limit_bytes=VMEM_LIMIT
+        ),
+        name="carry_back" if reverse else "carry",
+    )(total, rates)
+
+
+def sum_kernel(count, places, sizes, *refs):
+    parts, sum_ref = refs[: len(places)], refs[len(places)]
+    held, incoming, send_sem, recv_sem = refs[len(places) + 1 :]
+    me = lax.axis_index("seq")
+    bits = [1 << k for k in range(count.bit_length() - 1)]
+    peers = [{"seq": opposite(me, bit)} for bit in bits]
+    chunks, rows = held.shape[0], held.shape[1]
+    rounds = len(bits)
+    barrier = pltpu.get_barrier_semaphore()
+    for peer in peers:
+        pl.semaphore_signal(barrier, inc=1, device_id=peer, device_id_type=MESH)
+    for c in range(chunks):
+        for part, place, size in zip(parts, places, sizes):
+            low, high = max(place, c * rows), min(place + size, (c + 1) * rows)
+            if low < high:
+                held[c, low - c * rows : high - c * rows] = part[low - place : high - place].astype(held.dtype)
+        used = max(place + size for place, size in zip(places, sizes))
+        if used < (c + 1) * rows:
+            low = max(used - c * rows, 0)
+            held[c, low:] = jnp.zeros((rows - low, held.shape[2]), held.dtype)
+    pl.semaphore_wait(barrier, rounds)
+
+    sides = [lax.rem(lax.div(me, bit), 2) for bit in bits]
+    lows, lengths = [0], [rows]
+    for side in sides:
+        lengths.append(lengths[-1] // 2)
+        lows.append(lows[-1] + side * lengths[-1])
+
+    def span(low, length):
+        return pl.ds(pl.multiple_of(low, 16), length)
+
+    def copy(c, step):
+        if step < rounds:
+            k = step
+            other = lows[k] + (1 - sides[k]) * lengths[k + 1]
+            source = held.at[c, span(other, lengths[k + 1])]
+            target = incoming.at[c, pl.ds(rows - lengths[k], lengths[k + 1])]
+        else:
+            k = 2 * rounds - 1 - step
+            here = span(lows[k + 1], lengths[k + 1])
+            source, target = sum_ref.at[c, here], sum_ref.at[c, here]
+        return pltpu.make_async_remote_copy(
+            src_ref=source,
+            dst_ref=target,
+            send_sem=send_sem.at[c, step],
+            recv_sem=recv_sem.at[c, step],
+            device_id=peers[k],
+            device_id_type=MESH,
+        )
+
+    copy(0, 0).start()
+    for turn in range(2 * rounds + chunks - 1):
+        if turn + 1 < chunks:
+            copy(turn + 1, 0).start()
+        for c in range(max(0, turn - 2 * rounds + 1), min(chunks, turn + 1)):
+            step = turn - c
+            copy(c, step).wait()
+            if step < rounds:
+                kept = span(lows[step + 1], lengths[step + 1])
+                came = incoming[c, pl.ds(rows - lengths[step], lengths[step + 1])]
+                total = held[c, kept].astype(jnp.float32) + came.astype(jnp.float32)
+                if step < rounds - 1:
+                    held[c, kept] = total.astype(held.dtype)
+                else:
+                    sum_ref[c, kept] = total.astype(sum_ref.dtype)
+            if step < 2 * rounds - 1:
+                copy(c, step + 1).start()
+
+
+def summed(parts):
+    count = lax.axis_size("seq")
+    rounds = count.bit_length() - 1
+    width = parts[0].shape[1]
+    sizes = [part.shape[0] for part in parts]
+    places, used = [], 0
+    for size in sizes:
+        places.append(used)
+        used += -(-size // 16) * 16
+    chunk = 16 * count * max(1, 48 // count)
+    chunks = -(-used // chunk)
+    vmem = pl.BlockSpec(memory_space=pltpu.VMEM)
+    padded = [jnp.pad(part, ((0, -part.shape[0] % 16), (0, 0))) for part in parts]
+    total = pl.pallas_call(
+        partial(sum_kernel, count, places, [part.shape[0] for part in padded]),
+        in_specs=[vmem] * len(parts),
+        out_specs=vmem,
+        out_shape=jax.ShapeDtypeStruct((chunks, chunk, width), jnp.bfloat16),
+        scratch_shapes=[
+            pltpu.VMEM((chunks, chunk, width), jnp.bfloat16),
+            pltpu.VMEM((chunks, chunk, width), jnp.bfloat16),
+            pltpu.SemaphoreType.DMA((chunks, 2 * rounds)),
+            pltpu.SemaphoreType.DMA((chunks, 2 * rounds)),
+        ],
+        compiler_params=pltpu.CompilerParams(
+            collective_id=6, has_side_effects=True, vmem_limit_bytes=VMEM_LIMIT
+        ),
+        name="sum_late",
+    )(*padded).reshape(chunks * chunk, width)
+    return [total[place : place + size].astype(jnp.float32) for place, size in zip(places, sizes)]
 
 
 def to_steps(values):
@@ -130,6 +429,20 @@
     rows = values.shape[0]
     parts = values.reshape((rows // CHUNKS, CHUNKS) + values.shape[1:])
     return jnp.swapaxes(parts, 0, 1).reshape(values.shape)
+
+
+def stacked(*parts):
+    rows = sum(part.shape[0] for part in parts)
+    whole = jnp.concatenate([part.astype(jnp.bfloat16) for part in parts], 0)
+    return jnp.pad(whole, ((0, -rows % 16), (0, 0)))
+
+
+def unstacked(whole, parts):
+    out, first = [], 0
+    for part in parts:
+        out.append(whole[first : first + part.shape[0]].astype(jnp.float32))
+        first += part.shape[0]
+    return out
 
 
 def norm_apply(values, gain):
@@ -225,24 +538,9 @@
     tot_ref[STATE:, :] = total[0]
 
 
-def joined_over_devices(place_ref, all_ref, rate_ref, reverse):
-    count = all_ref.shape[0]
-    place = place_ref[0]
-    rates = rate_ref[...]
-
-    def turn(k, state):
-        source = count - 1 - k if reverse else k
-        part = all_ref[source]
-        reached = source > place if reverse else source < place
-        new = jnp.exp2(rates * part[STATE : STATE + 1]) * state + part[:STATE]
-        return jnp.where(reached, new, state)
-
-    return lax.fori_loop(0, count, turn, jnp.zeros((STATE, LANES), jnp.float32))
-
-
 def outputs_kernel(
-    halves, place_ref, step_ref, mixed_ref, break_ref, b_ref, c_ref, rate_ref, part_ref, sum_ref, all_ref,
-    skip_ref, gate_ref, scan_ref, gated_ref, entry_ref, b_wide, c_wide, device,
+    halves, step_ref, mixed_ref, break_ref, b_ref, c_ref, rate_ref, part_ref, sum_ref, device,
+    skip_ref, gate_ref, scan_ref, gated_ref, entry_ref, b_wide, c_wide,
 ):
     rows = step_ref.shape[0]
     steps = rows // (halves * CHUNKS)
@@ -253,7 +551,6 @@
         spread(c_wide, c_ref)
 
     rates = [full(rate_ref[n : n + 1, :]) for n in range(STATE)]
-    device[...] = joined_over_devices(place_ref, all_ref, rate_ref, False)
 
     def half(h, carry):
         state = []
@@ -289,9 +586,8 @@
 
 
 def grads_kernel(
-    halves, place_ref, step_ref, mixed_ref, break_ref, grad_ref, b_ref, c_ref, rate_ref, entry_ref, part_ref,
-    sum_ref, all_ref, step_out, mixed_out, b_out, c_out, rate_out, b_wide, c_wide, b_sum, c_sum, decays,
-    states, device,
+    halves, step_ref, mixed_ref, break_ref, grad_ref, b_ref, c_ref, rate_ref, entry_ref, part_ref, sum_ref,
+    device, step_out, mixed_out, b_out, c_out, rate_out, b_wide, c_wide, b_sum, c_sum, decays, states,
 ):
     rows = step_ref.shape[0]
     steps = rows // (halves * CHUNKS)
@@ -305,7 +601,6 @@
         b_sum[...] = jnp.zeros_like(b_sum)
         c_sum[...] = jnp.zeros_like(c_sum)
 
-    device[...] = joined_over_devices(place_ref, all_ref, rate_ref, True)
     zero = jnp.zeros((CHUNKS, LANES), jnp.float32)
 
     for first in (0, block):
@@ -384,8 +679,8 @@
 
 
 class Scan:
-    def __init__(self, rows, channels, halves, seq):
-        self.rows, self.channels, self.halves, self.seq = rows, channels, halves, seq
+    def __init__(self, rows, channels, halves):
+        self.rows, self.channels, self.halves = rows, channels, halves
         self.groups = channels // LANES
         row_spec = pl.BlockSpec((rows, LANES), lambda g: (0, g))
         fixed = lambda *shape: pl.BlockSpec(shape, lambda g: (0,) * len(shape))
@@ -396,15 +691,12 @@
         self.part_spec = pl.BlockSpec((halves, STATE, CHUNKS, LANES), lambda g: (0, 0, 0, g))
         self.sum_spec = pl.BlockSpec((halves, CHUNKS, LANES), lambda g: (0, 0, g))
         self.tot_spec = pl.BlockSpec((STATE + CHUNKS, LANES), lambda g: (0, g))
-        self.all_spec = pl.BlockSpec((seq, STATE + CHUNKS, LANES), lambda g: (0, 0, g))
         self.skip_spec = pl.BlockSpec((1, LANES), lambda g: (0, g))
-        self.place_spec = pl.BlockSpec(memory_space=pltpu.SMEM)
         self.row_f32 = jax.ShapeDtypeStruct((rows, channels), jnp.float32)
         self.part_f32 = jax.ShapeDtypeStruct((halves, STATE, CHUNKS, channels), jnp.float32)
         self.sum_f32 = jax.ShapeDtypeStruct((halves, CHUNKS, channels), jnp.float32)
         self.tot_f32 = jax.ShapeDtypeStruct((STATE + CHUNKS, channels), jnp.float32)
         self.wide = pltpu.VMEM((STATE, rows, LANES), jnp.float32)
-        self.device = pltpu.VMEM((STATE, LANES), jnp.float32)
 
     def params(self):
         return pltpu.CompilerParams(
@@ -430,13 +722,13 @@
             name="scan_ends_back" if reverse else "scan_ends",
         )(step, drive, breaks, maps, rates)
 
-    def outputs(self, place, step, mixed, breaks, b_in, c_out, rates, part, sums, every, skip, gate):
+    def outputs(self, step, mixed, breaks, b_in, c_out, rates, part, sums, device, skip, gate):
         return pl.pallas_call(
             partial(outputs_kernel, self.halves),
             grid=(self.groups,),
             in_specs=[
-                self.place_spec, self.row_spec, self.row_spec, self.break_spec, self.map_spec, self.map_spec,
-                self.rate_spec, self.part_spec, self.sum_spec, self.all_spec, self.skip_spec, self.row_spec,
+                self.row_spec, self.row_spec, self.break_spec, self.map_spec, self.map_spec, self.rate_spec,
+                self.part_spec, self.sum_spec, self.rate_spec, self.skip_spec, self.row_spec,
             ],
             out_specs=[self.row_spec, self.row_spec, self.part_spec],
             out_shape=[
@@ -444,21 +736,21 @@
                 jax.ShapeDtypeStruct((self.rows, self.channels), jnp.bfloat16),
                 self.part_f32,
             ],
-            scratch_shapes=[self.wide, self.wide, self.device],
+            scratch_shapes=[self.wide, self.wide],
             compiler_params=self.params(),
             cost_estimate=self.cost(7),
             name="scan_outputs",
-        )(place, step, mixed, breaks, b_in, c_out, rates, part, sums, every, skip, gate)
-
-    def grads(self, place, step, mixed, breaks, grad, b_in, c_out, rates, entry, part, sums, every):
+        )(step, mixed, breaks, b_in, c_out, rates, part, sums, device, skip, gate)
+
+    def grads(self, step, mixed, breaks, grad, b_in, c_out, rates, entry, part, sums, device):
         steps = self.rows // (self.halves * CHUNKS)
         block = STATE // 2
         return pl.pallas_call(
             partial(grads_kernel, self.halves),
             grid=(self.groups,),
             in_specs=[
-                self.place_spec, self.row_spec, self.row_spec, self.break_spec, self.row_spec, self.map_spec,
-                self.map_spec, self.rate_spec, self.part_spec, self.part_spec, self.sum_spec, self.all_spec,
+                self.row_spec, self.row_spec, self.break_spec, self.row_spec, self.map_spec, self.map_spec,
+                self.rate_spec, self.part_spec, self.part_spec, self.sum_spec, self.rate_spec,
             ],
             out_specs=[self.row_spec, self.row_spec, self.map_spec, self.map_spec, self.rate_spec],
             out_shape=[
@@ -472,12 +764,11 @@
                 self.wide, self.wide, self.wide, self.wide,
                 pltpu.VMEM((steps, block, CHUNKS, LANES), jnp.float32),
                 pltpu.VMEM((steps + 1, block, CHUNKS, LANES), jnp.float32),
-                self.device,
             ],
             compiler_params=self.params(),
             cost_estimate=self.cost(20),
             name="scan_grads",
-        )(place, step, mixed, breaks, grad, b_in, c_out, rates, entry, part, sums, every)
+        )(step, mixed, breaks, grad, b_in, c_out, rates, entry, part, sums, device)
 
 
 def over_tokens(values):
@@ -500,10 +791,8 @@
     gate_ref[...] = EXPERTS * jnp.sum(jnp.where(ids == route_ref[...], own, 0.0), 0, keepdims=True)
 
 
-def sinkhorn_back_kernel(place_ref, logit_ref, scaled_ref, row_ref, column_ref, route_ref, grad_ref, out_ref, held):
-    shape = logit_ref.shape
-    ids = lax.broadcasted_iota(jnp.int32, shape, 1)
-    grad = jnp.where(ids == route_ref[...], EXPERTS * grad_ref[...], 0.0)
+def sinkhorn_back_kernel(place_ref, logit_ref, scaled_ref, row_ref, column_ref, grad_ref, out_ref, held):
+    grad = grad_ref[...]
     for sweep in reversed(range(SINK)):
         scaled, row = scaled_ref[sweep], row_ref[sweep]
         inner = jnp.sum(grad * (scaled / row), 1, keepdims=True)
@@ -537,17 +826,17 @@
     )(place, logits, routes)
 
 
-def sinkhorn_back(place, logits, scaled, rows, columns, routes, grad):
+def sinkhorn_back(place, logits, scaled, rows, columns, grad):
     devices, experts, tokens = logits.shape
     return pl.pallas_call(
         sinkhorn_back_kernel,
-        in_specs=in_vmem(6),
+        in_specs=in_vmem(5),
         out_specs=in_vmem(1)[1],
         out_shape=jax.ShapeDtypeStruct((experts, tokens), jnp.float32),
         scratch_shapes=[pltpu.VMEM(logits.shape, jnp.float32)],
         compiler_params=pltpu.CompilerParams(vmem_limit_bytes=VMEM_LIMIT),
         name="sinkhorn_back",
-    )(place, logits, scaled, rows, columns, routes, grad)
+    )(place, logits, scaled, rows, columns, grad)
 
 
 def on_device(
@@ -571,9 +860,8 @@
     out_grad,
 ):
     tok_dev, model_width = block_in.shape
-    chan_count, seq_count = lax.axis_size("chan"), lax.axis_size("seq")
+    chan_count = lax.axis_size("chan")
     chan_place, seq_place = lax.axis_index("chan"), lax.axis_index("seq")
-    seq_ref = seq_place.astype(jnp.int32).reshape(1)
     dev_ref = (seq_place * chan_count + chan_place).astype(jnp.int32).reshape(1)
     steps = tok_dev // CHUNKS
     tok_seq = tok_dev * chan_count
@@ -589,7 +877,7 @@
     counts = jnp.dot((col_ids <= row_ids).astype(bf16), chosen, preferred_element_type=f32)
     rank = (jnp.sum(counts * chosen.astype(f32), 1) - 1.0).astype(jnp.int32)
     capacity = tok_dev * 5 // (4 * EXPERTS) + 1
-    capacity = -(-capacity // 8) * 8
+    capacity = -(-capacity // 16) * 16
     slot = to_steps(route_col * capacity + rank)
     route_steps = to_steps(route_col)
     slot_ids = lax.broadcasted_iota(jnp.int32, (1, EXPERTS * capacity), 1)
@@ -612,10 +900,6 @@
     residual = block_steps.astype(f32)
     normed, norm_back = jax.vjp(norm_apply, residual, norm_gain)
     gathered = chan_rows(normed.astype(bf16))
-    full_up = whole_expert(up_weight)
-    full_down = whole_expert(down_weight)
-    grad_arrived = to_experts(pack(grad_steps))
-    every_route = lax.all_gather(route_steps.reshape(1, tok_dev), ("seq", "chan"))
 
     inner_b = jnp.dot(gathered, in_weight[0], preferred_element_type=f32).astype(bf16)
     gate_z = jnp.dot(gathered, in_weight[1], preferred_element_type=f32)
@@ -658,19 +942,22 @@
         pads[axis] = (0, more)
         return jnp.pad(values, pads)
 
-    scan = Scan(tok_seq, padded_channels, chan_count, seq_count)
+    scan = Scan(tok_seq, padded_channels, chan_count)
     decay_rates = jnp.exp(a_log)
     rates = widened((-LOG2E * decay_rates).T)
     breaks = jnp.any(position[..., None] == starts, axis=-1).astype(f32) * BREAK
     breaks = jnp.broadcast_to(breaks.reshape(tok_seq, 1), (tok_seq, LANES))
     step_w, mixed_w = widened(step_size), widened(mixed)
     part, sums, total = scan.ends(False, step_w, mixed_w, breaks, b_in, rates)
-    every = lax.all_gather(total, "seq")
+    device_entry = carried(total, rates, False)
+    full_up = whole_expert(up_weight, None, device_entry)
+    grad_arrived = expert_rows_early(after(pack(grad_steps), device_entry)).reshape(-1, model_width)
     scan_out, gated_b, entry = scan.outputs(
-        seq_ref, step_w, mixed_w, breaks, b_in, c_out, rates, part, sums, every,
+        step_w, mixed_w, breaks, b_in, c_out, rates, part, sums, device_entry,
         widened(skip_gain[None]), widened(gate_z),
     )
     scan_out, gated_b = scan_out[:, :channels], gated_b[:, :channels]
+    full_down = whole_expert(down_weight, device_entry, gated_b)
 
     mixer_rows = chan_sums(
         lambda rows: jnp.dot(rows, out_weight, preferred_element_type=f32), gated_b
@@ -678,13 +965,17 @@
     hidden_one = residual + mixer_rows
     moe_in, moe_back = jax.vjp(norm_apply, hidden_one, moe_gain)
     logits = jnp.einsum("td,de->et", moe_in, router_weight, precision=HIGH)
-    every_logit = lax.all_gather(logits, ("seq", "chan"))
+    every_logit = gathered_everywhere(logits)
     gate_row, scaled, row_totals, columns = sinkhorn(
         dev_ref, every_logit, route_steps.reshape(1, tok_dev)
     )
     gate = gate_row.reshape(tok_dev)
 
-    arrived = to_experts(pack(moe_in.astype(bf16)))
+    gate_slots = jnp.einsum("ts,t->s", placer.astype(f32), gate, precision=HIGH)
+    gate_slots = jnp.pad(gate_slots.reshape(EXPERTS, 1, capacity), ((0, 0), (0, 7), (0, LANES - capacity)))
+    arrived, gate_arrived = expert_rows(1, pack(moe_in.astype(bf16)), gate_slots)
+    arrived = arrived.reshape(-1, model_width)
+    gate_arrived = gate_arrived[:, 0, :capacity].reshape(-1, 1)
     pre = jnp.dot(arrived, full_up, preferred_element_type=f32)
     act_b = jax.nn.gelu(pre, approximate=True).astype(bf16)
     expert_out = jnp.einsum("sf,df->sd", act_b, full_down, preferred_element_type=f32).astype(bf16)
@@ -693,27 +984,38 @@
     grad_rows_in = jnp.einsum(
         "sf,df->sd", plain_grad_pre.astype(bf16), full_up, preferred_element_type=f32
     ).astype(bf16)
-    expert_tok = unpack(to_tokens(expert_out))
-    plain_grad_part = unpack(to_tokens(grad_rows_in))
-
-    gate_slots = jnp.einsum("ts,t->s", placer.astype(f32), gate, precision=HIGH)
-    gate_slots = jnp.broadcast_to(gate_slots.reshape(EXPERTS, capacity, 1), (EXPERTS, capacity, LANES))
-    gate_arrived = to_experts(gate_slots)[:, 0:1]
+    blocks = (EXPERTS, capacity, model_width)
+
     grad_gated_rows = (grad_arrived.astype(f32) * gate_arrived).astype(bf16)
     grad_pre_b = (plain_grad_pre * gate_arrived).astype(bf16)
     down_part = jnp.einsum("sd,sf->df", grad_gated_rows, act_b, preferred_element_type=f32)
     up_part = jnp.einsum("sd,sf->df", arrived, grad_pre_b, preferred_element_type=f32)
-    down_grad = expert_grad_total(down_part.astype(bf16))
-    up_grad = expert_grad_total(up_part.astype(bf16))
+    own, share = expert_groups()
+    expert_grads = [
+        halved(part.astype(bf16).reshape(own, share, -1, part.shape[1]), 0) for part in (up_part, down_part)
+    ]
+    expert_back, grad_back = expert_rows(
+        2, after(expert_out, *expert_grads).reshape(blocks), grad_rows_in.reshape(blocks)
+    )
+    for stage in range(1, share.bit_length() - 1):
+        expert_grads = [halved(part, stage) for part in expert_grads]
+    expert_tok = unpack(after(expert_back, *expert_grads))
+    plain_grad_part = unpack(grad_back)
+    up_part, down_part = expert_grads
+    up_grad = to_owners(after(up_part.reshape(own, *up_part.shape[2:]), expert_back))
 
     block_out = from_steps((hidden_one + gate[:, None] * expert_tok).astype(bf16))
     grad_two = grad_steps.astype(f32)
     grad_gate = jnp.sum(expert_tok * grad_two, 1)
-    every_grad = lax.all_gather(grad_gate.reshape(1, tok_dev), ("seq", "chan"))
+    grad_probs = jnp.where(
+        route_steps[None] == lax.broadcasted_iota(jnp.int32, (EXPERTS, 1), 0),
+        EXPERTS * grad_gate[None],
+        0.0,
+    )
     grad_logits = sinkhorn_back(
-        dev_ref, every_logit, scaled, row_totals, columns, every_route, every_grad
-    )
-    router_grad = jnp.einsum("td,et->de", moe_in, grad_logits, precision=HIGH)
+        dev_ref, every_logit, scaled, row_totals, columns, gathered_everywhere(grad_probs)
+    )
+    router_grad = jnp.einsum("td,et->ed", moe_in, grad_logits, precision=HIGH)
     grad_moe_in = gate[:, None] * plain_grad_part + jnp.einsum(
         "et,de->td", grad_logits, router_weight, precision=HIGH
     )
@@ -727,19 +1029,20 @@
     grad_gate_z = (grad_gated * scan_out * silu_grad(gate_z)).astype(bf16)
     skip_grad = jnp.sum(grad_scan * mixed, 0)
     gate_weight_grad = jnp.einsum("td,te->de", gathered, grad_gate_z, preferred_element_type=f32)
-    early = lax.psum(
-        (out_weight_grad.astype(bf16), gate_weight_grad.astype(bf16), skip_grad.astype(bf16)), "seq"
-    )
+    gains = jnp.concatenate([moe_gain_grad[None], router_grad], 0)
+    gains = lax.psum(gains, "chan") if chan_count != 2 else gains + swapped(gains, "chan", 1)
     grad_scan_w = widened(grad_scan)
     back_part, back_sums, back_total = scan.ends(True, step_w, grad_scan_w, breaks, c_out, rates)
-    back_every = lax.all_gather(back_total, "seq")
+    back_entry = carried(after(back_total, up_grad), rates, True)
+    down_grad = to_owners(after(down_part.reshape(own, *down_part.shape[2:]), back_entry))
     step_grad, mixed_grad, b_grad, c_grad, rate_grad = scan.grads(
-        seq_ref, step_w, mixed_w, breaks, grad_scan_w, b_in, c_out, rates, entry, back_part, back_sums,
-        back_every,
-    )
+        step_w, mixed_w, breaks, grad_scan_w, b_in, c_out, rates, entry, back_part, back_sums,
+        back_entry,
+    )
+    step_grad = after(step_grad, down_grad)
     step_grad, mixed_grad = step_grad[:, :channels], mixed_grad[:, :channels]
     mixed_grad = mixed_grad + skip_gain * grad_scan
-    a_log_grad = -decay_rates * rate_grad[:, :channels].T
+    a_log_rows = -decay_rates.T * rate_grad[:, :channels]
     step_pre_grad = step_grad * jax.nn.sigmoid(step_pre)
     dt_bias_grad = jnp.sum(step_pre_grad, 0)
     dt_weight_grad = jnp.einsum("tr,te->re", low_rank, step_pre_grad, precision=HIGH)
@@ -748,7 +1051,7 @@
     mixed_grad = mixed_grad + jnp.einsum(
         "tp,ep->te", proj_grad_b, xproj_weight, preferred_element_type=f32
     )
-    xproj_grad = jnp.einsum("te,tp->ep", mixed_b, proj_grad_b, preferred_element_type=f32)
+    xproj_rows = jnp.einsum("te,tp->pe", mixed_b, proj_grad_b, preferred_element_type=f32)
     conv_grad = (mixed_grad * silu_grad(conv_pre)).reshape(shape4 + (channels,))
     conv_bias_grad = jnp.sum(conv_grad, (0, 1, 2))
     conv_weight_grad = jnp.stack(
@@ -783,21 +1086,29 @@
     residual_grad, norm_gain_grad = norm_back(normed_grad)
     in_grad = from_steps(residual_grad + grad_hidden)
 
-    late = (
-        inner_weight_grad, xproj_grad, dt_weight_grad, a_log_grad,
-        conv_weight_grad, conv_bias_grad, dt_bias_grad,
-    )
-    late, early = lax.optimization_barrier((tuple(part.astype(bf16) for part in late), early))
-    late = lax.psum(late, "seq")
+    norm_rows = norm_gain_grad[None]
+    norm_rows = lax.psum(norm_rows, "chan") if chan_count != 2 else norm_rows + swapped(norm_rows, "chan", 1)
+    pieces = (
+        xproj_rows, dt_weight_grad, a_log_rows, conv_weight_grad, conv_bias_grad[None], dt_bias_grad[None],
+        skip_grad[None], norm_rows.reshape(-1, channels), gains.reshape(-1, channels),
+    )
+    bounds = [sum(part.shape[0] for part in pieces[: k + 1]) for k in range(len(pieces) - 1)]
+    inner_weight_grad, gate_weight_grad, out_weight_grad, small = summed(
+        [
+            inner_weight_grad.astype(bf16), gate_weight_grad.astype(bf16),
+            out_weight_grad.astype(bf16).reshape(-1, channels), jnp.concatenate(pieces, 0),
+        ]
+    )
     (
-        inner_weight_grad, xproj_grad, dt_weight_grad, a_log_grad,
-        conv_weight_grad, conv_bias_grad, dt_bias_grad,
-    ) = (part.astype(f32) for part in late)
-    out_weight_grad, gate_weight_grad, skip_grad = (part.astype(f32) for part in early)
+        xproj_rows, dt_weight_grad, a_log_rows, conv_weight_grad, conv_bias_grad, dt_bias_grad, skip_grad,
+        norm_rows, gains,
+    ) = jnp.split(small, bounds, 0)
+    out_weight_grad = out_weight_grad.reshape(channels, model_width)
+    norm_gain_grad, gains = norm_rows.reshape(-1), gains.reshape(-1, model_width)
+    xproj_grad, a_log_grad = xproj_rows.T, a_log_rows.T
+    conv_bias_grad, dt_bias_grad, skip_grad = conv_bias_grad[0], dt_bias_grad[0], skip_grad[0]
+    moe_gain_grad, router_grad = gains[0], gains[1:].T
     in_weight_grad = jnp.stack([inner_weight_grad, gate_weight_grad])
-    norm_gain_grad, moe_gain_grad, router_grad = lax.psum(
-        (norm_gain_grad, moe_gain_grad, router_grad), ("seq", "chan")
-    )
     return (
         block_out,
         in_grad,
@@ -813,8 +1124,8 @@
         out_weight_grad,
         moe_gain_grad,
         router_grad,
-        up_grad,
-        down_grad,
+        up_grad.astype(f32),
+        down_grad.astype(f32),
     )
 
 

time: 1150 us -> 829 us (0.72)
  blocking collectives: 529 us -> 0 us
  Pallas kernels: 143 us -> 447 us
  waiting for transfers between devices: 126 us -> 74.5 us
  starting transfers between devices: 70.5 us -> 43.5 us
  matrix products: 140 us -> 121 us
    pallas_call x1 -> x8, Pallas kernels: 5.26 us -> 312 us  [the longest x1 122 us: summed(): pl.pallas_call(partial(sum_kernel, count, places, [part.shape[0] for part...]
    psum x3 -> x0, blocking collectives: 232 us -> none  [the longest x1 107 us: on_device(): lax.psum((out_weight_grad.astype(bf16), gate_weight_grad.astype(bf16), sk...]
    all_gather x2 -> x0, blocking collectives: 149 us -> none  [the longest x1 77.5 us: on_device(): lax.all_gather(route_steps.reshape(1, tok_dev), ('seq', 'chan'))]
    all_to_all x2 -> x0, blocking collectives: 105 us -> none  [across_experts(): lax.all_to_all(values, 'seq', split_axis=0, concat_axis=0, tiled=True, ax...]
    psum x2 -> x0, waiting for transfers between devices: 50 us -> none  [the longest x1 50 us: on_device(): late = lax.psum(late, 'seq')]
    unnamed x1 -> x0, blocking collectives: 43 us -> none
    all_to_all x12 -> x2, starting transfers between devices: 52.4 us -> 10.8 us  [to_owners(): lax.all_to_all(grad, 'seq', split_axis=0, concat_axis=0, tiled=True, axis...]
    ppermute x10 -> x22, waiting for transfers between devices: 50.4 us -> 74.2 us  [swapped(): lax.ppermute(value, axis, [(source, source ^ bit) for source in range(cou...]
  transfers between devices with their start and end apart: 30 -> 28, of which waited for: 13 -> 9; matrix products, arithmetic and copies ran while one was open for 19% -> 19% of each run, Pallas kernels for 11% -> 38%
where the time goes in v2:
time: 829 us; the launch traced here: 819 us
  Pallas kernels  447 us (54%)
  matrix products  121 us (15%)
  waiting for transfers between devices  74.5 us (9%)
  local copies, waits for them, and re-layouts  60.5 us (7%)
  other arithmetic  56.2 us (7%)
  starting transfers between devices  43.5 us (5%)
  between operations  16.2 us (2%)
    pallas_call x1, Pallas kernels, summed(): pl.pallas_call(partial(sum_kernel, count, places, [part.shape[0] for part...  122 us
    pallas_call x2, Pallas kernels, exchange(): pl.pallas_call(partial(exchange_kernel, own, share, chans, count), in_spe...  85.1 us
    ppermute x22, waiting for transfers between devices, swapped(): lax.ppermute(value, axis, [(source, source ^ bit) for source in range(cou...  74.2 us
    pallas_call x1, Pallas kernels, grads(): pl.pallas_call(partial(grads_kernel, self.halves), grid=(self.groups,), i...  73.1 us
    pallas_call x2, Pallas kernels, gathered_everywhere(): pl.pallas_call(partial(gather_kernel, devices, chans), in_specs=[pl.Block...  57.7 us
    pallas_call x2, Pallas kernels, carried(): pl.pallas_call(partial(carry_kernel, count, reverse), in_specs=[vmem, vme...  41.7 us
    pallas_call x2, Pallas kernels, ends(): pl.pallas_call(partial(ends_kernel, self.halves, reverse), grid=(self.gro...  33.9 us
    ppermute x22, starting transfers between devices, swapped(): lax.ppermute(value, axis, [(source, source ^ bit) for source in range(cou...  29.8 us
  transfers between devices with their start and end apart: 28, of which 9 were waited for; matrix products, arithmetic and copies ran while one was open for 19% of the time, Pallas kernels for 38%

profile of v2, /device:TPU:0, one launch (start us, length us, event | category | flops | bytes accessed | tf_op | source)
XLA Modules:
  0.0 819.0 jit_solution(10949481249275090446)
XLA Ops:
  7.3 3.0 copy.214
  14.5 2.9 collective-permute-start
  17.4 2.4 constant_dynamic-slice_fusion.9
  19.8 3.6 collective-permute-start.6
  24.7 9.4 %collective-permute-done = bf16[320,1152]{1,0:T(8,128)(2,1)S(1)} collective-permute-done((bf16[320,1152]{1,0:T(8,128)(2,1)}, bf16[320,1152]{1,0:T(8,128)(2,1)S(1)}, u32[]{:S(2)}, u32[]{:S(2)}) %collective-permute-start) | collective-permute-done | bytes 737312 | tf_op jit(solution)/shard_map/ppermute | solution.py:35
  36.0 4.6 fusion.8
  44.2 2.1 copy.121
  48.3 2.4 fusion.115
  53.7 6.6 collective-permute-done.2
  61.4 5.5 compare_select_fusion
  67.9 16.9 %scan_ends.1 = (f32[2,16,8,1152]{3,2,1,0:T(8,128)}, f32[2,8,1152]{2,1,0:T(8,128)}, f32[24,1152]{1,0:T(8,128)}) custom-call(f32[640,1152]{1,0:T(8,128)} %get-tuple-element.150.step_ref, f32[640,1152]{1,0:T(8,128)} %get-tuple-element.111.drive_ref.mixed_ref, f32[640,128]{1,0:T(8,128)} %broadcast_in_dim.38.break_ref, ...), custom_call_target="tpu_custom_call" | custom-call | flops 58982400 | bytes 8847360 | tf_op jit(solution)/shard_map/scan_ends/pallas_call | solution.py:713
  84.8 25.3 %carry.1.device = f32[16,1152]{1,0:T(8,128)} custom-call(f32[24,1152]{1,0:T(8,128)} %get-tuple-element.54.total_ref, f32[16,1152]{1,0:T(8,128)} %multiply_bitcast_fusion.rate_ref), custom_call_target="tpu_custom_call" | custom-call | tf_op jit(solution)/shard_map/carry/pallas_call | solution.py:301
  117.6 2.1 collective-permute-start.9
  122.1 6.3 fusion.29.gate_ref
  128.4 22.5 %scan_outputs.1 = (f32[640,1152]{1,0:T(8,128)}, bf16[640,1152]{1,0:T(8,128)(2,1)}, f32[2,16,8,1152]{3,2,1,0:T(8,128)}) custom-call(f32[640,1152]{1,0:T(8,128)} %get-tuple-element.150.step_ref, f32[640,1152]{1,0:T(8,128)} %get-tuple-element.111.drive_ref.mixed_ref, f32[640,128]{1,0:T(8,128)} %broadcast_in_dim.38.break_ref, ...), custom_call_target="tpu_custom_call" | custom-call | flops 82575360 | bytes 8847360 | tf_op jit(solution)/shard_map/scan_outputs/pallas_call | solution.py:726
  150.9 6.7 collective-permute-done.8
  164.0 2.4 convolution_convert_fusion.9
  168.0 11.1 %collective-permute-done.10 = bf16[4,64,1152]{2,1,0:T(8,128)(2,1)} collective-permute-done((bf16[4,64,1152]{2,1,0:T(8,128)(2,1)S(1)}, bf16[4,64,1152]{2,1,0:T(8,128)(2,1)}, u32[]{:S(2)}, u32[]{:S(2)}) %collective-permute-start.10) | collective-permute-done | bytes 589856 | tf_op jit(solution)/shard_map/ppermute | solution.py:35
  182.5 3.2 collective-permute-start.12
  186.9 6.5 collective-permute-done.3
  194.8 2.1 fusion.52.own_ref
  196.8 16.1 %gather_small.2.logit_ref = f32[32,8,320]{2,1,0:T(8,128)} custom-call(f32[8,320]{1,0:T(8,128)} %fusion.52.own_ref), custom_call_target="tpu_custom_call" | custom-call | tf_op jit(solution)/shard_map/gather_small/pallas_call | solution.py:240
  213.0 4.8 sinkhorn.1
  219.9 2.0 convolution_convert_fusion.8
  221.9 32.0 %expert_rows.2 = (bf16[8,64,1152]{2,1,0:T(8,128)(2,1)}, f32[8,8,128]{2,1,0:T(8,128)}) custom-call(bf16[8,64,1152]{2,1,0:T(8,128)(2,1)} %bitcast.246, f32[8,8,128]{2,1,0:T(8,128)} %pad.28.refs_1_), custom_call_target="tpu_custom_call" | custom-call | tf_op jit(solution)/shard_map/expert_rows/pallas_call | solution.py:185
  257.9 7.1 fusion.119
  265.1 2.6 copy-done.97
  267.7 6.3 convolution_convert_fusion
  274.0 10.4 %fusion.120 = f32[512,3072]{1,0:T(8,128)} fusion(bf16[512,1152]{1,0:T(8,128)(2,1)} %bitcast.250, bf16[1152,3072]{1,0:T(8,128)(2,1)} %bitcast.267), kind=kOutput, calls=%fused_computation.270 | convolution fusion | flops 3623878656 | bytes 14548992 | tf_op jit(solution)/shard_map/dot_general | solution.py:982
  284.5 8.9 %convolution_convert_fusion.1 = bf16[1152,3072]{1,0:T(8,128)(2,1)S(1)} fusion(bf16[512,1152]{1,0:T(8,128)(2,1)S(1)} %bitcast.274, f32[512]{0:T(512)S(1)} %mul.528, f32[512,3072]{1,0:T(8,128)S(1)} %copy-done.98, f32[512,3072]{1,0:T(8,128)} %fusion.120), kind=kOutput, calls=%fused_computation.1 | convolution fusion | flops 3660447744 | bytes 20842496 | tf_op jit(solution)/shard_map/sd,sf->df/dot_general | solution.py:992
  293.4 3.6 constant_dynamic-slice_fusion.3
  297.0 2.1 copy.200
  299.1 2.1 copy.199
  301.8 14.0 %fusion.13 = bf16[512,1152]{1,0:T(8,128)(2,1)} fusion(bf16[1152,3072]{1,0:T(8,128)(2,1)} %bitcast.266, f32[512,3072]{1,0:T(8,128)} %copy-done.97, f32[512,3072]{1,0:T(8,128)} %fusion.120), kind=kOutput, calls=%fused_computation.44 | convolution fusion | flops 3655925760 | bytes 20840448 | tf_op jit(solution)/shard_map/sf,df->sd/dot_general | solution.py:984
  315.8 3.3 fusion.1
  320.5 1.9 collective-permute-start.16
  323.1 3.6 fusion
  331.0 9.3 %convolution_convert_fusion.7 = bf16[512,1152]{1,0:T(8,128)(2,1)} fusion(bf16[1152,3072]{1,0:T(8,128)(2,1)S(1)} %bitcast.270, f32[512,3072]{1,0:T(8,128)} %copy-done.97), kind=kOutput, calls=%fused_computation.46 | convolution fusion | flops 3638624256 | bytes 14548992 | tf_op jit(solution)/shard_map/sf,df->sd/dot_general | solution.py:981
  340.3 53.1 %expert_rows.3 = (bf16[8,64,1152]{2,1,0:T(8,128)(2,1)}, bf16[8,64,1152]{2,1,0:T(8,128)(2,1)}) custom-call(bf16[8,64,1152]{2,1,0:T(8,128)(2,1)} %bitcast.254, bf16[8,64,1152]{2,1,0:T(8,128)(2,1)} %bitcast.252), custom_call_target="tpu_custom_call" | custom-call | tf_op jit(solution)/shard_map/expert_rows/pallas_call | solution.py:185
  393.4 3.9 add_convert_fusion.1
  397.3 6.0 all-to-all-start
  403.4 4.0 add_convert_fusion
  409.7 41.6 %gather_small.3.grad_ref = f32[32,8,320]{2,1,0:T(8,128)} custom-call(f32[8,320]{1,0:T(8,128)} %fusion.95.own_ref), custom_call_target="tpu_custom_call" | custom-call | tf_op jit(solution)/shard_map/gather_small/pallas_call | solution.py:240
  451.3 5.5 sinkhorn_back.1
  456.8 2.1 fusion.121
  461.3 17.8 %collective-permute-done.18 = bf16[320,1152]{1,0:T(8,128)(2,1)S(1)} collective-permute-done((bf16[320,1152]{1,0:T(8,128)(2,1)S(1)}, bf16[320,1152]{1,0:T(8,128)(2,1)S(1)}, u32[]{:S(2)}, u32[]{:S(2)}) %collective-permute-start.18) | collective-permute-done | bytes 737312 | tf_op jit(solution)/shard_map/ppermute | solution.py:35
  479.3 5.3 multiply_reduce_fusion
  484.6 17.1 %scan_ends_back.1 = (f32[2,16,8,1152]{3,2,1,0:T(8,128)}, f32[2,8,1152]{2,1,0:T(8,128)}, f32[24,1152]{1,0:T(8,128)}) custom-call(f32[640,1152]{1,0:T(8,128)} %get-tuple-element.150.step_ref, f32[640,1152]{1,0:T(8,128)} %get-tuple-element.107.drive_ref.grad_ref, f32[640,128]{1,0:T(8,128)} %broadcast_in_dim.38.break_ref, ...), custom_call_target="tpu_custom_call" | custom-call | flops 58982400 | bytes 8847360 | tf_op jit(solution)/shard_map/scan_ends_back/pallas_call | solution.py:713
  501.7 16.4 %carry_back.1.device = f32[16,1152]{1,0:T(8,128)} custom-call(f32[24,1152]{1,0:T(8,128)} %get-tuple-element.79.total_ref, f32[16,1152]{1,0:T(8,128)} %multiply_bitcast_fusion.rate_ref), custom_call_target="tpu_custom_call" | custom-call | tf_op jit(solution)/shard_map/carry_back/pallas_call | solution.py:301
  518.1 4.8 all-to-all-start.1
  525.0 3.4 collective-permute-done.23
  529.0 5.9 convolution_convert_fusion.2.refs_2_
  534.9 3.9 convolution_convert_fusion.3.refs_1_
  538.8 73.1 %scan_grads.1 = (f32[640,1152]{1,0:T(8,128)}, f32[640,1152]{1,0:T(8,128)}, f32[640,16]{1,0:T(8,128)}, f32[640,16]{1,0:T(8,128)}, f32[16,1152]{1,0:T(8,128)}) custom-call(f32[640,1152]{1,0:T(8,128)} %get-tuple-element.150.step_ref, f32[640,1152]{1,0:T(8,128)} %get-tuple-element.111.drive_ref.mixed_ref, f32[640,128]{1,0:T(8,128)} %broadcast_in_dim.38.break_ref, ...), custom_call_target="tpu_custom_call" | custom-call | flops 235929600 | bytes 8847360 | tf_op jit(solution)/shard_map/scan_grads/pallas_call | solution.py:748
  614.2 3.7 convert_element_type.297
  617.9 3.6 fusion.113
  622.1 3.0 fusion.122
  626.0 3.8 convert_element_type.298
  633.8 2.3 multiply_reduce_fusion.2
  648.2 3.9 convolution_convert_fusion.4.refs_0_
  652.1 12.7 %collective-permute-done.21 = bf16[320,1152]{1,0:T(8,128)(2,1)S(1)} collective-permute-done((bf16[320,1152]{1,0:T(8,128)(2,1)S(1)}, bf16[320,1152]{1,0:T(8,128)(2,1)S(1)}, u32[]{:S(2)}, u32[]{:S(2)}) %collective-permute-start.21) | collective-permute-done | bytes 737312 | tf_op jit(solution)/shard_map/ppermute | solution.py:35
  673.1 122.2 %sum_late.1 = bf16[5,768,1152]{2,1,0:T(8,128)(2,1)} custom-call(bf16[1152,1152]{1,0:T(8,128)(2,1)} %convolution_convert_fusion.4.refs_0_, bf16[1152,1152]{1,0:T(8,128)(2,1)} %convolution_convert_fusion.3.refs_1_, bf16[1152,1152]{1,0:T(8,128)(2,1)} %convolution_convert_fusion.2.refs_2_, f32[224,1152]{1,0:T(8,128)} %pad.34.refs_3_), custom_call_target="tpu_custom_call" | custom-call | tf_op jit(solution)/shard_map/sum_late/pallas_call | solution.py:403
  800.5 6.5 slice_convert_fusion
  806.9 4.8 maximum_convert_fusion
  (389 shorter events, 94.9 us)
Async XLA Ops:
  7.2 156.8 %copy-start = (bf16[1152,1152]{1,0:T(8,128)(2,1)S(1)}, bf16[1152,1152]{1,0:T(8,128)(2,1)}, u32[]{:S(2)}) copy-start(bf16[1152,1152]{1,0:T(8,128)(2,1)} %param.30) | copy-start | bytes 7962628
  7.2 250.7 %all-gather.3.cloned.1.call-start = ((), (), s32[]{:S(2)}) async-start(), calls=%async_computation.2 | async-start | bytes 8847360 | tf_op jit(solution)/shard_map/all_gather | solution.py:120
  12.0 22.1 %copy-start.75 = (f32[320]{0:T(512)}, f32[320]{0:T(512)S(1)}, u32[]{:S(2)}) copy-start(f32[320]{0:T(512)S(1)} %rsqrt.20) | copy-start | bytes 3844
  13.2 10.9 %copy-start.92 = (s32[4]{0:T(128)S(1)}, s32[4]{0:T(128)}, u32[]{:S(2)}) copy-start(s32[4]{0:T(128)} %param.20) | copy-start | bytes 52
  14.5 19.6 %collective-permute-start = (bf16[320,1152]{1,0:T(8,128)(2,1)}, bf16[320,1152]{1,0:T(8,128)(2,1)S(1)}, u32[]{:S(2)}, u32[]{:S(2)}) collective-permute-start(bf16[320,1152]{1,0:T(8,128)(2,1)} %multiply_convert_fusion.5), channel_id=1, source_target_pairs={{0,1},{1,0},{2,3},{3,2},{4,5},{5,4},{6,7},{7,6},{8,9},{9,8},{10,11... | collective-permute-start | bytes 2211848 | tf_op jit(solution)/shard_map/ppermute | solution.py:35
  19.8 90.3 %collective-permute-start.6 = (bf16[1,72,3072]{2,1,0:T(8,128)(2,1)}, bf16[1,72,3072]{2,1,0:T(8,128)(2,1)}, u32[]{:S(2)}, u32[]{:S(2)}) collective-permute-start(bf16[1,72,3072]{2,1,0:T(8,128)(2,1)} %get-tuple-element.129), channel_id=1, source_target_pairs={{0,24},{2,26},{4,28},{6,30},{8,16},{10,18},{12,20},{14,22},{16,8},... | collective-permute-start | bytes 1327112 | tf_op jit(solution)/shard_map/ppermute | solution.py:35
  23.4 86.7 %collective-permute-start.4 = (bf16[1,72,3072]{2,1,0:T(8,128)(2,1)}, bf16[1,72,3072]{2,1,0:T(8,128)(2,1)}, u32[]{:S(2)}, u32[]{:S(2)}) collective-permute-start(bf16[1,72,3072]{2,1,0:T(8,128)(2,1)} %get-tuple-element.130), channel_id=1, source_target_pairs={{0,8},{2,10},{4,12},{6,14},{8,0},{10,2},{12,4},{14,6},{16,24},{18,... | collective-permute-start | bytes 1327112 | tf_op jit(solution)/shard_map/ppermute | solution.py:35
  23.4 86.7 %collective-permute-start.5 = (bf16[1,72,3072]{2,1,0:T(8,128)(2,1)}, bf16[1,72,3072]{2,1,0:T(8,128)(2,1)}, u32[]{:S(2)}, u32[]{:S(2)}) collective-permute-start(bf16[1,72,3072]{2,1,0:T(8,128)(2,1)} %get-tuple-element.131), channel_id=1, source_target_pairs={{0,16},{2,18},{4,20},{6,22},{8,24},{10,26},{12,28},{14,30},{16,0},... | collective-permute-start | bytes 1327112 | tf_op jit(solution)/shard_map/ppermute | solution.py:35
  42.2 4.1 collective-permute-start.1
  50.7 16.3 %copy-start.14 = (bf16[640,1152]{1,0:T(8,128)(2,1)}, bf16[640,1152]{1,0:T(8,128)(2,1)S(1)}, u32[]{:S(2)}) copy-start(bf16[640,1152]{1,0:T(8,128)(2,1)S(1)} %get-tuple-element.112) | copy-start | bytes 4423684
  50.7 10.8 %copy-start.55 = (f32[72,1152]{1,0:T(8,128)S(1)}, f32[72,1152]{1,0:T(8,128)}, u32[]{:S(2)}) copy-start(f32[72,1152]{1,0:T(8,128)} %param.26) | copy-start | bytes 995332
  50.7 10.8 %copy-start.91 = (f32[1152]{0:T(1024)S(1)}, f32[1152]{0:T(1024)}, u32[]{:S(2)}) copy-start(f32[1152]{0:T(1024)} %param.27) | copy-start | bytes 13828
  51.3 9.1 %collective-permute-start.2 = (f32[640,104]{1,0:T(8,128)S(1)}, f32[640,104]{1,0:T(8,128)S(1)}, u32[]{:S(2)}, u32[]{:S(2)}) collective-permute-start(f32[640,104]{1,0:T(8,128)S(1)} %fusion.118), channel_id=1, source_target_pairs={{0,1},{1,0},{2,3},{3,2},{4,5},{5,4},{6,7},{7,6},{8,9},{9,8},{10,11... | collective-permute-start | bytes 798728 | tf_op jit(solution)/shard_map/ppermute | solution.py:35
  84.7 30.9 %copy-start.85 = (f32[1152]{0:T(1024)S(1)}, f32[1152]{0:T(1024)}, u32[]{:S(2)}) copy-start(f32[1152]{0:T(1024)} %param.29) | copy-start | bytes 13828
  111.9 10.2 %copy-start.39 = (bf16[320,1152]{1,0:T(8,128)(2,1)S(1)}, bf16[320,1152]{1,0:T(8,128)(2,1)}, u32[]{:S(2)}) copy-start(bf16[320,1152]{1,0:T(8,128)(2,1)} %copy-done.38) | copy-start | bytes 2211844
  115.6 158.4 %all-gather.5.cloned.1.call-start = ((), (), s32[]{:S(2)}) async-start(), calls=%async_computation.3 | async-start | bytes 8847360 | tf_op jit(solution)/shard_map/all_gather | solution.py:120
  117.6 33.3 %collective-permute-start.9 = (bf16[1,72,3072]{2,1,0:T(8,128)(2,1)S(1)}, bf16[1,72,3072]{2,1,0:T(8,128)(2,1)S(1)}, u32[]{:S(2)}, u32[]{:S(2)}) collective-permute-start(bf16[1,72,3072]{2,1,0:T(8,128)(2,1)S(1)} %get-tuple-element.132), channel_id=1, source_target_pairs={{0,24},{2,26},{4,28},{6,30},{8,16},{10,18},{12,20},{14,22},{16,8},... | collective-permute-start | bytes 1327112 | tf_op jit(solution)/shard_map/ppermute | solution.py:35
  119.7 37.9 %collective-permute-start.8 = (bf16[1,72,3072]{2,1,0:T(8,128)(2,1)S(1)}, bf16[1,72,3072]{2,1,0:T(8,128)(2,1)S(1)}, u32[]{:S(2)}, u32[]{:S(2)}) collective-permute-start(bf16[1,72,3072]{2,1,0:T(8,128)(2,1)S(1)} %get-tuple-element.133), channel_id=1, source_target_pairs={{0,16},{2,18},{4,20},{6,22},{8,24},{10,26},{12,28},{14,30},{16,0},... | collective-permute-start | bytes 1327112 | tf_op jit(solution)/shard_map/ppermute | solution.py:35
  121.0 36.6 %collective-permute-start.7 = (bf16[1,72,3072]{2,1,0:T(8,128)(2,1)S(1)}, bf16[1,72,3072]{2,1,0:T(8,128)(2,1)S(1)}, u32[]{:S(2)}, u32[]{:S(2)}) collective-permute-start(bf16[1,72,3072]{2,1,0:T(8,128)(2,1)S(1)} %get-tuple-element.134), channel_id=1, source_target_pairs={{0,8},{2,10},{4,12},{6,14},{8,0},{10,2},{12,4},{14,6},{16,24},{18,... | collective-permute-start | bytes 1327112 | tf_op jit(solution)/shard_map/ppermute | solution.py:35
  150.9 9.1 %copy-start.88 = (s32[320,1]{0,1:T(1,128)S(1)}, s32[320,1]{0,1:T(1,128)}, u32[]{:S(2)}) copy-start(s32[320,1]{0,1:T(1,128)} %param.19) | copy-start | bytes 3844
  150.9 9.7 %copy-start.21 = (bf16[320,1152]{1,0:T(8,128)(2,1)S(1)}, bf16[320,1152]{1,0:T(8,128)(2,1)}, u32[]{:S(2)}) copy-start(bf16[320,1152]{1,0:T(8,128)(2,1)} %param.35) | copy-start | bytes 2211844
  162.6 16.4 %collective-permute-start.10 = (bf16[4,64,1152]{2,1,0:T(8,128)(2,1)S(1)}, bf16[4,64,1152]{2,1,0:T(8,128)(2,1)}, u32[]{:S(2)}, u32[]{:S(2)}) collective-permute-start(bf16[4,64,1152]{2,1,0:T(8,128)(2,1)S(1)} %dynamic-slice_bitcast_fusion), channel_id=1, source_target_pairs={{0,1},{1,0},{2,3},{3,2},{4,5},{5,4},{6,7},{7,6},{8,9},{9,8},{10,11... | collective-permute-start | bytes 1769480 | tf_op jit(solution)/shard_map/ppermute | solution.py:35
  164.0 15.1 %copy-start.36 = (bf16[512,1152]{1,0:T(8,128)(2,1)S(1)}, bf16[512,1152]{1,0:T(8,128)(2,1)}, u32[]{:S(2)}) copy-start(bf16[512,1152]{1,0:T(8,128)(2,1)} %copy-done.35) | copy-start | bytes 3538948
  166.4 27.0 %copy-start.6 = (f32[8,40,1152]{2,1,0:T(8,128)S(1)}, f32[8,40,1152]{2,1,0:T(8,128)}, u32[]{:S(2)}) copy-start(f32[8,40,1152]{2,1,0:T(8,128)} %copy-done.5) | copy-start | bytes 4423684
  166.4 27.0 %copy-start.93 = (bf16[640,1152]{1,0:T(8,128)(2,1)S(1)}, bf16[640,1152]{1,0:T(8,128)(2,1)}, u32[]{:S(2)}) copy-start(bf16[640,1152]{1,0:T(8,128)(2,1)} %get-tuple-element.55) | copy-start | bytes 4423684
  166.4 27.0 %collective-permute-start.3 = (bf16[320,1152]{1,0:T(8,128)(2,1)S(1)}, bf16[320,1152]{1,0:T(8,128)(2,1)S(1)}, u32[]{:S(2)}, u32[]{:S(2)}) collective-permute-start(bf16[320,1152]{1,0:T(8,128)(2,1)S(1)} %convolution_convert_fusion.9), channel_id=1, source_target_pairs={{0,1},{1,0},{2,3},{3,2},{4,5},{5,4},{6,7},{7,6},{8,9},{9,8},{10,11... | collective-permute-start | bytes 2211848 | tf_op jit(solution)/shard_map/ppermute | solution.py:35
  181.3 75.9 %collective-permute-start.13 = (bf16[2,1,64,1152]{3,2,1,0:T(8,128)(2,1)}, bf16[2,1,64,1152]{3,2,1,0:T(8,128)(2,1)S(1)}, u32[]{:S(2)}, u32[]{:S(2)}) collective-permute-start(bf16[2,1,64,1152]{3,2,1,0:T(8,128)(2,1)} %get-tuple-element.141), channel_id=1, source_target_pairs={{0,24},{2,26},{4,28},{6,30},{8,16},{10,18},{12,20},{14,22},{16,8},... | collective-permute-start | bytes 884744 | tf_op jit(solution)/shard_map/ppermute | solution.py:35
  182.5 72.2 %collective-permute-start.11 = (bf16[2,1,64,1152]{3,2,1,0:T(8,128)(2,1)}, bf16[2,1,64,1152]{3,2,1,0:T(8,128)(2,1)}, u32[]{:S(2)}, u32[]{:S(2)}) collective-permute-start(bf16[2,1,64,1152]{3,2,1,0:T(8,128)(2,1)} %get-tuple-element.142), channel_id=1, source_target_pairs={{0,8},{2,10},{4,12},{6,14},{8,0},{10,2},{12,4},{14,6},{16,24},{18,... | collective-permute-start | bytes 884744 | tf_op jit(solution)/shard_map/ppermute | solution.py:35
  182.5 74.0 %collective-permute-start.12 = (bf16[2,1,64,1152]{3,2,1,0:T(8,128)(2,1)}, bf16[2,1,64,1152]{3,2,1,0:T(8,128)(2,1)S(1)}, u32[]{:S(2)}, u32[]{:S(2)}) collective-permute-start(bf16[2,1,64,1152]{3,2,1,0:T(8,128)(2,1)} %get-tuple-element.143), channel_id=1, source_target_pairs={{0,16},{2,18},{4,20},{6,22},{8,24},{10,26},{12,28},{14,30},{16,0},... | collective-permute-start | bytes 884744 | tf_op jit(solution)/shard_map/ppermute | solution.py:35
  194.7 25.1 %copy-start.2 = (f32[320,1152]{1,0:T(8,128)}, f32[320,1152]{1,0:T(8,128)S(1)}, u32[]{:S(2)}) copy-start(f32[320,1152]{1,0:T(8,128)S(1)} %get-tuple-element.153) | copy-start | bytes 4423684
  257.9 9.8 %copy-start.33 = (bf16[2,4,64,1152]{3,2,1,0:T(8,128)(2,1)S(1)}, bf16[2,4,64,1152]{3,2,1,0:T(8,128)(2,1)}, u32[]{:S(2)}) copy-start(bf16[2,4,64,1152]{3,2,1,0:T(8,128)(2,1)} %constant_dynamic-update-slice_fusion) | copy-start | bytes 3538948
  274.0 10.5 %copy-start.90 = (bf16[8,64,1152]{2,1,0:T(8,128)(2,1)S(1)}, bf16[8,64,1152]{2,1,0:T(8,128)(2,1)}, u32[]{:S(2)}) copy-start(bf16[8,64,1152]{2,1,0:T(8,128)(2,1)} %get-tuple-element.57) | copy-start | bytes 3538948
  274.0 10.5 %copy-start.98 = (f32[512,3072]{1,0:T(8,128)S(1)}, f32[512,3072]{1,0:T(8,128)}, u32[]{:S(2)}) copy-start(f32[512,3072]{1,0:T(8,128)} %copy-done.97) | copy-start | bytes 18874372
  274.0 19.3 %slice-start = ((s8[7077888]{0:T(1024)(128)(4,1)}), s8[4194304]{0:T(1024)(128)(4,1)S(1)}, s32[]{:S(2)}) async-start(s8[7077888]{0:T(1024)(128)(4,1)} %bitcast.234), calls=%async_computation.4 | async-start | bytes 8388608
  299.1 16.7 %collective-permute-start.14 = (bf16[4,2,72,3072]{3,2,0,1:T(8,128)(2,1)}, bf16[4,2,72,3072]{3,2,0,1:T(8,128)(2,1)}, u32[]{:S(2)}, u32[]{:S(2)}) collective-permute-start(bf16[4,2,72,3072]{3,2,0,1:T(8,128)(2,1)} %bitcast.225), channel_id=1, source_target_pairs={{0,2},{2,0},{4,6},{6,4},{8,10},{10,8},{12,14},{14,12},{16,18},{18,... | collective-permute-start | bytes 10616840 | tf_op jit(solution)/shard_map/ppermute | solution.py:35
  301.1 21.3 %collective-permute-start.15 = (bf16[4,2,72,3072]{3,2,0,1:T(8,128)(2,1)}, bf16[4,2,72,3072]{3,2,0,1:T(8,128)(2,1)}, u32[]{:S(2)}, u32[]{:S(2)}) collective-permute-start(bf16[4,2,72,3072]{3,2,0,1:T(8,128)(2,1)} %bitcast.224), channel_id=1, source_target_pairs={{0,2},{2,0},{4,6},{6,4},{8,10},{10,8},{12,14},{14,12},{16,18},{18,... | collective-permute-start | bytes 10616840 | tf_op jit(solution)/shard_map/ppermute | solution.py:35
  301.8 157.1 %copy-start.77 = (f32[320]{0:T(512)}, f32[320]{0:T(512)S(1)}, u32[]{:S(2)}) copy-start(f32[320]{0:T(512)S(1)} %reduce.10) | copy-start | bytes 3844
  301.8 14.0 %copy-start.11 = (bf16[4,2,1,72,3072]{4,3,2,1,0:T(8,128)(2,1)S(1)}, bf16[4,2,1,72,3072]{4,3,2,1,0:T(8,128)(2,1)}, u32[]{:S(2)}) copy-start(bf16[4,2,1,72,3072]{4,3,2,1,0:T(8,128)(2,1)} %get-tuple-element.159) | copy-start | bytes 10616836
  319.2 11.8 %slice-start.2 = ((s8[7077888]{0:T(1024)(128)(4,1)}), s8[4194304]{0:T(1024)(128)(4,1)S(1)}, s32[]{:S(2)}) async-start(s8[7077888]{0:T(1024)(128)(4,1)} %bitcast.268), calls=%async_computation.6 | async-start | bytes 8388608
  320.5 72.9 %collective-permute-start.16 = (bf16[4,1,72,3072]{3,2,0,1:T(8,128)(2,1)}, bf16[4,1,72,3072]{3,2,0,1:T(8,128)(2,1)}, u32[]{:S(2)}, u32[]{:S(2)}) collective-permute-start(bf16[4,1,72,3072]{3,2,0,1:T(8,128)(2,1)} %constant_dynamic-slice_fusion.1), channel_id=1, source_target_pairs={{0,4},{2,6},{4,0},{6,2},{8,12},{10,14},{12,8},{14,10},{16,20},{18,... | collective-permute-start | bytes 5308424 | tf_op jit(solution)/shard_map/ppermute | solution.py:35
  329.1 74.3 %collective-permute-start.17 = (bf16[4,1,72,3072]{3,2,0,1:T(8,128)(2,1)}, bf16[4,1,72,3072]{3,2,0,1:T(8,128)(2,1)}, u32[]{:S(2)}, u32[]{:S(2)}) collective-permute-start(bf16[4,1,72,3072]{3,2,0,1:T(8,128)(2,1)} %constant_dynamic-slice_fusion), channel_id=1, source_target_pairs={{0,4},{2,6},{4,0},{6,2},{8,12},{10,14},{12,8},{14,10},{16,20},{18,... | collective-permute-start | bytes 5308424 | tf_op jit(solution)/shard_map/ppermute | solution.py:35
  397.3 104.3 %all-to-all-start = ((bf16[4,72,3072]{2,1,0:T(8,128)(2,1)}), bf16[4,72,3072]{2,1,0:T(8,128)(2,1)}, u32[]{:S(2)}, u32[]{:S(2)}) async-start(bf16[4,72,3072]{2,1,0:T(8,128)(2,1)} %bitcast.239), calls=%async_computation | async-start | bytes 3538944 | tf_op jit(solution)/shard_map/all_to_all | solution.py:87
  459.8 19.4 %copy-start.12 = (f32[320,1152]{1,0:T(8,128)}, f32[320,1152]{1,0:T(8,128)S(1)}, u32[]{:S(2)}) copy-start(f32[320,1152]{1,0:T(8,128)S(1)} %get-tuple-element.156) | copy-start | bytes 4423684
  459.9 19.4 %copy-start.15 = (bf16[640,1152]{1,0:T(8,128)(2,1)S(1)}, bf16[640,1152]{1,0:T(8,128)(2,1)}, u32[]{:S(2)}) copy-start(bf16[640,1152]{1,0:T(8,128)(2,1)} %copy-done.14) | copy-start | bytes 4423684
  459.9 19.4 %copy-start.96 = (f32[640,1152]{1,0:T(8,128)S(1)}, f32[640,1152]{1,0:T(8,128)}, u32[]{:S(2)}) copy-start(f32[640,1152]{1,0:T(8,128)} %fusion.29.gate_ref) | copy-start | bytes 8847364
  459.9 19.4 %copy-start.99 = (f32[640,1152]{1,0:T(8,128)S(1)}, f32[640,1152]{1,0:T(8,128)}, u32[]{:S(2)}) copy-start(f32[640,1152]{1,0:T(8,128)} %get-tuple-element.86) | copy-start | bytes 8847364
  460.3 18.8 %collective-permute-start.18 = (bf16[320,1152]{1,0:T(8,128)(2,1)S(1)}, bf16[320,1152]{1,0:T(8,128)(2,1)S(1)}, u32[]{:S(2)}, u32[]{:S(2)}) collective-permute-start(bf16[320,1152]{1,0:T(8,128)(2,1)S(1)} %fusion.109), channel_id=1, source_target_pairs={{0,1},{1,0},{2,3},{3,2},{4,5},{5,4},{6,7},{7,6},{8,9},{9,8},{10,11... | collective-permute-start | bytes 2211848 | tf_op jit(solution)/shard_map/ppermute | solution.py:35
  501.6 21.3 %copy-start.4 = (f32[320,1152]{1,0:T(8,128)S(1)}, f32[320,1152]{1,0:T(8,128)}, u32[]{:S(2)}) copy-start(f32[320,1152]{1,0:T(8,128)} %copy-done.2) | copy-start | bytes 4423684
  501.6 21.3 %copy-start.63 = (f32[8,320]{1,0:T(8,128)S(1)}, f32[8,320]{1,0:T(8,128)}, u32[]{:S(2)}) copy-start(f32[8,320]{1,0:T(8,128)} %sinkhorn_back.1) | copy-start | bytes 30724
  501.6 26.7 %copy-start.87 = (f32[1152]{0:T(1024)S(1)}, f32[1152]{0:T(1024)}, u32[]{:S(2)}) copy-start(f32[1152]{0:T(1024)} %get-tuple-element.106) | copy-start | bytes 13828
  518.1 99.8 %all-to-all-start.1 = ((bf16[4,72,3072]{2,1,0:T(8,128)(2,1)}), bf16[4,72,3072]{2,1,0:T(8,128)(2,1)}, u32[]{:S(2)}, u32[]{:S(2)}) async-start(bf16[4,72,3072]{2,1,0:T(8,128)(2,1)} %bitcast.238), calls=%async_computation.1 | async-start | bytes 3538944 | tf_op jit(solution)/shard_map/all_to_all | solution.py:87
  523.9 4.4 collective-permute-start.23
  622.1 9.5 %copy-start.95 = (f32[640,1152]{1,0:T(8,128)S(1)}, f32[640,1152]{1,0:T(8,128)}, u32[]{:S(2)}) copy-start(f32[640,1152]{1,0:T(8,128)} %get-tuple-element.80) | copy-start | bytes 8847364
  625.1 6.5 collective-permute-start.19
  636.9 3.1 collective-permute-start.20
  645.5 19.3 %collective-permute-start.21 = (bf16[320,1152]{1,0:T(8,128)(2,1)S(1)}, bf16[320,1152]{1,0:T(8,128)(2,1)S(1)}, u32[]{:S(2)}, u32[]{:S(2)}) collective-permute-start(bf16[320,1152]{1,0:T(8,128)(2,1)S(1)} %fusion.26), channel_id=1, source_target_pairs={{0,1},{1,0},{2,3},{3,2},{4,5},{5,4},{6,7},{7,6},{8,9},{9,8},{10,11... | collective-permute-start | bytes 2211848 | tf_op jit(solution)/shard_map/ppermute | solution.py:35
  648.2 16.7 %copy-start.7 = (f32[8,40,1152]{2,1,0:T(8,128)S(1)}, f32[8,40,1152]{2,1,0:T(8,128)}, u32[]{:S(2)}) copy-start(f32[8,40,1152]{2,1,0:T(8,128)} %copy-done.5) | copy-start | bytes 4423684
  648.2 16.7 %copy-start.73 = (f32[1152]{0:T(1024)S(1)}, f32[1152]{0:T(1024)}, u32[]{:S(2)}) copy-start(f32[1152]{0:T(1024)} %param.21) | copy-start | bytes 13828
  648.2 16.7 %copy-start.76 = (f32[320]{0:T(512)S(1)}, f32[320]{0:T(512)}, u32[]{:S(2)}) copy-start(f32[320]{0:T(512)} %copy-done.75) | copy-start | bytes 3844
  652.1 14.5 %copy-start.81 = (f32[320]{0:T(512)S(1)}, f32[320]{0:T(512)}, u32[]{:S(2)}) copy-start(f32[320]{0:T(512)} %copy-done.80) | copy-start | bytes 3844
  652.1 15.9 %copy-start.13 = (f32[320,1152]{1,0:T(8,128)S(1)}, f32[320,1152]{1,0:T(8,128)}, u32[]{:S(2)}) copy-start(f32[320,1152]{1,0:T(8,128)} %copy-done.12) | copy-start | bytes 4423684
  652.1 15.9 %copy-start.23 = (f32[320,1152]{1,0:T(8,128)S(1)}, f32[320,1152]{1,0:T(8,128)}, u32[]{:S(2)}) copy-start(f32[320,1152]{1,0:T(8,128)} %get-tuple-element.155) | copy-start | bytes 4423684
  652.1 15.9 %copy-start.78 = (f32[320]{0:T(512)S(1)}, f32[320]{0:T(512)}, u32[]{:S(2)}) copy-start(f32[320]{0:T(512)} %copy-done.77) | copy-start | bytes 3844
  666.6 4.7 collective-permute-start.22
  (70 other events, 262.2 us)
Sparse Core Ops, SparseCore 0:
  115.7 50.5 all-gather.2
  168.4 55.0 all-gather.4

commit v3 on v2

--- a/solution.py
+++ b/solution.py
@@ -22,6 +22,8 @@
 LN2 = 0.6931471805599453
 BREAK = 1e30
 MESH = pl.DeviceIdType.MESH
+GELU_SCALE = 0.7978845608028654
+GELU_CUBE = 0.044715
 
 
 def passed_along(value, axis, steps):
@@ -117,8 +119,7 @@
         weight = after(weight, start)
     mine = across_experts(weight, 0, wait)
     groups = [[k * share + q for q in range(share)] for k in range(own)]
-    full = lax.all_gather(mine, "seq", axis=1, axis_index_groups=groups)
-    return full.reshape(own * share * features, hidden)
+    return lax.all_gather(mine, "seq", axis_index_groups=groups)
 
 
 def halved(grad, stage):
@@ -129,7 +130,11 @@
     sent = lax.dynamic_index_in_dim(pairs, 1 - side, 2, False)
     kept = lax.dynamic_index_in_dim(pairs, side, 2, False)
     came = swapped(sent, "seq", bit)
-    return (kept.astype(jnp.float32) + came.astype(jnp.float32)).astype(grad.dtype)
+    return added(kept, came)
+
+
+def added(kept, came):
+    return (kept.astype(jnp.float32) + came.astype(jnp.float32)).astype(kept.dtype)
 
 
 def after(value, *others):
@@ -318,85 +323,117 @@
     )(total, rates)
 
 
+class Halving:
+    def __init__(self, count, held, incoming, result, send_sem, recv_sem):
+        self.held, self.incoming, self.result = held, incoming, result
+        self.send_sem, self.recv_sem = send_sem, recv_sem
+        self.chunks, self.rows = held.shape[0], held.shape[1]
+        me = lax.axis_index("seq")
+        bits = [1 << k for k in range(count.bit_length() - 1)]
+        self.rounds = len(bits)
+        self.peers = [{"seq": opposite(me, bit)} for bit in bits]
+        self.sides = [lax.rem(lax.div(me, bit), 2) for bit in bits]
+        self.lows, self.lengths = [0], [self.rows]
+        for side in self.sides:
+            self.lengths.append(self.lengths[-1] // 2)
+            self.lows.append(self.lows[-1] + side * self.lengths[-1])
+        self.turns = 4 * self.rounds + self.chunks - 1
+
+    def greet(self):
+        barrier = pltpu.get_barrier_semaphore()
+        for peer in self.peers:
+            pl.semaphore_signal(barrier, inc=1, device_id=peer, device_id_type=MESH)
+
+    def greeted(self):
+        pl.semaphore_wait(pltpu.get_barrier_semaphore(), self.rounds)
+
+    def span(self, k, other=False):
+        low = self.lows[k]
+        if other:
+            low = self.lows[k - 1] + (1 - self.sides[k - 1]) * self.lengths[k]
+        return pl.ds(pl.multiple_of(low, 16), self.lengths[k])
+
+    def landing(self, step):
+        return pl.ds(self.rows - self.lengths[step], self.lengths[step + 1])
+
+    def copy(self, c, step):
+        if step < self.rounds:
+            k = step
+            source = self.held.at[c, self.span(k + 1, True)]
+            target = self.incoming.at[c, self.landing(step)]
+        else:
+            k = 2 * self.rounds - 1 - step
+            source = target = self.result.at[c, self.span(k + 1)]
+        return pltpu.make_async_remote_copy(
+            src_ref=source,
+            dst_ref=target,
+            send_sem=self.send_sem.at[c, step],
+            recv_sem=self.recv_sem.at[c, step],
+            device_id=self.peers[k],
+            device_id_type=MESH,
+        )
+
+    def start(self):
+        self.copy(0, 0).start()
+
+    def turn(self, turn):
+        if turn + 1 < self.chunks:
+            self.copy(turn + 1, 0).start()
+        for c in range(self.chunks):
+            step, odd = divmod(turn - c - 1, 2)
+            if odd or not 0 <= step < 2 * self.rounds:
+                continue
+            self.copy(c, step).wait()
+            if step < self.rounds:
+                kept = self.span(step + 1)
+                total = self.held[c, kept].astype(jnp.float32)
+                total = total + self.incoming[c, self.landing(step)].astype(jnp.float32)
+                target = self.held if step < self.rounds - 1 else self.result
+                target[c, kept] = total.astype(target.dtype)
+            if step < 2 * self.rounds - 1:
+                self.copy(c, step + 1).start()
+
+
+def sum_scratch(chunks, rows, width, count):
+    steps = 2 * (count.bit_length() - 1)
+    return [
+        pltpu.VMEM((chunks, rows, width), jnp.bfloat16),
+        pltpu.VMEM((chunks, rows, width), jnp.bfloat16),
+        pltpu.SemaphoreType.DMA((chunks, steps)),
+        pltpu.SemaphoreType.DMA((chunks, steps)),
+    ]
+
+
 def sum_kernel(count, places, sizes, *refs):
     parts, sum_ref = refs[: len(places)], refs[len(places)]
     held, incoming, send_sem, recv_sem = refs[len(places) + 1 :]
-    me = lax.axis_index("seq")
-    bits = [1 << k for k in range(count.bit_length() - 1)]
-    peers = [{"seq": opposite(me, bit)} for bit in bits]
-    chunks, rows = held.shape[0], held.shape[1]
-    rounds = len(bits)
-    barrier = pltpu.get_barrier_semaphore()
-    for peer in peers:
-        pl.semaphore_signal(barrier, inc=1, device_id=peer, device_id_type=MESH)
-    for c in range(chunks):
+    halving = Halving(count, held, incoming, sum_ref, send_sem, recv_sem)
+    rows = halving.rows
+    halving.greet()
+    used = max(place + size for place, size in zip(places, sizes))
+    for c in range(halving.chunks):
         for part, place, size in zip(parts, places, sizes):
             low, high = max(place, c * rows), min(place + size, (c + 1) * rows)
             if low < high:
                 held[c, low - c * rows : high - c * rows] = part[low - place : high - place].astype(held.dtype)
-        used = max(place + size for place, size in zip(places, sizes))
         if used < (c + 1) * rows:
             low = max(used - c * rows, 0)
             held[c, low:] = jnp.zeros((rows - low, held.shape[2]), held.dtype)
-    pl.semaphore_wait(barrier, rounds)
-
-    sides = [lax.rem(lax.div(me, bit), 2) for bit in bits]
-    lows, lengths = [0], [rows]
-    for side in sides:
-        lengths.append(lengths[-1] // 2)
-        lows.append(lows[-1] + side * lengths[-1])
-
-    def span(low, length):
-        return pl.ds(pl.multiple_of(low, 16), length)
-
-    def copy(c, step):
-        if step < rounds:
-            k = step
-            other = lows[k] + (1 - sides[k]) * lengths[k + 1]
-            source = held.at[c, span(other, lengths[k + 1])]
-            target = incoming.at[c, pl.ds(rows - lengths[k], lengths[k + 1])]
-        else:
-            k = 2 * rounds - 1 - step
-            here = span(lows[k + 1], lengths[k + 1])
-            source, target = sum_ref.at[c, here], sum_ref.at[c, here]
-        return pltpu.make_async_remote_copy(
-            src_ref=source,
-            dst_ref=target,
-            send_sem=send_sem.at[c, step],
-            recv_sem=recv_sem.at[c, step],
-            device_id=peers[k],
-            device_id_type=MESH,
-        )
-
-    copy(0, 0).start()
-    for turn in range(2 * rounds + chunks - 1):
-        if turn + 1 < chunks:
-            copy(turn + 1, 0).start()
-        for c in range(max(0, turn - 2 * rounds + 1), min(chunks, turn + 1)):
-            step = turn - c
-            copy(c, step).wait()
-            if step < rounds:
-                kept = span(lows[step + 1], lengths[step + 1])
-                came = incoming[c, pl.ds(rows - lengths[step], lengths[step + 1])]
-                total = held[c, kept].astype(jnp.float32) + came.astype(jnp.float32)
-                if step < rounds - 1:
-                    held[c, kept] = total.astype(held.dtype)
-                else:
-                    sum_ref[c, kept] = total.astype(sum_ref.dtype)
-            if step < 2 * rounds - 1:
-                copy(c, step + 1).start()
+    halving.greeted()
+    halving.start()
+    for turn in range(halving.turns):
+        halving.turn(turn)
 
 
 def summed(parts):
     count = lax.axis_size("seq")
-    rounds = count.bit_length() - 1
     width = parts[0].shape[1]
     sizes = [part.shape[0] for part in parts]
     places, used = [], 0
     for size in sizes:
         places.append(used)
         used += -(-size // 16) * 16
-    chunk = 16 * count * max(1, 48 // count)
+    chunk = 16 * count
     chunks = -(-used // chunk)
     vmem = pl.BlockSpec(memory_space=pltpu.VMEM)
     padded = [jnp.pad(part, ((0, -part.shape[0] % 16), (0, 0))) for part in parts]
@@ -405,12 +442,7 @@
         in_specs=[vmem] * len(parts),
         out_specs=vmem,
         out_shape=jax.ShapeDtypeStruct((chunks, chunk, width), jnp.bfloat16),
-        scratch_shapes=[
-            pltpu.VMEM((chunks, chunk, width), jnp.bfloat16),
-            pltpu.VMEM((chunks, chunk, width), jnp.bfloat16),
-            pltpu.SemaphoreType.DMA((chunks, 2 * rounds)),
-            pltpu.SemaphoreType.DMA((chunks, 2 * rounds)),
-        ],
+        scratch_shapes=sum_scratch(chunks, chunk, width, count),
         compiler_params=pltpu.CompilerParams(
             collective_id=6, has_side_effects=True, vmem_limit_bytes=VMEM_LIMIT
         ),
@@ -452,10 +484,6 @@
 def silu_grad(values):
     sigma = jax.nn.sigmoid(values)
     return sigma * (1.0 + values * (1.0 - sigma))
-
-
-def gelu_grad(values, upstream):
-    return jax.vjp(partial(jax.nn.gelu, approximate=True), values)[1](upstream)[0]
 
 
 def spread(target, source):
@@ -520,7 +548,7 @@
                     new.append(decay * state[n + 1] + drive * wide[n, at, :])
             return tuple(new)
 
-        out = lax.fori_loop(0, steps, body, (zero,) * (STATE + 1), unroll=2)
+        out = lax.fori_loop(0, steps, body, (zero,) * (STATE + 1), unroll=10)
         windows, sums = chunk_windows(out[0], not reverse)
         prior = shifted(sums, 1, not reverse)
         last = slice(0, 1) if reverse else slice(CHUNKS - 1, CHUNKS)
@@ -575,7 +603,7 @@
             scan_ref[at, :] = total
             return tuple(new)
 
-        lax.fori_loop(0, steps, body, tuple(state), unroll=2)
+        lax.fori_loop(0, steps, body, tuple(state), unroll=5)
         return carry
 
     lax.fori_loop(0, halves, half, 0)
@@ -585,17 +613,47 @@
     gated_ref[...] = (out * (gate * jax.nn.sigmoid(gate))).astype(gated_ref.dtype)
 
 
+def early_fills(first, second, held, own_sem):
+    rows, copies, place = held.shape[1], [], 0
+    for part in (first, second):
+        done = 0
+        while done < part.shape[0]:
+            c, low = (place + done) // rows, (place + done) % rows
+            length = min(rows - low, part.shape[0] - done)
+            copies.append(
+                pltpu.make_async_copy(
+                    part.at[pl.ds(done, length)], held.at[c, pl.ds(low, length)], own_sem.at[len(copies)]
+                )
+            )
+            done += length
+        place += part.shape[0]
+    return copies
+
+
 def grads_kernel(
-    halves, step_ref, mixed_ref, break_ref, grad_ref, b_ref, c_ref, rate_ref, entry_ref, part_ref, sum_ref,
-    device, step_out, mixed_out, b_out, c_out, rate_out, b_wide, c_wide, b_sum, c_sum, decays, states,
+    halves, count, groups, step_ref, mixed_ref, break_ref, grad_ref, b_ref, c_ref, rate_ref, entry_ref,
+    part_ref, sum_ref, device, first_early, second_early, step_out, mixed_out, b_out, c_out, rate_out, early_out,
+    b_wide, c_wide, b_sum, c_sum, decays, states, held, incoming, summed_early, send_sem, recv_sem, own_sem,
 ):
     rows = step_ref.shape[0]
     steps = rows // (halves * CHUNKS)
     group = pl.program_id(0)
     block = STATE // 2
+    halving = Halving(count, held, incoming, summed_early, send_sem, recv_sem)
+    slots = [[] for _ in range(2 * groups)]
+    for turn in range(halving.turns):
+        slots[turn * 2 * groups // halving.turns].append(turn)
 
     @pl.when(group == 0)
     def _():
+        halving.greet()
+        fills = early_fills(first_early, second_early, held, own_sem)
+        for fill in fills:
+            fill.start()
+        for fill in fills:
+            fill.wait()
+        halving.greeted()
+        halving.start()
         spread(b_wide, b_ref)
         spread(c_wide, c_ref)
         b_sum[...] = jnp.zeros_like(b_sum)
@@ -626,7 +684,7 @@
                     new.append(value)
                 return tuple(new)
 
-            lax.fori_loop(0, steps, ahead, tuple(entry), unroll=2)
+            lax.fori_loop(0, steps, ahead, tuple(entry), unroll=10)
 
             exits = [
                 part_ref[h, first + n]
@@ -664,15 +722,27 @@
                     mixed_out[at, :] += by_map
                 return tuple(flows + sums)
 
-            out = lax.fori_loop(0, steps, back, tuple(exits) + rate_sums)
+            out = lax.fori_loop(0, steps, back, tuple(exits) + rate_sums, unroll=5)
             return out[block:]
 
         rate_sums = lax.fori_loop(0, halves, half, (zero,) * block)
         for n in range(block):
             rate_out[first + n : first + n + 1, :] = jnp.sum(rate_sums[n], 0, keepdims=True)
 
-    @pl.when(group == pl.num_programs(0) - 1)
+        for g in range(groups):
+            turns = slots[2 * g + first // block]
+            if turns:
+
+                @pl.when(group == g)
+                def _(turns=turns):
+                    for turn in turns:
+                        halving.turn(turn)
+
+    @pl.when(group == groups - 1)
     def _():
+        result = pltpu.make_async_copy(summed_early, early_out, own_sem.at[0])
+        result.start()
+        result.wait()
         for n in range(STATE):
             b_out[:, n : n + 1] = jnp.sum(b_sum[n], -1, keepdims=True)
             c_out[:, n : n + 1] = jnp.sum(c_sum[n], -1, keepdims=True)
@@ -742,33 +812,49 @@
             name="scan_outputs",
         )(step, mixed, breaks, b_in, c_out, rates, part, sums, device, skip, gate)
 
-    def grads(self, step, mixed, breaks, grad, b_in, c_out, rates, entry, part, sums, device):
+    def grads(self, step, mixed, breaks, grad, b_in, c_out, rates, entry, part, sums, device, early):
+        count = lax.axis_size("seq")
+        width, total = early[0].shape[1], early[0].shape[0] + early[1].shape[0]
+        chunk = 16 * count
+        total = -(-total // chunk) * chunk
+        early = (early[0], jnp.pad(early[1], ((0, total - early[0].shape[0] - early[1].shape[0]), (0, 0))))
+        chunks = total // chunk
+        anywhere = pl.BlockSpec(memory_space=pl.ANY)
         steps = self.rows // (self.halves * CHUNKS)
         block = STATE // 2
         return pl.pallas_call(
-            partial(grads_kernel, self.halves),
+            partial(grads_kernel, self.halves, count, self.groups),
             grid=(self.groups,),
             in_specs=[
                 self.row_spec, self.row_spec, self.break_spec, self.row_spec, self.map_spec, self.map_spec,
-                self.rate_spec, self.part_spec, self.part_spec, self.sum_spec, self.rate_spec,
+                self.rate_spec, self.part_spec, self.part_spec, self.sum_spec, self.rate_spec, anywhere, anywhere,
             ],
-            out_specs=[self.row_spec, self.row_spec, self.map_spec, self.map_spec, self.rate_spec],
+            out_specs=[self.row_spec, self.row_spec, self.map_spec, self.map_spec, self.rate_spec, anywhere],
             out_shape=[
                 self.row_f32,
                 self.row_f32,
                 jax.ShapeDtypeStruct((self.rows, STATE), jnp.float32),
                 jax.ShapeDtypeStruct((self.rows, STATE), jnp.float32),
                 jax.ShapeDtypeStruct((STATE, self.channels), jnp.float32),
+                jax.ShapeDtypeStruct((chunks, chunk, width), jnp.bfloat16),
             ],
             scratch_shapes=[
                 self.wide, self.wide, self.wide, self.wide,
                 pltpu.VMEM((steps, block, CHUNKS, LANES), jnp.float32),
                 pltpu.VMEM((steps + 1, block, CHUNKS, LANES), jnp.float32),
+                pltpu.VMEM((chunks, chunk, width), jnp.bfloat16),
+                *sum_scratch(chunks, chunk, width, count)[1:2],
+                pltpu.VMEM((chunks, chunk, width), jnp.bfloat16),
+                *sum_scratch(chunks, chunk, width, count)[2:],
+                pltpu.SemaphoreType.DMA((chunks + 2,)),
             ],
-            compiler_params=self.params(),
+            compiler_params=pltpu.CompilerParams(
+                dimension_semantics=("arbitrary",), vmem_limit_bytes=VMEM_LIMIT, collective_id=7,
+                has_side_effects=True,
+            ),
             cost_estimate=self.cost(20),
             name="scan_grads",
-        )(step, mixed, breaks, grad, b_in, c_out, rates, entry, part, sums, device)
+        )(step, mixed, breaks, grad, b_in, c_out, rates, entry, part, sums, device, *early)
 
 
 def over_tokens(values):
@@ -837,6 +923,103 @@
         compiler_params=pltpu.CompilerParams(vmem_limit_bytes=VMEM_LIMIT),
         name="sinkhorn_back",
     )(place, logits, scaled, rows, columns, grad)
+
+
+def expert_kernel(
+    side_ref, rows_ref, grad_ref, gate_ref, up_ref, down_ref, out_ref, back_ref, up_kept, up_sent, down_kept,
+    down_sent, rows_t, grad_t, out_sum, back_sum, whole,
+):
+    step = pl.program_id(0)
+    features = up_kept.shape[1]
+
+    @pl.when(step == 0)
+    def _():
+        rows_t[...] = rows_ref[...].T
+        grad_t[...] = (grad_ref[...].astype(jnp.float32) * gate_ref[...]).astype(jnp.bfloat16).T
+
+    def parted(total, kept, sent):
+        whole[...] = total
+        first = side_ref[0] == 0
+        for k in range(kept.shape[0]):
+            low = whole[2 * k * features : (2 * k + 1) * features]
+            high = whole[(2 * k + 1) * features : (2 * k + 2) * features]
+            kept[k] = jnp.where(first, low, high).astype(kept.dtype)
+            sent[k] = jnp.where(first, high, low).astype(sent.dtype)
+
+    def dot(a, b, over=((1,), (0,))):
+        return lax.dot_general(a, b, (over, ((), ())), preferred_element_type=jnp.float32)
+
+    def joined(ref):
+        for q in range(ref.shape[0]):
+            for j in range(ref.shape[1]):
+                first = (j * ref.shape[0] + q) * features
+                whole[first : first + features] = ref[q, j].astype(jnp.float32)
+        return whole[...].astype(jnp.bfloat16)
+
+    across = ((1,), (1,))
+    up, down = joined(up_ref), joined(down_ref)
+    pre = dot(rows_ref[...], up)
+    square = pre * pre
+    bend = jnp.tanh(GELU_SCALE * (pre + GELU_CUBE * pre * square))
+    half = 0.5 * (1.0 + bend)
+    act = (pre * half).astype(jnp.bfloat16)
+    slope = half + 0.5 * pre * (1.0 - bend * bend) * (GELU_SCALE + 3.0 * GELU_SCALE * GELU_CUBE * square)
+    grad_pre = dot(grad_ref[...], down) * slope
+    out_part, back_part = dot(act, down, across), dot(grad_pre.astype(jnp.bfloat16), up, across)
+
+    @pl.when(step == 0)
+    def _():
+        out_sum[...] = out_part
+        back_sum[...] = back_part
+
+    @pl.when(step > 0)
+    def _():
+        out_sum[...] += out_part
+        back_sum[...] += back_part
+
+    parted(dot(grad_t[...], act), down_kept, down_sent)
+    parted(dot(rows_t[...], (grad_pre * gate_ref[...]).astype(jnp.bfloat16)), up_kept, up_sent)
+
+    @pl.when(step == pl.num_programs(0) - 1)
+    def _():
+        out_ref[...] = out_sum[...].astype(out_ref.dtype)
+        back_ref[...] = back_sum[...].astype(back_ref.dtype)
+
+
+def expert_passes(side, rows, grad, gate, up, down):
+    count, width = rows.shape
+    share, own, features, hidden = up.shape
+    tile = 512
+    blocks = width // (2 * features)
+    fixed = lambda *shape: pl.BlockSpec(shape, lambda k: (0,) * len(shape))
+    weight_spec = pl.BlockSpec((share, own, features, tile), lambda k: (0, 0, 0, k))
+    part_spec = pl.BlockSpec((blocks, features, tile), lambda k: (0, 0, k))
+    part_shape = jax.ShapeDtypeStruct((blocks, features, hidden), jnp.bfloat16)
+    row_shape = jax.ShapeDtypeStruct((count, width), jnp.bfloat16)
+    return pl.pallas_call(
+        expert_kernel,
+        grid=(hidden // tile,),
+        in_specs=[
+            pl.BlockSpec(memory_space=pltpu.SMEM), fixed(count, width), fixed(count, width), fixed(count, 1),
+            weight_spec, weight_spec,
+        ],
+        out_specs=[fixed(count, width), fixed(count, width)] + [part_spec] * 4,
+        out_shape=[row_shape, row_shape] + [part_shape] * 4,
+        scratch_shapes=[
+            pltpu.VMEM((width, count), jnp.bfloat16),
+            pltpu.VMEM((width, count), jnp.bfloat16),
+            pltpu.VMEM((count, width), jnp.float32),
+            pltpu.VMEM((count, width), jnp.float32),
+            pltpu.VMEM((width, tile), jnp.float32),
+        ],
+        compiler_params=pltpu.CompilerParams(
+            dimension_semantics=("arbitrary",), vmem_limit_bytes=VMEM_LIMIT
+        ),
+        cost_estimate=pl.CostEstimate(
+            flops=12 * count * width * hidden, bytes_accessed=8 * width * hidden, transcendentals=count * hidden
+        ),
+        name="expert_passes",
+    )(side, rows, grad, gate, up, down)
 
 
 def on_device(
@@ -976,24 +1159,18 @@
     arrived, gate_arrived = expert_rows(1, pack(moe_in.astype(bf16)), gate_slots)
     arrived = arrived.reshape(-1, model_width)
     gate_arrived = gate_arrived[:, 0, :capacity].reshape(-1, 1)
-    pre = jnp.dot(arrived, full_up, preferred_element_type=f32)
-    act_b = jax.nn.gelu(pre, approximate=True).astype(bf16)
-    expert_out = jnp.einsum("sf,df->sd", act_b, full_down, preferred_element_type=f32).astype(bf16)
-    grad_act = jnp.dot(grad_arrived, full_down, preferred_element_type=f32)
-    plain_grad_pre = gelu_grad(pre, grad_act)
-    grad_rows_in = jnp.einsum(
-        "sf,df->sd", plain_grad_pre.astype(bf16), full_up, preferred_element_type=f32
-    ).astype(bf16)
+    own, share = expert_groups()
+    features, hidden = up_weight.shape[1:]
+    side = lax.rem(seq_place, 2).astype(jnp.int32).reshape(1)
+    expert_out, grad_rows_in, up_kept, up_sent, down_kept, down_sent = expert_passes(
+        side, arrived, grad_arrived, gate_arrived, full_up, full_down
+    )
+    expert_grads = [
+        added(kept, swapped(sent, "seq", 1)).reshape(own, share // 2, features, hidden)
+        for kept, sent in ((up_kept, up_sent), (down_kept, down_sent))
+    ]
     blocks = (EXPERTS, capacity, model_width)
 
-    grad_gated_rows = (grad_arrived.astype(f32) * gate_arrived).astype(bf16)
-    grad_pre_b = (plain_grad_pre * gate_arrived).astype(bf16)
-    down_part = jnp.einsum("sd,sf->df", grad_gated_rows, act_b, preferred_element_type=f32)
-    up_part = jnp.einsum("sd,sf->df", arrived, grad_pre_b, preferred_element_type=f32)
-    own, share = expert_groups()
-    expert_grads = [
-        halved(part.astype(bf16).reshape(own, share, -1, part.shape[1]), 0) for part in (up_part, down_part)
-    ]
     expert_back, grad_back = expert_rows(
         2, after(expert_out, *expert_grads).reshape(blocks), grad_rows_in.reshape(blocks)
     )
@@ -1002,7 +1179,6 @@
     expert_tok = unpack(after(expert_back, *expert_grads))
     plain_grad_part = unpack(grad_back)
     up_part, down_part = expert_grads
-    up_grad = to_owners(after(up_part.reshape(own, *up_part.shape[2:]), expert_back))
 
     block_out = from_steps((hidden_one + gate[:, None] * expert_tok).astype(bf16))
     grad_two = grad_steps.astype(f32)
@@ -1012,9 +1188,9 @@
         EXPERTS * grad_gate[None],
         0.0,
     )
-    grad_logits = sinkhorn_back(
-        dev_ref, every_logit, scaled, row_totals, columns, gathered_everywhere(grad_probs)
-    )
+    every_grad = gathered_everywhere(grad_probs)
+    up_grad = to_owners(after(up_part.reshape(own, *up_part.shape[2:]), every_grad))
+    grad_logits = sinkhorn_back(dev_ref, every_logit, scaled, row_totals, columns, every_grad)
     router_grad = jnp.einsum("td,et->ed", moe_in, grad_logits, precision=HIGH)
     grad_moe_in = gate[:, None] * plain_grad_part + jnp.einsum(
         "et,de->td", grad_logits, router_weight, precision=HIGH
@@ -1034,12 +1210,12 @@
     grad_scan_w = widened(grad_scan)
     back_part, back_sums, back_total = scan.ends(True, step_w, grad_scan_w, breaks, c_out, rates)
     back_entry = carried(after(back_total, up_grad), rates, True)
-    down_grad = to_owners(after(down_part.reshape(own, *down_part.shape[2:]), back_entry))
-    step_grad, mixed_grad, b_grad, c_grad, rate_grad = scan.grads(
+    step_grad, mixed_grad, b_grad, c_grad, rate_grad, early = scan.grads(
         step_w, mixed_w, breaks, grad_scan_w, b_in, c_out, rates, entry, back_part, back_sums,
-        back_entry,
-    )
-    step_grad = after(step_grad, down_grad)
+        back_entry, (out_weight_grad.astype(bf16).reshape(-1, channels), gate_weight_grad.astype(bf16)),
+    )
+    early = early.reshape(-1, channels)
+    down_grad = to_owners(after(down_part.reshape(own, *down_part.shape[2:]), step_grad))
     step_grad, mixed_grad = step_grad[:, :channels], mixed_grad[:, :channels]
     mixed_grad = mixed_grad + skip_gain * grad_scan
     a_log_rows = -decay_rates.T * rate_grad[:, :channels]
@@ -1093,17 +1269,14 @@
         skip_grad[None], norm_rows.reshape(-1, channels), gains.reshape(-1, channels),
     )
     bounds = [sum(part.shape[0] for part in pieces[: k + 1]) for k in range(len(pieces) - 1)]
-    inner_weight_grad, gate_weight_grad, out_weight_grad, small = summed(
-        [
-            inner_weight_grad.astype(bf16), gate_weight_grad.astype(bf16),
-            out_weight_grad.astype(bf16).reshape(-1, channels), jnp.concatenate(pieces, 0),
-        ]
-    )
+    inner_weight_grad, small = summed([after(inner_weight_grad.astype(bf16), down_grad), jnp.concatenate(pieces, 0)])
+    early = after(early, small)
+    out_weight_grad = early[:model_width].reshape(channels, model_width).astype(f32)
+    gate_weight_grad = early[model_width : 2 * model_width].astype(f32)
     (
         xproj_rows, dt_weight_grad, a_log_rows, conv_weight_grad, conv_bias_grad, dt_bias_grad, skip_grad,
         norm_rows, gains,
     ) = jnp.split(small, bounds, 0)
-    out_weight_grad = out_weight_grad.reshape(channels, model_width)
     norm_gain_grad, gains = norm_rows.reshape(-1), gains.reshape(-1, model_width)
     xproj_grad, a_log_grad = xproj_rows.T, a_log_rows.T
     conv_bias_grad, dt_bias_grad, skip_grad = conv_bias_grad[0], dt_bias_grad[0], skip_grad[0]

time: 829 us -> 749 us (0.903)
  matrix products: 121 us -> 71 us
  Pallas kernels: 447 us -> 401 us
  other arithmetic: 56.2 us -> 65.3 us
  waiting for transfers between devices: 74.5 us -> 82.9 us
    pallas_call x1, Pallas kernels: 122 us -> 64.7 us  [summed(): pl.pallas_call(partial(sum_kernel, count, places, [part.shape[0] for part...]
    dot_general x6 -> x0, matrix products: 56 us -> none  [the longest x1 14 us: on_device(): jnp.einsum('sf,df->sd', plain_grad_pre.astype(bf16), full_up, preferred_e...]
    pallas_call x1 -> x2, Pallas kernels: 73.1 us -> 124 us  [the longest x1 89.2 us: grads(): pl.pallas_call(partial(grads_kernel, self.halves, count, self.groups), gr...]
    pallas_call x2, Pallas kernels: 57.7 us -> 27.7 us  [gathered_everywhere(): pl.pallas_call(partial(gather_kernel, devices, chans), in_specs=[pl.Block...]
    convert_element_type x4 -> x5, other arithmetic: 14.8 us -> 18.1 us  [the longest x4 15.1 us: added(): (kept.astype(jnp.float32) + came.astype(jnp.float32)).astype(kept.dtype)]
  transfers between devices with their start and end apart: 28 -> 28, of which waited for: 9 -> 11; matrix products, arithmetic and copies ran while one was open for 19% -> 19% of each run, Pallas kernels for 38% -> 24%
where the time goes in v3:
time: 749 us; the launch traced here: 738 us
  Pallas kernels  401 us (54%)
  waiting for transfers between devices  82.9 us (11%)
  matrix products  71 us (9%)
  other arithmetic  65.3 us (9%)
  local copies, waits for them, and re-layouts  59.2 us (8%)
  starting transfers between devices  42.1 us (6%)
  between operations  16.1 us (2%)
    pallas_call x1, Pallas kernels, grads(): pl.pallas_call(partial(grads_kernel, self.halves, count, self.groups), gr...  89.2 us
    pallas_call x2, Pallas kernels, exchange(): pl.pallas_call(partial(exchange_kernel, own, share, chans, count), in_spe...  85.6 us
    ppermute x22, waiting for transfers between devices, swapped(): lax.ppermute(value, axis, [(source, source ^ bit) for source in range(cou...  80.5 us
    pallas_call x1, Pallas kernels, summed(): pl.pallas_call(partial(sum_kernel, count, places, [part.shape[0] for part...  64.7 us
    pallas_call x2, Pallas kernels, carried(): pl.pallas_call(partial(carry_kernel, count, reverse), in_specs=[vmem, vme...  39.8 us
    pallas_call x1, Pallas kernels, expert_passes(): pl.pallas_call(expert_kernel, grid=(hidden // tile,), in_specs=[pl.BlockS...  35 us
    ppermute x22, starting transfers between devices, swapped(): lax.ppermute(value, axis, [(source, source ^ bit) for source in range(cou...  29.8 us
    pallas_call x2, Pallas kernels, ends(): pl.pallas_call(partial(ends_kernel, self.halves, reverse), grid=(self.gro...  27.9 us
  transfers between devices with their start and end apart: 28, of which 11 were waited for; matrix products, arithmetic and copies ran while one was open for 19% of the time, Pallas kernels for 24%

profile of v3, /device:TPU:0, one launch (start us, length us, event | category | flops | bytes accessed | tf_op | source)
XLA Modules:
  0.0 737.5 jit_solution(12516650330124739420)
XLA Ops:
  7.3 3.0 copy.228
  13.6 2.6 multiply_convert_fusion.1
  16.2 2.9 collective-permute-start
  19.1 2.4 constant_dynamic-slice_fusion.3
  21.5 3.6 collective-permute-start.10
  26.4 9.4 %collective-permute-done = bf16[320,1152]{1,0:T(8,128)(2,1)S(1)} collective-permute-done((bf16[320,1152]{1,0:T(8,128)(2,1)}, bf16[320,1152]{1,0:T(8,128)(2,1)S(1)}, u32[]{:S(2)}, u32[]{:S(2)}) %collective-permute-start) | collective-permute-done | bytes 737312 | tf_op jit(solution)/shard_map/ppermute | solution.py:37
  37.7 6.2 fusion.2
  46.9 2.1 copy.146
  50.9 2.5 fusion.100
  56.5 6.6 collective-permute-done.2
  64.2 5.5 compare_select_fusion
  70.6 14.0 %scan_ends.1 = (f32[2,16,8,1152]{3,2,1,0:T(8,128)}, f32[2,8,1152]{2,1,0:T(8,128)}, f32[24,1152]{1,0:T(8,128)}) custom-call(f32[640,1152]{1,0:T(8,128)} %get-tuple-element.159.step_ref, f32[640,1152]{1,0:T(8,128)} %get-tuple-element.125.drive_ref.mixed_ref, f32[640,128]{1,0:T(8,128)} %broadcast_in_dim.38.break_ref, ...), custom_call_target="tpu_custom_call" | custom-call | flops 58982400 | bytes 8847360 | tf_op jit(solution)/shard_map/scan_ends/pallas_call | solution.py:783
  84.6 24.3 %carry.1.device = f32[16,1152]{1,0:T(8,128)} custom-call(f32[24,1152]{1,0:T(8,128)} %get-tuple-element.61.total_ref, f32[16,1152]{1,0:T(8,128)} %multiply_bitcast_fusion.rate_ref), custom_call_target="tpu_custom_call" | custom-call | tf_op jit(solution)/shard_map/carry/pallas_call | solution.py:306
  116.5 2.1 collective-permute-start.13
  121.0 6.0 fusion.17.gate_ref
  127.0 20.7 %scan_outputs.1 = (f32[640,1152]{1,0:T(8,128)}, bf16[640,1152]{1,0:T(8,128)(2,1)}, f32[2,16,8,1152]{3,2,1,0:T(8,128)}) custom-call(f32[640,1152]{1,0:T(8,128)} %get-tuple-element.159.step_ref, f32[640,1152]{1,0:T(8,128)} %get-tuple-element.125.drive_ref.mixed_ref, f32[640,128]{1,0:T(8,128)} %broadcast_in_dim.38.break_ref, ...), custom_call_target="tpu_custom_call" | custom-call | flops 82575360 | bytes 8847360 | tf_op jit(solution)/shard_map/scan_outputs/pallas_call | solution.py:796
  147.7 8.8 %collective-permute-done.12 = bf16[1,72,3072]{2,1,0:T(8,128)(2,1)S(1)} collective-permute-done((bf16[1,72,3072]{2,1,0:T(8,128)(2,1)S(1)}, bf16[1,72,3072]{2,1,0:T(8,128)(2,1)S(1)}, u32[]{:S(2)}, u32[]{:S(2)}) %collective-permute-start.12) | collective-permute-done | bytes 442400 | tf_op jit(solution)/shard_map/ppermute | solution.py:37
  163.7 2.5 convolution_convert_fusion.6
  167.7 11.2 %collective-permute-done.4 = bf16[4,64,1152]{2,1,0:T(8,128)(2,1)} collective-permute-done((bf16[4,64,1152]{2,1,0:T(8,128)(2,1)}, bf16[4,64,1152]{2,1,0:T(8,128)(2,1)}, u32[]{:S(2)}, u32[]{:S(2)}) %collective-permute-start.4) | collective-permute-done | bytes 589856 | tf_op jit(solution)/shard_map/ppermute | solution.py:37
  182.3 3.2 collective-permute-start.6
  186.7 6.6 collective-permute-done.3
  193.3 2.9 multiply_reduce_fusion.8
  196.2 2.1 fusion.39.own_ref
  198.3 14.4 %gather_small.2.logit_ref = f32[32,8,320]{2,1,0:T(8,128)} custom-call(f32[8,320]{1,0:T(8,128)} %fusion.39.own_ref), custom_call_target="tpu_custom_call" | custom-call | tf_op jit(solution)/shard_map/gather_small/pallas_call | solution.py:245
  212.7 4.8 sinkhorn.1
  219.6 2.0 convolution_convert_fusion.5
  221.6 32.2 %expert_rows.2 = (bf16[8,64,1152]{2,1,0:T(8,128)(2,1)}, f32[8,8,128]{2,1,0:T(8,128)}) custom-call(bf16[8,64,1152]{2,1,0:T(8,128)(2,1)} %bitcast.237, f32[8,8,128]{2,1,0:T(8,128)} %pad.28.refs_1_), custom_call_target="tpu_custom_call" | custom-call | tf_op jit(solution)/shard_map/expert_rows/pallas_call | solution.py:190
  261.9 35.0 %expert_passes.1 = (bf16[512,1152]{1,0:T(8,128)(2,1)}, bf16[512,1152]{1,0:T(8,128)(2,1)}, bf16[8,72,3072]{2,1,0:T(8,128)(2,1)}, bf16[8,72,3072]{2,1,0:T(8,128)(2...) custom-call(s32[1]{0:T(128)} %bitcast.22.side_ref, bf16[512,1152]{1,0:T(8,128)(2,1)} %bitcast.257, ...), custom_call_target="tpu_custom_call" | custom-call | flops 21743271936 | bytes 28311552 | tf_op jit(solution)/shard_map/expert_passes/pallas_call | solution.py:999
  297.4 6.1 collective-permute-done.14
  303.5 4.4 add_convert_fusion.1
  309.3 1.9 collective-permute-start.15
  311.8 3.3 add_convert_fusion
  318.3 1.9 collective-permute-start.17
  321.6 53.4 %expert_rows.3 = (bf16[8,64,1152]{2,1,0:T(8,128)(2,1)}, bf16[8,64,1152]{2,1,0:T(8,128)(2,1)}) custom-call(bf16[8,64,1152]{2,1,0:T(8,128)(2,1)} %bitcast.241, bf16[8,64,1152]{2,1,0:T(8,128)(2,1)} %bitcast.242), custom_call_target="tpu_custom_call" | custom-call | tf_op jit(solution)/shard_map/expert_rows/pallas_call | solution.py:190
  375.0 4.0 fusion.1
  379.1 9.3 %collective-permute-done.17 = bf16[4,1,72,3072]{3,2,0,1:T(8,128)(2,1)} collective-permute-done((bf16[4,1,72,3072]{3,2,0,1:T(8,128)(2,1)}, bf16[4,1,72,3072]{3,2,0,1:T(8,128)(2,1)}, u32[]{:S(2)}, u32[]{:S(2)}) %collective-permute-start.17) | collective-permute-done | bytes 1769504 | tf_op jit(solution)/shard_map/ppermute | solution.py:37
  388.4 3.4 fusion
  394.2 13.3 %gather_small.3.grad_ref = f32[32,8,320]{2,1,0:T(8,128)} custom-call(f32[8,320]{1,0:T(8,128)} %fusion.82.own_ref), custom_call_target="tpu_custom_call" | custom-call | tf_op jit(solution)/shard_map/gather_small/pallas_call | solution.py:245
  407.5 5.4 sinkhorn_back.1
  412.9 2.1 fusion.104
  415.0 2.1 multiply_reduce_fusion.5
  424.3 4.8 all-to-all-start
  429.1 9.8 %collective-permute-done.23 = f32[9,1152]{1,0:T(8,128)} collective-permute-done((f32[9,1152]{1,0:T(8,128)}, f32[9,1152]{1,0:T(8,128)}, u32[]{:S(2)}, u32[]{:S(2)}) %collective-permute-start.23) | collective-permute-done | bytes 41504 | tf_op jit(solution)/shard_map/ppermute | solution.py:37
  441.7 6.1 multiply_reduce_fusion
  448.4 13.9 %scan_ends_back.1 = (f32[2,16,8,1152]{3,2,1,0:T(8,128)}, f32[2,8,1152]{2,1,0:T(8,128)}, f32[24,1152]{1,0:T(8,128)}) custom-call(f32[640,1152]{1,0:T(8,128)} %get-tuple-element.159.step_ref, f32[640,1152]{1,0:T(8,128)} %get-tuple-element.121.drive_ref.grad_ref, f32[640,128]{1,0:T(8,128)} %broadcast_in_dim.38.break_ref, ...), custom_call_target="tpu_custom_call" | custom-call | flops 58982400 | bytes 8847360 | tf_op jit(solution)/shard_map/scan_ends_back/pallas_call | solution.py:783
  462.4 3.9 convolution_convert_fusion.2.first_early
  466.4 3.9 convolution_convert_fusion.1.second_early
  471.4 15.5 %carry_back.1.device = f32[16,1152]{1,0:T(8,128)} custom-call(f32[24,1152]{1,0:T(8,128)} %get-tuple-element.91.total_ref, f32[16,1152]{1,0:T(8,128)} %multiply_bitcast_fusion.rate_ref), custom_call_target="tpu_custom_call" | custom-call | tf_op jit(solution)/shard_map/carry_back/pallas_call | solution.py:306
  486.9 89.2 %scan_grads.1 = (f32[640,1152]{1,0:T(8,128)}, f32[640,1152]{1,0:T(8,128)}, f32[640,16]{1,0:T(8,128)}, f32[640,16]{1,0:T(8,128)}, f32[16,1152]{1,0:T(8,128)}, /*index=5*/bf16[9,256,1152]{2,1,0:T(8,128)(2,1)}) custom-call(f32[640,1152]{1,0:T(8,128)} %get-tuple-element.159.step_ref, f32[640,1152]{1,0:T(8,128)} %get-tuple-element.125.drive_ref.mixed_ref, ...), custom_call_target="tpu_custom_call" | custom-call | flops 235929600 | bytes 8847360 | tf_op jit(solution)/shard_map/scan_grads/pallas_call | solution.py:825
  576.1 2.7 fusion.98
  579.4 3.0 fusion.105
  582.4 4.8 all-to-all-start.1
  591.7 3.8 convert_element_type.273
  597.6 3.8 fusion.97
  601.5 6.1 multiply_reduce_fusion.2
  619.3 3.9 convolution_convert_fusion.refs_0_
  623.3 12.6 %collective-permute-done.21 = bf16[320,1152]{1,0:T(8,128)(2,1)S(1)} collective-permute-done((bf16[320,1152]{1,0:T(8,128)(2,1)S(1)}, bf16[320,1152]{1,0:T(8,128)(2,1)S(1)}, u32[]{:S(2)}, u32[]{:S(2)}) %collective-permute-start.21) | collective-permute-done | bytes 737312 | tf_op jit(solution)/shard_map/ppermute | solution.py:37
  635.9 3.1 multiply_reduce_fusion.6
  640.1 2.4 fusion.32
  646.7 64.7 %sum_late.1 = bf16[6,256,1152]{2,1,0:T(8,128)(2,1)} custom-call(bf16[1152,1152]{1,0:T(8,128)(2,1)} %convolution_convert_fusion.refs_0_, f32[224,1152]{1,0:T(8,128)} %pad.34.refs_1_), custom_call_target="tpu_custom_call" | custom-call | tf_op jit(solution)/shard_map/sum_late/pallas_call | solution.py:440
  712.6 2.1 slice_bitcast_fusion
  718.8 2.9 slice_convert_fusion
  721.7 4.8 maximum_convert_fusion
  726.5 3.7 convert_element_type.274
  (373 shorter events, 99.5 us)
Async XLA Ops:
  7.2 156.5 %copy-start = (bf16[1152,1152]{1,0:T(8,128)(2,1)S(1)}, bf16[1152,1152]{1,0:T(8,128)(2,1)}, u32[]{:S(2)}) copy-start(bf16[1152,1152]{1,0:T(8,128)(2,1)} %param.30) | copy-start | bytes 7962628
  7.2 254.7 %all-gather.3.cloned.1.call-start = ((), (), s32[]{:S(2)}) async-start(), calls=%async_computation.2 | async-start | bytes 8847360 | tf_op jit(solution)/shard_map/all_gather | solution.py:122
  12.4 23.5 %copy-start.71 = (f32[320]{0:T(512)}, f32[320]{0:T(512)S(1)}, u32[]{:S(2)}) copy-start(f32[320]{0:T(512)S(1)} %rsqrt.20) | copy-start | bytes 3844
  13.6 12.3 %copy-start.93 = (s32[4]{0:T(128)S(1)}, s32[4]{0:T(128)}, u32[]{:S(2)}) copy-start(s32[4]{0:T(128)} %param.20) | copy-start | bytes 52
  16.2 19.6 %collective-permute-start = (bf16[320,1152]{1,0:T(8,128)(2,1)}, bf16[320,1152]{1,0:T(8,128)(2,1)S(1)}, u32[]{:S(2)}, u32[]{:S(2)}) collective-permute-start(bf16[320,1152]{1,0:T(8,128)(2,1)} %multiply_convert_fusion.1), channel_id=1, source_target_pairs={{0,1},{1,0},{2,3},{3,2},{4,5},{5,4},{6,7},{7,6},{8,9},{9,8},{10,11... | collective-permute-start | bytes 2211848 | tf_op jit(solution)/shard_map/ppermute | solution.py:37
  21.5 87.4 %collective-permute-start.10 = (bf16[1,72,3072]{2,1,0:T(8,128)(2,1)}, bf16[1,72,3072]{2,1,0:T(8,128)(2,1)}, u32[]{:S(2)}, u32[]{:S(2)}) collective-permute-start(bf16[1,72,3072]{2,1,0:T(8,128)(2,1)} %get-tuple-element.139), channel_id=1, source_target_pairs={{0,24},{2,26},{4,28},{6,30},{8,16},{10,18},{12,20},{14,22},{16,8},... | collective-permute-start | bytes 1327112 | tf_op jit(solution)/shard_map/ppermute | solution.py:37
  25.1 83.9 %collective-permute-start.8 = (bf16[1,72,3072]{2,1,0:T(8,128)(2,1)}, bf16[1,72,3072]{2,1,0:T(8,128)(2,1)}, u32[]{:S(2)}, u32[]{:S(2)}) collective-permute-start(bf16[1,72,3072]{2,1,0:T(8,128)(2,1)} %get-tuple-element.140), channel_id=1, source_target_pairs={{0,8},{2,10},{4,12},{6,14},{8,0},{10,2},{12,4},{14,6},{16,24},{18,... | collective-permute-start | bytes 1327112 | tf_op jit(solution)/shard_map/ppermute | solution.py:37
  25.1 83.8 %collective-permute-start.9 = (bf16[1,72,3072]{2,1,0:T(8,128)(2,1)}, bf16[1,72,3072]{2,1,0:T(8,128)(2,1)}, u32[]{:S(2)}, u32[]{:S(2)}) collective-permute-start(bf16[1,72,3072]{2,1,0:T(8,128)(2,1)} %get-tuple-element.141), channel_id=1, source_target_pairs={{0,16},{2,18},{4,20},{6,22},{8,24},{10,26},{12,28},{14,30},{16,0},... | collective-permute-start | bytes 1327112 | tf_op jit(solution)/shard_map/ppermute | solution.py:37
  44.9 4.1 collective-permute-start.1
  53.5 16.3 %copy-start.10 = (bf16[640,1152]{1,0:T(8,128)(2,1)}, bf16[640,1152]{1,0:T(8,128)(2,1)S(1)}, u32[]{:S(2)}) copy-start(bf16[640,1152]{1,0:T(8,128)(2,1)S(1)} %get-tuple-element.126) | copy-start | bytes 4423684
  53.5 10.8 %copy-start.47 = (f32[72,1152]{1,0:T(8,128)S(1)}, f32[72,1152]{1,0:T(8,128)}, u32[]{:S(2)}) copy-start(f32[72,1152]{1,0:T(8,128)} %param.26) | copy-start | bytes 995332
  53.5 10.8 %copy-start.92 = (f32[1152]{0:T(1024)S(1)}, f32[1152]{0:T(1024)}, u32[]{:S(2)}) copy-start(f32[1152]{0:T(1024)} %param.27) | copy-start | bytes 13828
  54.0 9.0 %collective-permute-start.2 = (f32[640,104]{1,0:T(8,128)S(1)}, f32[640,104]{1,0:T(8,128)S(1)}, u32[]{:S(2)}, u32[]{:S(2)}) collective-permute-start(f32[640,104]{1,0:T(8,128)S(1)} %fusion.103), channel_id=1, source_target_pairs={{0,1},{1,0},{2,3},{3,2},{4,5},{5,4},{6,7},{7,6},{8,9},{9,8},{10,11... | collective-permute-start | bytes 798728 | tf_op jit(solution)/shard_map/ppermute | solution.py:37
  84.6 29.9 %copy-start.87 = (f32[1152]{0:T(1024)S(1)}, f32[1152]{0:T(1024)}, u32[]{:S(2)}) copy-start(f32[1152]{0:T(1024)} %param.29) | copy-start | bytes 13828
  114.5 147.4 %all-gather.5.cloned.1.call-start = ((), (), s32[]{:S(2)}) async-start(), calls=%async_computation.3 | async-start | bytes 8847360 | tf_op jit(solution)/shard_map/all_gather | solution.py:122
  116.5 31.2 %collective-permute-start.13 = (bf16[1,72,3072]{2,1,0:T(8,128)(2,1)S(1)}, bf16[1,72,3072]{2,1,0:T(8,128)(2,1)S(1)}, u32[]{:S(2)}, u32[]{:S(2)}) collective-permute-start(bf16[1,72,3072]{2,1,0:T(8,128)(2,1)S(1)} %get-tuple-element.136), channel_id=1, source_target_pairs={{0,24},{2,26},{4,28},{6,30},{8,16},{10,18},{12,20},{14,22},{16,8},... | collective-permute-start | bytes 1327112 | tf_op jit(solution)/shard_map/ppermute | solution.py:37
  118.6 37.9 %collective-permute-start.12 = (bf16[1,72,3072]{2,1,0:T(8,128)(2,1)S(1)}, bf16[1,72,3072]{2,1,0:T(8,128)(2,1)S(1)}, u32[]{:S(2)}, u32[]{:S(2)}) collective-permute-start(bf16[1,72,3072]{2,1,0:T(8,128)(2,1)S(1)} %get-tuple-element.137), channel_id=1, source_target_pairs={{0,16},{2,18},{4,20},{6,22},{8,24},{10,26},{12,28},{14,30},{16,0},... | collective-permute-start | bytes 1327112 | tf_op jit(solution)/shard_map/ppermute | solution.py:37
  120.0 36.6 %collective-permute-start.11 = (bf16[1,72,3072]{2,1,0:T(8,128)(2,1)S(1)}, bf16[1,72,3072]{2,1,0:T(8,128)(2,1)S(1)}, u32[]{:S(2)}, u32[]{:S(2)}) collective-permute-start(bf16[1,72,3072]{2,1,0:T(8,128)(2,1)S(1)} %get-tuple-element.138), channel_id=1, source_target_pairs={{0,8},{2,10},{4,12},{6,14},{8,0},{10,2},{12,4},{14,6},{16,24},{18,... | collective-permute-start | bytes 1327112 | tf_op jit(solution)/shard_map/ppermute | solution.py:37
  147.7 11.3 %copy-start.91 = (s32[320,1]{0,1:T(1,128)S(1)}, s32[320,1]{0,1:T(1,128)}, u32[]{:S(2)}) copy-start(s32[320,1]{0,1:T(1,128)} %param.19) | copy-start | bytes 3844
  147.7 11.9 %copy-start.15 = (bf16[320,1152]{1,0:T(8,128)(2,1)S(1)}, bf16[320,1152]{1,0:T(8,128)(2,1)}, u32[]{:S(2)}) copy-start(bf16[320,1152]{1,0:T(8,128)(2,1)} %param.35) | copy-start | bytes 2211844
  162.4 16.6 %collective-permute-start.4 = (bf16[4,64,1152]{2,1,0:T(8,128)(2,1)}, bf16[4,64,1152]{2,1,0:T(8,128)(2,1)}, u32[]{:S(2)}, u32[]{:S(2)}) collective-permute-start(bf16[4,64,1152]{2,1,0:T(8,128)(2,1)} %dynamic-slice_bitcast_fusion.2), channel_id=1, source_target_pairs={{0,1},{1,0},{2,3},{3,2},{4,5},{5,4},{6,7},{7,6},{8,9},{9,8},{10,11... | collective-permute-start | bytes 1769480 | tf_op jit(solution)/shard_map/ppermute | solution.py:37
  163.7 15.3 %copy-start.30 = (bf16[512,1152]{1,0:T(8,128)(2,1)S(1)}, bf16[512,1152]{1,0:T(8,128)(2,1)}, u32[]{:S(2)}) copy-start(bf16[512,1152]{1,0:T(8,128)(2,1)} %copy-done.29) | copy-start | bytes 3538948
  166.1 27.1 %collective-permute-start.3 = (bf16[320,1152]{1,0:T(8,128)(2,1)S(1)}, bf16[320,1152]{1,0:T(8,128)(2,1)S(1)}, u32[]{:S(2)}, u32[]{:S(2)}) collective-permute-start(bf16[320,1152]{1,0:T(8,128)(2,1)S(1)} %convolution_convert_fusion.6), channel_id=1, source_target_pairs={{0,1},{1,0},{2,3},{3,2},{4,5},{5,4},{6,7},{7,6},{8,9},{9,8},{10,11... | collective-permute-start | bytes 2211848 | tf_op jit(solution)/shard_map/ppermute | solution.py:37
  180.2 13.1 %copy-start.94 = (bf16[640,1152]{1,0:T(8,128)(2,1)S(1)}, bf16[640,1152]{1,0:T(8,128)(2,1)}, u32[]{:S(2)}) copy-start(bf16[640,1152]{1,0:T(8,128)(2,1)} %get-tuple-element.62) | copy-start | bytes 4423684
  181.1 79.0 %collective-permute-start.7 = (bf16[2,1,64,1152]{3,2,1,0:T(8,128)(2,1)}, bf16[2,1,64,1152]{3,2,1,0:T(8,128)(2,1)}, u32[]{:S(2)}, u32[]{:S(2)}) collective-permute-start(bf16[2,1,64,1152]{3,2,1,0:T(8,128)(2,1)} %get-tuple-element.150), channel_id=1, source_target_pairs={{0,24},{2,26},{4,28},{6,30},{8,16},{10,18},{12,20},{14,22},{16,8},... | collective-permute-start | bytes 884744 | tf_op jit(solution)/shard_map/ppermute | solution.py:37
  182.3 74.5 %collective-permute-start.5 = (bf16[2,1,64,1152]{3,2,1,0:T(8,128)(2,1)}, bf16[2,1,64,1152]{3,2,1,0:T(8,128)(2,1)}, u32[]{:S(2)}, u32[]{:S(2)}) collective-permute-start(bf16[2,1,64,1152]{3,2,1,0:T(8,128)(2,1)} %get-tuple-element.151), channel_id=1, source_target_pairs={{0,8},{2,10},{4,12},{6,14},{8,0},{10,2},{12,4},{14,6},{16,24},{18,... | collective-permute-start | bytes 884744 | tf_op jit(solution)/shard_map/ppermute | solution.py:37
  182.3 76.2 %collective-permute-start.6 = (bf16[2,1,64,1152]{3,2,1,0:T(8,128)(2,1)}, bf16[2,1,64,1152]{3,2,1,0:T(8,128)(2,1)}, u32[]{:S(2)}, u32[]{:S(2)}) collective-permute-start(bf16[2,1,64,1152]{3,2,1,0:T(8,128)(2,1)} %get-tuple-element.152), channel_id=1, source_target_pairs={{0,16},{2,18},{4,20},{6,22},{8,24},{10,26},{12,28},{14,30},{16,0},... | collective-permute-start | bytes 884744 | tf_op jit(solution)/shard_map/ppermute | solution.py:37
  186.7 9.5 %copy-start.49 = (f32[1152]{0:T(1024)S(1)}, f32[1152]{0:T(1024)}, u32[]{:S(2)}) copy-start(f32[1152]{0:T(1024)} %param.31) | copy-start | bytes 13828
  186.7 9.5 %copy-start.56 = (f32[1152,8]{0,1:T(8,128)S(1)}, f32[1152,8]{0,1:T(8,128)}, u32[]{:S(2)}) copy-start(f32[1152,8]{0,1:T(8,128)} %param.32) | copy-start | bytes 110596
  186.7 30.8 %copy-start.74 = (s32[320]{0:T(512)S(1)}, s32[320]{0:T(512)}, u32[]{:S(2)}) copy-start(s32[320]{0:T(512)} %copy-done.73) | copy-start | bytes 3844
  196.1 23.4 %copy-start.2 = (f32[320,1152]{1,0:T(8,128)}, f32[320,1152]{1,0:T(8,128)S(1)}, u32[]{:S(2)}) copy-start(f32[320,1152]{1,0:T(8,128)S(1)} %get-tuple-element.162) | copy-start | bytes 4423684
  196.2 25.4 %copy-start.85 = (f32[320]{0:T(512)}, f32[320]{0:T(512)S(1)}, u32[]{:S(2)}) copy-start(f32[320]{0:T(512)S(1)} %get-tuple-element.161) | copy-start | bytes 3844
  196.2 222.9 %copy-start.58 = (f32[320]{0:T(512)}, f32[320]{0:T(512)S(1)}, u32[]{:S(2)}) copy-start(f32[320]{0:T(512)S(1)} %fusion.92) | copy-start | bytes 3844
  296.9 6.6 collective-permute-start.14
  296.9 14.3 %collective-permute-start.16 = (bf16[8,72,3072]{2,1,0:T(8,128)(2,1)}, bf16[8,72,3072]{2,1,0:T(8,128)(2,1)}, u32[]{:S(2)}, u32[]{:S(2)}) collective-permute-start(bf16[8,72,3072]{2,1,0:T(8,128)(2,1)} %get-tuple-element.80), channel_id=1, source_target_pairs={{0,2},{2,0},{4,6},{6,4},{8,10},{10,8},{12,14},{14,12},{16,18},{18,... | collective-permute-start | bytes 10616840 | tf_op jit(solution)/shard_map/ppermute | solution.py:37
  307.9 10.4 %copy-start.5 = (bf16[8,72,3072]{2,1,0:T(8,128)(2,1)}, bf16[8,72,3072]{2,1,0:T(8,128)(2,1)S(1)}, u32[]{:S(2)}) copy-start(bf16[8,72,3072]{2,1,0:T(8,128)(2,1)S(1)} %add_convert_fusion.1) | copy-start | bytes 10616836
  309.3 65.7 %collective-permute-start.15 = (bf16[4,1,72,3072]{3,2,0,1:T(8,128)(2,1)}, bf16[4,1,72,3072]{3,2,0,1:T(8,128)(2,1)}, u32[]{:S(2)}, u32[]{:S(2)}) collective-permute-start(bf16[4,1,72,3072]{3,2,0,1:T(8,128)(2,1)} %dynamic-slice_bitcast_fusion.1), channel_id=1, source_target_pairs={{0,4},{2,6},{4,0},{6,2},{8,12},{10,14},{12,8},{14,10},{16,20},{18,... | collective-permute-start | bytes 5308424 | tf_op jit(solution)/shard_map/ppermute | solution.py:37
  318.3 70.1 %collective-permute-start.17 = (bf16[4,1,72,3072]{3,2,0,1:T(8,128)(2,1)}, bf16[4,1,72,3072]{3,2,0,1:T(8,128)(2,1)}, u32[]{:S(2)}, u32[]{:S(2)}) collective-permute-start(bf16[4,1,72,3072]{3,2,0,1:T(8,128)(2,1)} %dynamic-slice_bitcast_fusion), channel_id=1, source_target_pairs={{0,4},{2,6},{4,0},{6,2},{8,12},{10,14},{12,8},{14,10},{16,20},{18,... | collective-permute-start | bytes 5308424 | tf_op jit(solution)/shard_map/ppermute | solution.py:37
  321.6 93.4 %copy-start.77 = (f32[320]{0:T(512)}, f32[320]{0:T(512)S(1)}, u32[]{:S(2)}) copy-start(f32[320]{0:T(512)S(1)} %reduce.10) | copy-start | bytes 3844
  375.0 13.4 %copy-start.7 = (bf16[8,72,3072]{2,1,0:T(8,128)(2,1)S(1)}, bf16[8,72,3072]{2,1,0:T(8,128)(2,1)}, u32[]{:S(2)}) copy-start(bf16[8,72,3072]{2,1,0:T(8,128)(2,1)} %copy-done.6) | copy-start | bytes 10616836
  379.1 12.7 %copy-start.28 = (bf16[8,64,1152]{2,1,0:T(8,128)(2,1)S(1)}, bf16[8,64,1152]{2,1,0:T(8,128)(2,1)}, u32[]{:S(2)}) copy-start(bf16[8,64,1152]{2,1,0:T(8,128)(2,1)} %get-tuple-element.81) | copy-start | bytes 3538948
  418.5 22.0 %collective-permute-start.18 = (bf16[320,1152]{1,0:T(8,128)(2,1)}, bf16[320,1152]{1,0:T(8,128)(2,1)S(1)}, u32[]{:S(2)}, u32[]{:S(2)}) collective-permute-start(bf16[320,1152]{1,0:T(8,128)(2,1)} %fusion.96), channel_id=1, source_target_pairs={{0,1},{1,0},{2,3},{3,2},{4,5},{5,4},{6,7},{7,6},{8,9},{9,8},{10,11... | collective-permute-start | bytes 2211848 | tf_op jit(solution)/shard_map/ppermute | solution.py:37
  420.7 18.2 %collective-permute-start.23 = (f32[9,1152]{1,0:T(8,128)}, f32[9,1152]{1,0:T(8,128)}, u32[]{:S(2)}, u32[]{:S(2)}) collective-permute-start(f32[9,1152]{1,0:T(8,128)} %pad_maximum_fusion.7), channel_id=1, source_target_pairs={{0,1},{1,0},{2,3},{3,2},{4,5},{5,4},{6,7},{7,6},{8,9},{9,8},{10,11... | collective-permute-start | bytes 124424 | tf_op jit(solution)/shard_map/ppermute | solution.py:37
  424.3 47.1 %all-to-all-start = ((bf16[4,72,3072]{2,1,0:T(8,128)(2,1)}), bf16[4,72,3072]{2,1,0:T(8,128)(2,1)}, u32[]{:S(2)}, u32[]{:S(2)}) async-start(bf16[4,72,3072]{2,1,0:T(8,128)(2,1)} %bitcast.227), calls=%async_computation | async-start | bytes 3538944 | tf_op jit(solution)/shard_map/all_to_all | solution.py:89
  429.1 12.6 %copy-start.11 = (bf16[640,1152]{1,0:T(8,128)(2,1)S(1)}, bf16[640,1152]{1,0:T(8,128)(2,1)}, u32[]{:S(2)}) copy-start(bf16[640,1152]{1,0:T(8,128)(2,1)} %copy-done.10) | copy-start | bytes 4423684
  447.8 18.5 %copy-start.26 = (bf16[640,1152]{1,0:T(8,128)(2,1)}, bf16[640,1152]{1,0:T(8,128)(2,1)S(1)}, u32[]{:S(2)}) copy-start(bf16[640,1152]{1,0:T(8,128)(2,1)S(1)} %get-tuple-element.127) | copy-start | bytes 4423684
  448.4 13.9 %copy-start.95 = (bf16[640,1152]{1,0:T(8,128)(2,1)S(1)}, bf16[640,1152]{1,0:T(8,128)(2,1)}, u32[]{:S(2)}) copy-start(bf16[640,1152]{1,0:T(8,128)(2,1)} %get-tuple-element.62) | copy-start | bytes 4423684
  486.9 89.2 %copy-start.21 = (f32[640,1152]{1,0:T(8,128)S(1)}, f32[640,1152]{1,0:T(8,128)}, u32[]{:S(2)}) copy-start(f32[640,1152]{1,0:T(8,128)} %get-tuple-element.160) | copy-start | bytes 8847364
  582.4 64.2 %all-to-all-start.1 = ((bf16[4,72,3072]{2,1,0:T(8,128)(2,1)}), bf16[4,72,3072]{2,1,0:T(8,128)(2,1)}, u32[]{:S(2)}, u32[]{:S(2)}) async-start(bf16[4,72,3072]{2,1,0:T(8,128)(2,1)} %bitcast.226), calls=%async_computation.1 | async-start | bytes 3538944 | tf_op jit(solution)/shard_map/all_to_all | solution.py:89
  590.1 7.3 collective-permute-start.19
  608.5 3.1 collective-permute-start.20
  617.1 18.8 %collective-permute-start.21 = (bf16[320,1152]{1,0:T(8,128)(2,1)S(1)}, bf16[320,1152]{1,0:T(8,128)(2,1)S(1)}, u32[]{:S(2)}, u32[]{:S(2)}) collective-permute-start(bf16[320,1152]{1,0:T(8,128)(2,1)S(1)} %fusion.14), channel_id=1, source_target_pairs={{0,1},{1,0},{2,3},{3,2},{4,5},{5,4},{6,7},{7,6},{8,9},{9,8},{10,11... | collective-permute-start | bytes 2211848 | tf_op jit(solution)/shard_map/ppermute | solution.py:37
  619.3 16.6 %copy-start.69 = (f32[1152]{0:T(1024)S(1)}, f32[1152]{0:T(1024)}, u32[]{:S(2)}) copy-start(f32[1152]{0:T(1024)} %param.21) | copy-start | bytes 13828
  619.3 16.6 %copy-start.72 = (f32[320]{0:T(512)S(1)}, f32[320]{0:T(512)}, u32[]{:S(2)}) copy-start(f32[320]{0:T(512)} %copy-done.71) | copy-start | bytes 3844
  623.3 16.8 %copy-start.81 = (f32[320]{0:T(512)S(1)}, f32[320]{0:T(512)}, u32[]{:S(2)}) copy-start(f32[320]{0:T(512)} %copy-done.80) | copy-start | bytes 3844
  623.3 16.8 %copy-start.4 = (f32[320,1152]{1,0:T(8,128)S(1)}, f32[320,1152]{1,0:T(8,128)}, u32[]{:S(2)}) copy-start(f32[320,1152]{1,0:T(8,128)} %copy-done.2) | copy-start | bytes 4423684
  623.3 16.8 %copy-start.9 = (f32[320,1152]{1,0:T(8,128)S(1)}, f32[320,1152]{1,0:T(8,128)}, u32[]{:S(2)}) copy-start(f32[320,1152]{1,0:T(8,128)} %copy-done.8) | copy-start | bytes 4423684
  623.3 16.8 %copy-start.16 = (bf16[320,1152]{1,0:T(8,128)(2,1)S(1)}, bf16[320,1152]{1,0:T(8,128)(2,1)}, u32[]{:S(2)}) copy-start(bf16[320,1152]{1,0:T(8,128)(2,1)} %param.35) | copy-start | bytes 2211844
  623.3 16.8 %copy-start.17 = (f32[320,1152]{1,0:T(8,128)S(1)}, f32[320,1152]{1,0:T(8,128)}, u32[]{:S(2)}) copy-start(f32[320,1152]{1,0:T(8,128)} %get-tuple-element.164) | copy-start | bytes 4423684
  623.3 16.8 %copy-start.59 = (f32[320]{0:T(512)S(1)}, f32[320]{0:T(512)}, u32[]{:S(2)}) copy-start(f32[320]{0:T(512)} %copy-done.58) | copy-start | bytes 3844
  623.3 16.8 %copy-start.76 = (f32[320]{0:T(512)S(1)}, f32[320]{0:T(512)}, u32[]{:S(2)}) copy-start(f32[320]{0:T(512)} %copy-done.75) | copy-start | bytes 3844
  623.3 16.8 %copy-start.78 = (f32[320]{0:T(512)S(1)}, f32[320]{0:T(512)}, u32[]{:S(2)}) copy-start(f32[320]{0:T(512)} %copy-done.77) | copy-start | bytes 3844
  639.1 5.8 collective-permute-start.22
  646.6 72.2 %slice-start = ((s8[5308416]{0:T(1024)(128)(4,1)}), s8[1114112]{0:T(1024)(128)(4,1)S(1)}, s32[]{:S(2)}) async-start(s8[5308416]{0:T(1024)(128)(4,1)} %bitcast.234), calls=%async_computation.4 | async-start | bytes 2228224
  (66 other events, 247.2 us)
Sparse Core Ops, SparseCore 0:
  114.6 50.5 all-gather.2
  167.3 55.0 all-gather.4

commit v4 on v3

--- a/solution.py
+++ b/solution.py
@@ -91,23 +91,6 @@
     )
 
 
-def expert_rows_early(packed):
-    own, share = expert_groups()
-    count = lax.axis_size("chan")
-    slots, width = packed.shape[1:]
-    if count == 2:
-        place = lax.axis_index("chan")
-        halves = packed.reshape(2, own, slots, width)
-        kept = lax.dynamic_index_in_dim(halves, place, 0, False)
-        came = swapped(lax.dynamic_index_in_dim(halves, 1 - place, 0, False), "chan", 1)
-        first = place == 0
-        arrived = jnp.stack([jnp.where(first, kept, came), jnp.where(first, came, kept)])
-    else:
-        arrived = lax.all_to_all(packed, "chan", split_axis=0, concat_axis=0, tiled=True)
-        arrived = arrived.reshape(count, own, slots, width)
-    return across_experts(arrived, 1).reshape(count * own, slots, width)
-
-
 def expert_rows(ident, *arrays):
     return exchange(ident, arrays)
 
@@ -141,6 +124,10 @@
     return lax.optimization_barrier((value,) + others)[0]
 
 
+def lasting(microseconds):
+    return pl.CostEstimate(flops=0, bytes_accessed=microseconds * 3_600_000, transcendentals=0)
+
+
 def opposite(place, bit):
     return place + bit - 2 * bit * lax.rem(lax.div(place, bit), 2)
 
@@ -152,57 +139,72 @@
     pl.semaphore_wait(barrier, len(targets))
 
 
+class Exchange:
+    def __init__(self, own, share, chans, sources, results, send_sem, recv_sem, own_sem):
+        seq, chan = lax.axis_index("seq"), lax.axis_index("chan")
+        column = lax.rem(seq, share)
+        me = chan * own + lax.div(seq, share)
+        total = own * chans
+        peers = [lax.rem(me + d, total) for d in range(1, total)]
+        self.targets = [(lax.rem(peer, own) * share + column, lax.div(peer, own)) for peer in peers]
+        self.copies = []
+        for k, (source, result) in enumerate(zip(sources, results)):
+            for d in range(total - 1):
+                self.copies.append(
+                    pltpu.make_async_remote_copy(
+                        src_ref=source.at[peers[d]],
+                        dst_ref=result.at[me],
+                        send_sem=send_sem.at[k, d],
+                        recv_sem=recv_sem.at[k, d],
+                        device_id=self.targets[d],
+                        device_id_type=MESH,
+                    )
+                )
+            self.copies.append(pltpu.make_async_copy(source.at[me], result.at[me], own_sem.at[k]))
+
+    def start(self):
+        greet(self.targets)
+        for copy in self.copies:
+            copy.start()
+
+    def wait(self):
+        for copy in self.copies:
+            copy.wait()
+
+
+def exchange_scratch(count):
+    others = expert_groups()[0] * lax.axis_size("chan") - 1
+    return [
+        pltpu.SemaphoreType.DMA((count, others)),
+        pltpu.SemaphoreType.DMA((count, others)),
+        pltpu.SemaphoreType.DMA((count,)),
+    ]
+
+
 def exchange_kernel(own, share, chans, count, *refs):
-    sources, results = refs[:count], refs[count : 2 * count]
-    send_sem, recv_sem, own_sem = refs[2 * count :]
-    seq, chan = lax.axis_index("seq"), lax.axis_index("chan")
-    column = lax.rem(seq, share)
-    me = chan * own + lax.div(seq, share)
-    total = own * chans
-    peers = [lax.rem(me + d, total) for d in range(1, total)]
-    targets = [(lax.rem(peer, own) * share + column, lax.div(peer, own)) for peer in peers]
-    greet(targets)
-    copies = []
-    for k in range(count):
-        for d in range(total - 1):
-            copies.append(
-                pltpu.make_async_remote_copy(
-                    src_ref=sources[k].at[peers[d]],
-                    dst_ref=results[k].at[me],
-                    send_sem=send_sem.at[k, d],
-                    recv_sem=recv_sem.at[k, d],
-                    device_id=targets[d],
-                    device_id_type=MESH,
-                )
-            )
-        copies.append(pltpu.make_async_copy(sources[k].at[me], results[k].at[me], own_sem.at[k]))
-    for copy in copies:
-        copy.start()
-    for copy in copies:
-        copy.wait()
+    rows = Exchange(own, share, chans, refs[:count], refs[count : 2 * count], *refs[2 * count :])
+    rows.start()
+    rows.wait()
 
 
 def exchange(ident, arrays):
     own, share = expert_groups()
     chans, count = lax.axis_size("chan"), len(arrays)
     anywhere = pl.BlockSpec(memory_space=pl.ANY)
-    others = own * chans - 1
     return pl.pallas_call(
         partial(exchange_kernel, own, share, chans, count),
         in_specs=[anywhere] * count,
         out_specs=[anywhere] * count,
         out_shape=[jax.ShapeDtypeStruct(part.shape, part.dtype) for part in arrays],
-        scratch_shapes=[
-            pltpu.SemaphoreType.DMA((count, others)),
-            pltpu.SemaphoreType.DMA((count, others)),
-            pltpu.SemaphoreType.DMA((count,)),
-        ],
+        scratch_shapes=exchange_scratch(count),
         compiler_params=pltpu.CompilerParams(collective_id=ident, has_side_effects=True),
+        cost_estimate=lasting(26 * count),
         name="expert_rows",
     )(*arrays)
 
 
-def gather_kernel(devices, chans, own_ref, every_ref, send_sem, recv_sem):
+def gather_kernel(devices, chans, passed, own_ref, *refs):
+    every_ref, send_sem, recv_sem = refs[passed], refs[-2], refs[-1]
     me = lax.axis_index("seq") * chans + lax.axis_index("chan")
     barrier = pltpu.get_barrier_semaphore()
 
@@ -239,28 +241,32 @@
     lax.fori_loop(1, devices, finish, 0)
 
 
-def gathered_everywhere(values):
+def gathered_everywhere(ident, values, *passed):
     chans = lax.axis_size("chan")
     devices = lax.axis_size("seq") * chans
-    return pl.pallas_call(
-        partial(gather_kernel, devices, chans),
-        in_specs=[pl.BlockSpec(memory_space=pltpu.VMEM)],
-        out_specs=pl.BlockSpec(memory_space=pltpu.VMEM),
-        out_shape=jax.ShapeDtypeStruct((devices,) + values.shape, values.dtype),
+    vmem, anywhere = pl.BlockSpec(memory_space=pltpu.VMEM), pl.BlockSpec(memory_space=pl.ANY)
+    out = pl.pallas_call(
+        partial(gather_kernel, devices, chans, len(passed)),
+        in_specs=[vmem] + [anywhere] * len(passed),
+        out_specs=[vmem] + [anywhere] * len(passed),
+        out_shape=[jax.ShapeDtypeStruct((devices,) + values.shape, values.dtype)]
+        + [jax.ShapeDtypeStruct(part.shape, part.dtype) for part in passed],
+        input_output_aliases={1 + k: 1 + k for k in range(len(passed))},
         scratch_shapes=[
             pltpu.SemaphoreType.DMA((devices - 1,)),
             pltpu.SemaphoreType.DMA((devices - 1,)),
         ],
         compiler_params=pltpu.CompilerParams(
-            collective_id=3, has_side_effects=True, vmem_limit_bytes=VMEM_LIMIT
+            collective_id=ident, has_side_effects=True, vmem_limit_bytes=VMEM_LIMIT
         ),
+        cost_estimate=lasting(12),
         name="gather_small",
-    )(values)
-
-
-def carry_kernel(
-    count, reverse, total_ref, rate_ref, entry_ref, ends_out, ends_in, sums_out, sums_in, ends_sems, sums_sems
-):
+    )(values, *passed)
+    return out if passed else out[0]
+
+
+def carry_kernel(count, reverse, total_ref, rate_ref, *refs):
+    entry_ref, ends_out, ends_in, sums_out, sums_in, ends_sems, sums_sems = refs[-7:]
     me = lax.axis_index("seq")
     bits = [1 << k for k in range(count.bit_length() - 1)]
     greet([{"seq": opposite(me, bit)} for bit in bits])
@@ -298,14 +304,14 @@
     entry_ref[...] = before
 
 
-def carried(total, rates, reverse):
+def carried(total, rates, reverse, *needed):
     count = lax.axis_size("seq")
     rounds = count.bit_length() - 1
     channels = rates.shape[1]
     vmem = pl.BlockSpec(memory_space=pltpu.VMEM)
     return pl.pallas_call(
         partial(carry_kernel, count, reverse),
-        in_specs=[vmem, vmem],
+        in_specs=[vmem, vmem] + [pl.BlockSpec(memory_space=pl.ANY)] * len(needed),
         out_specs=vmem,
         out_shape=jax.ShapeDtypeStruct(rates.shape, jnp.float32),
         scratch_shapes=[
@@ -319,8 +325,9 @@
         compiler_params=pltpu.CompilerParams(
             collective_id=5 if reverse else 4, has_side_effects=True, vmem_limit_bytes=VMEM_LIMIT
         ),
+        cost_estimate=lasting(14),
         name="carry_back" if reverse else "carry",
-    )(total, rates)
+    )(total, rates, *needed)
 
 
 class Halving:
@@ -446,6 +453,7 @@
         compiler_params=pltpu.CompilerParams(
             collective_id=6, has_side_effects=True, vmem_limit_bytes=VMEM_LIMIT
         ),
+        cost_estimate=lasting(60),
         name="sum_late",
     )(*padded).reshape(chunks * chunk, width)
     return [total[place : place + size].astype(jnp.float32) for place, size in zip(places, sizes)]
@@ -514,6 +522,21 @@
     for by, window in zip((1, 2, 4), windows):
         ends = ends + jnp.exp2(rate * window) * shifted(ends, by, down)
     return ends
+
+
+def ends_and_rows_kernel(halves, places, *refs):
+    ins, source, outs, result, wide, sems = refs[:5], refs[5], refs[6:9], refs[9], refs[10], refs[11:]
+    rows = Exchange(*places, [source], [result], *sems)
+
+    @pl.when(pl.program_id(0) == 0)
+    def _():
+        rows.start()
+
+    ends_kernel(halves, False, *ins, *outs, wide)
+
+    @pl.when(pl.program_id(0) == pl.num_programs(0) - 1)
+    def _():
+        rows.wait()
 
 
 def ends_kernel(halves, reverse, step_ref, drive_ref, break_ref, map_ref, rate_ref, part_ref, sum_ref, tot_ref, wide):
@@ -779,18 +802,30 @@
             flops=per_element * count, bytes_accessed=12 * self.rows * self.channels, transcendentals=count
         )
 
-    def ends(self, reverse, step, drive, breaks, maps, rates):
+    def ends(self, step, drive, breaks, maps, rates, blocks=None):
+        anywhere = [pl.BlockSpec(memory_space=pl.ANY)]
+        forward = blocks is not None
+        places = expert_groups() + (lax.axis_size("chan"),)
+        kernel = partial(ends_and_rows_kernel, self.halves, places) if forward else partial(ends_kernel, self.halves, True)
+        params = self.params()
+        if forward:
+            params = pltpu.CompilerParams(
+                dimension_semantics=("arbitrary",), vmem_limit_bytes=VMEM_LIMIT, collective_id=8,
+                has_side_effects=True,
+            )
         return pl.pallas_call(
-            partial(ends_kernel, self.halves, reverse),
+            kernel,
             grid=(self.groups,),
-            in_specs=[self.row_spec, self.row_spec, self.break_spec, self.map_spec, self.rate_spec],
-            out_specs=[self.part_spec, self.sum_spec, self.tot_spec],
-            out_shape=[self.part_f32, self.sum_f32, self.tot_f32],
-            scratch_shapes=[self.wide],
-            compiler_params=self.params(),
+            in_specs=[self.row_spec, self.row_spec, self.break_spec, self.map_spec, self.rate_spec]
+            + anywhere * forward,
+            out_specs=[self.part_spec, self.sum_spec, self.tot_spec] + anywhere * forward,
+            out_shape=[self.part_f32, self.sum_f32, self.tot_f32]
+            + ([jax.ShapeDtypeStruct(blocks.shape, blocks.dtype)] if forward else []),
+            scratch_shapes=[self.wide] + (exchange_scratch(1) if forward else []),
+            compiler_params=params,
             cost_estimate=self.cost(5),
-            name="scan_ends_back" if reverse else "scan_ends",
-        )(step, drive, breaks, maps, rates)
+            name="scan_ends" if forward else "scan_ends_back",
+        )(step, drive, breaks, maps, rates, *([blocks] if forward else []))
 
     def outputs(self, step, mixed, breaks, b_in, c_out, rates, part, sums, device, skip, gate):
         return pl.pallas_call(
@@ -926,25 +961,34 @@
 
 
 def expert_kernel(
-    side_ref, rows_ref, grad_ref, gate_ref, up_ref, down_ref, out_ref, back_ref, up_kept, up_sent, down_kept,
-    down_sent, rows_t, grad_t, out_sum, back_sum, whole,
+    share, rows_ref, grad_ref, gate_ref, up_ref, down_ref, out_ref, back_ref, up_kept, up_sent, down_kept,
+    down_sent, rows_t, grad_t, out_sum, back_sum, whole, half, held, sent, came, send_sem, recv_sem,
 ):
-    step = pl.program_id(0)
-    features = up_kept.shape[1]
+    step, last = pl.program_id(0), pl.num_programs(0) - 1
+    features = up_ref.shape[2]
+    me = lax.axis_index("seq")
+    side, next_side = lax.rem(me, 2), lax.rem(lax.div(me, 2), 2)
+    peer = {"seq": opposite(me, 1)}
+
+    def copy(k):
+        return pltpu.make_async_remote_copy(
+            src_ref=sent.at[k], dst_ref=came.at[k], send_sem=send_sem.at[k], recv_sem=recv_sem.at[k],
+            device_id=peer, device_id_type=MESH,
+        )
 
     @pl.when(step == 0)
     def _():
+        greet([peer])
         rows_t[...] = rows_ref[...].T
         grad_t[...] = (grad_ref[...].astype(jnp.float32) * gate_ref[...]).astype(jnp.bfloat16).T
 
-    def parted(total, kept, sent):
+    def halved_rows(total, which):
         whole[...] = total
-        first = side_ref[0] == 0
-        for k in range(kept.shape[0]):
+        for k in range(half.shape[0] // features):
             low = whole[2 * k * features : (2 * k + 1) * features]
             high = whole[(2 * k + 1) * features : (2 * k + 2) * features]
-            kept[k] = jnp.where(first, low, high).astype(kept.dtype)
-            sent[k] = jnp.where(first, high, low).astype(sent.dtype)
+            half[k * features : (k + 1) * features] = jnp.where(which == 0, low, high)
+        return half[...].astype(jnp.bfloat16)
 
     def dot(a, b, over=((1,), (0,))):
         return lax.dot_general(a, b, (over, ((), ())), preferred_element_type=jnp.float32)
@@ -956,52 +1000,74 @@
                 whole[first : first + features] = ref[q, j].astype(jnp.float32)
         return whole[...].astype(jnp.bfloat16)
 
-    across = ((1,), (1,))
-    up, down = joined(up_ref), joined(down_ref)
-    pre = dot(rows_ref[...], up)
-    square = pre * pre
-    bend = jnp.tanh(GELU_SCALE * (pre + GELU_CUBE * pre * square))
-    half = 0.5 * (1.0 + bend)
-    act = (pre * half).astype(jnp.bfloat16)
-    slope = half + 0.5 * pre * (1.0 - bend * bend) * (GELU_SCALE + 3.0 * GELU_SCALE * GELU_CUBE * square)
-    grad_pre = dot(grad_ref[...], down) * slope
-    out_part, back_part = dot(act, down, across), dot(grad_pre.astype(jnp.bfloat16), up, across)
-
-    @pl.when(step == 0)
+    def send(k, total):
+        held[k] = halved_rows(total, side)
+        sent[k] = halved_rows(total, 1 - side)
+        copy(k).start()
+
+    @pl.when(step < last)
     def _():
-        out_sum[...] = out_part
-        back_sum[...] = back_part
+        across = ((1,), (1,))
+        up, down = joined(up_ref), joined(down_ref)
+        pre = dot(rows_ref[...], up)
+        square = pre * pre
+        bend = jnp.tanh(GELU_SCALE * (pre + GELU_CUBE * pre * square))
+        rise = 0.5 * (1.0 + bend)
+        act = (pre * rise).astype(jnp.bfloat16)
+        slope = rise + 0.5 * pre * (1.0 - bend * bend) * (GELU_SCALE + 3.0 * GELU_SCALE * GELU_CUBE * square)
+        grad_pre = dot(grad_ref[...], down) * slope
+        out_part, back_part = dot(act, down, across), dot(grad_pre.astype(jnp.bfloat16), up, across)
+
+        @pl.when(step == 0)
+        def _():
+            out_sum[...] = out_part
+            back_sum[...] = back_part
+
+        @pl.when(step > 0)
+        def _():
+            out_sum[...] += out_part
+            back_sum[...] += back_part
+
+        send(2 * step, dot(grad_t[...], act))
+        send(2 * step + 1, dot(rows_t[...], (grad_pre * gate_ref[...]).astype(jnp.bfloat16)))
 
     @pl.when(step > 0)
     def _():
-        out_sum[...] += out_part
-        back_sum[...] += back_part
-
-    parted(dot(grad_t[...], act), down_kept, down_sent)
-    parted(dot(rows_t[...], (grad_pre * gate_ref[...]).astype(jnp.bfloat16)), up_kept, up_sent)
-
-    @pl.when(step == pl.num_programs(0) - 1)
+        for odd, kept_ref, sent_ref in ((0, down_kept, down_sent), (1, up_kept, up_sent)):
+            k = 2 * (step - 1) + odd
+            copy(k).wait()
+            total = held[k].astype(jnp.float32) + came[k].astype(jnp.float32)
+            half[...] = total
+            for g in range(half.shape[0] // (2 * features)):
+                low = half[2 * g * features : (2 * g + 1) * features]
+                high = half[(2 * g + 1) * features : (2 * g + 2) * features]
+                kept_ref[g] = jnp.where(next_side == 0, low, high).astype(kept_ref.dtype)
+                sent_ref[g] = jnp.where(next_side == 0, high, low).astype(sent_ref.dtype)
+
+    @pl.when(step == last)
     def _():
         out_ref[...] = out_sum[...].astype(out_ref.dtype)
         back_ref[...] = back_sum[...].astype(back_ref.dtype)
 
 
-def expert_passes(side, rows, grad, gate, up, down):
+def expert_passes(rows, grad, gate, up, down):
     count, width = rows.shape
     share, own, features, hidden = up.shape
     tile = 512
-    blocks = width // (2 * features)
+    tiles = hidden // tile
+    blocks = width // (4 * features)
     fixed = lambda *shape: pl.BlockSpec(shape, lambda k: (0,) * len(shape))
-    weight_spec = pl.BlockSpec((share, own, features, tile), lambda k: (0, 0, 0, k))
-    part_spec = pl.BlockSpec((blocks, features, tile), lambda k: (0, 0, k))
+    weight_spec = pl.BlockSpec(
+        (share, own, features, tile), lambda k: (0, 0, 0, jnp.minimum(k, tiles - 1))
+    )
+    part_spec = pl.BlockSpec((blocks, features, tile), lambda k: (0, 0, jnp.maximum(k - 1, 0)))
     part_shape = jax.ShapeDtypeStruct((blocks, features, hidden), jnp.bfloat16)
     row_shape = jax.ShapeDtypeStruct((count, width), jnp.bfloat16)
     return pl.pallas_call(
-        expert_kernel,
-        grid=(hidden // tile,),
+        partial(expert_kernel, share),
+        grid=(tiles + 1,),
         in_specs=[
-            pl.BlockSpec(memory_space=pltpu.SMEM), fixed(count, width), fixed(count, width), fixed(count, 1),
-            weight_spec, weight_spec,
+            fixed(count, width), fixed(count, width), fixed(count, 1), weight_spec, weight_spec,
         ],
         out_specs=[fixed(count, width), fixed(count, width)] + [part_spec] * 4,
         out_shape=[row_shape, row_shape] + [part_shape] * 4,
@@ -1011,15 +1077,22 @@
             pltpu.VMEM((count, width), jnp.float32),
             pltpu.VMEM((count, width), jnp.float32),
             pltpu.VMEM((width, tile), jnp.float32),
+            pltpu.VMEM((width // 2, tile), jnp.float32),
+            pltpu.VMEM((2 * tiles, width // 2, tile), jnp.bfloat16),
+            pltpu.VMEM((2 * tiles, width // 2, tile), jnp.bfloat16),
+            pltpu.VMEM((2 * tiles, width // 2, tile), jnp.bfloat16),
+            pltpu.SemaphoreType.DMA((2 * tiles,)),
+            pltpu.SemaphoreType.DMA((2 * tiles,)),
         ],
         compiler_params=pltpu.CompilerParams(
-            dimension_semantics=("arbitrary",), vmem_limit_bytes=VMEM_LIMIT
+            dimension_semantics=("arbitrary",), vmem_limit_bytes=VMEM_LIMIT, collective_id=9,
+            has_side_effects=True,
         ),
         cost_estimate=pl.CostEstimate(
             flops=12 * count * width * hidden, bytes_accessed=8 * width * hidden, transcendentals=count * hidden
         ),
         name="expert_passes",
-    )(side, rows, grad, gate, up, down)
+    )(rows, grad, gate, up, down)
 
 
 def on_device(
@@ -1131,10 +1204,10 @@
     breaks = jnp.any(position[..., None] == starts, axis=-1).astype(f32) * BREAK
     breaks = jnp.broadcast_to(breaks.reshape(tok_seq, 1), (tok_seq, LANES))
     step_w, mixed_w = widened(step_size), widened(mixed)
-    part, sums, total = scan.ends(False, step_w, mixed_w, breaks, b_in, rates)
+    part, sums, total, grad_arrived = scan.ends(step_w, mixed_w, breaks, b_in, rates, pack(grad_steps))
+    grad_arrived = grad_arrived.reshape(-1, model_width)
     device_entry = carried(total, rates, False)
     full_up = whole_expert(up_weight, None, device_entry)
-    grad_arrived = expert_rows_early(after(pack(grad_steps), device_entry)).reshape(-1, model_width)
     scan_out, gated_b, entry = scan.outputs(
         step_w, mixed_w, breaks, b_in, c_out, rates, part, sums, device_entry,
         widened(skip_gain[None]), widened(gate_z),
@@ -1148,7 +1221,7 @@
     hidden_one = residual + mixer_rows
     moe_in, moe_back = jax.vjp(norm_apply, hidden_one, moe_gain)
     logits = jnp.einsum("td,de->et", moe_in, router_weight, precision=HIGH)
-    every_logit = gathered_everywhere(logits)
+    every_logit = gathered_everywhere(3, logits)
     gate_row, scaled, row_totals, columns = sinkhorn(
         dev_ref, every_logit, route_steps.reshape(1, tok_dev)
     )
@@ -1161,22 +1234,18 @@
     gate_arrived = gate_arrived[:, 0, :capacity].reshape(-1, 1)
     own, share = expert_groups()
     features, hidden = up_weight.shape[1:]
-    side = lax.rem(seq_place, 2).astype(jnp.int32).reshape(1)
     expert_out, grad_rows_in, up_kept, up_sent, down_kept, down_sent = expert_passes(
-        side, arrived, grad_arrived, gate_arrived, full_up, full_down
-    )
+        arrived, grad_arrived, gate_arrived, full_up, full_down
+    )
+    blocks = (EXPERTS, capacity, model_width)
+    expert_back, grad_back = expert_rows(2, expert_out.reshape(blocks), grad_rows_in.reshape(blocks))
     expert_grads = [
-        added(kept, swapped(sent, "seq", 1)).reshape(own, share // 2, features, hidden)
+        added(kept, swapped(sent, "seq", 2)).reshape(own, share // 4, features, hidden)
         for kept, sent in ((up_kept, up_sent), (down_kept, down_sent))
     ]
-    blocks = (EXPERTS, capacity, model_width)
-
-    expert_back, grad_back = expert_rows(
-        2, after(expert_out, *expert_grads).reshape(blocks), grad_rows_in.reshape(blocks)
-    )
-    for stage in range(1, share.bit_length() - 1):
+    for stage in range(2, share.bit_length() - 1):
         expert_grads = [halved(part, stage) for part in expert_grads]
-    expert_tok = unpack(after(expert_back, *expert_grads))
+    expert_tok = unpack(expert_back)
     plain_grad_part = unpack(grad_back)
     up_part, down_part = expert_grads
 
@@ -1188,8 +1257,8 @@
         EXPERTS * grad_gate[None],
         0.0,
     )
-    every_grad = gathered_everywhere(grad_probs)
-    up_grad = to_owners(after(up_part.reshape(own, *up_part.shape[2:]), every_grad))
+    every_grad, up_part = gathered_everywhere(10, grad_probs, up_part)
+    up_grad = to_owners(up_part.reshape(own, *up_part.shape[2:]))
     grad_logits = sinkhorn_back(dev_ref, every_logit, scaled, row_totals, columns, every_grad)
     router_grad = jnp.einsum("td,et->ed", moe_in, grad_logits, precision=HIGH)
     grad_moe_in = gate[:, None] * plain_grad_part + jnp.einsum(
@@ -1208,8 +1277,8 @@
     gains = jnp.concatenate([moe_gain_grad[None], router_grad], 0)
     gains = lax.psum(gains, "chan") if chan_count != 2 else gains + swapped(gains, "chan", 1)
     grad_scan_w = widened(grad_scan)
-    back_part, back_sums, back_total = scan.ends(True, step_w, grad_scan_w, breaks, c_out, rates)
-    back_entry = carried(after(back_total, up_grad), rates, True)
+    back_part, back_sums, back_total = scan.ends(step_w, grad_scan_w, breaks, c_out, rates)
+    back_entry = carried(back_total, rates, True, up_grad, down_part)
     step_grad, mixed_grad, b_grad, c_grad, rate_grad, early = scan.grads(
         step_w, mixed_w, breaks, grad_scan_w, b_in, c_out, rates, entry, back_part, back_sums,
         back_entry, (out_weight_grad.astype(bf16).reshape(-1, channels), gate_weight_grad.astype(bf16)),
@@ -1270,7 +1339,6 @@
     )
     bounds = [sum(part.shape[0] for part in pieces[: k + 1]) for k in range(len(pieces) - 1)]
     inner_weight_grad, small = summed([after(inner_weight_grad.astype(bf16), down_grad), jnp.concatenate(pieces, 0)])
-    early = after(early, small)
     out_weight_grad = early[:model_width].reshape(channels, model_width).astype(f32)
     gate_weight_grad = early[model_width : 2 * model_width].astype(f32)
     (

time: 749 us -> 713 us (0.952)
  Pallas kernels: 401 us -> 425 us
  waiting for transfers between devices: 82.9 us -> 60.8 us
  local copies, waits for them, and re-layouts: 59.2 us -> 44.1 us
  other arithmetic: 65.3 us -> 53.4 us
    pallas_call x5, Pallas kernels: 90.6 us -> 127 us  [the longest x2 49 us: ends(): pl.pallas_call(kernel, grid=(self.groups,), in_specs=[self.row_spec, self...]
    ppermute x22 -> x16, waiting for transfers between devices: 80.5 us -> 59.6 us  [swapped(): lax.ppermute(value, axis, [(source, source ^ bit) for source in range(cou...]
    convert_element_type x4 -> x1, other arithmetic: 15.1 us -> 3.51 us  [added(): (kept.astype(jnp.float32) + came.astype(jnp.float32)).astype(kept.dtype)]
    pallas_call x2, Pallas kernels: 39.8 us -> 31.2 us  [carried(): pl.pallas_call(partial(carry_kernel, count, reverse), in_specs=[vmem, vme...]
    ppermute x22 -> x16, starting transfers between devices: 29.8 us -> 22.9 us  [swapped(): lax.ppermute(value, axis, [(source, source ^ bit) for source in range(cou...]
  transfers between devices with their start and end apart: 28 -> 22, of which waited for: 11 -> 7; matrix products, arithmetic and copies ran while one was open for 19% -> 18% of each run, Pallas kernels for 24% -> 31%
where the time goes in v4:
time: 713 us; the launch traced here: 708 us
  Pallas kernels  425 us (60%)
  matrix products  73.1 us (10%)
  waiting for transfers between devices  60.8 us (9%)
  other arithmetic  53.4 us (7%)
  local copies, waits for them, and re-layouts  44.1 us (6%)
  starting transfers between devices  35.4 us (5%)
  between operations  15.9 us (2%)
    pallas_call x1, Pallas kernels, grads(): pl.pallas_call(partial(grads_kernel, self.halves, count, self.groups), gr...  89.4 us
    pallas_call x2, Pallas kernels, exchange(): pl.pallas_call(partial(exchange_kernel, own, share, chans, count), in_spe...  86.4 us
    pallas_call x1, Pallas kernels, summed(): pl.pallas_call(partial(sum_kernel, count, places, [part.shape[0] for part...  60.9 us
    ppermute x16, waiting for transfers between devices, swapped(): lax.ppermute(value, axis, [(source, source ^ bit) for source in range(cou...  59.6 us
    pallas_call x2, Pallas kernels, ends(): pl.pallas_call(kernel, grid=(self.groups,), in_specs=[self.row_spec, self...  49 us
    pallas_call x1, Pallas kernels, expert_passes(): pl.pallas_call(partial(expert_kernel, share), grid=(tiles + 1,), in_specs...  41.4 us
    pallas_call x2, Pallas kernels, gathered_everywhere(): pl.pallas_call(partial(gather_kernel, devices, chans, len(passed)), in_sp...  36.1 us
    pallas_call x2, Pallas kernels, carried(): pl.pallas_call(partial(carry_kernel, count, reverse), in_specs=[vmem, vme...  31.2 us
  transfers between devices with their start and end apart: 22, of which 7 were waited for; matrix products, arithmetic and copies ran while one was open for 18% of the time, Pallas kernels for 31%

profile of v4, /device:TPU:0, one launch (start us, length us, event | category | flops | bytes accessed | tf_op | source)
XLA Modules:
  0.0 707.7 jit_solution(10482248295198817123)
XLA Ops:
  7.3 3.1 copy.215
  13.7 2.6 multiply_convert_fusion.1
  16.3 2.9 collective-permute-start
  19.3 2.4 constant_dynamic-slice_fusion.3
  21.6 3.6 collective-permute-start.6
  28.2 7.7 %collective-permute-done = bf16[320,1152]{1,0:T(8,128)(2,1)S(1)} collective-permute-done((bf16[320,1152]{1,0:T(8,128)(2,1)}, bf16[320,1152]{1,0:T(8,128)(2,1)S(1)}, u32[]{:S(2)}, u32[]{:S(2)}) %collective-permute-start) | collective-permute-done | bytes 737312 | tf_op jit(solution)/shard_map/ppermute | solution.py:37
  36.0 1.9 broadcast_select_fusion.3
  37.9 6.2 fusion
  47.4 2.1 copy.139
  51.5 2.4 fusion.94
  54.6 1.8 collective-permute-start.2
  56.4 2.0 convolution_convert_fusion.5
  58.3 5.3 collective-permute-done.2
  64.8 5.5 compare_select_fusion
  71.2 35.1 %scan_ends.1 = (f32[2,16,8,1152]{3,2,1,0:T(8,128)}, f32[2,8,1152]{2,1,0:T(8,128)}, f32[24,1152]{1,0:T(8,128)}, bf16[8,64,1152]{2,1,0:T(8,128)(2,1)}) custom-call(f32[640,1152]{1,0:T(8,128)} %get-tuple-element.150.refs_0_.step_ref, f32[640,1152]{1,0:T(8,128)} %get-tuple-element.121.refs_1_.mixed_ref, f32[640,128]{1,0:T(8,128)} %broadcast_in_dim.38.refs_2_.break_ref, ...), custom_call_target="tpu_custom_call" | custom-call | flops 58982400 | bytes 8847360 | tf_op jit(solution)/shard_map/scan_ends/pallas_call | solution.py:816
  106.3 15.5 %carry.1.device = f32[16,1152]{1,0:T(8,128)} custom-call(f32[24,1152]{1,0:T(8,128)} %get-tuple-element.59.total_ref, f32[16,1152]{1,0:T(8,128)} %multiply_bitcast_fusion.refs_4_.rate_ref), custom_call_target="tpu_custom_call" | custom-call | bytes 50400000 | tf_op jit(solution)/shard_map/carry/pallas_call | solution.py:312
  121.9 1.8 bitcast_dynamic-update-slice_fusion.5
  123.7 1.9 bitcast_dynamic-update-slice_fusion.4
  130.5 3.4 collective-permute-start.7
  133.9 6.0 fusion.15.gate_ref
  139.9 20.5 %scan_outputs.1 = (f32[640,1152]{1,0:T(8,128)}, bf16[640,1152]{1,0:T(8,128)(2,1)}, f32[2,16,8,1152]{3,2,1,0:T(8,128)}) custom-call(f32[640,1152]{1,0:T(8,128)} %get-tuple-element.150.refs_0_.step_ref, f32[640,1152]{1,0:T(8,128)} %get-tuple-element.121.refs_1_.mixed_ref, f32[640,128]{1,0:T(8,128)} %broadcast_in_dim.38.refs_2_.break_ref, ...), custom_call_target="tpu_custom_call" | custom-call | flops 82575360 | bytes 8847360 | tf_op jit(solution)/shard_map/scan_outputs/pallas_call | solution.py:831
  160.4 7.1 collective-permute-done.8
  169.9 3.2 convolution_convert_fusion.6
  175.3 14.3 %collective-permute-done.3 = bf16[320,1152]{1,0:T(8,128)(2,1)} collective-permute-done((bf16[320,1152]{1,0:T(8,128)(2,1)}, bf16[320,1152]{1,0:T(8,128)(2,1)}, u32[]{:S(2)}, u32[]{:S(2)}) %collective-permute-start.3) | collective-permute-done | bytes 737312 | tf_op jit(solution)/shard_map/ppermute | solution.py:37
  189.5 3.4 multiply_reduce_fusion.8
  193.0 2.1 fusion.38.own_ref
  195.1 15.2 %gather_small.2.logit_ref = f32[32,8,320]{2,1,0:T(8,128)} custom-call(f32[8,320]{1,0:T(8,128)} %fusion.38.own_ref), custom_call_target="tpu_custom_call" | custom-call | bytes 43200000 | tf_op jit(solution)/shard_map/gather_small/pallas_call | solution.py:248
  210.2 4.8 sinkhorn.1
  217.1 2.0 convolution_convert_fusion.4
  219.1 33.0 %expert_rows.2 = (bf16[8,64,1152]{2,1,0:T(8,128)(2,1)}, f32[8,8,128]{2,1,0:T(8,128)}) custom-call(bf16[8,64,1152]{2,1,0:T(8,128)(2,1)} %bitcast.202, f32[8,8,128]{2,1,0:T(8,128)} %pad.28.refs_1_), custom_call_target="tpu_custom_call" | custom-call | bytes 187200000 | tf_op jit(solution)/shard_map/expert_rows/pallas_call | solution.py:194
  253.8 41.4 %expert_passes.1 = (bf16[512,1152]{1,0:T(8,128)(2,1)}, bf16[512,1152]{1,0:T(8,128)(2,1)}, bf16[4,72,3072]{2,1,0:T(8,128)(2,1)}, bf16[4,72,3072]{2,1,0:T(8,128)(2...) custom-call(bf16[512,1152]{1,0:T(8,128)(2,1)} %bitcast.219, bf16[512,1152]{1,0:T(8,128)(2,1)} %bitcast.221, ...), custom_call_target="tpu_custom_call" | custom-call | flops 21743271936 | bytes 28311552 | tf_op jit(solution)/shard_map/expert_passes/pallas_call | solution.py:1066
  295.3 2.5 collective-permute-start.10
  298.7 53.4 %expert_rows.3 = (bf16[8,64,1152]{2,1,0:T(8,128)(2,1)}, bf16[8,64,1152]{2,1,0:T(8,128)(2,1)}) custom-call(bf16[8,64,1152]{2,1,0:T(8,128)(2,1)} %bitcast.206, bf16[8,64,1152]{2,1,0:T(8,128)(2,1)} %bitcast.207), custom_call_target="tpu_custom_call" | custom-call | bytes 187200000 | tf_op jit(solution)/shard_map/expert_rows/pallas_call | solution.py:194
  352.1 3.1 fusion.29
  355.9 3.4 fusion.28.refs_0_
  359.2 21.0 %gather_small.3 = (f32[32,8,320]{2,1,0:T(8,128)}, bf16[4,1,72,3072]{3,2,1,0:T(8,128)(2,1)}) custom-call(f32[8,320]{1,0:T(8,128)} %fusion.76.own_ref, bf16[4,1,72,3072]{3,2,1,0:T(8,128)(2,1)} %fusion.28.refs_0_), custom_call_target="tpu_custom_call", output_to_operand_aliasing={{1}: (1, {})} | custom-call | bytes 43200000 | tf_op jit(solution)/shard_map/gather_small/pallas_call | solution.py:248
  380.2 4.6 all-to-all-start
  384.8 5.4 sinkhorn_back.1
  390.3 2.0 fusion.98
  392.4 2.1 multiply_reduce_fusion.5
  398.1 3.5 add_convert_fusion
  402.3 13.5 %collective-permute-done.11 = bf16[320,1152]{1,0:T(8,128)(2,1)S(1)} collective-permute-done((bf16[320,1152]{1,0:T(8,128)(2,1)S(1)}, bf16[320,1152]{1,0:T(8,128)(2,1)S(1)}, u32[]{:S(2)}, u32[]{:S(2)}) %collective-permute-start.11) | collective-permute-done | bytes 737312 | tf_op jit(solution)/shard_map/ppermute | solution.py:37
  415.9 4.5 multiply_reduce_fusion
  421.0 13.9 %scan_ends_back.1 = (f32[2,16,8,1152]{3,2,1,0:T(8,128)}, f32[2,8,1152]{2,1,0:T(8,128)}, f32[24,1152]{1,0:T(8,128)}) custom-call(f32[640,1152]{1,0:T(8,128)} %get-tuple-element.150.refs_0_.step_ref, f32[640,1152]{1,0:T(8,128)} %get-tuple-element.117.drive_ref.grad_ref, f32[640,128]{1,0:T(8,128)} %broadcast_in_dim.38.refs_2_.break_ref, ...), custom_call_target="tpu_custom_call" | custom-call | flops 58982400 | bytes 8847360 | tf_op jit(solution)/shard_map/scan_ends_back/pallas_call | solution.py:816
  435.0 4.0 convolution_convert_fusion.2.first_early
  438.9 4.0 convolution_convert_fusion.1.second_early
  442.9 15.6 %carry_back.1.device = f32[16,1152]{1,0:T(8,128)} custom-call(f32[24,1152]{1,0:T(8,128)} %get-tuple-element.85.total_ref, f32[16,1152]{1,0:T(8,128)} %multiply_bitcast_fusion.refs_4_.rate_ref, bf16[4,72,3072]{2,1,0:T(8,128)(2,1)} %all-to-all-done.refs_0_, bf16[4,1,72,3072]{3,2,1,0:T(8,128)(2,1)} %bitcast.191), custom_call_target="tpu_custom_call" | custom-call | bytes 50400000 | tf_op jit(solution)/shard_map/carry_back/pallas_call | solution.py:312
  458.6 89.4 %scan_grads.1 = (f32[640,1152]{1,0:T(8,128)}, f32[640,1152]{1,0:T(8,128)}, f32[640,16]{1,0:T(8,128)}, f32[640,16]{1,0:T(8,128)}, f32[16,1152]{1,0:T(8,128)}, /*index=5*/bf16[9,256,1152]{2,1,0:T(8,128)(2,1)}) custom-call(f32[640,1152]{1,0:T(8,128)} %get-tuple-element.150.refs_0_.step_ref, f32[640,1152]{1,0:T(8,128)} %get-tuple-element.121.refs_1_.mixed_ref, ...), custom_call_target="tpu_custom_call" | custom-call | flops 235929600 | bytes 8847360 | tf_op jit(solution)/shard_map/scan_grads/pallas_call | solution.py:860
  548.0 2.7 fusion.92
  551.2 3.0 fusion.99
  554.2 4.9 all-to-all-start.1
  563.2 6.5 slice_convert_fusion
  569.8 3.8 convert_element_type.225
  573.6 1.8 fusion.72
  575.7 3.8 fusion.91
  579.6 6.0 multiply_reduce_fusion.2
  597.4 3.9 convolution_convert_fusion.refs_0_
  601.4 11.8 %collective-permute-done.15 = bf16[320,1152]{1,0:T(8,128)(2,1)S(1)} collective-permute-done((bf16[320,1152]{1,0:T(8,128)(2,1)S(1)}, bf16[320,1152]{1,0:T(8,128)(2,1)S(1)}, u32[]{:S(2)}, u32[]{:S(2)}) %collective-permute-start.15) | collective-permute-done | bytes 737312 | tf_op jit(solution)/shard_map/ppermute | solution.py:37
  613.3 3.1 multiply_reduce_fusion.6
  617.5 2.4 fusion.31
  624.0 60.9 %sum_late.1 = bf16[6,256,1152]{2,1,0:T(8,128)(2,1)} custom-call(bf16[1152,1152]{1,0:T(8,128)(2,1)} %convolution_convert_fusion.refs_0_, f32[224,1152]{1,0:T(8,128)} %pad.34.refs_1_), custom_call_target="tpu_custom_call" | custom-call | bytes 216000000 | tf_op jit(solution)/shard_map/sum_late/pallas_call | solution.py:447
  686.0 2.1 slice_bitcast_fusion.1
  692.2 4.8 maximum_convert_fusion
  697.0 3.7 convert_element_type.226
  (349 shorter events, 60.7 us)
Async XLA Ops:
  7.2 162.7 %copy-start = (bf16[1152,1152]{1,0:T(8,128)(2,1)S(1)}, bf16[1152,1152]{1,0:T(8,128)(2,1)}, u32[]{:S(2)}) copy-start(bf16[1152,1152]{1,0:T(8,128)(2,1)} %param.30) | copy-start | bytes 7962628
  7.2 246.6 %all-gather.3.cloned.1.call-start = ((), (), s32[]{:S(2)}) async-start(), calls=%async_computation.2 | async-start | bytes 8847360 | tf_op jit(solution)/shard_map/all_gather | solution.py:105
  12.4 9.2 %copy-start.81 = (f32[320]{0:T(512)}, f32[320]{0:T(512)S(1)}, u32[]{:S(2)}) copy-start(f32[320]{0:T(512)S(1)} %add.262) | copy-start | bytes 3844
  12.5 23.5 %copy-start.72 = (f32[320]{0:T(512)}, f32[320]{0:T(512)S(1)}, u32[]{:S(2)}) copy-start(f32[320]{0:T(512)S(1)} %rsqrt.20) | copy-start | bytes 3844
  13.7 12.4 %copy-start.91 = (s32[320,1]{0,1:T(1,128)S(1)}, s32[320,1]{0,1:T(1,128)}, u32[]{:S(2)}) copy-start(s32[320,1]{0,1:T(1,128)} %param.19) | copy-start | bytes 3844
  13.7 12.7 %copy-start.94 = (s32[4]{0:T(128)S(1)}, s32[4]{0:T(128)}, u32[]{:S(2)}) copy-start(s32[4]{0:T(128)} %param.20) | copy-start | bytes 52
  13.7 13.9 %copy-start.48 = (f32[1152,16]{0,1:T(8,128)S(1)}, f32[1152,16]{0,1:T(8,128)}, u32[]{:S(2)}) copy-start(f32[1152,16]{0,1:T(8,128)} %param.28) | copy-start | bytes 221188
  16.3 19.6 %collective-permute-start = (bf16[320,1152]{1,0:T(8,128)(2,1)}, bf16[320,1152]{1,0:T(8,128)(2,1)S(1)}, u32[]{:S(2)}, u32[]{:S(2)}) collective-permute-start(bf16[320,1152]{1,0:T(8,128)(2,1)} %multiply_convert_fusion.1), channel_id=1, source_target_pairs={{0,1},{1,0},{2,3},{3,2},{4,5},{5,4},{6,7},{7,6},{8,9},{9,8},{10,11... | collective-permute-start | bytes 2211848 | tf_op jit(solution)/shard_map/ppermute | solution.py:37
  21.6 100.2 %collective-permute-start.6 = (bf16[1,72,3072]{2,1,0:T(8,128)(2,1)}, bf16[1,72,3072]{2,1,0:T(8,128)(2,1)}, u32[]{:S(2)}, u32[]{:S(2)}) collective-permute-start(bf16[1,72,3072]{2,1,0:T(8,128)(2,1)} %get-tuple-element.135), channel_id=1, source_target_pairs={{0,24},{2,26},{4,28},{6,30},{8,16},{10,18},{12,20},{14,22},{16,8},... | collective-permute-start | bytes 1327112 | tf_op jit(solution)/shard_map/ppermute | solution.py:37
  25.2 96.6 %collective-permute-start.4 = (bf16[1,72,3072]{2,1,0:T(8,128)(2,1)}, bf16[1,72,3072]{2,1,0:T(8,128)(2,1)}, u32[]{:S(2)}, u32[]{:S(2)}) collective-permute-start(bf16[1,72,3072]{2,1,0:T(8,128)(2,1)} %get-tuple-element.136), channel_id=1, source_target_pairs={{0,8},{2,10},{4,12},{6,14},{8,0},{10,2},{12,4},{14,6},{16,24},{18,... | collective-permute-start | bytes 1327112 | tf_op jit(solution)/shard_map/ppermute | solution.py:37
  25.3 96.6 %collective-permute-start.5 = (bf16[1,72,3072]{2,1,0:T(8,128)(2,1)}, bf16[1,72,3072]{2,1,0:T(8,128)(2,1)}, u32[]{:S(2)}, u32[]{:S(2)}) collective-permute-start(bf16[1,72,3072]{2,1,0:T(8,128)(2,1)} %get-tuple-element.137), channel_id=1, source_target_pairs={{0,16},{2,18},{4,20},{6,22},{8,24},{10,26},{12,28},{14,30},{16,0},... | collective-permute-start | bytes 1327112 | tf_op jit(solution)/shard_map/ppermute | solution.py:37
  26.3 17.7 %copy-start.70 = (s32[8,40]{1,0:T(8,128)}, s32[8,40]{1,0:T(8,128)S(1)}, u32[]{:S(2)}) copy-start(s32[8,40]{1,0:T(8,128)S(1)} %squeeze.33) | copy-start | bytes 3844
  27.6 19.7 %copy-start.68 = (f32[2,40,8]{1,2,0:T(8,128)}, f32[2,40,8]{1,2,0:T(8,128)S(1)}, u32[]{:S(2)}) copy-start(f32[2,40,8]{1,2,0:T(8,128)S(1)} %get-tuple-element.147) | copy-start | bytes 7684
  37.8 8.7 %copy-start.80 = (f32[4,1152]{1,0:T(4,128)S(1)}, f32[4,1152]{1,0:T(4,128)}, u32[]{:S(2)}) copy-start(f32[4,1152]{1,0:T(4,128)} %param.23) | copy-start | bytes 55300
  37.8 9.2 %copy-start.75 = (f32[2,40,8]{1,2,0:T(8,128)S(1)}, f32[2,40,8]{1,2,0:T(8,128)}, u32[]{:S(2)}) copy-start(f32[2,40,8]{1,2,0:T(8,128)} %get-tuple-element.148) | copy-start | bytes 7684
  37.9 9.3 %copy-start.74 = (f32[2,40,8]{1,2,0:T(8,128)S(1)}, f32[2,40,8]{1,2,0:T(8,128)}, u32[]{:S(2)}) copy-start(f32[2,40,8]{1,2,0:T(8,128)} %get-tuple-element.149) | copy-start | bytes 7684
  45.1 4.5 collective-permute-start.1
  54.0 10.8 %copy-start.7 = (bf16[640,1152]{1,0:T(8,128)(2,1)}, bf16[640,1152]{1,0:T(8,128)(2,1)S(1)}, u32[]{:S(2)}) copy-start(bf16[640,1152]{1,0:T(8,128)(2,1)S(1)} %get-tuple-element.122) | copy-start | bytes 4423684
  54.5 10.2 %copy-start.43 = (f32[72,1152]{1,0:T(8,128)S(1)}, f32[72,1152]{1,0:T(8,128)}, u32[]{:S(2)}) copy-start(f32[72,1152]{1,0:T(8,128)} %param.26) | copy-start | bytes 995332
  54.6 10.2 %copy-start.93 = (f32[1152]{0:T(1024)S(1)}, f32[1152]{0:T(1024)}, u32[]{:S(2)}) copy-start(f32[1152]{0:T(1024)} %param.27) | copy-start | bytes 13828
  54.6 9.1 %collective-permute-start.2 = (f32[640,104]{1,0:T(8,128)S(1)}, f32[640,104]{1,0:T(8,128)S(1)}, u32[]{:S(2)}, u32[]{:S(2)}) collective-permute-start(f32[640,104]{1,0:T(8,128)S(1)} %fusion.97), channel_id=1, source_target_pairs={{0,1},{1,0},{2,3},{3,2},{4,5},{5,4},{6,7},{7,6},{8,9},{9,8},{10,11... | collective-permute-start | bytes 798728 | tf_op jit(solution)/shard_map/ppermute | solution.py:37
  106.3 21.2 %copy-start.88 = (f32[1152]{0:T(1024)S(1)}, f32[1152]{0:T(1024)}, u32[]{:S(2)}) copy-start(f32[1152]{0:T(1024)} %param.29) | copy-start | bytes 13828
  127.4 126.5 %all-gather.5.cloned.1.call-start = ((), (), s32[]{:S(2)}) async-start(), calls=%async_computation.3 | async-start | bytes 8847360 | tf_op jit(solution)/shard_map/all_gather | solution.py:105
  129.4 31.0 %collective-permute-start.9 = (bf16[1,72,3072]{2,1,0:T(8,128)(2,1)S(1)}, bf16[1,72,3072]{2,1,0:T(8,128)(2,1)S(1)}, u32[]{:S(2)}, u32[]{:S(2)}) collective-permute-start(bf16[1,72,3072]{2,1,0:T(8,128)(2,1)S(1)} %get-tuple-element.132), channel_id=1, source_target_pairs={{0,24},{2,26},{4,28},{6,30},{8,16},{10,18},{12,20},{14,22},{16,8},... | collective-permute-start | bytes 1327112 | tf_op jit(solution)/shard_map/ppermute | solution.py:37
  129.5 38.0 %collective-permute-start.8 = (bf16[1,72,3072]{2,1,0:T(8,128)(2,1)S(1)}, bf16[1,72,3072]{2,1,0:T(8,128)(2,1)S(1)}, u32[]{:S(2)}, u32[]{:S(2)}) collective-permute-start(bf16[1,72,3072]{2,1,0:T(8,128)(2,1)S(1)} %get-tuple-element.133), channel_id=1, source_target_pairs={{0,16},{2,18},{4,20},{6,22},{8,24},{10,26},{12,28},{14,30},{16,0},... | collective-permute-start | bytes 1327112 | tf_op jit(solution)/shard_map/ppermute | solution.py:37
  130.5 37.0 %collective-permute-start.7 = (bf16[1,72,3072]{2,1,0:T(8,128)(2,1)S(1)}, bf16[1,72,3072]{2,1,0:T(8,128)(2,1)S(1)}, u32[]{:S(2)}, u32[]{:S(2)}) collective-permute-start(bf16[1,72,3072]{2,1,0:T(8,128)(2,1)S(1)} %get-tuple-element.134), channel_id=1, source_target_pairs={{0,8},{2,10},{4,12},{6,14},{8,0},{10,2},{12,4},{14,6},{16,24},{18,... | collective-permute-start | bytes 1327112 | tf_op jit(solution)/shard_map/ppermute | solution.py:37
  173.1 16.4 %collective-permute-start.3 = (bf16[320,1152]{1,0:T(8,128)(2,1)}, bf16[320,1152]{1,0:T(8,128)(2,1)}, u32[]{:S(2)}, u32[]{:S(2)}) collective-permute-start(bf16[320,1152]{1,0:T(8,128)(2,1)} %convolution_convert_fusion.6), channel_id=1, source_target_pairs={{0,1},{1,0},{2,3},{3,2},{4,5},{5,4},{6,7},{7,6},{8,9},{9,8},{10,11... | collective-permute-start | bytes 2211848 | tf_op jit(solution)/shard_map/ppermute | solution.py:37
  175.3 17.7 %copy-start.45 = (f32[1152]{0:T(1024)S(1)}, f32[1152]{0:T(1024)}, u32[]{:S(2)}) copy-start(f32[1152]{0:T(1024)} %param.31) | copy-start | bytes 13828
  175.3 17.7 %copy-start.52 = (f32[1152,8]{0,1:T(8,128)S(1)}, f32[1152,8]{0,1:T(8,128)}, u32[]{:S(2)}) copy-start(f32[1152,8]{0,1:T(8,128)} %param.32) | copy-start | bytes 110596
  192.9 24.2 %copy-start.2 = (f32[320,1152]{1,0:T(8,128)}, f32[320,1152]{1,0:T(8,128)S(1)}, u32[]{:S(2)}) copy-start(f32[320,1152]{1,0:T(8,128)S(1)} %get-tuple-element.153) | copy-start | bytes 4423684
  192.9 59.2 %copy-start.86 = (f32[320]{0:T(512)}, f32[320]{0:T(512)S(1)}, u32[]{:S(2)}) copy-start(f32[320]{0:T(512)S(1)} %get-tuple-element.152) | copy-start | bytes 3844
  193.0 204.0 %copy-start.55 = (f32[320]{0:T(512)}, f32[320]{0:T(512)S(1)}, u32[]{:S(2)}) copy-start(f32[320]{0:T(512)S(1)} %fusion.86) | copy-start | bytes 3844
  253.8 44.0 %copy-start.69 = (f32[2,40,8]{1,2,0:T(8,128)S(1)}, f32[2,40,8]{1,2,0:T(8,128)}, u32[]{:S(2)}) copy-start(f32[2,40,8]{1,2,0:T(8,128)} %copy-done.68) | copy-start | bytes 7684
  253.8 44.8 %copy-start.92 = (f32[1,320]{1,0:T(1,128)S(1)}, f32[1,320]{1,0:T(1,128)}, u32[]{:S(2)}) copy-start(f32[1,320]{1,0:T(1,128)} %get-tuple-element.61) | copy-start | bytes 3844
  295.3 60.6 %collective-permute-start.10 = (bf16[4,72,3072]{2,1,0:T(8,128)(2,1)}, bf16[4,72,3072]{2,1,0:T(8,128)(2,1)}, u32[]{:S(2)}, u32[]{:S(2)}) collective-permute-start(bf16[4,72,3072]{2,1,0:T(8,128)(2,1)} %get-tuple-element.80), channel_id=1, source_target_pairs={{0,4},{2,6},{4,0},{6,2},{8,12},{10,14},{12,8},{14,10},{16,20},{18,... | collective-permute-start | bytes 5308424 | tf_op jit(solution)/shard_map/ppermute | solution.py:37
  298.6 93.7 %copy-start.78 = (f32[320]{0:T(512)}, f32[320]{0:T(512)S(1)}, u32[]{:S(2)}) copy-start(f32[320]{0:T(512)S(1)} %reduce.11) | copy-start | bytes 3844
  298.6 99.5 %collective-permute-start.12 = (bf16[4,72,3072]{2,1,0:T(8,128)(2,1)}, bf16[4,72,3072]{2,1,0:T(8,128)(2,1)}, u32[]{:S(2)}, u32[]{:S(2)}) collective-permute-start(bf16[4,72,3072]{2,1,0:T(8,128)(2,1)} %get-tuple-element.88), channel_id=1, source_target_pairs={{0,4},{2,6},{4,0},{6,2},{8,12},{10,14},{12,8},{14,10},{16,20},{18,... | collective-permute-start | bytes 5308424 | tf_op jit(solution)/shard_map/ppermute | solution.py:37
  380.2 62.7 %all-to-all-start = ((bf16[4,72,3072]{2,1,0:T(8,128)(2,1)}), bf16[4,72,3072]{2,1,0:T(8,128)(2,1)}, u32[]{:S(2)}, u32[]{:S(2)}) async-start(bf16[4,72,3072]{2,1,0:T(8,128)(2,1)} %bitcast.192), calls=%async_computation | async-start | bytes 3538944 | tf_op jit(solution)/shard_map/all_to_all | solution.py:89
  395.5 6.1 collective-permute-start.17
  397.4 18.3 %collective-permute-start.11 = (bf16[320,1152]{1,0:T(8,128)(2,1)S(1)}, bf16[320,1152]{1,0:T(8,128)(2,1)S(1)}, u32[]{:S(2)}, u32[]{:S(2)}) collective-permute-start(bf16[320,1152]{1,0:T(8,128)(2,1)S(1)} %fusion.90), channel_id=1, source_target_pairs={{0,1},{1,0},{2,3},{3,2},{4,5},{5,4},{6,7},{7,6},{8,9},{9,8},{10,11... | collective-permute-start | bytes 2211848 | tf_op jit(solution)/shard_map/ppermute | solution.py:37
  398.1 17.8 %copy-start.98 = (f32[640,1152]{1,0:T(8,128)S(1)}, f32[640,1152]{1,0:T(8,128)}, u32[]{:S(2)}) copy-start(f32[640,1152]{1,0:T(8,128)} %fusion.15.gate_ref) | copy-start | bytes 8847364
  398.1 17.8 %copy-start.99 = (f32[640,1152]{1,0:T(8,128)S(1)}, f32[640,1152]{1,0:T(8,128)}, u32[]{:S(2)}) copy-start(f32[640,1152]{1,0:T(8,128)} %get-tuple-element.89) | copy-start | bytes 8847364
  401.6 14.3 %copy-start.8 = (bf16[640,1152]{1,0:T(8,128)(2,1)S(1)}, bf16[640,1152]{1,0:T(8,128)(2,1)}, u32[]{:S(2)}) copy-start(bf16[640,1152]{1,0:T(8,128)(2,1)} %copy-done.7) | copy-start | bytes 4423684
  420.4 18.6 %copy-start.25 = (bf16[640,1152]{1,0:T(8,128)(2,1)}, bf16[640,1152]{1,0:T(8,128)(2,1)S(1)}, u32[]{:S(2)}) copy-start(bf16[640,1152]{1,0:T(8,128)(2,1)S(1)} %get-tuple-element.123) | copy-start | bytes 4423684
  421.0 14.0 %copy-start.95 = (bf16[640,1152]{1,0:T(8,128)(2,1)S(1)}, bf16[640,1152]{1,0:T(8,128)(2,1)}, u32[]{:S(2)}) copy-start(bf16[640,1152]{1,0:T(8,128)(2,1)} %get-tuple-element.60) | copy-start | bytes 4423684
  458.5 89.4 %copy-start.18 = (f32[640,1152]{1,0:T(8,128)S(1)}, f32[640,1152]{1,0:T(8,128)}, u32[]{:S(2)}) copy-start(f32[640,1152]{1,0:T(8,128)} %get-tuple-element.151) | copy-start | bytes 8847364
  554.2 69.8 %all-to-all-start.1 = ((bf16[4,72,3072]{2,1,0:T(8,128)(2,1)}), bf16[4,72,3072]{2,1,0:T(8,128)(2,1)}, u32[]{:S(2)}, u32[]{:S(2)}) async-start(bf16[4,72,3072]{2,1,0:T(8,128)(2,1)} %add_convert_fusion), calls=%async_computation.1 | async-start | bytes 3538944 | tf_op jit(solution)/shard_map/all_to_all | solution.py:89
  560.3 9.5 %copy-start.39 = (f32[640,16]{0,1:T(8,128)}, f32[640,16]{0,1:T(8,128)S(1)}, u32[]{:S(2)}) copy-start(f32[640,16]{0,1:T(8,128)S(1)} %copy.157) | copy-start | bytes 122884
  562.1 13.4 %collective-permute-start.13 = (f32[640,104]{0,1:T(8,128)S(1)}, f32[640,104]{0,1:T(8,128)S(1)}, u32[]{:S(2)}, u32[]{:S(2)}) collective-permute-start(f32[640,104]{0,1:T(8,128)S(1)} %pad_maximum_fusion.5), channel_id=1, source_target_pairs={{0,1},{1,0},{2,3},{3,2},{4,5},{5,4},{6,7},{7,6},{8,9},{9,8},{10,11... | collective-permute-start | bytes 798728 | tf_op jit(solution)/shard_map/ppermute | solution.py:37
  563.2 12.3 %copy-start.97 = (f32[640,1152]{1,0:T(8,128)S(1)}, f32[640,1152]{1,0:T(8,128)}, u32[]{:S(2)}) copy-start(f32[640,1152]{1,0:T(8,128)} %get-tuple-element.90) | copy-start | bytes 8847364
  586.4 3.1 collective-permute-start.14
  595.1 18.2 %collective-permute-start.15 = (bf16[320,1152]{1,0:T(8,128)(2,1)S(1)}, bf16[320,1152]{1,0:T(8,128)(2,1)S(1)}, u32[]{:S(2)}, u32[]{:S(2)}) collective-permute-start(bf16[320,1152]{1,0:T(8,128)(2,1)S(1)} %fusion.12), channel_id=1, source_target_pairs={{0,1},{1,0},{2,3},{3,2},{4,5},{5,4},{6,7},{7,6},{8,9},{9,8},{10,11... | collective-permute-start | bytes 2211848 | tf_op jit(solution)/shard_map/ppermute | solution.py:37
  597.4 15.8 %copy-start.66 = (f32[1152]{0:T(1024)S(1)}, f32[1152]{0:T(1024)}, u32[]{:S(2)}) copy-start(f32[1152]{0:T(1024)} %param.21) | copy-start | bytes 13828
  597.4 15.8 %copy-start.73 = (f32[320]{0:T(512)S(1)}, f32[320]{0:T(512)}, u32[]{:S(2)}) copy-start(f32[320]{0:T(512)} %copy-done.72) | copy-start | bytes 3844
  601.4 16.1 %copy-start.82 = (f32[320]{0:T(512)S(1)}, f32[320]{0:T(512)}, u32[]{:S(2)}) copy-start(f32[320]{0:T(512)} %copy-done.81) | copy-start | bytes 3844
  601.4 16.1 %copy-start.4 = (f32[320,1152]{1,0:T(8,128)S(1)}, f32[320,1152]{1,0:T(8,128)}, u32[]{:S(2)}) copy-start(f32[320,1152]{1,0:T(8,128)} %copy-done.2) | copy-start | bytes 4423684
  601.4 16.1 %copy-start.6 = (f32[320,1152]{1,0:T(8,128)S(1)}, f32[320,1152]{1,0:T(8,128)}, u32[]{:S(2)}) copy-start(f32[320,1152]{1,0:T(8,128)} %copy-done.5) | copy-start | bytes 4423684
  601.4 16.1 %copy-start.14 = (bf16[320,1152]{1,0:T(8,128)(2,1)S(1)}, bf16[320,1152]{1,0:T(8,128)(2,1)}, u32[]{:S(2)}) copy-start(bf16[320,1152]{1,0:T(8,128)(2,1)} %param.35) | copy-start | bytes 2211844
  601.4 16.1 %copy-start.15 = (f32[320,1152]{1,0:T(8,128)S(1)}, f32[320,1152]{1,0:T(8,128)}, u32[]{:S(2)}) copy-start(f32[320,1152]{1,0:T(8,128)} %get-tuple-element.155) | copy-start | bytes 4423684
  601.4 16.1 %copy-start.56 = (f32[320]{0:T(512)S(1)}, f32[320]{0:T(512)}, u32[]{:S(2)}) copy-start(f32[320]{0:T(512)} %copy-done.55) | copy-start | bytes 3844
  601.4 16.1 %copy-start.77 = (f32[320]{0:T(512)S(1)}, f32[320]{0:T(512)}, u32[]{:S(2)}) copy-start(f32[320]{0:T(512)} %copy-done.76) | copy-start | bytes 3844
  601.4 16.1 %copy-start.79 = (f32[320]{0:T(512)S(1)}, f32[320]{0:T(512)}, u32[]{:S(2)}) copy-start(f32[320]{0:T(512)} %copy-done.78) | copy-start | bytes 3844
  616.4 5.9 collective-permute-start.16
  692.2 8.5 %copy-start.1 = (bf16[1152,1152]{1,0:T(8,128)(2,1)S(1)}, bf16[1152,1152]{1,0:T(8,128)(2,1)}, u32[]{:S(2)}) copy-start(bf16[1152,1152]{1,0:T(8,128)(2,1)} %param.30) | copy-start | bytes 7962628
  (60 other events, 218.7 us)
Sparse Core Ops, SparseCore 0:
  127.5 50.0 all-gather.2
  179.1 55.0 all-gather.4

commit v5 on v4

--- a/solution.py
+++ b/solution.py
@@ -203,42 +203,89 @@
     )(*arrays)
 
 
-def gather_kernel(devices, chans, passed, own_ref, *refs):
-    every_ref, send_sem, recv_sem = refs[passed], refs[-2], refs[-1]
-    me = lax.axis_index("seq") * chans + lax.axis_index("chan")
-    barrier = pltpu.get_barrier_semaphore()
-
-    def target(d):
-        peer = lax.rem(me + d, devices)
-        return (lax.div(peer, chans), lax.rem(peer, chans))
-
-    def copy(d):
+class Gather:
+    def __init__(self, devices, chans, own_ref, every_ref, send_sem, recv_sem):
+        self.devices, self.chans = devices, chans
+        self.own_ref, self.every_ref = own_ref, every_ref
+        self.send_sem, self.recv_sem = send_sem, recv_sem
+        self.me = lax.axis_index("seq") * chans + lax.axis_index("chan")
+
+    def target(self, d):
+        peer = lax.rem(self.me + d, self.devices)
+        return (lax.div(peer, self.chans), lax.rem(peer, self.chans))
+
+    def copy(self, d):
         return pltpu.make_async_remote_copy(
-            src_ref=own_ref,
-            dst_ref=every_ref.at[me],
-            send_sem=send_sem.at[d - 1],
-            recv_sem=recv_sem.at[d - 1],
-            device_id=target(d),
+            src_ref=self.own_ref,
+            dst_ref=self.every_ref.at[self.me],
+            send_sem=self.send_sem.at[d - 1],
+            recv_sem=self.recv_sem.at[d - 1],
+            device_id=self.target(d),
             device_id_type=MESH,
         )
 
-    def signal(d, carry):
-        pl.semaphore_signal(barrier, inc=1, device_id=target(d), device_id_type=MESH)
-        return carry
-
-    def start(d, carry):
-        copy(d).start()
-        return carry
-
-    def finish(d, carry):
-        copy(d).wait()
-        return carry
-
-    lax.fori_loop(1, devices, signal, 0)
-    every_ref[me] = own_ref[...]
-    pl.semaphore_wait(barrier, devices - 1)
-    lax.fori_loop(1, devices, start, 0)
-    lax.fori_loop(1, devices, finish, 0)
+    def each(self, act):
+        def turn(d, carry):
+            act(d)
+            return carry
+
+        lax.fori_loop(1, self.devices, turn, 0)
+
+    def greet(self):
+        barrier = pltpu.get_barrier_semaphore()
+        self.each(
+            lambda d: pl.semaphore_signal(barrier, inc=1, device_id=self.target(d), device_id_type=MESH)
+        )
+        self.every_ref[self.me] = self.own_ref[...]
+        pl.semaphore_wait(barrier, self.devices - 1)
+
+    def start(self):
+        self.each(lambda d: self.copy(d).start())
+
+    def wait(self):
+        self.each(lambda d: self.copy(d).wait())
+
+
+def gather_kernel(devices, chans, passed, own_ref, *refs):
+    gather = Gather(devices, chans, own_ref, refs[passed], refs[-2], refs[-1])
+    gather.greet()
+    gather.start()
+    gather.wait()
+
+
+def rows_and_gather_kernel(
+    places, devices, source, own_ref, result, every_ref, rows_send, rows_recv, rows_own, send_sem, recv_sem
+):
+    gather = Gather(devices, places[2], own_ref, every_ref, send_sem, recv_sem)
+    rows = Exchange(*places, [source], [result], rows_send, rows_recv, rows_own)
+    gather.greet()
+    gather.start()
+    for copy in rows.copies:
+        copy.start()
+    gather.wait()
+    rows.wait()
+
+
+def rows_and_gather(packed, values):
+    chans = lax.axis_size("chan")
+    devices = lax.axis_size("seq") * chans
+    vmem, anywhere = pl.BlockSpec(memory_space=pltpu.VMEM), pl.BlockSpec(memory_space=pl.ANY)
+    return pl.pallas_call(
+        partial(rows_and_gather_kernel, expert_groups() + (chans,), devices),
+        in_specs=[anywhere, vmem],
+        out_specs=[anywhere, vmem],
+        out_shape=[
+            jax.ShapeDtypeStruct(packed.shape, packed.dtype),
+            jax.ShapeDtypeStruct((devices,) + values.shape, values.dtype),
+        ],
+        scratch_shapes=exchange_scratch(1)
+        + [pltpu.SemaphoreType.DMA((devices - 1,)), pltpu.SemaphoreType.DMA((devices - 1,))],
+        compiler_params=pltpu.CompilerParams(
+            collective_id=1, has_side_effects=True, vmem_limit_bytes=VMEM_LIMIT
+        ),
+        cost_estimate=lasting(34),
+        name="rows_and_gather",
+    )(packed, values)
 
 
 def gathered_everywhere(ident, values, *passed):
@@ -525,8 +572,8 @@
 
 
 def ends_and_rows_kernel(halves, places, *refs):
-    ins, source, outs, result, wide, sems = refs[:5], refs[5], refs[6:9], refs[9], refs[10], refs[11:]
-    rows = Exchange(*places, [source], [result], *sems)
+    ins, sources, outs, results, wide, sems = refs[:5], refs[5:7], refs[7:10], refs[10:12], refs[12], refs[13:]
+    rows = Exchange(*places, sources, results, *sems)
 
     @pl.when(pl.program_id(0) == 0)
     def _():
@@ -673,11 +720,11 @@
         fills = early_fills(first_early, second_early, held, own_sem)
         for fill in fills:
             fill.start()
+        spread(b_wide, b_ref)
         for fill in fills:
             fill.wait()
         halving.greeted()
         halving.start()
-        spread(b_wide, b_ref)
         spread(c_wide, c_ref)
         b_sum[...] = jnp.zeros_like(b_sum)
         c_sum[...] = jnp.zeros_like(c_sum)
@@ -803,7 +850,7 @@
         )
 
     def ends(self, step, drive, breaks, maps, rates, blocks=None):
-        anywhere = [pl.BlockSpec(memory_space=pl.ANY)]
+        anywhere = [pl.BlockSpec(memory_space=pl.ANY)] * 2
         forward = blocks is not None
         places = expert_groups() + (lax.axis_size("chan"),)
         kernel = partial(ends_and_rows_kernel, self.halves, places) if forward else partial(ends_kernel, self.halves, True)
@@ -820,12 +867,12 @@
             + anywhere * forward,
             out_specs=[self.part_spec, self.sum_spec, self.tot_spec] + anywhere * forward,
             out_shape=[self.part_f32, self.sum_f32, self.tot_f32]
-            + ([jax.ShapeDtypeStruct(blocks.shape, blocks.dtype)] if forward else []),
-            scratch_shapes=[self.wide] + (exchange_scratch(1) if forward else []),
+            + ([jax.ShapeDtypeStruct(part.shape, part.dtype) for part in blocks] if forward else []),
+            scratch_shapes=[self.wide] + (exchange_scratch(2) if forward else []),
             compiler_params=params,
             cost_estimate=self.cost(5),
             name="scan_ends" if forward else "scan_ends_back",
-        )(step, drive, breaks, maps, rates, *([blocks] if forward else []))
+        )(step, drive, breaks, maps, rates, *(blocks if forward else []))
 
     def outputs(self, step, mixed, breaks, b_in, c_out, rates, part, sums, device, skip, gate):
         return pl.pallas_call(
@@ -896,7 +943,7 @@
     return jnp.sum(jnp.sum(values, 0), -1, keepdims=True)
 
 
-def sinkhorn_kernel(place_ref, logit_ref, route_ref, gate_ref, scaled_ref, row_ref, column_ref):
+def sinkhorn_kernel(place_ref, logit_ref, route_ref, gate_ref, scaled_ref, row_ref, column_ref, every_ref):
     probs = jnp.exp(logit_ref[...])
     for sweep in range(SINK):
         column = over_tokens(probs)
@@ -906,6 +953,8 @@
         row_ref[sweep] = row
         column_ref[sweep] = jnp.broadcast_to(column, column_ref.shape[1:])
         probs = scaled / row
+    ids = lax.broadcasted_iota(jnp.int32, probs.shape, 1)
+    every_ref[...] = EXPERTS * jnp.sum(jnp.where(ids == place_ref[1], probs, 0.0), 1, keepdims=True)
     place = place_ref[0]
     own = scaled_ref[SINK - 1, place] / row_ref[SINK - 1, place]
     ids = lax.broadcasted_iota(jnp.int32, own.shape, 0)
@@ -935,12 +984,13 @@
     return pl.pallas_call(
         sinkhorn_kernel,
         in_specs=in_vmem(2),
-        out_specs=in_vmem(4)[1:],
+        out_specs=in_vmem(5)[1:],
         out_shape=[
             f32(1, tokens),
             f32(SINK, devices, experts, tokens),
             f32(SINK, devices, 1, tokens),
             f32(SINK, experts, LANES),
+            f32(devices, 1, tokens),
         ],
         compiler_params=pltpu.CompilerParams(vmem_limit_bytes=VMEM_LIMIT),
         name="sinkhorn",
@@ -1118,7 +1168,9 @@
     tok_dev, model_width = block_in.shape
     chan_count = lax.axis_size("chan")
     chan_place, seq_place = lax.axis_index("chan"), lax.axis_index("seq")
-    dev_ref = (seq_place * chan_count + chan_place).astype(jnp.int32).reshape(1)
+    own, share = expert_groups()
+    held_expert = chan_place * own + seq_place // share
+    dev_ref = jnp.stack([seq_place * chan_count + chan_place, held_expert]).astype(jnp.int32)
     steps = tok_dev // CHUNKS
     tok_seq = tok_dev * chan_count
     channels = in_weight.shape[2]
@@ -1204,7 +1256,13 @@
     breaks = jnp.any(position[..., None] == starts, axis=-1).astype(f32) * BREAK
     breaks = jnp.broadcast_to(breaks.reshape(tok_seq, 1), (tok_seq, LANES))
     step_w, mixed_w = widened(step_size), widened(mixed)
-    part, sums, total, grad_arrived = scan.ends(step_w, mixed_w, breaks, b_in, rates, pack(grad_steps))
+    token_slots = jnp.einsum(
+        "ts,t->s", placer.astype(f32), 1.0 + lax.broadcasted_iota(f32, (tok_dev,), 0), precision=HIGH
+    )
+    token_slots = jnp.pad(token_slots.reshape(EXPERTS, 1, capacity), ((0, 0), (0, 7), (0, LANES - capacity)))
+    part, sums, total, grad_arrived, token_arrived = scan.ends(
+        step_w, mixed_w, breaks, b_in, rates, (pack(grad_steps), token_slots)
+    )
     grad_arrived = grad_arrived.reshape(-1, model_width)
     device_entry = carried(total, rates, False)
     full_up = whole_expert(up_weight, None, device_entry)
@@ -1221,18 +1279,21 @@
     hidden_one = residual + mixer_rows
     moe_in, moe_back = jax.vjp(norm_apply, hidden_one, moe_gain)
     logits = jnp.einsum("td,de->et", moe_in, router_weight, precision=HIGH)
-    every_logit = gathered_everywhere(3, logits)
-    gate_row, scaled, row_totals, columns = sinkhorn(
+    arrived, every_logit = rows_and_gather(pack(moe_in.astype(bf16)), logits)
+    gate_row, scaled, row_totals, columns, every_gate = sinkhorn(
         dev_ref, every_logit, route_steps.reshape(1, tok_dev)
     )
     gate = gate_row.reshape(tok_dev)
 
-    gate_slots = jnp.einsum("ts,t->s", placer.astype(f32), gate, precision=HIGH)
-    gate_slots = jnp.pad(gate_slots.reshape(EXPERTS, 1, capacity), ((0, 0), (0, 7), (0, LANES - capacity)))
-    arrived, gate_arrived = expert_rows(1, pack(moe_in.astype(bf16)), gate_slots)
     arrived = arrived.reshape(-1, model_width)
-    gate_arrived = gate_arrived[:, 0, :capacity].reshape(-1, 1)
-    own, share = expert_groups()
+    senders = lax.dynamic_index_in_dim(
+        every_gate.reshape(own, share, chan_count, tok_dev), seq_place % share, 1, False
+    )
+    senders = jnp.swapaxes(senders, 0, 1).reshape(EXPERTS, 1, tok_dev)
+    token_ids = 1.0 + lax.broadcasted_iota(f32, (1, 1, tok_dev), 2)
+    gate_arrived = jnp.sum(
+        jnp.where(token_arrived[:, 0, :capacity, None] == token_ids, senders, 0.0), -1
+    ).reshape(-1, 1)
     features, hidden = up_weight.shape[1:]
     expert_out, grad_rows_in, up_kept, up_sent, down_kept, down_sent = expert_passes(
         arrived, grad_arrived, gate_arrived, full_up, full_down

time: 713 us -> 707 us (level)
  Pallas kernels: 425 us -> 414 us
    pallas_call x1 -> x2, Pallas kernels: 4.78 us -> 45.2 us  [the longest x1 40.4 us: rows_and_gather(): pl.pallas_call(partial(rows_and_gather_kernel, expert_groups() + (chans,)...]
    pallas_call x2 -> x1, Pallas kernels: 86.4 us -> 54.7 us  [exchange(): pl.pallas_call(partial(exchange_kernel, own, share, chans, count), in_spe...]
    pallas_call x2 -> x1, Pallas kernels: 36.1 us -> 18.1 us  [gathered_everywhere(): pl.pallas_call(partial(gather_kernel, devices, chans, len(passed)), in_sp...]
  transfers between devices with their start and end apart: 22 -> 22, of which waited for: 7 -> 7; matrix products, arithmetic and copies ran while one was open for 18% -> 19% of each run, Pallas kernels for 31% -> 30%
where the time goes in v5:
time: 707 us; the launch traced here: 702 us
  Pallas kernels  414 us (59%)
  matrix products  72 us (10%)
  waiting for transfers between devices  58.8 us (8%)
  other arithmetic  56.6 us (8%)
  local copies, waits for them, and re-layouts  47 us (7%)
  starting transfers between devices  37.2 us (5%)
  between operations  16 us (2%)
    pallas_call x1, Pallas kernels, grads(): pl.pallas_call(partial(grads_kernel, self.halves, count, self.groups), gr...  87.5 us
    pallas_call x1, Pallas kernels, summed(): pl.pallas_call(partial(sum_kernel, count, places, [part.shape[0] for part...  60.8 us
    ppermute x16, waiting for transfers between devices, swapped(): lax.ppermute(value, axis, [(source, source ^ bit) for source in range(cou...  57.6 us
    pallas_call x1, Pallas kernels, exchange(): pl.pallas_call(partial(exchange_kernel, own, share, chans, count), in_spe...  54.7 us
    pallas_call x2, Pallas kernels, ends(): pl.pallas_call(kernel, grid=(self.groups,), in_specs=[self.row_spec, self...  51.1 us
    pallas_call x1, Pallas kernels, expert_passes(): pl.pallas_call(partial(expert_kernel, share), grid=(tiles + 1,), in_specs...  41.4 us
    pallas_call x1, Pallas kernels, rows_and_gather(): pl.pallas_call(partial(rows_and_gather_kernel, expert_groups() + (chans,)...  40.4 us
    pallas_call x2, Pallas kernels, carried(): pl.pallas_call(partial(carry_kernel, count, reverse), in_specs=[vmem, vme...  29.8 us
  transfers between devices with their start and end apart: 22, of which 7 were waited for; matrix products, arithmetic and copies ran while one was open for 19% of the time, Pallas kernels for 30%

profile of v5, /device:TPU:0, one launch (start us, length us, event | category | flops | bytes accessed | tf_op | source)
XLA Modules:
  0.0 701.8 jit_solution(9824359104548809864)
XLA Ops:
  7.3 3.1 copy.221
  13.7 2.6 multiply_convert_fusion.1
  16.3 2.9 collective-permute-start
  19.3 2.4 constant_dynamic-slice_fusion.3
  21.6 3.6 collective-permute-start.6
  29.1 6.8 collective-permute-done
  36.0 1.8 broadcast_select_fusion.3
  37.9 6.2 fusion
  47.9 2.1 copy.142
  52.0 2.4 fusion.92
  55.1 1.8 collective-permute-start.2
  56.9 2.0 convolution_convert_fusion.5
  58.9 5.3 collective-permute-done.2
  65.3 5.5 compare_select_fusion
  71.7 37.1 %scan_ends.1 = (f32[2,16,8,1152]{3,2,1,0:T(8,128)}, f32[2,8,1152]{2,1,0:T(8,128)}, f32[24,1152]{1,0:T(8,128)}, bf16[8,64,1152]{2,1,0:T(8,128)(2,1)}, f32[8,8,128]{2,1,0:T(8,128)}) custom-call(f32[640,1152]{1,0:T(8,128)} %get-tuple-element.154.refs_0_.step_ref, f32[640,1152]{1,0:T(8,128)} %get-tuple-element.125.refs_1_.mixed_ref, ...), custom_call_target="tpu_custom_call" | custom-call | flops 58982400 | bytes 8847360 | tf_op jit(solution)/shard_map/scan_ends/pallas_call | solution.py:863
  108.8 14.1 %carry.1.device = f32[16,1152]{1,0:T(8,128)} custom-call(f32[24,1152]{1,0:T(8,128)} %get-tuple-element.61.total_ref, f32[16,1152]{1,0:T(8,128)} %multiply_bitcast_fusion.refs_4_.rate_ref), custom_call_target="tpu_custom_call" | custom-call | bytes 50400000 | tf_op jit(solution)/shard_map/carry/pallas_call | solution.py:359
  123.0 1.8 bitcast_dynamic-update-slice_fusion.5
  124.8 1.9 bitcast_dynamic-update-slice_fusion.4
  126.7 1.8 bitcast_dynamic-update-slice_fusion.3
  130.6 1.6 collective-permute-start.9
  132.3 2.8 collective-permute-start.7
  135.1 6.0 fusion.15.gate_ref
  141.1 20.4 %scan_outputs.1 = (f32[640,1152]{1,0:T(8,128)}, bf16[640,1152]{1,0:T(8,128)(2,1)}, f32[2,16,8,1152]{3,2,1,0:T(8,128)}) custom-call(f32[640,1152]{1,0:T(8,128)} %get-tuple-element.154.refs_0_.step_ref, f32[640,1152]{1,0:T(8,128)} %get-tuple-element.125.refs_1_.mixed_ref, f32[640,128]{1,0:T(8,128)} %broadcast_in_dim.81.refs_2_.break_ref, ...), custom_call_target="tpu_custom_call" | custom-call | flops 82575360 | bytes 8847360 | tf_op jit(solution)/shard_map/scan_outputs/pallas_call | solution.py:878
  161.5 7.3 %collective-permute-done.8 = bf16[1,72,3072]{2,1,0:T(8,128)(2,1)S(1)} collective-permute-done((bf16[1,72,3072]{2,1,0:T(8,128)(2,1)S(1)}, bf16[1,72,3072]{2,1,0:T(8,128)(2,1)S(1)}, u32[]{:S(2)}, u32[]{:S(2)}) %collective-permute-start.8) | collective-permute-done | bytes 442400 | tf_op jit(solution)/shard_map/ppermute | solution.py:37
  171.2 3.2 convolution_convert_fusion.6
  178.6 12.3 %collective-permute-done.3 = bf16[320,1152]{1,0:T(8,128)(2,1)} collective-permute-done((bf16[320,1152]{1,0:T(8,128)(2,1)}, bf16[320,1152]{1,0:T(8,128)(2,1)}, u32[]{:S(2)}, u32[]{:S(2)}) %collective-permute-start.3) | collective-permute-done | bytes 737312 | tf_op jit(solution)/shard_map/ppermute | solution.py:37
  190.8 3.3 multiply_reduce_fusion.8
  194.2 2.1 fusion.38.own_ref
  196.3 2.0 convolution_convert_fusion.4
  198.3 40.4 %rows_and_gather.1 = (bf16[8,64,1152]{2,1,0:T(8,128)(2,1)}, f32[32,8,320]{2,1,0:T(8,128)}) custom-call(bf16[8,64,1152]{2,1,0:T(8,128)(2,1)} %bitcast.204, f32[8,320]{1,0:T(8,128)} %fusion.38.own_ref), custom_call_target="tpu_custom_call" | custom-call | bytes 122400000 | tf_op jit(solution)/shard_map/rows_and_gather/pallas_call | solution.py:273
  238.8 4.8 sinkhorn.1
  247.7 41.4 %expert_passes.1 = (bf16[512,1152]{1,0:T(8,128)(2,1)}, bf16[512,1152]{1,0:T(8,128)(2,1)}, bf16[4,72,3072]{2,1,0:T(8,128)(2,1)}, bf16[4,72,3072]{2,1,0:T(8,128)(2...) custom-call(bf16[512,1152]{1,0:T(8,128)(2,1)} %bitcast.224, bf16[512,1152]{1,0:T(8,128)(2,1)} %bitcast.226, ...), custom_call_target="tpu_custom_call" | custom-call | flops 21743271936 | bytes 28311552 | tf_op jit(solution)/shard_map/expert_passes/pallas_call | solution.py:1116
  293.4 54.7 %expert_rows.1 = (bf16[8,64,1152]{2,1,0:T(8,128)(2,1)}, bf16[8,64,1152]{2,1,0:T(8,128)(2,1)}) custom-call(bf16[8,64,1152]{2,1,0:T(8,128)(2,1)} %bitcast.208, bf16[8,64,1152]{2,1,0:T(8,128)(2,1)} %bitcast.209), custom_call_target="tpu_custom_call" | custom-call | bytes 187200000 | tf_op jit(solution)/shard_map/expert_rows/pallas_call | solution.py:194
  348.2 3.1 fusion.29
  351.9 3.4 fusion.28.refs_0_
  355.3 18.1 %gather_small.1 = (f32[32,8,320]{2,1,0:T(8,128)}, bf16[4,1,72,3072]{3,2,1,0:T(8,128)(2,1)}) custom-call(f32[8,320]{1,0:T(8,128)} %fusion.75.own_ref, bf16[4,1,72,3072]{3,2,1,0:T(8,128)(2,1)} %fusion.28.refs_0_), custom_call_target="tpu_custom_call", output_to_operand_aliasing={{1}: (1, {})} | custom-call | bytes 43200000 | tf_op jit(solution)/shard_map/gather_small/pallas_call | solution.py:295
  373.4 6.5 all-to-all-start
  379.9 5.4 sinkhorn_back.1
  385.3 2.1 fusion.96
  387.5 2.1 multiply_reduce_fusion.5
  393.2 3.5 add_convert_fusion
  397.4 13.5 %collective-permute-done.11 = bf16[320,1152]{1,0:T(8,128)(2,1)S(1)} collective-permute-done((bf16[320,1152]{1,0:T(8,128)(2,1)S(1)}, bf16[320,1152]{1,0:T(8,128)(2,1)S(1)}, u32[]{:S(2)}, u32[]{:S(2)}) %collective-permute-start.11) | collective-permute-done | bytes 737312 | tf_op jit(solution)/shard_map/ppermute | solution.py:37
  411.0 4.4 multiply_reduce_fusion
  416.1 14.0 %scan_ends_back.1 = (f32[2,16,8,1152]{3,2,1,0:T(8,128)}, f32[2,8,1152]{2,1,0:T(8,128)}, f32[24,1152]{1,0:T(8,128)}) custom-call(f32[640,1152]{1,0:T(8,128)} %get-tuple-element.154.refs_0_.step_ref, f32[640,1152]{1,0:T(8,128)} %get-tuple-element.121.drive_ref.grad_ref, f32[640,128]{1,0:T(8,128)} %broadcast_in_dim.81.refs_2_.break_ref, ...), custom_call_target="tpu_custom_call" | custom-call | flops 58982400 | bytes 8847360 | tf_op jit(solution)/shard_map/scan_ends_back/pallas_call | solution.py:863
  430.1 4.0 convolution_convert_fusion.2.first_early
  434.1 4.0 convolution_convert_fusion.1.second_early
  438.0 15.6 %carry_back.1.device = f32[16,1152]{1,0:T(8,128)} custom-call(f32[24,1152]{1,0:T(8,128)} %get-tuple-element.89.total_ref, f32[16,1152]{1,0:T(8,128)} %multiply_bitcast_fusion.refs_4_.rate_ref, bf16[4,72,3072]{2,1,0:T(8,128)(2,1)} %all-to-all-done.refs_0_, bf16[4,1,72,3072]{3,2,1,0:T(8,128)(2,1)} %bitcast.193), custom_call_target="tpu_custom_call" | custom-call | bytes 50400000 | tf_op jit(solution)/shard_map/carry_back/pallas_call | solution.py:359
  453.7 87.5 %scan_grads.1 = (f32[640,1152]{1,0:T(8,128)}, f32[640,1152]{1,0:T(8,128)}, f32[640,16]{1,0:T(8,128)}, f32[640,16]{1,0:T(8,128)}, f32[16,1152]{1,0:T(8,128)}, /*index=5*/bf16[9,256,1152]{2,1,0:T(8,128)(2,1)}) custom-call(f32[640,1152]{1,0:T(8,128)} %get-tuple-element.154.refs_0_.step_ref, f32[640,1152]{1,0:T(8,128)} %get-tuple-element.125.refs_1_.mixed_ref, ...), custom_call_target="tpu_custom_call" | custom-call | flops 235929600 | bytes 8847360 | tf_op jit(solution)/shard_map/scan_grads/pallas_call | solution.py:907
  541.2 2.7 fusion.90
  544.5 3.0 fusion.97
  547.5 4.9 all-to-all-start.1
  556.3 6.5 slice_convert_fusion
  562.8 3.8 convert_element_type.225
  566.7 1.8 fusion.71
  568.7 3.8 fusion.89
  572.6 6.0 multiply_reduce_fusion.2
  590.7 3.9 convolution_convert_fusion.refs_0_
  594.7 12.5 %collective-permute-done.15 = bf16[320,1152]{1,0:T(8,128)(2,1)S(1)} collective-permute-done((bf16[320,1152]{1,0:T(8,128)(2,1)S(1)}, bf16[320,1152]{1,0:T(8,128)(2,1)S(1)}, u32[]{:S(2)}, u32[]{:S(2)}) %collective-permute-start.15) | collective-permute-done | bytes 737312 | tf_op jit(solution)/shard_map/ppermute | solution.py:37
  607.2 3.1 multiply_reduce_fusion.6
  611.7 2.4 fusion.31
  618.2 60.8 %sum_late.1 = bf16[6,256,1152]{2,1,0:T(8,128)(2,1)} custom-call(bf16[1152,1152]{1,0:T(8,128)(2,1)} %convolution_convert_fusion.refs_0_, f32[224,1152]{1,0:T(8,128)} %pad.34.refs_1_), custom_call_target="tpu_custom_call" | custom-call | bytes 216000000 | tf_op jit(solution)/shard_map/sum_late/pallas_call | solution.py:494
  680.1 2.1 slice_bitcast_fusion.1
  686.3 4.8 maximum_convert_fusion
  691.1 3.7 convert_element_type.226
  (365 shorter events, 65.2 us)
Async XLA Ops:
  7.2 164.0 %copy-start = (bf16[1152,1152]{1,0:T(8,128)(2,1)S(1)}, bf16[1152,1152]{1,0:T(8,128)(2,1)}, u32[]{:S(2)}) copy-start(bf16[1152,1152]{1,0:T(8,128)(2,1)} %param.30) | copy-start | bytes 7962628
  7.2 240.5 %all-gather.3.cloned.1.call-start = ((), (), s32[]{:S(2)}) async-start(), calls=%async_computation.2 | async-start | bytes 8847360 | tf_op jit(solution)/shard_map/all_gather | solution.py:105
  12.4 9.2 %copy-start.84 = (f32[320]{0:T(512)}, f32[320]{0:T(512)S(1)}, u32[]{:S(2)}) copy-start(f32[320]{0:T(512)S(1)} %add.282) | copy-start | bytes 3844
  12.4 23.5 %copy-start.72 = (f32[320]{0:T(512)}, f32[320]{0:T(512)S(1)}, u32[]{:S(2)}) copy-start(f32[320]{0:T(512)S(1)} %rsqrt.20) | copy-start | bytes 3844
  13.7 12.4 %copy-start.96 = (s32[320,1]{0,1:T(1,128)S(1)}, s32[320,1]{0,1:T(1,128)}, u32[]{:S(2)}) copy-start(s32[320,1]{0,1:T(1,128)} %param.19) | copy-start | bytes 3844
  13.7 12.7 %copy-start.98 = (s32[4]{0:T(128)S(1)}, s32[4]{0:T(128)}, u32[]{:S(2)}) copy-start(s32[4]{0:T(128)} %param.20) | copy-start | bytes 52
  13.7 14.8 %copy-start.48 = (f32[1152,16]{0,1:T(8,128)S(1)}, f32[1152,16]{0,1:T(8,128)}, u32[]{:S(2)}) copy-start(f32[1152,16]{0,1:T(8,128)} %param.28) | copy-start | bytes 221188
  16.3 19.6 %collective-permute-start = (bf16[320,1152]{1,0:T(8,128)(2,1)}, bf16[320,1152]{1,0:T(8,128)(2,1)S(1)}, u32[]{:S(2)}, u32[]{:S(2)}) collective-permute-start(bf16[320,1152]{1,0:T(8,128)(2,1)} %multiply_convert_fusion.1), channel_id=1, source_target_pairs={{0,1},{1,0},{2,3},{3,2},{4,5},{5,4},{6,7},{7,6},{8,9},{9,8},{10,11... | collective-permute-start | bytes 2211848 | tf_op jit(solution)/shard_map/ppermute | solution.py:37
  21.6 101.3 %collective-permute-start.6 = (bf16[1,72,3072]{2,1,0:T(8,128)(2,1)}, bf16[1,72,3072]{2,1,0:T(8,128)(2,1)}, u32[]{:S(2)}, u32[]{:S(2)}) collective-permute-start(bf16[1,72,3072]{2,1,0:T(8,128)(2,1)} %get-tuple-element.139), channel_id=1, source_target_pairs={{0,24},{2,26},{4,28},{6,30},{8,16},{10,18},{12,20},{14,22},{16,8},... | collective-permute-start | bytes 1327112 | tf_op jit(solution)/shard_map/ppermute | solution.py:37
  25.2 97.8 %collective-permute-start.4 = (bf16[1,72,3072]{2,1,0:T(8,128)(2,1)}, bf16[1,72,3072]{2,1,0:T(8,128)(2,1)}, u32[]{:S(2)}, u32[]{:S(2)}) collective-permute-start(bf16[1,72,3072]{2,1,0:T(8,128)(2,1)} %get-tuple-element.140), channel_id=1, source_target_pairs={{0,8},{2,10},{4,12},{6,14},{8,0},{10,2},{12,4},{14,6},{16,24},{18,... | collective-permute-start | bytes 1327112 | tf_op jit(solution)/shard_map/ppermute | solution.py:37
  25.2 97.7 %collective-permute-start.5 = (bf16[1,72,3072]{2,1,0:T(8,128)(2,1)}, bf16[1,72,3072]{2,1,0:T(8,128)(2,1)}, u32[]{:S(2)}, u32[]{:S(2)}) collective-permute-start(bf16[1,72,3072]{2,1,0:T(8,128)(2,1)} %get-tuple-element.141), channel_id=1, source_target_pairs={{0,16},{2,18},{4,20},{6,22},{8,24},{10,26},{12,28},{14,30},{16,0},... | collective-permute-start | bytes 1327112 | tf_op jit(solution)/shard_map/ppermute | solution.py:37
  28.5 18.7 %copy-start.68 = (f32[2,40,8]{1,2,0:T(8,128)}, f32[2,40,8]{1,2,0:T(8,128)S(1)}, u32[]{:S(2)}) copy-start(f32[2,40,8]{1,2,0:T(8,128)S(1)} %get-tuple-element.151) | copy-start | bytes 7684
  37.8 8.7 %copy-start.83 = (f32[4,1152]{1,0:T(4,128)S(1)}, f32[4,1152]{1,0:T(4,128)}, u32[]{:S(2)}) copy-start(f32[4,1152]{1,0:T(4,128)} %param.23) | copy-start | bytes 55300
  37.8 9.1 %copy-start.75 = (f32[2,40,8]{1,2,0:T(8,128)S(1)}, f32[2,40,8]{1,2,0:T(8,128)}, u32[]{:S(2)}) copy-start(f32[2,40,8]{1,2,0:T(8,128)} %get-tuple-element.152) | copy-start | bytes 7684
  37.8 9.2 %copy-start.74 = (f32[2,40,8]{1,2,0:T(8,128)S(1)}, f32[2,40,8]{1,2,0:T(8,128)}, u32[]{:S(2)}) copy-start(f32[2,40,8]{1,2,0:T(8,128)} %get-tuple-element.153) | copy-start | bytes 7684
  45.0 5.0 collective-permute-start.1
  54.5 10.8 %copy-start.7 = (bf16[640,1152]{1,0:T(8,128)(2,1)}, bf16[640,1152]{1,0:T(8,128)(2,1)S(1)}, u32[]{:S(2)}) copy-start(bf16[640,1152]{1,0:T(8,128)(2,1)S(1)} %get-tuple-element.126) | copy-start | bytes 4423684
  55.0 10.2 %copy-start.43 = (f32[72,1152]{1,0:T(8,128)S(1)}, f32[72,1152]{1,0:T(8,128)}, u32[]{:S(2)}) copy-start(f32[72,1152]{1,0:T(8,128)} %param.26) | copy-start | bytes 995332
  55.1 10.2 %copy-start.97 = (f32[1152]{0:T(1024)S(1)}, f32[1152]{0:T(1024)}, u32[]{:S(2)}) copy-start(f32[1152]{0:T(1024)} %param.27) | copy-start | bytes 13828
  55.1 9.1 %collective-permute-start.2 = (f32[640,104]{1,0:T(8,128)S(1)}, f32[640,104]{1,0:T(8,128)S(1)}, u32[]{:S(2)}, u32[]{:S(2)}) collective-permute-start(f32[640,104]{1,0:T(8,128)S(1)} %fusion.95), channel_id=1, source_target_pairs={{0,1},{1,0},{2,3},{3,2},{4,5},{5,4},{6,7},{7,6},{8,9},{9,8},{10,11... | collective-permute-start | bytes 798728 | tf_op jit(solution)/shard_map/ppermute | solution.py:37
  108.8 19.8 %copy-start.92 = (f32[1152]{0:T(1024)S(1)}, f32[1152]{0:T(1024)}, u32[]{:S(2)}) copy-start(f32[1152]{0:T(1024)} %param.29) | copy-start | bytes 13828
  128.6 119.2 %all-gather.5.cloned.1.call-start = ((), (), s32[]{:S(2)}) async-start(), calls=%async_computation.3 | async-start | bytes 8847360 | tf_op jit(solution)/shard_map/all_gather | solution.py:105
  130.6 30.9 %collective-permute-start.9 = (bf16[1,72,3072]{2,1,0:T(8,128)(2,1)S(1)}, bf16[1,72,3072]{2,1,0:T(8,128)(2,1)S(1)}, u32[]{:S(2)}, u32[]{:S(2)}) collective-permute-start(bf16[1,72,3072]{2,1,0:T(8,128)(2,1)S(1)} %get-tuple-element.136), channel_id=1, source_target_pairs={{0,24},{2,26},{4,28},{6,30},{8,16},{10,18},{12,20},{14,22},{16,8},... | collective-permute-start | bytes 1327112 | tf_op jit(solution)/shard_map/ppermute | solution.py:37
  132.2 36.6 %collective-permute-start.8 = (bf16[1,72,3072]{2,1,0:T(8,128)(2,1)S(1)}, bf16[1,72,3072]{2,1,0:T(8,128)(2,1)S(1)}, u32[]{:S(2)}, u32[]{:S(2)}) collective-permute-start(bf16[1,72,3072]{2,1,0:T(8,128)(2,1)S(1)} %get-tuple-element.137), channel_id=1, source_target_pairs={{0,16},{2,18},{4,20},{6,22},{8,24},{10,26},{12,28},{14,30},{16,0},... | collective-permute-start | bytes 1327112 | tf_op jit(solution)/shard_map/ppermute | solution.py:37
  132.3 36.5 %collective-permute-start.7 = (bf16[1,72,3072]{2,1,0:T(8,128)(2,1)S(1)}, bf16[1,72,3072]{2,1,0:T(8,128)(2,1)S(1)}, u32[]{:S(2)}, u32[]{:S(2)}) collective-permute-start(bf16[1,72,3072]{2,1,0:T(8,128)(2,1)S(1)} %get-tuple-element.138), channel_id=1, source_target_pairs={{0,8},{2,10},{4,12},{6,14},{8,0},{10,2},{12,4},{14,6},{16,24},{18,... | collective-permute-start | bytes 1327112 | tf_op jit(solution)/shard_map/ppermute | solution.py:37
  174.4 16.4 %collective-permute-start.3 = (bf16[320,1152]{1,0:T(8,128)(2,1)}, bf16[320,1152]{1,0:T(8,128)(2,1)}, u32[]{:S(2)}, u32[]{:S(2)}) collective-permute-start(bf16[320,1152]{1,0:T(8,128)(2,1)} %convolution_convert_fusion.6), channel_id=1, source_target_pairs={{0,1},{1,0},{2,3},{3,2},{4,5},{5,4},{6,7},{7,6},{8,9},{9,8},{10,11... | collective-permute-start | bytes 2211848 | tf_op jit(solution)/shard_map/ppermute | solution.py:37
  178.6 15.7 %copy-start.45 = (f32[1152]{0:T(1024)S(1)}, f32[1152]{0:T(1024)}, u32[]{:S(2)}) copy-start(f32[1152]{0:T(1024)} %param.31) | copy-start | bytes 13828
  178.6 15.7 %copy-start.52 = (f32[1152,8]{0,1:T(8,128)S(1)}, f32[1152,8]{0,1:T(8,128)}, u32[]{:S(2)}) copy-start(f32[1152,8]{0,1:T(8,128)} %param.32) | copy-start | bytes 110596
  194.2 44.6 %copy-start.90 = (f32[320]{0:T(512)}, f32[320]{0:T(512)S(1)}, u32[]{:S(2)}) copy-start(f32[320]{0:T(512)S(1)} %get-tuple-element.156) | copy-start | bytes 3844
  194.2 197.9 %copy-start.55 = (f32[320]{0:T(512)}, f32[320]{0:T(512)S(1)}, u32[]{:S(2)}) copy-start(f32[320]{0:T(512)S(1)} %fusion.85) | copy-start | bytes 3844
  247.7 42.8 %copy-start.69 = (f32[2,40,8]{1,2,0:T(8,128)S(1)}, f32[2,40,8]{1,2,0:T(8,128)}, u32[]{:S(2)}) copy-start(f32[2,40,8]{1,2,0:T(8,128)} %copy-done.68) | copy-start | bytes 7684
  289.1 62.8 %collective-permute-start.10 = (bf16[4,72,3072]{2,1,0:T(8,128)(2,1)}, bf16[4,72,3072]{2,1,0:T(8,128)(2,1)}, u32[]{:S(2)}, u32[]{:S(2)}) collective-permute-start(bf16[4,72,3072]{2,1,0:T(8,128)(2,1)} %get-tuple-element.84), channel_id=1, source_target_pairs={{0,4},{2,6},{4,0},{6,2},{8,12},{10,14},{12,8},{14,10},{16,20},{18,... | collective-permute-start | bytes 5308424 | tf_op jit(solution)/shard_map/ppermute | solution.py:37
  292.0 95.4 %copy-start.81 = (f32[320]{0:T(512)}, f32[320]{0:T(512)S(1)}, u32[]{:S(2)}) copy-start(f32[320]{0:T(512)S(1)} %reduce.11) | copy-start | bytes 3844
  292.0 101.2 %collective-permute-start.12 = (bf16[4,72,3072]{2,1,0:T(8,128)(2,1)}, bf16[4,72,3072]{2,1,0:T(8,128)(2,1)}, u32[]{:S(2)}, u32[]{:S(2)}) collective-permute-start(bf16[4,72,3072]{2,1,0:T(8,128)(2,1)} %get-tuple-element.92), channel_id=1, source_target_pairs={{0,4},{2,6},{4,0},{6,2},{8,12},{10,14},{12,8},{14,10},{16,20},{18,... | collective-permute-start | bytes 5308424 | tf_op jit(solution)/shard_map/ppermute | solution.py:37
  293.4 57.9 %copy-start.94 = (s32[320]{0:T(512)S(1)}, s32[320]{0:T(512)}, u32[]{:S(2)}) copy-start(s32[320]{0:T(512)} %eq.89) | copy-start | bytes 3844
  373.4 64.6 %all-to-all-start = ((bf16[4,72,3072]{2,1,0:T(8,128)(2,1)}), bf16[4,72,3072]{2,1,0:T(8,128)(2,1)}, u32[]{:S(2)}, u32[]{:S(2)}) async-start(bf16[4,72,3072]{2,1,0:T(8,128)(2,1)} %bitcast.194), calls=%async_computation | async-start | bytes 3538944 | tf_op jit(solution)/shard_map/all_to_all | solution.py:89
  379.9 7.5 %copy-start.3 = (f32[320,1152]{1,0:T(8,128)S(1)}, f32[320,1152]{1,0:T(8,128)}, u32[]{:S(2)}) copy-start(f32[320,1152]{1,0:T(8,128)} %copy-done.2) | copy-start | bytes 4423684
  390.6 6.1 collective-permute-start.17
  392.6 18.3 %collective-permute-start.11 = (bf16[320,1152]{1,0:T(8,128)(2,1)S(1)}, bf16[320,1152]{1,0:T(8,128)(2,1)S(1)}, u32[]{:S(2)}, u32[]{:S(2)}) collective-permute-start(bf16[320,1152]{1,0:T(8,128)(2,1)S(1)} %fusion.88), channel_id=1, source_target_pairs={{0,1},{1,0},{2,3},{3,2},{4,5},{5,4},{6,7},{7,6},{8,9},{9,8},{10,11... | collective-permute-start | bytes 2211848 | tf_op jit(solution)/shard_map/ppermute | solution.py:37
  393.2 17.8 %copy-start.102 = (f32[640,1152]{1,0:T(8,128)S(1)}, f32[640,1152]{1,0:T(8,128)}, u32[]{:S(2)}) copy-start(f32[640,1152]{1,0:T(8,128)} %fusion.15.gate_ref) | copy-start | bytes 8847364
  393.2 17.8 %copy-start.103 = (f32[640,1152]{1,0:T(8,128)S(1)}, f32[640,1152]{1,0:T(8,128)}, u32[]{:S(2)}) copy-start(f32[640,1152]{1,0:T(8,128)} %get-tuple-element.93) | copy-start | bytes 8847364
  396.7 14.3 %copy-start.8 = (bf16[640,1152]{1,0:T(8,128)(2,1)S(1)}, bf16[640,1152]{1,0:T(8,128)(2,1)}, u32[]{:S(2)}) copy-start(bf16[640,1152]{1,0:T(8,128)(2,1)} %copy-done.7) | copy-start | bytes 4423684
  415.4 18.6 %copy-start.25 = (bf16[640,1152]{1,0:T(8,128)(2,1)}, bf16[640,1152]{1,0:T(8,128)(2,1)S(1)}, u32[]{:S(2)}) copy-start(bf16[640,1152]{1,0:T(8,128)(2,1)S(1)} %get-tuple-element.127) | copy-start | bytes 4423684
  416.1 14.0 %copy-start.99 = (bf16[640,1152]{1,0:T(8,128)(2,1)S(1)}, bf16[640,1152]{1,0:T(8,128)(2,1)}, u32[]{:S(2)}) copy-start(bf16[640,1152]{1,0:T(8,128)(2,1)} %get-tuple-element.62) | copy-start | bytes 4423684
  453.7 87.5 %copy-start.18 = (f32[640,1152]{1,0:T(8,128)S(1)}, f32[640,1152]{1,0:T(8,128)}, u32[]{:S(2)}) copy-start(f32[640,1152]{1,0:T(8,128)} %get-tuple-element.155) | copy-start | bytes 8847364
  547.5 70.7 %all-to-all-start.1 = ((bf16[4,72,3072]{2,1,0:T(8,128)(2,1)}), bf16[4,72,3072]{2,1,0:T(8,128)(2,1)}, u32[]{:S(2)}, u32[]{:S(2)}) async-start(bf16[4,72,3072]{2,1,0:T(8,128)(2,1)} %add_convert_fusion), calls=%async_computation.1 | async-start | bytes 3538944 | tf_op jit(solution)/shard_map/all_to_all | solution.py:89
  553.6 9.2 %copy-start.39 = (f32[640,16]{0,1:T(8,128)}, f32[640,16]{0,1:T(8,128)S(1)}, u32[]{:S(2)}) copy-start(f32[640,16]{0,1:T(8,128)S(1)} %copy.161) | copy-start | bytes 122884
  554.7 8.1 %copy-start.41 = (f32[640,16]{0,1:T(8,128)}, f32[640,16]{0,1:T(8,128)S(1)}, u32[]{:S(2)}) copy-start(f32[640,16]{0,1:T(8,128)S(1)} %copy.162) | copy-start | bytes 122884
  555.4 13.1 %collective-permute-start.13 = (f32[640,104]{0,1:T(8,128)S(1)}, f32[640,104]{0,1:T(8,128)S(1)}, u32[]{:S(2)}, u32[]{:S(2)}) collective-permute-start(f32[640,104]{0,1:T(8,128)S(1)} %pad_maximum_fusion.5), channel_id=1, source_target_pairs={{0,1},{1,0},{2,3},{3,2},{4,5},{5,4},{6,7},{7,6},{8,9},{9,8},{10,11... | collective-permute-start | bytes 798728 | tf_op jit(solution)/shard_map/ppermute | solution.py:37
  556.3 12.3 %copy-start.101 = (f32[640,1152]{1,0:T(8,128)S(1)}, f32[640,1152]{1,0:T(8,128)}, u32[]{:S(2)}) copy-start(f32[640,1152]{1,0:T(8,128)} %get-tuple-element.94) | copy-start | bytes 8847364
  579.5 3.1 collective-permute-start.14
  588.1 19.1 %collective-permute-start.15 = (bf16[320,1152]{1,0:T(8,128)(2,1)S(1)}, bf16[320,1152]{1,0:T(8,128)(2,1)S(1)}, u32[]{:S(2)}, u32[]{:S(2)}) collective-permute-start(bf16[320,1152]{1,0:T(8,128)(2,1)S(1)} %fusion.12), channel_id=1, source_target_pairs={{0,1},{1,0},{2,3},{3,2},{4,5},{5,4},{6,7},{7,6},{8,9},{9,8},{10,11... | collective-permute-start | bytes 2211848 | tf_op jit(solution)/shard_map/ppermute | solution.py:37
  590.7 16.5 %copy-start.66 = (f32[1152]{0:T(1024)S(1)}, f32[1152]{0:T(1024)}, u32[]{:S(2)}) copy-start(f32[1152]{0:T(1024)} %param.21) | copy-start | bytes 13828
  590.7 16.5 %copy-start.73 = (f32[320]{0:T(512)S(1)}, f32[320]{0:T(512)}, u32[]{:S(2)}) copy-start(f32[320]{0:T(512)} %copy-done.72) | copy-start | bytes 3844
  594.7 16.9 %copy-start.85 = (f32[320]{0:T(512)S(1)}, f32[320]{0:T(512)}, u32[]{:S(2)}) copy-start(f32[320]{0:T(512)} %copy-done.84) | copy-start | bytes 3844
  594.7 17.0 %copy-start.4 = (f32[320,1152]{1,0:T(8,128)S(1)}, f32[320,1152]{1,0:T(8,128)}, u32[]{:S(2)}) copy-start(f32[320,1152]{1,0:T(8,128)} %copy-done.2) | copy-start | bytes 4423684
  594.7 17.0 %copy-start.6 = (f32[320,1152]{1,0:T(8,128)S(1)}, f32[320,1152]{1,0:T(8,128)}, u32[]{:S(2)}) copy-start(f32[320,1152]{1,0:T(8,128)} %copy-done.5) | copy-start | bytes 4423684
  594.7 17.0 %copy-start.14 = (bf16[320,1152]{1,0:T(8,128)(2,1)S(1)}, bf16[320,1152]{1,0:T(8,128)(2,1)}, u32[]{:S(2)}) copy-start(bf16[320,1152]{1,0:T(8,128)(2,1)} %param.35) | copy-start | bytes 2211844
  594.7 17.0 %copy-start.15 = (f32[320,1152]{1,0:T(8,128)S(1)}, f32[320,1152]{1,0:T(8,128)}, u32[]{:S(2)}) copy-start(f32[320,1152]{1,0:T(8,128)} %get-tuple-element.159) | copy-start | bytes 4423684
  594.7 17.0 %copy-start.56 = (f32[320]{0:T(512)S(1)}, f32[320]{0:T(512)}, u32[]{:S(2)}) copy-start(f32[320]{0:T(512)} %copy-done.55) | copy-start | bytes 3844
  594.7 17.0 %copy-start.80 = (f32[320]{0:T(512)S(1)}, f32[320]{0:T(512)}, u32[]{:S(2)}) copy-start(f32[320]{0:T(512)} %copy-done.79) | copy-start | bytes 3844
  594.7 17.0 %copy-start.82 = (f32[320]{0:T(512)S(1)}, f32[320]{0:T(512)}, u32[]{:S(2)}) copy-start(f32[320]{0:T(512)} %copy-done.81) | copy-start | bytes 3844
  610.4 6.1 collective-permute-start.16
  686.3 8.5 %copy-start.1 = (bf16[1152,1152]{1,0:T(8,128)(2,1)S(1)}, bf16[1152,1152]{1,0:T(8,128)(2,1)}, u32[]{:S(2)}) copy-start(bf16[1152,1152]{1,0:T(8,128)(2,1)} %param.30) | copy-start | bytes 7962628
  (64 other events, 222.6 us)
Sparse Core Ops, SparseCore 0:
  128.7 49.4 all-gather.2
  179.7 55.0 all-gather.4

commit v6 on v5

--- a/solution.py
+++ b/solution.py
@@ -1401,7 +1401,7 @@
     bounds = [sum(part.shape[0] for part in pieces[: k + 1]) for k in range(len(pieces) - 1)]
     inner_weight_grad, small = summed([after(inner_weight_grad.astype(bf16), down_grad), jnp.concatenate(pieces, 0)])
     out_weight_grad = early[:model_width].reshape(channels, model_width).astype(f32)
-    gate_weight_grad = early[model_width : 2 * model_width].astype(f32)
+    gate_weight_grad = early[model_width : 2 * model_width]
     (
         xproj_rows, dt_weight_grad, a_log_rows, conv_weight_grad, conv_bias_grad, dt_bias_grad, skip_grad,
         norm_rows, gains,
@@ -1410,7 +1410,7 @@
     xproj_grad, a_log_grad = xproj_rows.T, a_log_rows.T
     conv_bias_grad, dt_bias_grad, skip_grad = conv_bias_grad[0], dt_bias_grad[0], skip_grad[0]
     moe_gain_grad, router_grad = gains[0], gains[1:].T
-    in_weight_grad = jnp.stack([inner_weight_grad, gate_weight_grad])
+    in_weight_grad = jnp.stack([inner_weight_grad.astype(bf16), gate_weight_grad]).astype(f32)
     return (
         block_out,
         in_grad,

time: 707 us -> 707 us (level)
  no operation moved by 1% of the time
where the time goes in v6:
time: 707 us; the launch traced here: 702 us
  Pallas kernels  414 us (59%)
  matrix products  72 us (10%)
  waiting for transfers between devices  58.8 us (8%)
  other arithmetic  56.6 us (8%)
  local copies, waits for them, and re-layouts  47 us (7%)
  starting transfers between devices  37.2 us (5%)
  between operations  16 us (2%)
    pallas_call x1, Pallas kernels, grads(): pl.pallas_call(partial(grads_kernel, self.halves, count, self.groups), gr...  87.5 us
    pallas_call x1, Pallas kernels, summed(): pl.pallas_call(partial(sum_kernel, count, places, [part.shape[0] for part...  60.8 us
    ppermute x16, waiting for transfers between devices, swapped(): lax.ppermute(value, axis, [(source, source ^ bit) for source in range(cou...  57.6 us
    pallas_call x1, Pallas kernels, exchange(): pl.pallas_call(partial(exchange_kernel, own, share, chans, count), in_spe...  54.7 us
    pallas_call x2, Pallas kernels, ends(): pl.pallas_call(kernel, grid=(self.groups,), in_specs=[self.row_spec, self...  51.1 us
    pallas_call x1, Pallas kernels, expert_passes(): pl.pallas_call(partial(expert_kernel, share), grid=(tiles + 1,), in_specs...  41.4 us
    pallas_call x1, Pallas kernels, rows_and_gather(): pl.pallas_call(partial(rows_and_gather_kernel, expert_groups() + (chans,)...  40.4 us
    pallas_call x2, Pallas kernels, carried(): pl.pallas_call(partial(carry_kernel, count, reverse), in_specs=[vmem, vme...  29.8 us
  transfers between devices with their start and end apart: 22, of which 7 were waited for; matrix products, arithmetic and copies ran while one was open for 19% of the time, Pallas kernels for 30%

profile of v6, /device:TPU:0, one launch (start us, length us, event | category | flops | bytes accessed | tf_op | source)
XLA Modules:
  0.0 701.8 jit_solution(9824359104548809864)
XLA Ops:
  7.3 3.1 copy.221
  13.7 2.6 multiply_convert_fusion.1
  16.3 2.9 collective-permute-start
  19.3 2.4 constant_dynamic-slice_fusion.3
  21.6 3.6 collective-permute-start.6
  29.1 6.8 collective-permute-done
  36.0 1.8 broadcast_select_fusion.3
  37.9 6.2 fusion
  47.9 2.1 copy.142
  52.0 2.4 fusion.92
  55.1 1.8 collective-permute-start.2
  56.9 2.0 convolution_convert_fusion.5
  58.9 5.3 collective-permute-done.2
  65.3 5.5 compare_select_fusion
  71.7 37.1 %scan_ends.1 = (f32[2,16,8,1152]{3,2,1,0:T(8,128)}, f32[2,8,1152]{2,1,0:T(8,128)}, f32[24,1152]{1,0:T(8,128)}, bf16[8,64,1152]{2,1,0:T(8,128)(2,1)}, f32[8,8,128]{2,1,0:T(8,128)}) custom-call(f32[640,1152]{1,0:T(8,128)} %get-tuple-element.154.refs_0_.step_ref, f32[640,1152]{1,0:T(8,128)} %get-tuple-element.125.refs_1_.mixed_ref, ...), custom_call_target="tpu_custom_call" | custom-call | flops 58982400 | bytes 8847360 | tf_op jit(solution)/shard_map/scan_ends/pallas_call | solution.py:863
  108.8 14.1 %carry.1.device = f32[16,1152]{1,0:T(8,128)} custom-call(f32[24,1152]{1,0:T(8,128)} %get-tuple-element.61.total_ref, f32[16,1152]{1,0:T(8,128)} %multiply_bitcast_fusion.refs_4_.rate_ref), custom_call_target="tpu_custom_call" | custom-call | bytes 50400000 | tf_op jit(solution)/shard_map/carry/pallas_call | solution.py:359
  123.0 1.8 bitcast_dynamic-update-slice_fusion.5
  124.8 1.9 bitcast_dynamic-update-slice_fusion.4
  126.7 1.8 bitcast_dynamic-update-slice_fusion.3
  130.6 1.6 collective-permute-start.9
  132.3 2.8 collective-permute-start.7
  135.1 6.0 fusion.15.gate_ref
  141.1 20.4 %scan_outputs.1 = (f32[640,1152]{1,0:T(8,128)}, bf16[640,1152]{1,0:T(8,128)(2,1)}, f32[2,16,8,1152]{3,2,1,0:T(8,128)}) custom-call(f32[640,1152]{1,0:T(8,128)} %get-tuple-element.154.refs_0_.step_ref, f32[640,1152]{1,0:T(8,128)} %get-tuple-element.125.refs_1_.mixed_ref, f32[640,128]{1,0:T(8,128)} %broadcast_in_dim.81.refs_2_.break_ref, ...), custom_call_target="tpu_custom_call" | custom-call | flops 82575360 | bytes 8847360 | tf_op jit(solution)/shard_map/scan_outputs/pallas_call | solution.py:878
  161.5 7.3 %collective-permute-done.8 = bf16[1,72,3072]{2,1,0:T(8,128)(2,1)S(1)} collective-permute-done((bf16[1,72,3072]{2,1,0:T(8,128)(2,1)S(1)}, bf16[1,72,3072]{2,1,0:T(8,128)(2,1)S(1)}, u32[]{:S(2)}, u32[]{:S(2)}) %collective-permute-start.8) | collective-permute-done | bytes 442400 | tf_op jit(solution)/shard_map/ppermute | solution.py:37
  171.2 3.2 convolution_convert_fusion.6
  178.6 12.3 %collective-permute-done.3 = bf16[320,1152]{1,0:T(8,128)(2,1)} collective-permute-done((bf16[320,1152]{1,0:T(8,128)(2,1)}, bf16[320,1152]{1,0:T(8,128)(2,1)}, u32[]{:S(2)}, u32[]{:S(2)}) %collective-permute-start.3) | collective-permute-done | bytes 737312 | tf_op jit(solution)/shard_map/ppermute | solution.py:37
  190.8 3.3 multiply_reduce_fusion.8
  194.2 2.1 fusion.38.own_ref
  196.3 2.0 convolution_convert_fusion.4
  198.3 40.4 %rows_and_gather.1 = (bf16[8,64,1152]{2,1,0:T(8,128)(2,1)}, f32[32,8,320]{2,1,0:T(8,128)}) custom-call(bf16[8,64,1152]{2,1,0:T(8,128)(2,1)} %bitcast.204, f32[8,320]{1,0:T(8,128)} %fusion.38.own_ref), custom_call_target="tpu_custom_call" | custom-call | bytes 122400000 | tf_op jit(solution)/shard_map/rows_and_gather/pallas_call | solution.py:273
  238.8 4.8 sinkhorn.1
  247.7 41.4 %expert_passes.1 = (bf16[512,1152]{1,0:T(8,128)(2,1)}, bf16[512,1152]{1,0:T(8,128)(2,1)}, bf16[4,72,3072]{2,1,0:T(8,128)(2,1)}, bf16[4,72,3072]{2,1,0:T(8,128)(2...) custom-call(bf16[512,1152]{1,0:T(8,128)(2,1)} %bitcast.224, bf16[512,1152]{1,0:T(8,128)(2,1)} %bitcast.226, ...), custom_call_target="tpu_custom_call" | custom-call | flops 21743271936 | bytes 28311552 | tf_op jit(solution)/shard_map/expert_passes/pallas_call | solution.py:1116
  293.4 54.7 %expert_rows.1 = (bf16[8,64,1152]{2,1,0:T(8,128)(2,1)}, bf16[8,64,1152]{2,1,0:T(8,128)(2,1)}) custom-call(bf16[8,64,1152]{2,1,0:T(8,128)(2,1)} %bitcast.208, bf16[8,64,1152]{2,1,0:T(8,128)(2,1)} %bitcast.209), custom_call_target="tpu_custom_call" | custom-call | bytes 187200000 | tf_op jit(solution)/shard_map/expert_rows/pallas_call | solution.py:194
  348.2 3.1 fusion.29
  351.9 3.4 fusion.28.refs_0_
  355.3 18.1 %gather_small.1 = (f32[32,8,320]{2,1,0:T(8,128)}, bf16[4,1,72,3072]{3,2,1,0:T(8,128)(2,1)}) custom-call(f32[8,320]{1,0:T(8,128)} %fusion.75.own_ref, bf16[4,1,72,3072]{3,2,1,0:T(8,128)(2,1)} %fusion.28.refs_0_), custom_call_target="tpu_custom_call", output_to_operand_aliasing={{1}: (1, {})} | custom-call | bytes 43200000 | tf_op jit(solution)/shard_map/gather_small/pallas_call | solution.py:295
  373.4 6.5 all-to-all-start
  379.9 5.4 sinkhorn_back.1
  385.3 2.1 fusion.96
  387.5 2.1 multiply_reduce_fusion.5
  393.2 3.5 add_convert_fusion
  397.4 13.5 %collective-permute-done.11 = bf16[320,1152]{1,0:T(8,128)(2,1)S(1)} collective-permute-done((bf16[320,1152]{1,0:T(8,128)(2,1)S(1)}, bf16[320,1152]{1,0:T(8,128)(2,1)S(1)}, u32[]{:S(2)}, u32[]{:S(2)}) %collective-permute-start.11) | collective-permute-done | bytes 737312 | tf_op jit(solution)/shard_map/ppermute | solution.py:37
  411.0 4.4 multiply_reduce_fusion
  416.1 14.0 %scan_ends_back.1 = (f32[2,16,8,1152]{3,2,1,0:T(8,128)}, f32[2,8,1152]{2,1,0:T(8,128)}, f32[24,1152]{1,0:T(8,128)}) custom-call(f32[640,1152]{1,0:T(8,128)} %get-tuple-element.154.refs_0_.step_ref, f32[640,1152]{1,0:T(8,128)} %get-tuple-element.121.drive_ref.grad_ref, f32[640,128]{1,0:T(8,128)} %broadcast_in_dim.81.refs_2_.break_ref, ...), custom_call_target="tpu_custom_call" | custom-call | flops 58982400 | bytes 8847360 | tf_op jit(solution)/shard_map/scan_ends_back/pallas_call | solution.py:863
  430.1 4.0 convolution_convert_fusion.2.first_early
  434.1 4.0 convolution_convert_fusion.1.second_early
  438.0 15.6 %carry_back.1.device = f32[16,1152]{1,0:T(8,128)} custom-call(f32[24,1152]{1,0:T(8,128)} %get-tuple-element.89.total_ref, f32[16,1152]{1,0:T(8,128)} %multiply_bitcast_fusion.refs_4_.rate_ref, bf16[4,72,3072]{2,1,0:T(8,128)(2,1)} %all-to-all-done.refs_0_, bf16[4,1,72,3072]{3,2,1,0:T(8,128)(2,1)} %bitcast.193), custom_call_target="tpu_custom_call" | custom-call | bytes 50400000 | tf_op jit(solution)/shard_map/carry_back/pallas_call | solution.py:359
  453.7 87.5 %scan_grads.1 = (f32[640,1152]{1,0:T(8,128)}, f32[640,1152]{1,0:T(8,128)}, f32[640,16]{1,0:T(8,128)}, f32[640,16]{1,0:T(8,128)}, f32[16,1152]{1,0:T(8,128)}, /*index=5*/bf16[9,256,1152]{2,1,0:T(8,128)(2,1)}) custom-call(f32[640,1152]{1,0:T(8,128)} %get-tuple-element.154.refs_0_.step_ref, f32[640,1152]{1,0:T(8,128)} %get-tuple-element.125.refs_1_.mixed_ref, ...), custom_call_target="tpu_custom_call" | custom-call | flops 235929600 | bytes 8847360 | tf_op jit(solution)/shard_map/scan_grads/pallas_call | solution.py:907
  541.2 2.7 fusion.90
  544.5 3.0 fusion.97
  547.5 4.9 all-to-all-start.1
  556.3 6.5 slice_convert_fusion
  562.8 3.8 convert_element_type.229
  566.7 1.8 fusion.71
  568.7 3.8 fusion.89
  572.6 6.0 multiply_reduce_fusion.2
  590.7 3.9 convolution_convert_fusion.refs_0_
  594.7 12.5 %collective-permute-done.15 = bf16[320,1152]{1,0:T(8,128)(2,1)S(1)} collective-permute-done((bf16[320,1152]{1,0:T(8,128)(2,1)S(1)}, bf16[320,1152]{1,0:T(8,128)(2,1)S(1)}, u32[]{:S(2)}, u32[]{:S(2)}) %collective-permute-start.15) | collective-permute-done | bytes 737312 | tf_op jit(solution)/shard_map/ppermute | solution.py:37
  607.2 3.1 multiply_reduce_fusion.6
  611.7 2.4 fusion.31
  618.2 60.8 %sum_late.1 = bf16[6,256,1152]{2,1,0:T(8,128)(2,1)} custom-call(bf16[1152,1152]{1,0:T(8,128)(2,1)} %convolution_convert_fusion.refs_0_, f32[224,1152]{1,0:T(8,128)} %pad.34.refs_1_), custom_call_target="tpu_custom_call" | custom-call | bytes 216000000 | tf_op jit(solution)/shard_map/sum_late/pallas_call | solution.py:494
  680.1 2.1 slice_bitcast_fusion.1
  686.3 4.8 maximum_convert_fusion
  691.1 3.7 convert_element_type.230
  (365 shorter events, 65.2 us)
Async XLA Ops:
  7.2 164.0 %copy-start = (bf16[1152,1152]{1,0:T(8,128)(2,1)S(1)}, bf16[1152,1152]{1,0:T(8,128)(2,1)}, u32[]{:S(2)}) copy-start(bf16[1152,1152]{1,0:T(8,128)(2,1)} %param.30) | copy-start | bytes 7962628
  7.2 240.5 %all-gather.3.cloned.1.call-start = ((), (), s32[]{:S(2)}) async-start(), calls=%async_computation.2 | async-start | bytes 8847360 | tf_op jit(solution)/shard_map/all_gather | solution.py:105
  12.4 9.2 %copy-start.84 = (f32[320]{0:T(512)}, f32[320]{0:T(512)S(1)}, u32[]{:S(2)}) copy-start(f32[320]{0:T(512)S(1)} %add.282) | copy-start | bytes 3844
  12.4 23.5 %copy-start.72 = (f32[320]{0:T(512)}, f32[320]{0:T(512)S(1)}, u32[]{:S(2)}) copy-start(f32[320]{0:T(512)S(1)} %rsqrt.20) | copy-start | bytes 3844
  13.7 12.4 %copy-start.96 = (s32[320,1]{0,1:T(1,128)S(1)}, s32[320,1]{0,1:T(1,128)}, u32[]{:S(2)}) copy-start(s32[320,1]{0,1:T(1,128)} %param.19) | copy-start | bytes 3844
  13.7 12.7 %copy-start.98 = (s32[4]{0:T(128)S(1)}, s32[4]{0:T(128)}, u32[]{:S(2)}) copy-start(s32[4]{0:T(128)} %param.20) | copy-start | bytes 52
  13.7 14.8 %copy-start.48 = (f32[1152,16]{0,1:T(8,128)S(1)}, f32[1152,16]{0,1:T(8,128)}, u32[]{:S(2)}) copy-start(f32[1152,16]{0,1:T(8,128)} %param.28) | copy-start | bytes 221188
  16.3 19.6 %collective-permute-start = (bf16[320,1152]{1,0:T(8,128)(2,1)}, bf16[320,1152]{1,0:T(8,128)(2,1)S(1)}, u32[]{:S(2)}, u32[]{:S(2)}) collective-permute-start(bf16[320,1152]{1,0:T(8,128)(2,1)} %multiply_convert_fusion.1), channel_id=1, source_target_pairs={{0,1},{1,0},{2,3},{3,2},{4,5},{5,4},{6,7},{7,6},{8,9},{9,8},{10,11... | collective-permute-start | bytes 2211848 | tf_op jit(solution)/shard_map/ppermute | solution.py:37
  21.6 101.3 %collective-permute-start.6 = (bf16[1,72,3072]{2,1,0:T(8,128)(2,1)}, bf16[1,72,3072]{2,1,0:T(8,128)(2,1)}, u32[]{:S(2)}, u32[]{:S(2)}) collective-permute-start(bf16[1,72,3072]{2,1,0:T(8,128)(2,1)} %get-tuple-element.139), channel_id=1, source_target_pairs={{0,24},{2,26},{4,28},{6,30},{8,16},{10,18},{12,20},{14,22},{16,8},... | collective-permute-start | bytes 1327112 | tf_op jit(solution)/shard_map/ppermute | solution.py:37
  25.2 97.8 %collective-permute-start.4 = (bf16[1,72,3072]{2,1,0:T(8,128)(2,1)}, bf16[1,72,3072]{2,1,0:T(8,128)(2,1)}, u32[]{:S(2)}, u32[]{:S(2)}) collective-permute-start(bf16[1,72,3072]{2,1,0:T(8,128)(2,1)} %get-tuple-element.140), channel_id=1, source_target_pairs={{0,8},{2,10},{4,12},{6,14},{8,0},{10,2},{12,4},{14,6},{16,24},{18,... | collective-permute-start | bytes 1327112 | tf_op jit(solution)/shard_map/ppermute | solution.py:37
  25.2 97.7 %collective-permute-start.5 = (bf16[1,72,3072]{2,1,0:T(8,128)(2,1)}, bf16[1,72,3072]{2,1,0:T(8,128)(2,1)}, u32[]{:S(2)}, u32[]{:S(2)}) collective-permute-start(bf16[1,72,3072]{2,1,0:T(8,128)(2,1)} %get-tuple-element.141), channel_id=1, source_target_pairs={{0,16},{2,18},{4,20},{6,22},{8,24},{10,26},{12,28},{14,30},{16,0},... | collective-permute-start | bytes 1327112 | tf_op jit(solution)/shard_map/ppermute | solution.py:37
  28.5 18.7 %copy-start.68 = (f32[2,40,8]{1,2,0:T(8,128)}, f32[2,40,8]{1,2,0:T(8,128)S(1)}, u32[]{:S(2)}) copy-start(f32[2,40,8]{1,2,0:T(8,128)S(1)} %get-tuple-element.151) | copy-start | bytes 7684
  37.8 8.7 %copy-start.83 = (f32[4,1152]{1,0:T(4,128)S(1)}, f32[4,1152]{1,0:T(4,128)}, u32[]{:S(2)}) copy-start(f32[4,1152]{1,0:T(4,128)} %param.23) | copy-start | bytes 55300
  37.8 9.1 %copy-start.75 = (f32[2,40,8]{1,2,0:T(8,128)S(1)}, f32[2,40,8]{1,2,0:T(8,128)}, u32[]{:S(2)}) copy-start(f32[2,40,8]{1,2,0:T(8,128)} %get-tuple-element.152) | copy-start | bytes 7684
  37.8 9.2 %copy-start.74 = (f32[2,40,8]{1,2,0:T(8,128)S(1)}, f32[2,40,8]{1,2,0:T(8,128)}, u32[]{:S(2)}) copy-start(f32[2,40,8]{1,2,0:T(8,128)} %get-tuple-element.153) | copy-start | bytes 7684
  45.0 5.0 collective-permute-start.1
  54.5 10.8 %copy-start.7 = (bf16[640,1152]{1,0:T(8,128)(2,1)}, bf16[640,1152]{1,0:T(8,128)(2,1)S(1)}, u32[]{:S(2)}) copy-start(bf16[640,1152]{1,0:T(8,128)(2,1)S(1)} %get-tuple-element.126) | copy-start | bytes 4423684
  55.0 10.2 %copy-start.43 = (f32[72,1152]{1,0:T(8,128)S(1)}, f32[72,1152]{1,0:T(8,128)}, u32[]{:S(2)}) copy-start(f32[72,1152]{1,0:T(8,128)} %param.26) | copy-start | bytes 995332
  55.1 10.2 %copy-start.97 = (f32[1152]{0:T(1024)S(1)}, f32[1152]{0:T(1024)}, u32[]{:S(2)}) copy-start(f32[1152]{0:T(1024)} %param.27) | copy-start | bytes 13828
  55.1 9.1 %collective-permute-start.2 = (f32[640,104]{1,0:T(8,128)S(1)}, f32[640,104]{1,0:T(8,128)S(1)}, u32[]{:S(2)}, u32[]{:S(2)}) collective-permute-start(f32[640,104]{1,0:T(8,128)S(1)} %fusion.95), channel_id=1, source_target_pairs={{0,1},{1,0},{2,3},{3,2},{4,5},{5,4},{6,7},{7,6},{8,9},{9,8},{10,11... | collective-permute-start | bytes 798728 | tf_op jit(solution)/shard_map/ppermute | solution.py:37
  108.8 19.8 %copy-start.92 = (f32[1152]{0:T(1024)S(1)}, f32[1152]{0:T(1024)}, u32[]{:S(2)}) copy-start(f32[1152]{0:T(1024)} %param.29) | copy-start | bytes 13828
  128.6 119.2 %all-gather.5.cloned.1.call-start = ((), (), s32[]{:S(2)}) async-start(), calls=%async_computation.3 | async-start | bytes 8847360 | tf_op jit(solution)/shard_map/all_gather | solution.py:105
  130.6 30.9 %collective-permute-start.9 = (bf16[1,72,3072]{2,1,0:T(8,128)(2,1)S(1)}, bf16[1,72,3072]{2,1,0:T(8,128)(2,1)S(1)}, u32[]{:S(2)}, u32[]{:S(2)}) collective-permute-start(bf16[1,72,3072]{2,1,0:T(8,128)(2,1)S(1)} %get-tuple-element.136), channel_id=1, source_target_pairs={{0,24},{2,26},{4,28},{6,30},{8,16},{10,18},{12,20},{14,22},{16,8},... | collective-permute-start | bytes 1327112 | tf_op jit(solution)/shard_map/ppermute | solution.py:37
  132.2 36.6 %collective-permute-start.8 = (bf16[1,72,3072]{2,1,0:T(8,128)(2,1)S(1)}, bf16[1,72,3072]{2,1,0:T(8,128)(2,1)S(1)}, u32[]{:S(2)}, u32[]{:S(2)}) collective-permute-start(bf16[1,72,3072]{2,1,0:T(8,128)(2,1)S(1)} %get-tuple-element.137), channel_id=1, source_target_pairs={{0,16},{2,18},{4,20},{6,22},{8,24},{10,26},{12,28},{14,30},{16,0},... | collective-permute-start | bytes 1327112 | tf_op jit(solution)/shard_map/ppermute | solution.py:37
  132.3 36.5 %collective-permute-start.7 = (bf16[1,72,3072]{2,1,0:T(8,128)(2,1)S(1)}, bf16[1,72,3072]{2,1,0:T(8,128)(2,1)S(1)}, u32[]{:S(2)}, u32[]{:S(2)}) collective-permute-start(bf16[1,72,3072]{2,1,0:T(8,128)(2,1)S(1)} %get-tuple-element.138), channel_id=1, source_target_pairs={{0,8},{2,10},{4,12},{6,14},{8,0},{10,2},{12,4},{14,6},{16,24},{18,... | collective-permute-start | bytes 1327112 | tf_op jit(solution)/shard_map/ppermute | solution.py:37
  174.4 16.4 %collective-permute-start.3 = (bf16[320,1152]{1,0:T(8,128)(2,1)}, bf16[320,1152]{1,0:T(8,128)(2,1)}, u32[]{:S(2)}, u32[]{:S(2)}) collective-permute-start(bf16[320,1152]{1,0:T(8,128)(2,1)} %convolution_convert_fusion.6), channel_id=1, source_target_pairs={{0,1},{1,0},{2,3},{3,2},{4,5},{5,4},{6,7},{7,6},{8,9},{9,8},{10,11... | collective-permute-start | bytes 2211848 | tf_op jit(solution)/shard_map/ppermute | solution.py:37
  178.6 15.7 %copy-start.45 = (f32[1152]{0:T(1024)S(1)}, f32[1152]{0:T(1024)}, u32[]{:S(2)}) copy-start(f32[1152]{0:T(1024)} %param.31) | copy-start | bytes 13828
  178.6 15.7 %copy-start.52 = (f32[1152,8]{0,1:T(8,128)S(1)}, f32[1152,8]{0,1:T(8,128)}, u32[]{:S(2)}) copy-start(f32[1152,8]{0,1:T(8,128)} %param.32) | copy-start | bytes 110596
  194.2 44.6 %copy-start.90 = (f32[320]{0:T(512)}, f32[320]{0:T(512)S(1)}, u32[]{:S(2)}) copy-start(f32[320]{0:T(512)S(1)} %get-tuple-element.156) | copy-start | bytes 3844
  194.2 197.9 %copy-start.55 = (f32[320]{0:T(512)}, f32[320]{0:T(512)S(1)}, u32[]{:S(2)}) copy-start(f32[320]{0:T(512)S(1)} %fusion.85) | copy-start | bytes 3844
  247.7 42.8 %copy-start.69 = (f32[2,40,8]{1,2,0:T(8,128)S(1)}, f32[2,40,8]{1,2,0:T(8,128)}, u32[]{:S(2)}) copy-start(f32[2,40,8]{1,2,0:T(8,128)} %copy-done.68) | copy-start | bytes 7684
  289.1 62.8 %collective-permute-start.10 = (bf16[4,72,3072]{2,1,0:T(8,128)(2,1)}, bf16[4,72,3072]{2,1,0:T(8,128)(2,1)}, u32[]{:S(2)}, u32[]{:S(2)}) collective-permute-start(bf16[4,72,3072]{2,1,0:T(8,128)(2,1)} %get-tuple-element.84), channel_id=1, source_target_pairs={{0,4},{2,6},{4,0},{6,2},{8,12},{10,14},{12,8},{14,10},{16,20},{18,... | collective-permute-start | bytes 5308424 | tf_op jit(solution)/shard_map/ppermute | solution.py:37
  292.0 95.4 %copy-start.81 = (f32[320]{0:T(512)}, f32[320]{0:T(512)S(1)}, u32[]{:S(2)}) copy-start(f32[320]{0:T(512)S(1)} %reduce.11) | copy-start | bytes 3844
  292.0 101.2 %collective-permute-start.12 = (bf16[4,72,3072]{2,1,0:T(8,128)(2,1)}, bf16[4,72,3072]{2,1,0:T(8,128)(2,1)}, u32[]{:S(2)}, u32[]{:S(2)}) collective-permute-start(bf16[4,72,3072]{2,1,0:T(8,128)(2,1)} %get-tuple-element.92), channel_id=1, source_target_pairs={{0,4},{2,6},{4,0},{6,2},{8,12},{10,14},{12,8},{14,10},{16,20},{18,... | collective-permute-start | bytes 5308424 | tf_op jit(solution)/shard_map/ppermute | solution.py:37
  293.4 57.9 %copy-start.94 = (s32[320]{0:T(512)S(1)}, s32[320]{0:T(512)}, u32[]{:S(2)}) copy-start(s32[320]{0:T(512)} %eq.89) | copy-start | bytes 3844
  373.4 64.6 %all-to-all-start = ((bf16[4,72,3072]{2,1,0:T(8,128)(2,1)}), bf16[4,72,3072]{2,1,0:T(8,128)(2,1)}, u32[]{:S(2)}, u32[]{:S(2)}) async-start(bf16[4,72,3072]{2,1,0:T(8,128)(2,1)} %bitcast.194), calls=%async_computation | async-start | bytes 3538944 | tf_op jit(solution)/shard_map/all_to_all | solution.py:89
  379.9 7.5 %copy-start.3 = (f32[320,1152]{1,0:T(8,128)S(1)}, f32[320,1152]{1,0:T(8,128)}, u32[]{:S(2)}) copy-start(f32[320,1152]{1,0:T(8,128)} %copy-done.2) | copy-start | bytes 4423684
  390.6 6.1 collective-permute-start.17
  392.6 18.3 %collective-permute-start.11 = (bf16[320,1152]{1,0:T(8,128)(2,1)S(1)}, bf16[320,1152]{1,0:T(8,128)(2,1)S(1)}, u32[]{:S(2)}, u32[]{:S(2)}) collective-permute-start(bf16[320,1152]{1,0:T(8,128)(2,1)S(1)} %fusion.88), channel_id=1, source_target_pairs={{0,1},{1,0},{2,3},{3,2},{4,5},{5,4},{6,7},{7,6},{8,9},{9,8},{10,11... | collective-permute-start | bytes 2211848 | tf_op jit(solution)/shard_map/ppermute | solution.py:37
  393.2 17.8 %copy-start.102 = (f32[640,1152]{1,0:T(8,128)S(1)}, f32[640,1152]{1,0:T(8,128)}, u32[]{:S(2)}) copy-start(f32[640,1152]{1,0:T(8,128)} %fusion.15.gate_ref) | copy-start | bytes 8847364
  393.2 17.8 %copy-start.103 = (f32[640,1152]{1,0:T(8,128)S(1)}, f32[640,1152]{1,0:T(8,128)}, u32[]{:S(2)}) copy-start(f32[640,1152]{1,0:T(8,128)} %get-tuple-element.93) | copy-start | bytes 8847364
  396.7 14.3 %copy-start.8 = (bf16[640,1152]{1,0:T(8,128)(2,1)S(1)}, bf16[640,1152]{1,0:T(8,128)(2,1)}, u32[]{:S(2)}) copy-start(bf16[640,1152]{1,0:T(8,128)(2,1)} %copy-done.7) | copy-start | bytes 4423684
  415.4 18.6 %copy-start.25 = (bf16[640,1152]{1,0:T(8,128)(2,1)}, bf16[640,1152]{1,0:T(8,128)(2,1)S(1)}, u32[]{:S(2)}) copy-start(bf16[640,1152]{1,0:T(8,128)(2,1)S(1)} %get-tuple-element.127) | copy-start | bytes 4423684
  416.1 14.0 %copy-start.99 = (bf16[640,1152]{1,0:T(8,128)(2,1)S(1)}, bf16[640,1152]{1,0:T(8,128)(2,1)}, u32[]{:S(2)}) copy-start(bf16[640,1152]{1,0:T(8,128)(2,1)} %get-tuple-element.62) | copy-start | bytes 4423684
  453.7 87.5 %copy-start.18 = (f32[640,1152]{1,0:T(8,128)S(1)}, f32[640,1152]{1,0:T(8,128)}, u32[]{:S(2)}) copy-start(f32[640,1152]{1,0:T(8,128)} %get-tuple-element.155) | copy-start | bytes 8847364
  547.5 70.7 %all-to-all-start.1 = ((bf16[4,72,3072]{2,1,0:T(8,128)(2,1)}), bf16[4,72,3072]{2,1,0:T(8,128)(2,1)}, u32[]{:S(2)}, u32[]{:S(2)}) async-start(bf16[4,72,3072]{2,1,0:T(8,128)(2,1)} %add_convert_fusion), calls=%async_computation.1 | async-start | bytes 3538944 | tf_op jit(solution)/shard_map/all_to_all | solution.py:89
  553.6 9.2 %copy-start.39 = (f32[640,16]{0,1:T(8,128)}, f32[640,16]{0,1:T(8,128)S(1)}, u32[]{:S(2)}) copy-start(f32[640,16]{0,1:T(8,128)S(1)} %copy.161) | copy-start | bytes 122884
  554.7 8.1 %copy-start.41 = (f32[640,16]{0,1:T(8,128)}, f32[640,16]{0,1:T(8,128)S(1)}, u32[]{:S(2)}) copy-start(f32[640,16]{0,1:T(8,128)S(1)} %copy.162) | copy-start | bytes 122884
  555.4 13.1 %collective-permute-start.13 = (f32[640,104]{0,1:T(8,128)S(1)}, f32[640,104]{0,1:T(8,128)S(1)}, u32[]{:S(2)}, u32[]{:S(2)}) collective-permute-start(f32[640,104]{0,1:T(8,128)S(1)} %pad_maximum_fusion.5), channel_id=1, source_target_pairs={{0,1},{1,0},{2,3},{3,2},{4,5},{5,4},{6,7},{7,6},{8,9},{9,8},{10,11... | collective-permute-start | bytes 798728 | tf_op jit(solution)/shard_map/ppermute | solution.py:37
  556.3 12.3 %copy-start.101 = (f32[640,1152]{1,0:T(8,128)S(1)}, f32[640,1152]{1,0:T(8,128)}, u32[]{:S(2)}) copy-start(f32[640,1152]{1,0:T(8,128)} %get-tuple-element.94) | copy-start | bytes 8847364
  579.5 3.1 collective-permute-start.14
  588.1 19.1 %collective-permute-start.15 = (bf16[320,1152]{1,0:T(8,128)(2,1)S(1)}, bf16[320,1152]{1,0:T(8,128)(2,1)S(1)}, u32[]{:S(2)}, u32[]{:S(2)}) collective-permute-start(bf16[320,1152]{1,0:T(8,128)(2,1)S(1)} %fusion.12), channel_id=1, source_target_pairs={{0,1},{1,0},{2,3},{3,2},{4,5},{5,4},{6,7},{7,6},{8,9},{9,8},{10,11... | collective-permute-start | bytes 2211848 | tf_op jit(solution)/shard_map/ppermute | solution.py:37
  590.7 16.5 %copy-start.66 = (f32[1152]{0:T(1024)S(1)}, f32[1152]{0:T(1024)}, u32[]{:S(2)}) copy-start(f32[1152]{0:T(1024)} %param.21) | copy-start | bytes 13828
  590.7 16.5 %copy-start.73 = (f32[320]{0:T(512)S(1)}, f32[320]{0:T(512)}, u32[]{:S(2)}) copy-start(f32[320]{0:T(512)} %copy-done.72) | copy-start | bytes 3844
  594.7 16.9 %copy-start.85 = (f32[320]{0:T(512)S(1)}, f32[320]{0:T(512)}, u32[]{:S(2)}) copy-start(f32[320]{0:T(512)} %copy-done.84) | copy-start | bytes 3844
  594.7 17.0 %copy-start.4 = (f32[320,1152]{1,0:T(8,128)S(1)}, f32[320,1152]{1,0:T(8,128)}, u32[]{:S(2)}) copy-start(f32[320,1152]{1,0:T(8,128)} %copy-done.2) | copy-start | bytes 4423684
  594.7 17.0 %copy-start.6 = (f32[320,1152]{1,0:T(8,128)S(1)}, f32[320,1152]{1,0:T(8,128)}, u32[]{:S(2)}) copy-start(f32[320,1152]{1,0:T(8,128)} %copy-done.5) | copy-start | bytes 4423684
  594.7 17.0 %copy-start.14 = (bf16[320,1152]{1,0:T(8,128)(2,1)S(1)}, bf16[320,1152]{1,0:T(8,128)(2,1)}, u32[]{:S(2)}) copy-start(bf16[320,1152]{1,0:T(8,128)(2,1)} %param.35) | copy-start | bytes 2211844
  594.7 17.0 %copy-start.15 = (f32[320,1152]{1,0:T(8,128)S(1)}, f32[320,1152]{1,0:T(8,128)}, u32[]{:S(2)}) copy-start(f32[320,1152]{1,0:T(8,128)} %get-tuple-element.159) | copy-start | bytes 4423684
  594.7 17.0 %copy-start.56 = (f32[320]{0:T(512)S(1)}, f32[320]{0:T(512)}, u32[]{:S(2)}) copy-start(f32[320]{0:T(512)} %copy-done.55) | copy-start | bytes 3844
  594.7 17.0 %copy-start.80 = (f32[320]{0:T(512)S(1)}, f32[320]{0:T(512)}, u32[]{:S(2)}) copy-start(f32[320]{0:T(512)} %copy-done.79) | copy-start | bytes 3844
  594.7 17.0 %copy-start.82 = (f32[320]{0:T(512)S(1)}, f32[320]{0:T(512)}, u32[]{:S(2)}) copy-start(f32[320]{0:T(512)} %copy-done.81) | copy-start | bytes 3844
  610.4 6.1 collective-permute-start.16
  686.3 8.5 %copy-start.1 = (bf16[1152,1152]{1,0:T(8,128)(2,1)S(1)}, bf16[1152,1152]{1,0:T(8,128)(2,1)}, u32[]{:S(2)}) copy-start(bf16[1152,1152]{1,0:T(8,128)(2,1)} %param.30) | copy-start | bytes 7962628
  (64 other events, 222.6 us)
Sparse Core Ops, SparseCore 0:
  128.7 49.4 all-gather.2
  179.7 55.0 all-gather.4
